TPU v7x, 32 devices: a whole 2x2x4 slice. The times are simulated.
32 devices in a mesh: groups: 2 (over y), gx: 16 (over z, x, core).
Axes of the slice: x: 2, y: 2, z: 4, core: 2. Of those that a mesh axis runs over, the one named last changes fastest.
Arguments:
- iterate: float32 [128, 64, 128], P(('groups', 'gx')), parts along dimension 0, may hold values from -6 to 6
- source: float32 [128, 64, 128], P(('groups', 'gx')), parts along dimension 0, may hold values from -24 to 24
- phase_field: float32 [128, 64, 128], P(('groups', 'gx')), parts along dimension 0, may hold values from 0 to 1
- block_owner: int32 [32], P('groups'), parts along dimension 0, may hold values from 0 to 15, each once
Outputs:
- solved: float32 [128, 64, 128], P(('groups', 'gx')), parts along dimension 0
- owned_correction: float32 [32, 16, 32], P(('groups', 'gx')), parts along dimension 0
There are 2 independent parts, one for each index of `groups`. A program takes and returns all parts, laid end to end along the dimension named above; each array names one. Nothing has to cross between parts.
Inputs may be any that keep to these rules, and one draw needn't show every extreme that they name: `block_owner`: each block index appears exactly once.
All inputs are finite; a program needn't handle non-finite values.
Results may differ from a plain program's by a relative error of at most 0.00002.
Values sent between devices are 32-bit elements; how exact they have to be, the bound alone decides.
No kernel may reach another device: no remote copies, remote signals or barrier semaphores. Data moves between devices by JAX's collectives and lax.ppermute only.
A program may use at most 64 MiB of HBM per device.

v0:
```python
import jax
import jax.numpy as jnp
from jax import lax
from jax.sharding import PartitionSpec as P

LEVELS = 6
SWEEPS = 1
COARSE_SWEEPS = 4


stiffness = 100.0
epsilon = 0.01


def with_halo(cells, sides, width):
    for axis, dim in sides:
        count = lax.axis_size(axis)
        ends = count - 1
        head = lax.slice_in_dim(cells, 0, width, axis=dim)
        tail = lax.slice_in_dim(cells, cells.shape[dim] - width, cells.shape[dim], axis=dim)
        cells = jnp.concatenate(
            [
                lax.ppermute(tail, axis, [(i, (i + 1) % count) for i in range(ends)]),
                cells,
                lax.ppermute(head, axis, [((i + 1) % count, i) for i in range(ends)]),
            ],
            axis=dim,
        )
    return cells


def from_behind(block, axis, distance):
    devices = range(lax.axis_size(axis))
    route = [(i - distance, i) for i in devices if i - distance in devices]
    return lax.ppermute(block, axis, route)


def next_along(values, along):
    widths = [(0, 0)] * values.ndim
    widths[along] = (0, 1)
    return lax.slice_in_dim(jnp.pad(values, widths), 1, values.shape[along] + 1, axis=along)


def prev_along(values, along):
    widths = [(0, 0)] * values.ndim
    widths[along] = (1, 0)
    return lax.slice_in_dim(jnp.pad(values, widths), 0, values.shape[along], axis=along)


def pad_layers(values):
    widths = [(1, 1)] + [(0, 0)] * (values.ndim - 1)
    return jnp.pad(values, widths)


def neighbours(padded, faces_x, faces_y, faces_z):
    middle = padded[1:-1]
    low_y = prev_along(faces_y, 1)
    low_z = prev_along(faces_z, 2)
    summed = faces_x[1:] * padded[2:] + faces_x[:-1] * padded[:-2]
    summed = summed + faces_y * next_along(middle, 1) + low_y * prev_along(middle, 1)
    summed = summed + faces_z * next_along(middle, 2) + low_z * prev_along(middle, 2)
    weight = faces_x[1:] + faces_x[:-1] + faces_y + low_y + faces_z + low_z
    return (middle, summed, weight)


def relax_colour(padded, source_p, coeffs_p, mask_p, mass_term):
    middle, summed, weight = neighbours(
        padded, coeffs_p[:-1, 0], coeffs_p[1:-1, 1], coeffs_p[1:-1, 2]
    )
    return jnp.where(mask_p[1:-1], (source_p[1:-1] + summed) / (mass_term + weight), middle)


def apply_operator(padded, coeffs_p, mass_term):
    middle, summed, weight = neighbours(
        padded, coeffs_p[:-1, 0], coeffs_p[1:-1, 1], coeffs_p[1:-1, 2]
    )
    return (mass_term + weight) * middle - summed


def colours(first_layer, layers, height, depth_cells):
    parity = (
        (first_layer + jnp.arange(layers))[:, None, None]
        + jnp.arange(height)[None, :, None]
        + jnp.arange(depth_cells)[None, None, :]
    )
    parity = parity % 2
    return (parity == 0, parity == 1)


def restrict(values):
    layers, height, depth_cells = values.shape
    return values.reshape(layers // 2, 2, height // 2, 2, depth_cells // 2, 2).sum(axis=(1, 3, 5))


def prolong(values):
    return jnp.repeat(jnp.repeat(jnp.repeat(values, 2, axis=0), 2, axis=1), 2, axis=2)


def coarsen(coeffs):
    layers, height, depth_cells = (coeffs.shape[0], coeffs.shape[2], coeffs.shape[3])
    faces_x = (
        coeffs[1::2, 0].reshape(layers // 2, height // 2, 2, depth_cells // 2, 2).sum(axis=(2, 4))
    )
    faces_y = (
        coeffs[:, 1, 1::2, :]
        .reshape(layers // 2, 2, height // 2, depth_cells // 2, 2)
        .sum(axis=(1, 4))
    )
    faces_z = (
        coeffs[:, 2, :, 1::2]
        .reshape(layers // 2, 2, height // 2, 2, depth_cells // 2)
        .sum(axis=(1, 3))
    )
    return jnp.stack([faces_x, faces_y, faces_z], 1)


def outer_layers(values, width):
    return with_halo(values, (("gx", 0),), width)


def slab_edges(values):
    edge_list = []
    for offset in (8, -8):
        edge_layer = values[-1:] if offset > 0 else values[:1]
        edge_list.append(from_behind(edge_layer, "gx", offset))
    return jnp.concatenate([edge_list[0], values, edge_list[1]], 0)


def coarse_level(level, field, source, coeffs):
    layers, height, depth_cells = field.shape
    first_layer = lax.axis_index("gx") // 8 * layers
    mass_term = 8.0 ** (level - 1)
    coeffs_one = slab_edges(coeffs)
    source_one = pad_layers(source)
    even_cells, odd_cells = colours(first_layer - 1, layers + 2, height, depth_cells)

    def smooth(current, turns):
        for sweep_turn in range(turns):
            current = relax_colour(
                slab_edges(current), source_one, coeffs_one, even_cells, mass_term
            )
            current = relax_colour(
                slab_edges(current), source_one, coeffs_one, odd_cells, mass_term
            )
        return current

    if level == LEVELS:
        return smooth(field, COARSE_SWEEPS)
    field = smooth(field, SWEEPS)
    residual = source - apply_operator(slab_edges(field), coeffs_one, mass_term)
    coarse_source = restrict(residual)
    coarse_fix = coarse_level(
        level + 1, jnp.zeros_like(coarse_source), coarse_source, coarsen(coeffs)
    )
    return smooth(field + prolong(coarse_fix), SWEEPS)


def coarse_solve(residual, coarse_coeffs):
    bundle = jnp.concatenate([residual[:, None], coarse_coeffs], 1)
    position = lax.axis_index("gx")
    for offset in (1, 2, 4):
        arrivals = []
        for distance in (offset, -offset):
            arrivals.append(from_behind(bundle, "gx", distance))
        upper = position // offset % 2 == 1
        bundle = jnp.where(
            upper,
            jnp.concatenate([arrivals[0], bundle], 0),
            jnp.concatenate([bundle, arrivals[1]], 0),
        )
    slab_source = bundle[:, 0]
    holding = coarse_level(3, jnp.zeros_like(slab_source), slab_source, bundle[:, 1:])
    block_rows = residual.shape[0]
    start_row = position % 8 * block_rows
    own_block = lax.dynamic_slice_in_dim(holding, start_row, block_rows, 0)
    return (own_block, own_block)


def fine_level(level, field, source, coeffs, deeper):
    layers, height, depth_cells = field.shape
    first_layer = lax.axis_index("gx") * layers
    mass_term = 8.0 ** (level - 1)
    coeffs_one = outer_layers(coeffs, 1)
    source_one = pad_layers(source)
    even_cells, odd_cells = colours(first_layer - 1, layers + 2, height, depth_cells)

    def smooth(current):
        current = relax_colour(
            outer_layers(current, 1), source_one, coeffs_one, even_cells, mass_term
        )
        current = relax_colour(
            outer_layers(current, 1), source_one, coeffs_one, odd_cells, mass_term
        )
        return current

    field = smooth(field)
    residual = source - apply_operator(outer_layers(field, 1), coeffs_one, mass_term)
    coarse_fix, third_fix = deeper(restrict(residual), coarsen(coeffs))
    field = smooth(field + prolong(coarse_fix))
    return (field, third_fix)


def middle_level(residual, coarse_coeffs):
    return fine_level(2, jnp.zeros_like(residual), residual, coarse_coeffs, coarse_solve)


def on_device(iterate, source, phase_field, block_owner):
    layers, height, depth_cells = iterate.shape
    position = lax.axis_index("gx")
    total_layers = layers * lax.axis_size("gx")
    cell_coef = stiffness * (phase_field * phase_field + epsilon)
    next_layer = outer_layers(cell_coef, 1)[2:]
    global_x = position * layers + jnp.arange(layers)
    keep_y = (jnp.arange(height) < height - 1)[None, :, None]
    keep_z = (jnp.arange(depth_cells) < depth_cells - 1)[None, None, :]
    faces_x = jnp.where(
        (global_x < total_layers - 1)[:, None, None], 0.5 * (cell_coef + next_layer), 0.0
    )
    faces_y = jnp.where(keep_y, 0.5 * (cell_coef + next_along(cell_coef, 1)), 0.0)
    faces_z = jnp.where(keep_z, 0.5 * (cell_coef + next_along(cell_coef, 2)), 0.0)
    coeffs = jnp.stack([faces_x, faces_y, faces_z], 1)
    solved, third_fix = fine_level(1, iterate, source, coeffs, middle_level)
    target = block_owner[position] * third_fix.shape[0]
    shard_rows = lax.all_gather(third_fix, "gx", axis=0, tiled=True)
    row_ids = jnp.arange(shard_rows.shape[0])
    chosen = row_ids[None, :] == (target + jnp.arange(jnp.zeros_like(third_fix).shape[0]))[:, None]
    owned = jnp.sum(jnp.where(chosen[:, :, None, None], shard_rows[None], 0.0), axis=1)
    return (solved, owned)


def solution(mesh):
    placed = (
        P(("groups", "gx"), None, None),
        P(("groups", "gx"), None, None),
        P(("groups", "gx"), None, None),
        P("groups"),
    )
    return jax.shard_map(
        on_device,
        mesh=mesh,
        in_specs=placed,
        out_specs=(P(("groups", "gx"), None, None), P(("groups", "gx"), None, None)),
        check_vma=False,
    )
```

profile of v0, /device:TPU:0, one launch (start us, length us, event | category | flops | bytes accessed | tf_op | source)
XLA Modules:
  0.0 343.8 jit_solution(11935072212124103848)
XLA Ops:
  8.8 6.4 %collective-permute-start.3 = (f32[1,64,128]{2,1,0:T(8,128)S(1)}, f32[1,64,128]{2,1,0:T(8,128)S(1)}, u32[]{:S(2)}, u32[]{:S(2)}) collective-permute-start(f32[1,64,128]{2,1,0:T(8,128)S(1)} %get-tuple-element.50), channel_id=1, source_target_pairs={{0,1},{1,2},{2,3},{3,4},{4,5},{5,6},{6,7},{7,8},{8,9},{9,10},{10,1... | collective-permute-start | bytes 98312 | tf_op jit(solution)/shard_map/ppermute | solution.py:23
  30.4 5.5 %reshape_squeeze.37 = f32[2,32,2,64,2]{4,3,2,1,0:T(8,128)} reshape(f32[2,1,64,128]{3,2,0,1:T(8,128)S(1)} %slice.1267) | data formatting | bytes 131072 | tf_op jit(solution)/shard_map/reshape;squeeze | solution.py:102
  40.3 4.9 %collective-permute-start.7 = (f32[1,64,128]{2,1,0:T(8,128)S(1)}, f32[1,64,128]{2,1,0:T(8,128)S(1)}, u32[]{:S(2)}, u32[]{:S(2)}) collective-permute-start(f32[1,64,128]{2,1,0:T(8,128)S(1)} %get-tuple-element.43), channel_id=1, source_target_pairs={{0,1},{1,2},{2,3},{3,4},{4,5},{5,6},{6,7},{7,8},{8,9},{9,10},{10,1... | collective-permute-start | bytes 98312 | tf_op jit(solution)/shard_map/ppermute | solution.py:23
  45.3 7.4 %collective-permute-start.23 = (f32[1,16,32]{2,1,0:T(8,128)S(1)}, f32[1,16,32]{2,1,0:T(8,128)S(1)}, u32[]{:S(2)}, u32[]{:S(2)}) collective-permute-start(f32[1,16,32]{2,1,0:T(8,128)S(1)} %broadcast.569), channel_id=1, source_target_pairs={{0,8},{1,9},{2,10},{3,11},{4,12},{5,13},{6,14},{7,15},{16,24},{17,... | collective-permute-start | bytes 6152 | tf_op jit(solution)/shard_map/ppermute | solution.py:35
  54.4 9.8 %reshape.316 = f32[2,2,32,2,64,2]{5,4,3,2,1,0:T(8,128)} reshape(f32[4,64,128]{2,1,0:T(8,128)S(1)} %fusion.31) | data formatting | bytes 262144 | tf_op jit(solution)/shard_map/reshape | solution.py:92
  76.9 4.9 %collective-permute-start.14 = (f32[1,32,64]{2,1,0:T(8,128)S(1)}, f32[1,32,64]{2,1,0:T(8,128)S(1)}, u32[]{:S(2)}, u32[]{:S(2)}) collective-permute-start(f32[1,32,64]{2,1,0:T(8,128)S(1)} %get-tuple-element.70), channel_id=1, source_target_pairs={{0,1},{1,2},{2,3},{3,4},{4,5},{5,6},{6,7},{7,8},{8,9},{9,10},{10,1... | collective-permute-start | bytes 24584 | tf_op jit(solution)/shard_map/ppermute | solution.py:23
  92.6 6.5 %collective-permute-start.17 = (f32[2,4,16,32]{3,2,1,0:T(8,128)S(1)}, f32[2,4,16,32]{3,2,1,0:T(8,128)S(1)}, u32[]{:S(2)}, u32[]{:S(2)}) collective-permute-start(f32[2,4,16,32]{3,2,1,0:T(8,128)S(1)} %maximum_select_fusion.2), channel_id=1, source_target_pairs={{0,2},{1,3},{2,4},{3,5},{4,6},{5,7},{6,8},{7,9},{8,10},{9,11},{10,... | collective-permute-start | bytes 49160 | tf_op jit(solution)/shard_map/ppermute | solution.py:35
  101.0 5.7 %collective-permute-done.18 = f32[2,4,16,32]{3,2,1,0:T(8,128)S(1)} collective-permute-done((f32[2,4,16,32]{3,2,1,0:T(8,128)S(1)}, f32[2,4,16,32]{3,2,1,0:T(8,128)S(1)}, u32[]{:S(2)}, u32[]{:S(2)}) %collective-permute-start.18) | collective-permute-done | bytes 16416 | tf_op jit(solution)/shard_map/ppermute | solution.py:35
  113.4 6.4 %collective-permute-start.30 = (f32[1,8,16]{2,1,0:T(8,128)S(1)}, f32[1,8,16]{2,1,0:T(8,128)S(1)}, u32[]{:S(2)}, u32[]{:S(2)}) collective-permute-start(f32[1,8,16]{2,1,0:T(8,128)S(1)} %broadcast.572), channel_id=1, source_target_pairs={{0,8},{1,9},{2,10},{3,11},{4,12},{5,13},{6,14},{7,15},{16,24},{17,... | collective-permute-start | bytes 1544 | tf_op jit(solution)/shard_map/ppermute | solution.py:35
  126.2 5.4 %collective-permute-start.25 = (f32[1,16,32]{2,1,0:T(8,128)S(1)}, f32[1,16,32]{2,1,0:T(8,128)S(1)}, u32[]{:S(2)}, u32[]{:S(2)}) collective-permute-start(f32[1,16,32]{2,1,0:T(8,128)S(1)} %get-tuple-element.64), channel_id=1, source_target_pairs={{0,8},{1,9},{2,10},{3,11},{4,12},{5,13},{6,14},{7,15},{16,24},{17,... | collective-permute-start | bytes 6152 | tf_op jit(solution)/shard_map/ppermute | solution.py:35
  135.2 5.6 %collective-permute-start.27 = (f32[1,16,32]{2,1,0:T(8,128)S(1)}, f32[1,16,32]{2,1,0:T(8,128)S(1)}, u32[]{:S(2)}, u32[]{:S(2)}) collective-permute-start(f32[1,16,32]{2,1,0:T(8,128)S(1)} %get-tuple-element.62), channel_id=1, source_target_pairs={{0,8},{1,9},{2,10},{3,11},{4,12},{5,13},{6,14},{7,15},{16,24},{17,... | collective-permute-start | bytes 6152 | tf_op jit(solution)/shard_map/ppermute | solution.py:35
  142.7 4.3 %collective-permute-start.29 = (f32[1,3,8,16]{3,2,0,1:T(8,128)S(1)}, f32[1,3,8,16]{3,2,0,1:T(8,128)S(1)}, u32[]{:S(2)}, u32[]{:S(2)}) collective-permute-start(f32[1,3,8,16]{3,2,0,1:T(8,128)S(1)} %pad_maximum_fusion.50), channel_id=1, source_target_pairs={{0,8},{1,9},{2,10},{3,11},{4,12},{5,13},{6,14},{7,15},{16,24},{17,... | collective-permute-start | bytes 4616 | tf_op jit(solution)/shard_map/ppermute | solution.py:35
  150.7 5.4 %collective-permute-start.32 = (f32[1,8,16]{2,1,0:T(8,128)S(1)}, f32[1,8,16]{2,1,0:T(8,128)S(1)}, u32[]{:S(2)}, u32[]{:S(2)}) collective-permute-start(f32[1,8,16]{2,1,0:T(8,128)S(1)} %get-tuple-element.80), channel_id=1, source_target_pairs={{0,8},{1,9},{2,10},{3,11},{4,12},{5,13},{6,14},{7,15},{16,24},{17,... | collective-permute-start | bytes 1544 | tf_op jit(solution)/shard_map/ppermute | solution.py:35
  158.8 5.4 %collective-permute-start.34 = (f32[1,8,16]{2,1,0:T(8,128)S(1)}, f32[1,8,16]{2,1,0:T(8,128)S(1)}, u32[]{:S(2)}, u32[]{:S(2)}) collective-permute-start(f32[1,8,16]{2,1,0:T(8,128)S(1)} %get-tuple-element.78), channel_id=1, source_target_pairs={{0,8},{1,9},{2,10},{3,11},{4,12},{5,13},{6,14},{7,15},{16,24},{17,... | collective-permute-start | bytes 1544 | tf_op jit(solution)/shard_map/ppermute | solution.py:35
  166.0 4.7 %collective-permute-start.36 = (f32[1,3,4,8]{3,2,0,1:T(4,128)S(1)}, f32[1,3,4,8]{3,2,0,1:T(4,128)S(1)}, u32[]{:S(2)}, u32[]{:S(2)}) collective-permute-start(f32[1,3,4,8]{3,2,0,1:T(4,128)S(1)} %pad_maximum_fusion.52), channel_id=1, source_target_pairs={{0,8},{1,9},{2,10},{3,11},{4,12},{5,13},{6,14},{7,15},{16,24},{17,... | collective-permute-start | bytes 1160 | tf_op jit(solution)/shard_map/ppermute | solution.py:35
  173.4 5.4 %collective-permute-start.39 = (f32[1,4,8]{2,1,0:T(4,128)S(1)}, f32[1,4,8]{2,1,0:T(4,128)S(1)}, u32[]{:S(2)}, u32[]{:S(2)}) collective-permute-start(f32[1,4,8]{2,1,0:T(4,128)S(1)} %get-tuple-element.88), channel_id=1, source_target_pairs={{0,8},{1,9},{2,10},{3,11},{4,12},{5,13},{6,14},{7,15},{16,24},{17,... | collective-permute-start | bytes 392 | tf_op jit(solution)/shard_map/ppermute | solution.py:35
  181.6 5.4 %collective-permute-start.41 = (f32[1,4,8]{2,1,0:T(4,128)S(1)}, f32[1,4,8]{2,1,0:T(4,128)S(1)}, u32[]{:S(2)}, u32[]{:S(2)}) collective-permute-start(f32[1,4,8]{2,1,0:T(4,128)S(1)} %get-tuple-element.86), channel_id=1, source_target_pairs={{0,8},{1,9},{2,10},{3,11},{4,12},{5,13},{6,14},{7,15},{16,24},{17,... | collective-permute-start | bytes 392 | tf_op jit(solution)/shard_map/ppermute | solution.py:35
  191.0 5.4 %collective-permute-start.46 = (f32[1,2,4]{2,1,0:T(2,128)S(1)}, f32[1,2,4]{2,1,0:T(2,128)S(1)}, u32[]{:S(2)}, u32[]{:S(2)}) collective-permute-start(f32[1,2,4]{2,1,0:T(2,128)S(1)} %get-tuple-element.8), channel_id=1, source_target_pairs={{0,8},{1,9},{2,10},{3,11},{4,12},{5,13},{6,14},{7,15},{16,24},{17,... | collective-permute-start | bytes 104 | tf_op jit(solution)/shard_map/ppermute | solution.py:35
  199.1 5.4 %collective-permute-start.48 = (f32[1,2,4]{2,1,0:T(2,128)S(1)}, f32[1,2,4]{2,1,0:T(2,128)S(1)}, u32[]{:S(2)}, u32[]{:S(2)}) collective-permute-start(f32[1,2,4]{2,1,0:T(2,128)S(1)} %get-tuple-element.6), channel_id=1, source_target_pairs={{0,8},{1,9},{2,10},{3,11},{4,12},{5,13},{6,14},{7,15},{16,24},{17,... | collective-permute-start | bytes 104 | tf_op jit(solution)/shard_map/ppermute | solution.py:35
  207.2 5.4 %collective-permute-start.50 = (f32[1,2,4]{2,1,0:T(2,128)S(1)}, f32[1,2,4]{2,1,0:T(2,128)S(1)}, u32[]{:S(2)}, u32[]{:S(2)}) collective-permute-start(f32[1,2,4]{2,1,0:T(2,128)S(1)} %divide_select_fusion.5), channel_id=1, source_target_pairs={{0,8},{1,9},{2,10},{3,11},{4,12},{5,13},{6,14},{7,15},{16,24},{17,... | collective-permute-start | bytes 104 | tf_op jit(solution)/shard_map/ppermute | solution.py:35
  215.3 5.4 %collective-permute-start.52 = (f32[1,2,4]{2,1,0:T(2,128)S(1)}, f32[1,2,4]{2,1,0:T(2,128)S(1)}, u32[]{:S(2)}, u32[]{:S(2)}) collective-permute-start(f32[1,2,4]{2,1,0:T(2,128)S(1)} %divide_select_fusion.4), channel_id=1, source_target_pairs={{0,8},{1,9},{2,10},{3,11},{4,12},{5,13},{6,14},{7,15},{16,24},{17,... | collective-permute-start | bytes 104 | tf_op jit(solution)/shard_map/ppermute | solution.py:35
  223.4 5.4 %collective-permute-start.54 = (f32[1,2,4]{2,1,0:T(2,128)S(1)}, f32[1,2,4]{2,1,0:T(2,128)S(1)}, u32[]{:S(2)}, u32[]{:S(2)}) collective-permute-start(f32[1,2,4]{2,1,0:T(2,128)S(1)} %divide_select_fusion.3), channel_id=1, source_target_pairs={{0,8},{1,9},{2,10},{3,11},{4,12},{5,13},{6,14},{7,15},{16,24},{17,... | collective-permute-start | bytes 104 | tf_op jit(solution)/shard_map/ppermute | solution.py:35
  231.5 5.4 %collective-permute-start.56 = (f32[1,2,4]{2,1,0:T(2,128)S(1)}, f32[1,2,4]{2,1,0:T(2,128)S(1)}, u32[]{:S(2)}, u32[]{:S(2)}) collective-permute-start(f32[1,2,4]{2,1,0:T(2,128)S(1)} %divide_select_fusion.2), channel_id=1, source_target_pairs={{0,8},{1,9},{2,10},{3,11},{4,12},{5,13},{6,14},{7,15},{16,24},{17,... | collective-permute-start | bytes 104 | tf_op jit(solution)/shard_map/ppermute | solution.py:35
  239.6 5.4 %collective-permute-start.58 = (f32[1,2,4]{2,1,0:T(2,128)S(1)}, f32[1,2,4]{2,1,0:T(2,128)S(1)}, u32[]{:S(2)}, u32[]{:S(2)}) collective-permute-start(f32[1,2,4]{2,1,0:T(2,128)S(1)} %divide_select_fusion.1), channel_id=1, source_target_pairs={{0,8},{1,9},{2,10},{3,11},{4,12},{5,13},{6,14},{7,15},{16,24},{17,... | collective-permute-start | bytes 104 | tf_op jit(solution)/shard_map/ppermute | solution.py:35
  247.9 5.4 %collective-permute-start.60 = (f32[1,4,8]{2,1,0:T(4,128)S(1)}, f32[1,4,8]{2,1,0:T(4,128)S(1)}, u32[]{:S(2)}, u32[]{:S(2)}) collective-permute-start(f32[1,4,8]{2,1,0:T(4,128)S(1)} %get-tuple-element.84), channel_id=1, source_target_pairs={{0,8},{1,9},{2,10},{3,11},{4,12},{5,13},{6,14},{7,15},{16,24},{17,... | collective-permute-start | bytes 392 | tf_op jit(solution)/shard_map/ppermute | solution.py:35
  256.0 5.4 %collective-permute-start.62 = (f32[1,4,8]{2,1,0:T(4,128)S(1)}, f32[1,4,8]{2,1,0:T(4,128)S(1)}, u32[]{:S(2)}, u32[]{:S(2)}) collective-permute-start(f32[1,4,8]{2,1,0:T(4,128)S(1)} %get-tuple-element.82), channel_id=1, source_target_pairs={{0,8},{1,9},{2,10},{3,11},{4,12},{5,13},{6,14},{7,15},{16,24},{17,... | collective-permute-start | bytes 392 | tf_op jit(solution)/shard_map/ppermute | solution.py:35
  264.3 5.4 %collective-permute-start.64 = (f32[1,8,16]{2,1,0:T(8,128)S(1)}, f32[1,8,16]{2,1,0:T(8,128)S(1)}, u32[]{:S(2)}, u32[]{:S(2)}) collective-permute-start(f32[1,8,16]{2,1,0:T(8,128)S(1)} %get-tuple-element.76), channel_id=1, source_target_pairs={{0,8},{1,9},{2,10},{3,11},{4,12},{5,13},{6,14},{7,15},{16,24},{17,... | collective-permute-start | bytes 1544 | tf_op jit(solution)/shard_map/ppermute | solution.py:35
  272.5 5.4 %collective-permute-start.66 = (f32[1,8,16]{2,1,0:T(8,128)S(1)}, f32[1,8,16]{2,1,0:T(8,128)S(1)}, u32[]{:S(2)}, u32[]{:S(2)}) collective-permute-start(f32[1,8,16]{2,1,0:T(8,128)S(1)} %get-tuple-element.74), channel_id=1, source_target_pairs={{0,8},{1,9},{2,10},{3,11},{4,12},{5,13},{6,14},{7,15},{16,24},{17,... | collective-permute-start | bytes 1544 | tf_op jit(solution)/shard_map/ppermute | solution.py:35
  280.9 5.4 %collective-permute-start.68 = (f32[1,16,32]{2,1,0:T(8,128)S(1)}, f32[1,16,32]{2,1,0:T(8,128)S(1)}, u32[]{:S(2)}, u32[]{:S(2)}) collective-permute-start(f32[1,16,32]{2,1,0:T(8,128)S(1)} %get-tuple-element.60), channel_id=1, source_target_pairs={{0,8},{1,9},{2,10},{3,11},{4,12},{5,13},{6,14},{7,15},{16,24},{17,... | collective-permute-start | bytes 6152 | tf_op jit(solution)/shard_map/ppermute | solution.py:35
  289.2 5.4 %collective-permute-start.70 = (f32[1,16,32]{2,1,0:T(8,128)S(1)}, f32[1,16,32]{2,1,0:T(8,128)S(1)}, u32[]{:S(2)}, u32[]{:S(2)}) collective-permute-start(f32[1,16,32]{2,1,0:T(8,128)S(1)} %get-tuple-element.56), channel_id=1, source_target_pairs={{0,8},{1,9},{2,10},{3,11},{4,12},{5,13},{6,14},{7,15},{16,24},{17,... | collective-permute-start | bytes 6152 | tf_op jit(solution)/shard_map/ppermute | solution.py:35
  309.5 4.9 %collective-permute-start.76 = (f32[1,64,128]{2,1,0:T(8,128)S(1)}, f32[1,64,128]{2,1,0:T(8,128)S(1)}, u32[]{:S(2)}, u32[]{:S(2)}) collective-permute-start(f32[1,64,128]{2,1,0:T(8,128)S(1)} %get-tuple-element.41), channel_id=1, source_target_pairs={{0,1},{1,2},{2,3},{3,4},{4,5},{5,6},{6,7},{7,8},{8,9},{9,10},{10,1... | collective-permute-start | bytes 98312 | tf_op jit(solution)/shard_map/ppermute | solution.py:23
  315.1 22.4 %all_gather.3 = f32[16,16,32]{2,1,0:T(8,128)S(1)} all-gather(f32[1,16,32]{2,1,0:T(8,128)S(1)} %dynamic-slice_select_fusion), channel_id=1, replica_groups=mesh['groups'=2,'gx'=16] {'gx'}, dimensions={0}, use_global_device_ids=true | all-gather | bytes 34816 | tf_op jit(solution)/shard_map/all_gather | solution.py:224
  (327 shorter events, 143.7 us)
Async XLA Ops:
  0.7 67.6 %collective-permute-start.10 = (f32[1,32,64]{2,1,0:T(8,128)S(1)}, f32[1,32,64]{2,1,0:T(8,128)S(1)}, u32[]{:S(2)}, u32[]{:S(2)}) collective-permute-start(f32[1,32,64]{2,1,0:T(8,128)S(1)} %broadcast.566), channel_id=1, source_target_pairs={{0,1},{1,2},{2,3},{3,4},{4,5},{5,6},{6,7},{7,8},{8,9},{9,10},{10,1... | collective-permute-start | bytes 24584 | tf_op jit(solution)/shard_map/ppermute | solution.py:23
  3.1 66.4 %collective-permute-start.8 = (f32[1,32,64]{2,1,0:T(8,128)S(1)}, f32[1,32,64]{2,1,0:T(8,128)S(1)}, u32[]{:S(2)}, u32[]{:S(2)}) collective-permute-start(f32[1,32,64]{2,1,0:T(8,128)S(1)} %broadcast.566), channel_id=1, source_target_pairs={{1,0},{2,1},{3,2},{4,3},{5,4},{6,5},{7,6},{8,7},{9,8},{10,9},{11,1... | collective-permute-start | bytes 24584 | tf_op jit(solution)/shard_map/ppermute | solution.py:25
  5.4 10.5 %collective-permute-start = (f32[1,64,128]{2,1,0:T(8,128)S(1)}, f32[1,64,128]{2,1,0:T(8,128)S(1)}, u32[]{:S(2)}, u32[]{:S(2)}) collective-permute-start(f32[1,64,128]{2,1,0:T(8,128)S(1)} %slice.1523), channel_id=1, source_target_pairs={{1,0},{2,1},{3,2},{4,3},{5,4},{6,5},{7,6},{8,7},{9,8},{10,9},{11,1... | collective-permute-start | bytes 98312 | tf_op jit(solution)/shard_map/ppermute | solution.py:25
  7.5 12.3 %collective-permute-start.1 = (f32[1,64,128]{2,1,0:T(8,128)S(1)}, f32[1,64,128]{2,1,0:T(8,128)S(1)}, u32[]{:S(2)}, u32[]{:S(2)}) collective-permute-start(f32[1,64,128]{2,1,0:T(8,128)S(1)} %get-tuple-element.49), channel_id=1, source_target_pairs={{1,0},{2,1},{3,2},{4,3},{5,4},{6,5},{7,6},{8,7},{9,8},{10,9},{11,1... | collective-permute-start | bytes 98312 | tf_op jit(solution)/shard_map/ppermute | solution.py:25
  8.8 12.3 %collective-permute-start.3 = (f32[1,64,128]{2,1,0:T(8,128)S(1)}, f32[1,64,128]{2,1,0:T(8,128)S(1)}, u32[]{:S(2)}, u32[]{:S(2)}) collective-permute-start(f32[1,64,128]{2,1,0:T(8,128)S(1)} %get-tuple-element.50), channel_id=1, source_target_pairs={{0,1},{1,2},{2,3},{3,4},{4,5},{5,6},{6,7},{7,8},{8,9},{9,10},{10,1... | collective-permute-start | bytes 98312 | tf_op jit(solution)/shard_map/ppermute | solution.py:23
  19.8 105.0 %collective-permute-start.21 = (f32[1,16,32]{2,1,0:T(8,128)S(1)}, f32[1,16,32]{2,1,0:T(8,128)S(1)}, u32[]{:S(2)}, u32[]{:S(2)}) collective-permute-start(f32[1,16,32]{2,1,0:T(8,128)S(1)} %broadcast.569), channel_id=1, source_target_pairs={{8,0},{9,1},{10,2},{11,3},{12,4},{13,5},{14,6},{15,7},{24,16},{25,... | collective-permute-start | bytes 6152 | tf_op jit(solution)/shard_map/ppermute | solution.py:35
  22.9 15.8 %collective-permute-start.4 = (f32[1,64,128]{2,1,0:T(8,128)S(1)}, f32[1,64,128]{2,1,0:T(8,128)S(1)}, u32[]{:S(2)}, u32[]{:S(2)}) collective-permute-start(f32[1,64,128]{2,1,0:T(8,128)S(1)} %get-tuple-element.44), channel_id=1, source_target_pairs={{1,0},{2,1},{3,2},{4,3},{5,4},{6,5},{7,6},{8,7},{9,8},{10,9},{11,1... | collective-permute-start | bytes 98312 | tf_op jit(solution)/shard_map/ppermute | solution.py:25
  24.2 14.5 %collective-permute-start.5 = (f32[1,64,128]{2,1,0:T(8,128)S(1)}, f32[1,64,128]{2,1,0:T(8,128)S(1)}, u32[]{:S(2)}, u32[]{:S(2)}) collective-permute-start(f32[1,64,128]{2,1,0:T(8,128)S(1)} %get-tuple-element.45), channel_id=1, source_target_pairs={{0,1},{1,2},{2,3},{3,4},{4,5},{5,6},{6,7},{7,8},{8,9},{9,10},{10,1... | collective-permute-start | bytes 98312 | tf_op jit(solution)/shard_map/ppermute | solution.py:23
  40.3 12.4 %collective-permute-start.7 = (f32[1,64,128]{2,1,0:T(8,128)S(1)}, f32[1,64,128]{2,1,0:T(8,128)S(1)}, u32[]{:S(2)}, u32[]{:S(2)}) collective-permute-start(f32[1,64,128]{2,1,0:T(8,128)S(1)} %get-tuple-element.43), channel_id=1, source_target_pairs={{0,1},{1,2},{2,3},{3,4},{4,5},{5,6},{6,7},{7,8},{8,9},{9,10},{10,1... | collective-permute-start | bytes 98312 | tf_op jit(solution)/shard_map/ppermute | solution.py:23
  45.3 79.4 %collective-permute-start.23 = (f32[1,16,32]{2,1,0:T(8,128)S(1)}, f32[1,16,32]{2,1,0:T(8,128)S(1)}, u32[]{:S(2)}, u32[]{:S(2)}) collective-permute-start(f32[1,16,32]{2,1,0:T(8,128)S(1)} %broadcast.569), channel_id=1, source_target_pairs={{0,8},{1,9},{2,10},{3,11},{4,12},{5,13},{6,14},{7,15},{16,24},{17,... | collective-permute-start | bytes 6152 | tf_op jit(solution)/shard_map/ppermute | solution.py:35
  52.7 16.9 %collective-permute-start.9 = (f32[1,3,32,64]{3,2,0,1:T(8,128)S(1)}, f32[1,3,32,64]{3,2,0,1:T(8,128)S(1)}, u32[]{:S(2)}, u32[]{:S(2)}) collective-permute-start(f32[1,3,32,64]{3,2,0,1:T(8,128)S(1)} %pad_maximum_fusion.25), channel_id=1, source_target_pairs={{0,1},{1,2},{2,3},{3,4},{4,5},{5,6},{6,7},{7,8},{8,9},{9,10},{10,1... | collective-permute-start | bytes 73736 | tf_op jit(solution)/shard_map/ppermute | solution.py:23
  68.3 79.7 %collective-permute-start.28 = (f32[1,8,16]{2,1,0:T(8,128)S(1)}, f32[1,8,16]{2,1,0:T(8,128)S(1)}, u32[]{:S(2)}, u32[]{:S(2)}) collective-permute-start(f32[1,8,16]{2,1,0:T(8,128)S(1)} %broadcast.572), channel_id=1, source_target_pairs={{8,0},{9,1},{10,2},{11,3},{12,4},{13,5},{14,6},{15,7},{24,16},{25,... | collective-permute-start | bytes 1544 | tf_op jit(solution)/shard_map/ppermute | solution.py:35
  75.6 7.6 %collective-permute-start.13 = (f32[1,32,64]{2,1,0:T(8,128)S(1)}, f32[1,32,64]{2,1,0:T(8,128)S(1)}, u32[]{:S(2)}, u32[]{:S(2)}) collective-permute-start(f32[1,32,64]{2,1,0:T(8,128)S(1)} %get-tuple-element.69), channel_id=1, source_target_pairs={{1,0},{2,1},{3,2},{4,3},{5,4},{6,5},{7,6},{8,7},{9,8},{10,9},{11,1... | collective-permute-start | bytes 24584 | tf_op jit(solution)/shard_map/ppermute | solution.py:25
  92.6 8.4 %collective-permute-start.17 = (f32[2,4,16,32]{3,2,1,0:T(8,128)S(1)}, f32[2,4,16,32]{3,2,1,0:T(8,128)S(1)}, u32[]{:S(2)}, u32[]{:S(2)}) collective-permute-start(f32[2,4,16,32]{3,2,1,0:T(8,128)S(1)} %maximum_select_fusion.2), channel_id=1, source_target_pairs={{0,2},{1,3},{2,4},{3,5},{4,6},{5,7},{6,8},{7,9},{8,10},{9,11},{10,... | collective-permute-start | bytes 49160 | tf_op jit(solution)/shard_map/ppermute | solution.py:35
  99.1 7.6 %collective-permute-start.18 = (f32[2,4,16,32]{3,2,1,0:T(8,128)S(1)}, f32[2,4,16,32]{3,2,1,0:T(8,128)S(1)}, u32[]{:S(2)}, u32[]{:S(2)}) collective-permute-start(f32[2,4,16,32]{3,2,1,0:T(8,128)S(1)} %maximum_select_fusion.2), channel_id=1, source_target_pairs={{2,0},{3,1},{4,2},{5,3},{6,4},{7,5},{8,6},{9,7},{10,8},{11,9},{12,... | collective-permute-start | bytes 49160 | tf_op jit(solution)/shard_map/ppermute | solution.py:35
  109.8 10.0 %collective-permute-start.20 = (f32[4,4,16,32]{3,2,1,0:T(8,128)S(1)}, f32[4,4,16,32]{3,2,1,0:T(8,128)S(1)}, u32[]{:S(2)}, u32[]{:S(2)}) collective-permute-start(f32[4,4,16,32]{3,2,1,0:T(8,128)S(1)} %maximum_select_fusion.1), channel_id=1, source_target_pairs={{4,0},{5,1},{6,2},{7,3},{8,4},{9,5},{10,6},{11,7},{12,8},{13,9},{1... | collective-permute-start | bytes 98312 | tf_op jit(solution)/shard_map/ppermute | solution.py:35
  113.4 35.8 %collective-permute-start.30 = (f32[1,8,16]{2,1,0:T(8,128)S(1)}, f32[1,8,16]{2,1,0:T(8,128)S(1)}, u32[]{:S(2)}, u32[]{:S(2)}) collective-permute-start(f32[1,8,16]{2,1,0:T(8,128)S(1)} %broadcast.572), channel_id=1, source_target_pairs={{0,8},{1,9},{2,10},{3,11},{4,12},{5,13},{6,14},{7,15},{16,24},{17,... | collective-permute-start | bytes 1544 | tf_op jit(solution)/shard_map/ppermute | solution.py:35
  123.3 47.6 %collective-permute-start.35 = (f32[1,4,8]{2,1,0:T(4,128)S(1)}, f32[1,4,8]{2,1,0:T(4,128)S(1)}, u32[]{:S(2)}, u32[]{:S(2)}) collective-permute-start(f32[1,4,8]{2,1,0:T(4,128)S(1)} %broadcast.575), channel_id=1, source_target_pairs={{8,0},{9,1},{10,2},{11,3},{12,4},{13,5},{14,6},{15,7},{24,16},{25,... | collective-permute-start | bytes 392 | tf_op jit(solution)/shard_map/ppermute | solution.py:35
  124.9 8.8 %collective-permute-start.24 = (f32[1,16,32]{2,1,0:T(8,128)S(1)}, f32[1,16,32]{2,1,0:T(8,128)S(1)}, u32[]{:S(2)}, u32[]{:S(2)}) collective-permute-start(f32[1,16,32]{2,1,0:T(8,128)S(1)} %get-tuple-element.63), channel_id=1, source_target_pairs={{8,0},{9,1},{10,2},{11,3},{12,4},{13,5},{14,6},{15,7},{24,16},{25,... | collective-permute-start | bytes 6152 | tf_op jit(solution)/shard_map/ppermute | solution.py:35
  126.2 7.5 %collective-permute-start.25 = (f32[1,16,32]{2,1,0:T(8,128)S(1)}, f32[1,16,32]{2,1,0:T(8,128)S(1)}, u32[]{:S(2)}, u32[]{:S(2)}) collective-permute-start(f32[1,16,32]{2,1,0:T(8,128)S(1)} %get-tuple-element.64), channel_id=1, source_target_pairs={{0,8},{1,9},{2,10},{3,11},{4,12},{5,13},{6,14},{7,15},{16,24},{17,... | collective-permute-start | bytes 6152 | tf_op jit(solution)/shard_map/ppermute | solution.py:35
  133.9 7.5 %collective-permute-start.26 = (f32[1,16,32]{2,1,0:T(8,128)S(1)}, f32[1,16,32]{2,1,0:T(8,128)S(1)}, u32[]{:S(2)}, u32[]{:S(2)}) collective-permute-start(f32[1,16,32]{2,1,0:T(8,128)S(1)} %get-tuple-element.61), channel_id=1, source_target_pairs={{8,0},{9,1},{10,2},{11,3},{12,4},{13,5},{14,6},{15,7},{24,16},{25,... | collective-permute-start | bytes 6152 | tf_op jit(solution)/shard_map/ppermute | solution.py:35
  135.2 7.5 %collective-permute-start.27 = (f32[1,16,32]{2,1,0:T(8,128)S(1)}, f32[1,16,32]{2,1,0:T(8,128)S(1)}, u32[]{:S(2)}, u32[]{:S(2)}) collective-permute-start(f32[1,16,32]{2,1,0:T(8,128)S(1)} %get-tuple-element.62), channel_id=1, source_target_pairs={{0,8},{1,9},{2,10},{3,11},{4,12},{5,13},{6,14},{7,15},{16,24},{17,... | collective-permute-start | bytes 6152 | tf_op jit(solution)/shard_map/ppermute | solution.py:35
  141.4 29.6 %collective-permute-start.37 = (f32[1,4,8]{2,1,0:T(4,128)S(1)}, f32[1,4,8]{2,1,0:T(4,128)S(1)}, u32[]{:S(2)}, u32[]{:S(2)}) collective-permute-start(f32[1,4,8]{2,1,0:T(4,128)S(1)} %broadcast.575), channel_id=1, source_target_pairs={{0,8},{1,9},{2,10},{3,11},{4,12},{5,13},{6,14},{7,15},{16,24},{17,... | collective-permute-start | bytes 392 | tf_op jit(solution)/shard_map/ppermute | solution.py:35
  147.9 40.6 %collective-permute-start.42 = (f32[1,2,4]{2,1,0:T(2,128)S(1)}, f32[1,2,4]{2,1,0:T(2,128)S(1)}, u32[]{:S(2)}, u32[]{:S(2)}) collective-permute-start(f32[1,2,4]{2,1,0:T(2,128)S(1)} %broadcast.578), channel_id=1, source_target_pairs={{8,0},{9,1},{10,2},{11,3},{12,4},{13,5},{14,6},{15,7},{24,16},{25,... | collective-permute-start | bytes 104 | tf_op jit(solution)/shard_map/ppermute | solution.py:35
  149.4 6.9 %collective-permute-start.31 = (f32[1,8,16]{2,1,0:T(8,128)S(1)}, f32[1,8,16]{2,1,0:T(8,128)S(1)}, u32[]{:S(2)}, u32[]{:S(2)}) collective-permute-start(f32[1,8,16]{2,1,0:T(8,128)S(1)} %get-tuple-element.79), channel_id=1, source_target_pairs={{8,0},{9,1},{10,2},{11,3},{12,4},{13,5},{14,6},{15,7},{24,16},{25,... | collective-permute-start | bytes 1544 | tf_op jit(solution)/shard_map/ppermute | solution.py:35
  157.5 7.2 %collective-permute-start.33 = (f32[1,8,16]{2,1,0:T(8,128)S(1)}, f32[1,8,16]{2,1,0:T(8,128)S(1)}, u32[]{:S(2)}, u32[]{:S(2)}) collective-permute-start(f32[1,8,16]{2,1,0:T(8,128)S(1)} %get-tuple-element.77), channel_id=1, source_target_pairs={{8,0},{9,1},{10,2},{11,3},{12,4},{13,5},{14,6},{15,7},{24,16},{25,... | collective-permute-start | bytes 1544 | tf_op jit(solution)/shard_map/ppermute | solution.py:35
  158.8 7.2 %collective-permute-start.34 = (f32[1,8,16]{2,1,0:T(8,128)S(1)}, f32[1,8,16]{2,1,0:T(8,128)S(1)}, u32[]{:S(2)}, u32[]{:S(2)}) collective-permute-start(f32[1,8,16]{2,1,0:T(8,128)S(1)} %get-tuple-element.78), channel_id=1, source_target_pairs={{0,8},{1,9},{2,10},{3,11},{4,12},{5,13},{6,14},{7,15},{16,24},{17,... | collective-permute-start | bytes 1544 | tf_op jit(solution)/shard_map/ppermute | solution.py:35
  164.7 23.9 %collective-permute-start.44 = (f32[1,2,4]{2,1,0:T(2,128)S(1)}, f32[1,2,4]{2,1,0:T(2,128)S(1)}, u32[]{:S(2)}, u32[]{:S(2)}) collective-permute-start(f32[1,2,4]{2,1,0:T(2,128)S(1)} %broadcast.578), channel_id=1, source_target_pairs={{0,8},{1,9},{2,10},{3,11},{4,12},{5,13},{6,14},{7,15},{16,24},{17,... | collective-permute-start | bytes 104 | tf_op jit(solution)/shard_map/ppermute | solution.py:35
  180.2 8.1 %collective-permute-start.40 = (f32[1,4,8]{2,1,0:T(4,128)S(1)}, f32[1,4,8]{2,1,0:T(4,128)S(1)}, u32[]{:S(2)}, u32[]{:S(2)}) collective-permute-start(f32[1,4,8]{2,1,0:T(4,128)S(1)} %get-tuple-element.85), channel_id=1, source_target_pairs={{8,0},{9,1},{10,2},{11,3},{12,4},{13,5},{14,6},{15,7},{24,16},{25,... | collective-permute-start | bytes 392 | tf_op jit(solution)/shard_map/ppermute | solution.py:35
  280.9 6.8 %collective-permute-start.68 = (f32[1,16,32]{2,1,0:T(8,128)S(1)}, f32[1,16,32]{2,1,0:T(8,128)S(1)}, u32[]{:S(2)}, u32[]{:S(2)}) collective-permute-start(f32[1,16,32]{2,1,0:T(8,128)S(1)} %get-tuple-element.60), channel_id=1, source_target_pairs={{0,8},{1,9},{2,10},{3,11},{4,12},{5,13},{6,14},{7,15},{16,24},{17,... | collective-permute-start | bytes 6152 | tf_op jit(solution)/shard_map/ppermute | solution.py:35
  308.2 29.2 %collective-permute-start.75 = (f32[1,64,128]{2,1,0:T(8,128)S(1)}, f32[1,64,128]{2,1,0:T(8,128)S(1)}, u32[]{:S(2)}, u32[]{:S(2)}) collective-permute-start(f32[1,64,128]{2,1,0:T(8,128)S(1)} %get-tuple-element.40), channel_id=1, source_target_pairs={{1,0},{2,1},{3,2},{4,3},{5,4},{6,5},{7,6},{8,7},{9,8},{10,9},{11,1... | collective-permute-start | bytes 98312 | tf_op jit(solution)/shard_map/ppermute | solution.py:25
  309.5 27.9 %collective-permute-start.76 = (f32[1,64,128]{2,1,0:T(8,128)S(1)}, f32[1,64,128]{2,1,0:T(8,128)S(1)}, u32[]{:S(2)}, u32[]{:S(2)}) collective-permute-start(f32[1,64,128]{2,1,0:T(8,128)S(1)} %get-tuple-element.41), channel_id=1, source_target_pairs={{0,1},{1,2},{2,3},{3,4},{4,5},{5,6},{6,7},{7,8},{8,9},{9,10},{10,1... | collective-permute-start | bytes 98312 | tf_op jit(solution)/shard_map/ppermute | solution.py:23
  (49 other events, 560.9 us)
where the time goes:
time: 347 us; the launch traced here: 344 us
  starting transfers between devices  239 us (69%)
  waiting for transfers between devices  36.1 us (10%)
  local copies, waits for them, and re-layouts  25 us (7%)
  blocking collectives  22.4 us (6%)
  other arithmetic  18.3 us (5%)
    ppermute x56, starting transfers between devices, from_behind(): return lax.ppermute(block, axis, route)  180 us
    ppermute x12, starting transfers between devices, with_halo(): lax.ppermute(tail, axis, [(i, (i + 1) % count) for i in range(ends)])  45.6 us
    ppermute x56, waiting for transfers between devices, from_behind(): return lax.ppermute(block, axis, route)  34.1 us
    all_gather x1, blocking collectives, on_device(): shard_rows = lax.all_gather(third_fix, 'gx', axis=0, tiled=True)  22.4 us
    ppermute x11, starting transfers between devices, with_halo(): lax.ppermute(head, axis, [((i + 1) % count, i) for i in range(ends)])  14.2 us
    reshape x3, local copies, waits for them, and re-layouts, restrict(): values.reshape(layers // 2, 2, height // 2, 2, depth_cells // 2, 2)  10.5 us
  transfers between devices with their start and end apart: 79, of which 26 were waited for; matrix products, arithmetic and copies ran while one was open for 12% of the time, Pallas kernels for 0%

commit v1 on v0

v1 whole, which is shorter than its diff:
```python
import jax
import jax.numpy as jnp
from jax import lax
from jax.experimental import pallas as pl
from jax.experimental.pallas import tpu as pltpu
from jax.sharding import PartitionSpec as P

STIFFNESS = 100.0
EPSILON = 0.01
COARSE_SWEEPS = 4
PAD = 8


def from_behind(block, distance):
    devices = range(lax.axis_size("gx"))
    route = [(i - distance, i) for i in devices if i - distance in devices]
    return lax.ppermute(block, "gx", route)


def lanes_of(shape):
    return lax.broadcasted_iota(jnp.int32, shape, len(shape) - 1)


def rows_of(shape):
    return lax.broadcasted_iota(jnp.int32, shape, len(shape) - 2)


def ahead(values, step, axis):
    return pltpu.roll(values, values.shape[axis] - step, axis)


def behind(values, step, axis):
    return pltpu.roll(values, step, axis)


def with_partner(values, step, axis):
    index = lax.broadcasted_iota(jnp.int32, values.shape, axis)
    partner = jnp.where((index & step) == 0, ahead(values, step, axis), behind(values, step, axis))
    return values + partner


def even_row_sum(scratch, rows):
    return scratch[pl.ds(0, rows, 2), :] + scratch[pl.ds(1, rows, 2), :]


def fine_down_kernel(
    where_ref, iterate, source, phase, from_left, from_right,
    coarse_out, field_out, source_out, fx_out, fy_out, fz_out, inv_out,
    cell, e, fx, fy, fz, fzl, inv, held, pair,
):
    layers, height, depth = iterate.shape
    window = 3 * layers
    position, last = where_ref[0], where_ref[1]
    body = pl.ds(PAD, height)
    up, down = pl.ds(PAD + 1, height), pl.ds(PAD - 1, height)
    row, lane = rows_of((height, depth)), lanes_of((height, depth))
    even_sum = ((row + lane) & 1) == 0

    def pick(kind, w):
        if w < layers:
            return from_left[(0, layers, 2 * layers - 1)[kind] + w - (kind == 1)]
        if w < 2 * layers:
            return (iterate, source, phase)[kind][w - layers]
        return from_right[(0, layers, 2 * layers - 1)[kind] + w - 2 * layers]

    edge = jnp.zeros((PAD, depth), jnp.float32)
    for w in range(window):
        for padded in (e, fy):
            padded[w, :PAD] = edge
            padded[w, PAD + height:] = edge
        e[w, body] = pick(0, w)
        value = pick(2, w)
        cell[w, body] = STIFFNESS * (value * value + EPSILON)
        cell[w, PAD + height:] = edge
    for w in range(window):
        here = cell[w, body]
        if w < window - 1:
            face = 0.5 * (here + cell[w + 1, body])
            if w == layers - 1:
                face = jnp.where(position > 0, face, 0.0)
            if w == 2 * layers - 1:
                face = jnp.where(position < last, face, 0.0)
            fx[w] = face
        fy[w, body] = jnp.where(row < height - 1, 0.5 * (here + cell[w, up]), 0.0)
        face = jnp.where(lane < depth - 1, 0.5 * (here + ahead(here, 1, 1)), 0.0)
        fz[w] = face
        fzl[w] = behind(face, 1, 1)
    for w in range(1, window - 1):
        weight = fx[w] + fx[w - 1] + fy[w, body] + fy[w, down] + fz[w] + fzl[w]
        inv[w] = 1.0 / (1.0 + weight)

    def neigh(w):
        here = e[w, body]
        total = fx[w] * e[w + 1, body] + fx[w - 1] * e[w - 1, body]
        total = total + fy[w, body] * e[w, up] + fy[w, down] * e[w, down]
        return total + fz[w] * ahead(here, 1, 1) + fzl[w] * behind(here, 1, 1)

    def mask(w, odd):
        return even_sum if (w + odd) % 2 == 0 else ~even_sum

    for w in range(1, window - 1):
        total = pick(1, w) + neigh(w)
        if layers <= w < 2 * layers:
            held[w - layers] = total
        e[w, body] = jnp.where(mask(w, 0), total * inv[w], e[w, body])
    for w in range(2, window - 2):
        total = (pick(1, w) + neigh(w)) * inv[w]
        e[w, body] = jnp.where(mask(w, 1), total, e[w, body])

    first = layers - 2
    for w in range(first, window - first):
        field_out[w - first] = e[w, body]
    first = layers - 1
    for w in range(first - 1, window - first):
        fx_out[w - first + 1] = fx[w]
    for w in range(first, window - first):
        source_out[w - first] = pick(1, w)
        fy_out[w - first] = fy[w]
        fz_out[w - first] = fz[w]
        inv_out[w - first] = inv[w]

    half = height // 2
    lane = lanes_of((half, depth))
    first_of_two = (lane & 1) == 0

    def residual(w):
        return jnp.where(mask(w, 0), pick(1, w) + neigh(w) - held[w - layers], 0.0)

    def merged(one, two):
        return jnp.where(first_of_two, one, two)

    def slabs(make, reduce_rows, reduce_lanes):
        found = []
        for t in range(2):
            pair[t] = make(layers + 2 * t)
            found.append(reduce_lanes(reduce_rows(pair.at[t])))
        return merged(found[0], found[1])

    def both_rows(scratch):
        return even_row_sum(scratch, half)

    def odd_rows(scratch):
        return scratch[pl.ds(1, half, 2), :]

    def both_lanes(values):
        return with_partner(values, 1, 1)

    def odd_lanes(values):
        return jnp.where(first_of_two, ahead(values, 1, 1), values)

    coarse_out[0] = slabs(lambda w: residual(w) + residual(w + 1), both_rows, both_lanes)
    coarse_out[1] = slabs(lambda w: fx[w + 1], both_rows, both_lanes)
    coarse_out[2] = slabs(lambda w: fy[w, body] + fy[w + 1, body], odd_rows, both_lanes)
    coarse_out[3] = slabs(lambda w: fz[w] + fz[w + 1], both_rows, odd_lanes)


class Level:
    def __init__(self, mass, source, faces, row_step, lane_step):
        self.source, self.row_step, self.lane_step = source, row_step, lane_step
        self.fx, self.fy, self.fz = faces
        self.layers, rows, lanes = source.shape
        nothing = jnp.zeros_like(source[:1])
        self.nothing = nothing
        self.fxl = jnp.concatenate([nothing, self.fx[:-1]], 0)
        self.fyl = behind(self.fy, row_step, 1)
        self.fzl = behind(self.fz, lane_step, 2)
        weight = self.fx + self.fxl + self.fy + self.fyl + self.fz + self.fzl
        self.inv = 1.0 / (mass + weight)
        shape = source.shape
        total = lax.broadcasted_iota(jnp.int32, shape, 0)
        total = total + rows_of(shape) // row_step + lanes_of(shape) // lane_step
        self.even = (total & 1) == 0

    def neigh(self, e):
        upper = jnp.concatenate([e[1:], self.nothing], 0)
        lower = jnp.concatenate([self.nothing, e[:-1]], 0)
        total = self.fx * upper + self.fxl * lower
        total = total + self.fy * ahead(e, self.row_step, 1) + self.fyl * behind(e, self.row_step, 1)
        return total + self.fz * ahead(e, self.lane_step, 2) + self.fzl * behind(e, self.lane_step, 2)

    def start(self):
        e = jnp.where(self.even, self.source * self.inv, 0.0)
        return self.odd_update(e)

    def even_update(self, e):
        return jnp.where(self.even, (self.source + self.neigh(e)) * self.inv, e)

    def odd_update(self, e):
        return jnp.where(self.even, e, (self.source + self.neigh(e)) * self.inv)

    def residual(self, e):
        return jnp.where(self.even, self.neigh(e), 0.0)

    def pairs(self, values):
        halves = values.reshape(self.layers // 2, 2, *values.shape[1:])
        return halves[:, 0] + halves[:, 1]

    def coarse_faces(self):
        row_bit = (rows_of(self.fx.shape) & self.row_step) != 0
        lane_bit = (lanes_of(self.fx.shape) & self.lane_step) != 0
        odd_layers = self.fx.reshape(self.layers // 2, 2, *self.fx.shape[1:])[:, 1]
        fx = self.in_plane(odd_layers)
        fy = self.in_plane(self.pairs(jnp.where(row_bit, self.fy, 0.0)))
        fz = self.in_plane(self.pairs(jnp.where(lane_bit, self.fz, 0.0)))
        return fx, fy, fz

    def in_plane(self, values):
        return with_partner(with_partner(values, self.row_step, 1), self.lane_step, 2)

    def restricted(self, values):
        return self.in_plane(self.pairs(values))


def doubled_layers(values):
    layers = values.shape[0]
    both = jnp.concatenate([values[:, None], values[:, None]], 1)
    return both.reshape(2 * layers, *values.shape[1:])


def small_cycle(mass, source, faces, row_step, lane_step, deeper):
    level = Level(mass, source, faces, row_step, lane_step)
    e = level.start()
    if deeper == 0:
        for turn in range(COARSE_SWEEPS - 1):
            e = level.odd_update(level.even_update(e))
        return e
    fix = small_cycle(
        8.0 * mass, level.restricted(level.residual(e)), level.coarse_faces(),
        2 * row_step, 2 * lane_step, deeper - 1,
    )
    e = e + doubled_layers(fix)
    return level.odd_update(level.even_update(e))


def chunked(count, size, body):
    size = min(size, count)
    if count == size:
        body(0)
    else:
        lax.fori_loop(0, count // size, lambda i, c: (body(i * size), c)[1], 0)


def coarse_kernel(
    where_ref, gathered, field, source, fx_in, fy_in, fz_in, inv_in,
    solved, owned,
    s2, fx2, fxl2, fy2, fz2, fzl2, inv2, e2,
    s3, fx3, fy3, fz3, fzl3, inv3, e3, pair3, small,
    e1, cor,
):
    blocks, _, half, lanes = gathered.shape
    height = 2 * half
    quarter = half // 2
    position, owner = where_ref[0], where_ref[2]
    total = blocks + 4

    body2, up2, down2 = pl.ds(PAD, half), pl.ds(PAD + 1, half), pl.ds(PAD - 1, half)
    row, lane = rows_of((half, lanes)), lanes_of((half, lanes))
    first_of_two = (lane & 1) == 0
    even2 = ((row + (lane & 1) + (lane >> 1)) & 1) == 0
    edge = jnp.zeros((PAD, lanes), jnp.float32)
    blank = jnp.zeros((half, lanes), jnp.float32)
    for j in (0, 1, total - 2, total - 1):
        for plain in (s2, fx2, fxl2, fz2, fzl2, inv2):
            plain[j] = blank
        for padded in (e2, fy2):
            padded[j] = jnp.zeros((half + 2 * PAD, lanes), jnp.float32)

    def setup2(at):
        for i in range(4):
            j = at + i
            s2[j + 2] = gathered[j, 0]
            fx2[j + 2] = gathered[j, 1]
            fy2[j + 2, body2] = gathered[j, 2]
            fz2[j + 2] = gathered[j, 3]
            fzl2[j + 2] = behind(gathered[j, 3], 2, 1)
            for padded in (e2, fy2):
                padded[j + 2, :PAD] = edge
                padded[j + 2, PAD + half:] = edge

    chunked(blocks, 4, setup2)

    def weights2(at):
        for i in range(4):
            j = at + i + 2
            low = jnp.where(first_of_two, ahead(fx2[j - 1], 1, 1), behind(fx2[j], 1, 1))
            weight = fx2[j] + low + fy2[j, body2] + fy2[j, down2] + fz2[j] + fzl2[j]
            inverse = 1.0 / (8.0 + weight)
            fxl2[j] = low
            inv2[j] = inverse
            e2[j, body2] = jnp.where(even2, s2[j] * inverse, 0.0)

    chunked(blocks, 4, weights2)

    def neigh2(at, count):
        here = [e2[at + i, body2] for i in range(-1, count + 1)]
        after = [ahead(v, 1, 1) for v in here]
        before = [behind(v, 1, 1) for v in here]
        found = []
        for i in range(count):
            j = at + i
            upper = jnp.where(first_of_two, after[i + 1], before[i + 2])
            lower = jnp.where(first_of_two, after[i], before[i + 1])
            sums = fx2[j] * upper + fxl2[j] * lower
            sums = sums + fy2[j, body2] * e2[j, up2] + fy2[j, down2] * e2[j, down2]
            sums = sums + fz2[j] * ahead(here[i + 1], 2, 1) + fzl2[j] * behind(here[i + 1], 2, 1)
            found.append(sums)
        return here[1:-1], found

    def update2(at, count, even):
        here, sums = neigh2(at, count)
        fresh = []
        for i in range(count):
            value = (s2[at + i] + sums[i]) * inv2[at + i]
            fresh.append(jnp.where(even2, value, here[i]) if even else jnp.where(even2, here[i], value))
        for i in range(count):
            e2[at + i, body2] = fresh[i]

    chunked(blocks, 4, lambda at: update2(at + 2, 4, False))

    body3, up3, down3 = pl.ds(PAD, quarter), pl.ds(PAD + 1, quarter), pl.ds(PAD - 1, quarter)
    row, lane = rows_of((quarter, lanes)), lanes_of((quarter, lanes))
    parity3 = row + (lane >> 2)
    odd_layer = (lane & 1) != 0
    odd_depth = (lane & 2) != 0
    edge3 = jnp.zeros((quarter + 2 * PAD, lanes), jnp.float32)
    for j in (0, blocks + 1):
        e3[j] = edge3
    fx3[0] = jnp.zeros((quarter, lanes), jnp.float32)

    def group(values):
        return with_partner(with_partner(values, 1, 1), 2, 1)

    def restrict2(at):
        _, sums = neigh2(at + 2, 4)
        for i in range(4):
            pair3[i] = jnp.where(even2, sums[i], 0.0)
        for i in range(4):
            j = at + i
            s3[j] = group(even_row_sum(pair3.at[i], quarter))
            fxs = fx2[j + 2, pl.ds(0, quarter, 2), :] + fx2[j + 2, pl.ds(1, quarter, 2), :]
            fx3[j + 1] = group(jnp.where(odd_layer, fxs, 0.0))
            fy3[j] = edge3
            fy3[j, body3] = group(fy2[j + 2, pl.ds(PAD + 1, quarter, 2), :])
            fzs = fz2[j + 2, pl.ds(0, quarter, 2), :] + fz2[j + 2, pl.ds(1, quarter, 2), :]
            face = group(jnp.where(odd_depth, fzs, 0.0))
            fz3[j] = face
            fzl3[j] = behind(face, 4, 1)

    chunked(blocks, 4, restrict2)

    def is_even3(j):
        return ((parity3 + j) & 1) == 0

    def weights3(at):
        for i in range(4):
            j = at + i
            weight = fx3[j + 1] + fx3[j] + fy3[j, body3] + fy3[j, down3] + fz3[j] + fzl3[j]
            inverse = 1.0 / (64.0 + weight)
            inv3[j] = inverse
            e3[j + 1] = edge3
            e3[j + 1, body3] = jnp.where(is_even3(j), s3[j] * inverse, 0.0)

    chunked(blocks, 4, weights3)

    def neigh3(j):
        here = e3[j + 1, body3]
        sums = fx3[j + 1] * e3[j + 2, body3] + fx3[j] * e3[j, body3]
        sums = sums + fy3[j, body3] * e3[j + 1, up3] + fy3[j, down3] * e3[j + 1, down3]
        return here, sums + fz3[j] * ahead(here, 4, 1) + fzl3[j] * behind(here, 4, 1)

    def update3(at, count, even):
        fresh = []
        for i in range(count):
            j = at + i
            here, sums = neigh3(j)
            value = (s3[j] + sums) * inv3[j]
            where = is_even3(j)
            fresh.append(jnp.where(where, value, here) if even else jnp.where(where, here, value))
        for i in range(count):
            e3[at + i + 1, body3] = fresh[i]

    chunked(blocks, 8, lambda at: update3(at, 8, False))

    def restrict3(at):
        for i in range(0, 4, 2):
            j = at + i
            parts = []
            for k in (j, j + 1):
                _, sums = neigh3(k)
                parts.append(jnp.where(is_even3(k), sums, 0.0))
            pair3[i, :quarter] = parts[0] + parts[1]
            pair3[i + 1, :quarter] = fz3[j] + fz3[j + 1]
        for i in range(0, 4, 2):
            j = at + i
            out = (at + i) // 2
            small[0, out] = with_partner(even_row_sum(pair3.at[i], PAD), 4, 1)
            fxs = fx3[j + 2, pl.ds(0, PAD, 2), :] + fx3[j + 2, pl.ds(1, PAD, 2), :]
            small[1, out] = with_partner(fxs, 4, 1)
            fys = fy3[j, pl.ds(PAD + 1, PAD, 2), :] + fy3[j + 1, pl.ds(PAD + 1, PAD, 2), :]
            small[2, out] = with_partner(fys, 4, 1)
            fzs = even_row_sum(pair3.at[i + 1], PAD)
            odd = (lanes_of((PAD, lanes)) & 4) != 0
            small[3, out] = with_partner(jnp.where(odd, fzs, 0.0), 4, 1)

    chunked(blocks, 4, restrict3)

    small[0] = small_cycle(512.0, small[0], (small[1], small[2], small[3]), 1, 8, 2)

    def prolong3(at):
        for i in range(4):
            j = at + i
            fix = small[0, j // 2]
            pair3[i, pl.ds(0, PAD, 2), :] = fix
            pair3[i, pl.ds(1, PAD, 2), :] = fix
        for i in range(4):
            j = at + i
            e3[j + 1, body3] = e3[j + 1, body3] + pair3[i, :quarter]

    chunked(blocks, 4, prolong3)
    chunked(blocks, 8, lambda at: update3(at, 8, True))
    chunked(blocks, 8, lambda at: update3(at, 8, False))

    wide, narrow = lanes_of((lanes, lanes)), rows_of((lanes, lanes))
    take = jnp.where(narrow == 4 * wide, 1.0, 0.0)
    block = jnp.dot(
        e3[owner + 1, body3], take, precision=lax.Precision.HIGHEST, preferred_element_type=jnp.float32
    )
    owned[0] = block[:, : lanes // 4]

    for k in range(5):
        j = position + k
        inside = (j >= 2) & (j < blocks + 2)
        third = jnp.clip(j - 1, 1, blocks)
        fix = jnp.where(inside, e3[third, body3], 0.0)
        pair3[0, pl.ds(0, quarter, 2), :] = fix
        pair3[0, pl.ds(1, quarter, 2), :] = fix
        e2[j, body2] = e2[j, body2] + pair3[0]
    update2(position + 1, 3, True)
    update2(position + 1, 3, False)

    body1, up1, down1 = pl.ds(PAD, height), pl.ds(PAD + 1, height), pl.ds(PAD - 1, height)
    rows, lane = rows_of((height, lanes)), lanes_of((height, lanes))
    even_sum = ((rows + lane) & 1) == 0
    lane = lanes_of((half, lanes))
    count = field.shape[0]
    for w in range(0, count, 2):
        coarse_layer = w // 2 - 1
        packed = e2[position + 2 + coarse_layer // 2, body2]
        if coarse_layer % 2 == 0:
            plain = jnp.where(first_of_two, packed, behind(packed, 1, 1))
        else:
            plain = jnp.where(first_of_two, ahead(packed, 1, 1), packed)
        cor[pl.ds(0, half, 2), :] = plain
        cor[pl.ds(1, half, 2), :] = plain
        fix = cor[...]
        for v in (w, w + 1):
            e1[v, :PAD] = edge
            e1[v, PAD + height:] = edge
            e1[v, body1] = field[v] + fix

    def smoothed1(w, even):
        here = e1[w, body1]
        face = fz_in[w - 1]
        sums = fx_in[w] * e1[w + 1, body1] + fx_in[w - 1] * e1[w - 1, body1]
        sums = sums + fy_in[w - 1, body1] * e1[w, up1] + fy_in[w - 1, down1] * e1[w, down1]
        sums = sums + face * ahead(here, 1, 1) + behind(face, 1, 1) * behind(here, 1, 1)
        value = (source[w - 1] + sums) * inv_in[w - 1]
        keep = even_sum if (w + even) % 2 == 0 else ~even_sum
        return jnp.where(keep, here, value)

    for w in range(1, count - 1):
        e1[w, body1] = smoothed1(w, 1)
    for w in range(2, count - 2):
        solved[w - 2] = smoothed1(w, 0)


def f32(*shape):
    return jax.ShapeDtypeStruct(shape, jnp.float32)


def vmem(*shape):
    return pltpu.VMEM(shape, jnp.float32)


def on_device(iterate, source, phase_field, block_owner):
    layers, height, depth = iterate.shape
    position = lax.axis_index("gx")
    blocks = lax.axis_size("gx")
    where = jnp.stack([position, jnp.full_like(position, blocks - 1), block_owner[position]]).astype(jnp.int32)
    to_left = jnp.concatenate([iterate, source[:-1], phase_field], 0)
    to_right = jnp.concatenate([iterate, source[1:], phase_field], 0)
    from_left = from_behind(to_right, 1)
    from_right = from_behind(to_left, -1)
    window = 3 * layers
    half, quarter = height // 2, height // 4
    padded = height + 2 * PAD
    scalar = pl.BlockSpec(memory_space=pltpu.SMEM)
    whole = pl.BlockSpec(memory_space=pltpu.VMEM)
    coarse, field, source1, fx, fy, fz, inv = pl.pallas_call(
        fine_down_kernel,
        out_shape=(
            f32(4, half, depth), f32(layers + 4, height, depth), f32(layers + 2, height, depth),
            f32(layers + 3, height, depth), f32(layers + 2, padded, depth), f32(layers + 2, height, depth),
            f32(layers + 2, height, depth),
        ),
        in_specs=[scalar] + [whole] * 5,
        out_specs=[whole] * 7,
        scratch_shapes=[
            vmem(window, padded, depth), vmem(window, padded, depth), vmem(window, height, depth),
            vmem(window, padded, depth), vmem(window, height, depth), vmem(window, height, depth),
            vmem(window, height, depth), vmem(layers, height, depth), vmem(2, height, depth),
        ],
        compiler_params=pltpu.CompilerParams(vmem_limit_bytes=48 * 2**20),
    )(where, iterate, source, phase_field, from_left, from_right)
    gathered = lax.all_gather(coarse, "gx", axis=0, tiled=False)
    total = blocks + 4
    padded2, padded3 = half + 2 * PAD, quarter + 2 * PAD
    solved, owned = pl.pallas_call(
        coarse_kernel,
        out_shape=(f32(layers, height, depth), f32(1, quarter, depth // 4)),
        in_specs=[scalar] + [whole] * 7,
        out_specs=[whole] * 2,
        scratch_shapes=[
            vmem(total, half, depth), vmem(total, half, depth), vmem(total, half, depth),
            vmem(total, padded2, depth), vmem(total, half, depth), vmem(total, half, depth),
            vmem(total, half, depth), vmem(total, padded2, depth),
            vmem(blocks, quarter, depth), vmem(blocks + 1, quarter, depth), vmem(blocks, padded3, depth),
            vmem(blocks, quarter, depth), vmem(blocks, quarter, depth), vmem(blocks, quarter, depth),
            vmem(blocks + 2, padded3, depth), vmem(4, half, depth), vmem(4, blocks // 2, PAD, depth),
            vmem(layers + 4, padded, depth), vmem(height, depth),
        ],
        compiler_params=pltpu.CompilerParams(vmem_limit_bytes=56 * 2**20),
    )(where, gathered, field, source1, fx, fy, fz, inv)
    return solved, owned


def solution(mesh):
    split = P(("groups", "gx"), None, None)
    return jax.shard_map(
        on_device,
        mesh=mesh,
        in_specs=(split, split, split, P("groups")),
        out_specs=(split, split),
        check_vma=False,
    )
```

time: 347 us -> 85.3 us (0.25)
  starting transfers between devices: 239 us -> 4.38 us
  blocking collectives: 22.4 us -> 0 us
  local copies, waits for them, and re-layouts: 25 us -> 6.39 us
  other arithmetic: 18.3 us -> 0.79 us
  Pallas kernels: 0 us -> 12.4 us
  between operations: 2.61 us -> 14.1 us
  waiting for transfers between devices: 36.1 us -> 47 us
    ppermute x79 -> x2, starting transfers between devices: 239 us -> 4.34 us  [from_behind(): return lax.ppermute(block, 'gx', route)]
    all_gather x0 -> x1, waiting for transfers between devices: none -> 46.9 us  [on_device(): gathered = lax.all_gather(coarse, 'gx', axis=0, tiled=False)]
    ppermute x79 -> x2, waiting for transfers between devices: 36.1 us -> 0.01 us  [from_behind(): return lax.ppermute(block, 'gx', route)]
    all_gather x1 -> x0, blocking collectives: 22.4 us -> none  [on_device(): shard_rows = lax.all_gather(third_fix, 'gx', axis=0, tiled=True)]
    pallas_call x0 -> x2, Pallas kernels: none -> 12.4 us  [the longest x1 10 us: on_device(): pl.pallas_call(coarse_kernel, out_shape=(f32(layers, height, depth), f32(...]
    reshape x9 -> x0, local copies, waits for them, and re-layouts: 11 us -> none  [the longest x3 10.5 us: restrict(): values.reshape(layers // 2, 2, height // 2, 2, depth_cells // 2, 2)]
    reduce_sum x27 -> x0, other arithmetic: 9.5 us -> none  [the longest x7 4.7 us: restrict(): values.reshape(layers // 2, 2, height // 2, 2, depth_cells // 2, 2)]
    another operation x9 -> x0, local copies, waits for them, and re-layouts: 6.25 us -> none  [the longest x4 6.24 us: coarsen(): coeffs[1::2, 0].reshape(layers // 2, height // 2, 2, depth_cells // 2, 2)]
  transfers between devices with their start and end apart: 79 -> 3, of which waited for: 26 -> 1; matrix products, arithmetic and copies ran while one was open for 12% -> 2% of each run, Pallas kernels for 0% -> 0%
where the time goes in v1:
time: 85.3 us; the launch traced here: 85.1 us
  waiting for transfers between devices  47 us (55%)
  between operations  14.1 us (17%)
  Pallas kernels  12.4 us (15%)
  local copies, waits for them, and re-layouts  6.39 us (7%)
  starting transfers between devices  4.38 us (5%)
    all_gather x1, waiting for transfers between devices, on_device(): gathered = lax.all_gather(coarse, 'gx', axis=0, tiled=False)  46.9 us
    pallas_call x1, Pallas kernels, on_device(): pl.pallas_call(coarse_kernel, out_shape=(f32(layers, height, depth), f32(...  10 us
    unnamed x22, local copies, waits for them, and re-layouts  4.8 us
    ppermute x2, starting transfers between devices, from_behind(): return lax.ppermute(block, 'gx', route)  4.34 us
    pallas_call x1, Pallas kernels, on_device(): pl.pallas_call(fine_down_kernel, out_shape=(f32(4, half, depth), f32(laye...  2.44 us
  transfers between devices with their start and end apart: 3, of which 1 were waited for; matrix products, arithmetic and copies ran while one was open for 2% of the time, Pallas kernels for 0%

profile of v1, /device:TPU:0, one launch (start us, length us, event | category | flops | bytes accessed | tf_op | source)
XLA Modules:
  0.0 85.1 jit_solution(8986698307061023794)
XLA Ops:
  7.2 0.0 copy-start.2
  7.2 0.0 copy-start.1
  7.2 0.0 all-gather.3.cloned.1.call-start
  7.2 1.0 %fusion = (f32[3,64,128]{2,1,0:T(8,128)S(1)}, f32[3,64,128]{2,1,0:T(8,128)S(1)}) fusion(f32[4,64,128]{2,1,0:T(8,128)} %source.1), kind=kLoop, calls=%fused_computation.5 | loop fusion | bytes 393216 | tf_op jit(solution)/shard_map/slice | solution.py:490
  8.2 0.0 copy-done.2
  8.3 0.0 copy-done.1
  8.3 0.0 copy-start
  8.3 0.1 pad_maximum_fusion
  8.4 1.3 %collective-permute-start.1 = (f32[11,64,128]{2,1,0:T(8,128)S(1)}, f32[11,64,128]{2,1,0:T(8,128)S(1)}, u32[]{:S(2)}, u32[]{:S(2)}) collective-permute-start(f32[11,64,128]{2,1,0:T(8,128)S(1)} %get-tuple-element.16), channel_id=1, source_target_pairs={{1,0},{2,1},{3,2},{4,3},{5,4},{6,5},{7,6},{8,7},{9,8},{10,9},{11,1... | collective-permute-start | bytes 1081352 | tf_op jit(solution)/shard_map/ppermute | solution.py:17
  9.7 3.1 %collective-permute-start = (f32[11,64,128]{2,1,0:T(8,128)S(1)}, f32[11,64,128]{2,1,0:T(8,128)S(1)}, u32[]{:S(2)}, u32[]{:S(2)}) collective-permute-start(f32[11,64,128]{2,1,0:T(8,128)S(1)} %get-tuple-element.17), channel_id=1, source_target_pairs={{0,1},{1,2},{2,3},{3,4},{4,5},{5,6},{6,7},{7,8},{8,9},{9,10},{10,1... | collective-permute-start | bytes 1081352 | tf_op jit(solution)/shard_map/ppermute | solution.py:17
  12.7 0.0 copy-start.10
  12.7 0.6 copy-done.10
  13.4 0.6 dynamic_slice.3
  14.0 0.7 pad_add_fusion.where_ref
  14.7 0.0 copy-start.9
  14.7 0.0 collective-permute-done.1.from_right
  14.7 0.0 collective-permute-done.from_left
  14.7 0.0 copy-done
  14.7 2.4 %shard_map.59 = (f32[4,32,128]{2,1,0:T(8,128)}, f32[8,64,128]{2,1,0:T(8,128)S(1)}, f32[6,64,128]{2,1,0:T(8,128)S(1)}, f32[7,64,128]{2,1,0:T(8,128)S(1)}, f32[6,8...) custom-call(s32[3]{0:T(128)S(1)} %pad_add_fusion.where_ref, f32[4,64,128]{2,1,0:T(8,128)S(1)} %copy-done.1, ...), custom_call_target="tpu_custom_call" | custom-call | tf_op jit(solution)/shard_map/pallas_call | solution.py:499
  17.1 0.0 copy-done.9
  17.1 0.0 copy-start.3
  17.1 0.7 copy-done.3
  17.9 0.7 copy-done.4
  18.6 0.0 copy-start.5
  18.6 0.7 copy-done.5
  19.3 0.0 copy-start.6
  19.3 0.7 copy-done.6
  19.9 0.7 copy-done.7
  20.6 0.7 copy-done.8
  21.3 0.0 all-gather.3.cloned.1.call-update
  21.3 46.9 %all-gather.3.cloned.1.call-done = f32[64,32,128]{2,1,0:T(8,128)} async-done(((f32[4,32,128]{2,1,0:T(8,128)}), f32[64,32,128]{2,1,0:T(8,128)}) %all-gather.3.cloned.1.call-update) | async-done | bytes 1048592 | tf_op jit(solution)/shard_map/all_gather | solution.py:515
  68.3 10.0 %shard_map.60 = (f32[4,64,128]{2,1,0:T(8,128)}, f32[1,16,32]{2,1,0:T(8,128)}) custom-call(s32[3]{0:T(128)} %copy-done.9, f32[16,4,32,128]{3,2,1,0:T(8,128)} %bitcast.2, f32[8,64,128]{2,1,0:T(8,128)} %copy-done.3, f32[6,64,128]{2,1,0:T(8,128)} %copy-done.6, f32[7,64,128]{2,1,0:T(8,128)} %copy-done.5, f32[6,80,128]{2,1,0:T(8,128)} %copy-done.4, ...), custom_call_target="tpu_custom_call" | custom-call | tf_op jit(solution)/shard_map/pallas_call | solution.py:518
  (3 shorter events, 0.0 us)
Async XLA Ops:
  7.2 1.1 %copy-start.2 = (f32[4,64,128]{2,1,0:T(8,128)S(1)}, f32[4,64,128]{2,1,0:T(8,128)}, u32[]{:S(2)}) copy-start(f32[4,64,128]{2,1,0:T(8,128)} %phase.1) | copy-start | bytes 393220
  7.2 1.1 %copy-start.1 = (f32[4,64,128]{2,1,0:T(8,128)S(1)}, f32[4,64,128]{2,1,0:T(8,128)}, u32[]{:S(2)}) copy-start(f32[4,64,128]{2,1,0:T(8,128)} %iterate.1) | copy-start | bytes 393220
  7.2 61.1 %all-gather.3.cloned.1.call-start = ((), (), s32[]{:S(2)}) async-start(), calls=%async_computation | async-start | bytes 1114112 | tf_op jit(solution)/shard_map/all_gather | solution.py:515
  8.3 6.4 %copy-start = (f32[4,64,128]{2,1,0:T(8,128)S(1)}, f32[4,64,128]{2,1,0:T(8,128)}, u32[]{:S(2)}) copy-start(f32[4,64,128]{2,1,0:T(8,128)} %source.1) | copy-start | bytes 393220
  8.4 6.3 %collective-permute-start.1 = (f32[11,64,128]{2,1,0:T(8,128)S(1)}, f32[11,64,128]{2,1,0:T(8,128)S(1)}, u32[]{:S(2)}, u32[]{:S(2)}) collective-permute-start(f32[11,64,128]{2,1,0:T(8,128)S(1)} %get-tuple-element.16), channel_id=1, source_target_pairs={{1,0},{2,1},{3,2},{4,3},{5,4},{6,5},{7,6},{8,7},{9,8},{10,9},{11,1... | collective-permute-start | bytes 1081352 | tf_op jit(solution)/shard_map/ppermute | solution.py:17
  9.7 5.0 %collective-permute-start = (f32[11,64,128]{2,1,0:T(8,128)S(1)}, f32[11,64,128]{2,1,0:T(8,128)S(1)}, u32[]{:S(2)}, u32[]{:S(2)}) collective-permute-start(f32[11,64,128]{2,1,0:T(8,128)S(1)} %get-tuple-element.17), channel_id=1, source_target_pairs={{0,1},{1,2},{2,3},{3,4},{4,5},{5,6},{6,7},{7,8},{8,9},{9,10},{10,1... | collective-permute-start | bytes 1081352 | tf_op jit(solution)/shard_map/ppermute | solution.py:17
  12.7 0.7 copy-start.10
  14.7 2.5 %copy-start.9 = (s32[3]{0:T(128)}, s32[3]{0:T(128)S(1)}, u32[]{:S(2)}) copy-start(s32[3]{0:T(128)S(1)} %pad_add_fusion.where_ref) | copy-start | bytes 40
  17.1 0.7 copy-start.3
  17.9 0.7 copy-start.4
  18.6 0.7 copy-start.5
  19.3 0.7 copy-start.6
  19.9 0.7 copy-start.7
  20.6 0.7 copy-start.8
Sparse Core Ops, SparseCore 0:
  21.4 46.7 all-gather.2

commit v2 on v1

v2 whole, which is shorter than its diff:
```python
import jax
import jax.numpy as jnp
from jax import lax
from jax.experimental import pallas as pl
from jax.experimental.pallas import tpu as pltpu
from jax.sharding import PartitionSpec as P

STIFFNESS = 100.0
EPSILON = 0.01
COARSE_SWEEPS = 4
PAD = 8


def from_behind(block, distance):
    devices = range(lax.axis_size("gx"))
    route = [(i - distance, i) for i in devices if i - distance in devices]
    return lax.ppermute(block, "gx", route)


def lanes_of(shape):
    return lax.broadcasted_iota(jnp.int32, shape, len(shape) - 1)


def rows_of(shape):
    return lax.broadcasted_iota(jnp.int32, shape, len(shape) - 2)


def ahead(values, step, axis):
    return pltpu.roll(values, values.shape[axis] - step, axis)


def behind(values, step, axis):
    return pltpu.roll(values, step, axis)


def with_partner(values, step, axis):
    index = lax.broadcasted_iota(jnp.int32, values.shape, axis)
    partner = jnp.where((index & step) == 0, ahead(values, step, axis), behind(values, step, axis))
    return values + partner


def even_row_sum(scratch, rows):
    return scratch[pl.ds(0, rows, 2), :] + scratch[pl.ds(1, rows, 2), :]


def edge_kernel(iterate, source, phase, to_left, to_right):
    layers, height, depth = iterate.shape
    row, lane = rows_of((height, depth)), lanes_of((height, depth))
    even_sum = ((row + lane) & 1) == 0
    odd_lane = (lanes_of((height // 2, depth)) & 1) != 0
    cell = []
    for w in range(layers):
        value = phase[w]
        cell.append(STIFFNESS * (value * value + EPSILON))
    for out, near, step in ((to_left, 0, 1), (to_right, layers - 1, -1)):
        inner, far = near + step, near + 2 * step
        here, e = cell[inner], iterate[inner]
        face_near, face_far = 0.5 * (here + cell[near]), 0.5 * (here + cell[far])
        fy = jnp.where(row < height - 1, 0.5 * (here + ahead(here, 1, 0)), 0.0)
        fz = jnp.where(lane < depth - 1, 0.5 * (here + ahead(here, 1, 1)), 0.0)
        fyl, fzl = behind(fy, 1, 0), behind(fz, 1, 1)
        total = face_near * iterate[near] + face_far * iterate[far]
        total = total + fy * ahead(e, 1, 0) + fyl * behind(e, 1, 0)
        total = total + fz * ahead(e, 1, 1) + fzl * behind(e, 1, 1)
        weight = 1.0 + (face_near + face_far + fy + fyl + fz + fzl)
        even = even_sum if inner % 2 == 0 else ~even_sum
        out[:height] = cell[near]
        out[height:2 * height] = here
        out[2 * height:3 * height] = source[near]
        out[3 * height:4 * height] = jnp.where(even, (source[inner] + total) / weight, e)
        out[4 * height:] = odd_cells(iterate.at[near], height // 2, odd_lane if near % 2 == 0 else ~odd_lane)


def odd_cells(ref, rows, first):
    return jnp.where(first, ref[pl.ds(0, rows, 2), :], ref[pl.ds(1, rows, 2), :])


def into_both_rows(ref, values):
    rows = values.shape[0]
    ref[pl.ds(0, rows, 2), :] = values
    ref[pl.ds(1, rows, 2), :] = values


def fine_down_kernel(
    where_ref, iterate, source, phase, from_left, from_right,
    to_left, to_right, field_out, source_out, fx, fy, fz, inv,
    cell, e, fzl, held, pair,
):
    layers, height, depth = iterate.shape
    window = layers + 4
    position, last = where_ref[0], where_ref[1]
    body = pl.ds(PAD, height)
    up, down = pl.ds(PAD + 1, height), pl.ds(PAD - 1, height)
    row, lane = rows_of((height, depth)), lanes_of((height, depth))
    even_sum = ((row + lane) & 1) == 0
    half = height // 2

    def part(ref, k):
        return ref[k * height:(k + 1) * height]

    edge = jnp.zeros((PAD, depth), jnp.float32)
    for w in range(window):
        for padded in (e, fy):
            padded[w, :PAD] = edge
            padded[w, PAD + height:] = edge
        cell[w, PAD + height:] = edge
    for ref, outer, inner in ((from_left, 0, 1), (from_right, window - 1, window - 2)):
        cell[inner, body] = part(ref, 0)
        cell[outer, body] = part(ref, 1)
        source_out[inner] = part(ref, 2)
        e[outer, body] = part(ref, 3)
        into_both_rows(pair.at[0], ref[4 * height:])
        e[inner, body] = pair[0]
    for w in range(layers):
        value = phase[w]
        cell[w + 2, body] = STIFFNESS * (value * value + EPSILON)
        e[w + 2, body] = iterate[w]
        source_out[w + 2] = source[w]
    for w in range(window):
        here = cell[w, body]
        if w < window - 1:
            face = 0.5 * (here + cell[w + 1, body])
            if w == 1:
                face = jnp.where(position > 0, face, 0.0)
            if w == window - 3:
                face = jnp.where(position < last, face, 0.0)
            fx[w] = face
        if 0 < w < window - 1:
            fy[w, body] = jnp.where(row < height - 1, 0.5 * (here + cell[w, up]), 0.0)
            face = jnp.where(lane < depth - 1, 0.5 * (here + ahead(here, 1, 1)), 0.0)
            fz[w] = face
            fzl[w] = behind(face, 1, 1)
    for w in range(1, window - 1):
        weight = fx[w] + fx[w - 1] + fy[w, body] + fy[w, down] + fz[w] + fzl[w]
        inv[w] = 1.0 / (1.0 + weight)

    def neigh(w):
        here = e[w, body]
        total = fx[w] * e[w + 1, body] + fx[w - 1] * e[w - 1, body]
        total = total + fy[w, body] * e[w, up] + fy[w, down] * e[w, down]
        return total + fz[w] * ahead(here, 1, 1) + fzl[w] * behind(here, 1, 1)

    def mask(w, odd):
        return even_sum if (w + odd) % 2 == 0 else ~even_sum

    for w in range(1, window - 1):
        total = source_out[w] + neigh(w)
        if 2 <= w < layers + 2:
            held[w - 2] = total
        e[w, body] = jnp.where(mask(w, 0), total * inv[w], e[w, body])
    for w in range(1, window - 1):
        total = (source_out[w] + neigh(w)) * inv[w]
        e[w, body] = jnp.where(mask(w, 1), total, e[w, body])
        field_out[w] = e[w, body]

    lane = lanes_of((half, depth))
    first_of_two = (lane & 1) == 0

    def residual(w):
        return jnp.where(mask(w, 0), source_out[w] + neigh(w) - held[w - 2], 0.0)

    def slabs(make, reduce_rows, reduce_lanes, start=2):
        found = []
        for t in range(2):
            pair[t] = make(start + 2 * t)
            found.append(reduce_lanes(reduce_rows(pair.at[t])))
        return jnp.where(first_of_two, found[0], found[1])

    def both_rows(scratch):
        return even_row_sum(scratch, half)

    def odd_rows(scratch):
        return scratch[pl.ds(1, half, 2), :]

    def both_lanes(values):
        return with_partner(values, 1, 1)

    def odd_lanes(values):
        return jnp.where(first_of_two, ahead(values, 1, 1), values)

    coarse_source = slabs(lambda w: residual(w) + residual(w + 1), both_rows, both_lanes)
    coarse_fy = slabs(lambda w: fy[w, body] + fy[w + 1, body], odd_rows, both_lanes)
    coarse_fz = slabs(lambda w: fz[w] + fz[w + 1], both_rows, odd_lanes)
    to_left[1] = slabs(lambda w: fx[w + 1], both_rows, both_lanes)
    to_right[1] = slabs(lambda w: fx[w - 1], both_rows, both_lanes)
    for out in (to_left, to_right):
        out[0], out[2], out[3] = coarse_source, coarse_fy, coarse_fz
    odd_lane = ~first_of_two
    for out, w in ((to_left, 3), (to_right, window - 4)):
        pair[0] = e[w, body]
        out[4] = odd_cells(pair.at[0], half, odd_lane if w % 2 == 0 else ~odd_lane)


def neigh2(e2, fx2, fxl2, fy2, fz2, fzl2, first_of_two, tiles):
    half = fx2.shape[1]
    body, up, down = pl.ds(PAD, half), pl.ds(PAD + 1, half), pl.ds(PAD - 1, half)
    needed = range(tiles[0], tiles[-1] + 3)
    here = {j: e2[j, body] for j in needed}
    after = {j: ahead(here[j], 1, 1) for j in needed}
    before = {j: behind(here[j], 1, 1) for j in needed}
    found = []
    for j in tiles:
        k = j + 1
        upper = jnp.where(first_of_two, after[k], before[k + 1])
        lower = jnp.where(first_of_two, after[k - 1], before[k])
        sums = fx2[j] * upper + fxl2[j] * lower
        sums = sums + fy2[j, body] * e2[k, up] + fy2[j, down] * e2[k, down]
        sums = sums + fz2[j] * ahead(here[k], 2, 1) + fzl2[j] * behind(here[k], 2, 1)
        found.append(sums)
    return found


def parities2(half, lanes):
    row, lane = rows_of((half, lanes)), lanes_of((half, lanes))
    return (lane & 1) == 0, ((row + (lane & 1) + (lane >> 1)) & 1) == 0


def group(values):
    return with_partner(with_partner(values, 1, 1), 2, 1)


def middle_down_kernel(
    where_ref, own_left, own_right, from_left, from_right,
    slots, e2_out, s2, fx2, fxl2, fy2, fz2, inv2,
    e2, fzl2, pair,
):
    _, half, lanes = own_left.shape
    quarter = half // 2
    position = where_ref[0]
    first_of_two, even2 = parities2(half, lanes)
    body, down = pl.ds(PAD, half), pl.ds(PAD - 1, half)
    edge = jnp.zeros((PAD, lanes), jnp.float32)
    for j in range(5):
        e2[j] = jnp.zeros((half + 2 * PAD, lanes), jnp.float32)
    for j, ref in enumerate((from_left, own_left, from_right)):
        s2[j] = ref[0]
        fy2[j, :PAD] = edge
        fy2[j, body] = ref[2]
        fy2[j, PAD + half:] = edge
        fz2[j] = ref[3]
        fzl2[j] = behind(ref[3], 2, 1)
    fx2[0] = jnp.where(first_of_two, ahead(from_left[1], 1, 1), behind(own_right[1], 1, 1))
    fx2[1] = own_left[1]
    fx2[2] = from_right[1]
    fxl2[0] = from_left[1]
    fxl2[1] = own_right[1]
    fxl2[2] = jnp.where(first_of_two, ahead(own_left[1], 1, 1), behind(from_right[1], 1, 1))
    for j in range(3):
        weight = fx2[j] + fxl2[j] + fy2[j, body] + fy2[j, down] + fz2[j] + fzl2[j]
        inverse = 1.0 / (8.0 + weight)
        inv2[j] = inverse
        e2[j + 1, body] = jnp.where(even2, s2[j] * inverse, 0.0)

    def neigh(tiles):
        return neigh2(e2, fx2, fxl2, fy2, fz2, fzl2, first_of_two, tiles)

    fresh = [
        jnp.where(even2, e2[j + 1, body], (s2[j] + sums) * inv2[j]) for j, sums in enumerate(neigh((0, 1, 2)))
    ]
    for j in range(3):
        e2[j + 1, body] = fresh[j]
        e2_out[j] = fresh[j]
    pair[0] = jnp.where(even2, neigh((1,))[0], 0.0)
    lane = lanes_of((quarter, lanes))
    odd_layer, odd_depth, item = (lane & 1) != 0, (lane & 2) != 0, lane & 3
    source = group(even_row_sum(pair.at[0], quarter))
    fx = group(jnp.where(odd_layer, even_row_sum(fx2.at[1], quarter), 0.0))
    fy = group(fy2[1, pl.ds(PAD + 1, quarter, 2), :])
    fz = group(jnp.where(odd_depth, even_row_sum(fz2.at[1], quarter), 0.0))
    tile = jnp.where(item == 0, source, jnp.where(item == 1, fx, jnp.where(item == 2, fy, fz)))
    first = (((lane & 1) + (lane >> 1)) & 1) != 0
    pair[0] = jnp.where(first_of_two, fresh[2], fresh[1])
    pair[1] = jnp.where(first_of_two, fresh[1], fresh[0])
    for_left = odd_cells(pair.at[0], quarter, first)
    for_right = odd_cells(pair.at[1], quarter, first)
    for d in range(slots.shape[0]):
        slots[d, 0] = tile
        slots[d, 1] = jnp.where(position < d, for_right, for_left)


class Level:
    def __init__(self, mass, source, faces, row_step, lane_step):
        self.source, self.row_step, self.lane_step = source, row_step, lane_step
        self.fx, self.fy, self.fz = faces
        self.layers, rows, lanes = source.shape
        nothing = jnp.zeros_like(source[:1])
        self.nothing = nothing
        self.fxl = jnp.concatenate([nothing, self.fx[:-1]], 0)
        self.fyl = behind(self.fy, row_step, 1)
        self.fzl = behind(self.fz, lane_step, 2)
        weight = self.fx + self.fxl + self.fy + self.fyl + self.fz + self.fzl
        self.inv = 1.0 / (mass + weight)
        shape = source.shape
        total = lax.broadcasted_iota(jnp.int32, shape, 0)
        total = total + rows_of(shape) // row_step + lanes_of(shape) // lane_step
        self.even = (total & 1) == 0

    def neigh(self, e):
        upper = jnp.concatenate([e[1:], self.nothing], 0)
        lower = jnp.concatenate([self.nothing, e[:-1]], 0)
        total = self.fx * upper + self.fxl * lower
        total = total + self.fy * ahead(e, self.row_step, 1) + self.fyl * behind(e, self.row_step, 1)
        return total + self.fz * ahead(e, self.lane_step, 2) + self.fzl * behind(e, self.lane_step, 2)

    def start(self):
        e = jnp.where(self.even, self.source * self.inv, 0.0)
        return self.odd_update(e)

    def even_update(self, e):
        return jnp.where(self.even, (self.source + self.neigh(e)) * self.inv, e)

    def odd_update(self, e):
        return jnp.where(self.even, e, (self.source + self.neigh(e)) * self.inv)

    def residual(self, e):
        return jnp.where(self.even, self.neigh(e), 0.0)

    def pairs(self, values):
        halves = values.reshape(self.layers // 2, 2, *values.shape[1:])
        return halves[:, 0] + halves[:, 1]

    def coarse_faces(self):
        row_bit = (rows_of(self.fx.shape) & self.row_step) != 0
        lane_bit = (lanes_of(self.fx.shape) & self.lane_step) != 0
        odd_layers = self.fx.reshape(self.layers // 2, 2, *self.fx.shape[1:])[:, 1]
        fx = self.in_plane(odd_layers)
        fy = self.in_plane(self.pairs(jnp.where(row_bit, self.fy, 0.0)))
        fz = self.in_plane(self.pairs(jnp.where(lane_bit, self.fz, 0.0)))
        return fx, fy, fz

    def in_plane(self, values):
        return with_partner(with_partner(values, self.row_step, 1), self.lane_step, 2)

    def restricted(self, values):
        return self.in_plane(self.pairs(values))


def doubled_layers(values):
    layers = values.shape[0]
    both = jnp.concatenate([values[:, None], values[:, None]], 1)
    return both.reshape(2 * layers, *values.shape[1:])


def small_cycle(mass, source, faces, row_step, lane_step, deeper):
    level = Level(mass, source, faces, row_step, lane_step)
    e = level.start()
    if deeper == 0:
        for turn in range(COARSE_SWEEPS - 1):
            e = level.odd_update(level.even_update(e))
        return e
    fix = small_cycle(
        8.0 * mass, level.restricted(level.residual(e)), level.coarse_faces(),
        2 * row_step, 2 * lane_step, deeper - 1,
    )
    e = e + doubled_layers(fix)
    return level.odd_update(level.even_update(e))


def chunked(count, size, body):
    size = min(size, count)
    if count == size:
        body(0)
    else:
        lax.fori_loop(0, count // size, lambda i, c: (body(i * size), c)[1], 0)


def coarse_kernel(
    where_ref, gathered, e2_in, s2, fx2, fxl2, fy2, fz2, inv2,
    field, source, fx_in, fy_in, fz_in, inv_in, from_left, from_right,
    solved, owned,
    s3, fx3, fy3, fz3, fzl3, inv3, e3, pair3, small, e2, fzl2, e1, cor,
):
    blocks, _, quarter, lanes = gathered.shape
    half, height = 2 * quarter, 4 * quarter
    position, last, owner = where_ref[0], where_ref[1], where_ref[2]

    body3, up3, down3 = pl.ds(PAD, quarter), pl.ds(PAD + 1, quarter), pl.ds(PAD - 1, quarter)
    row, lane = rows_of((quarter, lanes)), lanes_of((quarter, lanes))
    parity3 = row + (lane >> 2)
    item = lane & 3
    edge3 = jnp.zeros((quarter + 2 * PAD, lanes), jnp.float32)
    for j in (0, blocks + 1):
        e3[j] = edge3
    fx3[0] = jnp.zeros((quarter, lanes), jnp.float32)

    def unpack(at):
        for i in range(4):
            j = at + i
            tile = gathered[j, 0]
            moved = {0: tile}
            for step in (1, 2, 3):
                moved[step] = ahead(tile, step, 1)
                moved[-step] = behind(tile, step, 1)
            spread = []
            for k in range(4):
                value = moved[k]
                for slot in (1, 2, 3):
                    value = jnp.where(item == slot, moved[k - slot], value)
                spread.append(value)
            s3[j] = spread[0]
            fx3[j + 1] = spread[1]
            fy3[j] = edge3
            fy3[j, body3] = spread[2]
            fz3[j] = spread[3]
            fzl3[j] = behind(spread[3], 4, 1)

    chunked(blocks, 4, unpack)

    def is_even3(j):
        return ((parity3 + j) & 1) == 0

    def weights3(at):
        for i in range(4):
            j = at + i
            weight = fx3[j + 1] + fx3[j] + fy3[j, body3] + fy3[j, down3] + fz3[j] + fzl3[j]
            inverse = 1.0 / (64.0 + weight)
            inv3[j] = inverse
            e3[j + 1] = edge3
            e3[j + 1, body3] = jnp.where(is_even3(j), s3[j] * inverse, 0.0)

    chunked(blocks, 4, weights3)

    def neigh3(j):
        here = e3[j + 1, body3]
        sums = fx3[j + 1] * e3[j + 2, body3] + fx3[j] * e3[j, body3]
        sums = sums + fy3[j, body3] * e3[j + 1, up3] + fy3[j, down3] * e3[j + 1, down3]
        return here, sums + fz3[j] * ahead(here, 4, 1) + fzl3[j] * behind(here, 4, 1)

    def update3(at, count, even):
        fresh = []
        for i in range(count):
            j = at + i
            here, sums = neigh3(j)
            value = (s3[j] + sums) * inv3[j]
            where = is_even3(j)
            fresh.append(jnp.where(where, value, here) if even else jnp.where(where, here, value))
        for i in range(count):
            e3[at + i + 1, body3] = fresh[i]

    chunked(blocks, 8, lambda at: update3(at, 8, False))

    def restrict3(at):
        for i in range(0, 4, 2):
            j = at + i
            parts = []
            for k in (j, j + 1):
                _, sums = neigh3(k)
                parts.append(jnp.where(is_even3(k), sums, 0.0))
            pair3[i, :quarter] = parts[0] + parts[1]
            pair3[i + 1, :quarter] = fz3[j] + fz3[j + 1]
        for i in range(0, 4, 2):
            j = at + i
            out = (at + i) // 2
            small[0, out] = with_partner(even_row_sum(pair3.at[i], PAD), 4, 1)
            fxs = fx3[j + 2, pl.ds(0, PAD, 2), :] + fx3[j + 2, pl.ds(1, PAD, 2), :]
            small[1, out] = with_partner(fxs, 4, 1)
            fys = fy3[j, pl.ds(PAD + 1, PAD, 2), :] + fy3[j + 1, pl.ds(PAD + 1, PAD, 2), :]
            small[2, out] = with_partner(fys, 4, 1)
            fzs = even_row_sum(pair3.at[i + 1], PAD)
            odd = (lanes_of((PAD, lanes)) & 4) != 0
            small[3, out] = with_partner(jnp.where(odd, fzs, 0.0), 4, 1)

    chunked(blocks, 4, restrict3)

    small[0] = small_cycle(512.0, small[0], (small[1], small[2], small[3]), 1, 8, 2)

    def prolong3(at):
        for i in range(4):
            j = at + i
            fix = small[0, j // 2]
            pair3[i, pl.ds(0, PAD, 2), :] = fix
            pair3[i, pl.ds(1, PAD, 2), :] = fix
        for i in range(4):
            j = at + i
            e3[j + 1, body3] = e3[j + 1, body3] + pair3[i, :quarter]

    chunked(blocks, 4, prolong3)
    chunked(blocks, 8, lambda at: update3(at, 8, True))
    chunked(blocks, 8, lambda at: update3(at, 8, False))

    wide, narrow = lanes_of((lanes, lanes)), rows_of((lanes, lanes))
    take = jnp.where(narrow == 4 * wide, 1.0, 0.0)
    block = jnp.dot(
        e3[owner + 1, body3], take, precision=lax.Precision.HIGHEST, preferred_element_type=jnp.float32
    )
    owned[0] = block[:, : lanes // 4]

    first_of_two, even2 = parities2(half, lanes)
    body2 = pl.ds(PAD, half)
    edge = jnp.zeros((PAD, lanes), jnp.float32)
    left = gathered[jnp.maximum(position - 1, 0), 1]
    right = gathered[jnp.minimum(position + 1, last), 1]
    into_both_rows(pair3.at[0], left)
    into_both_rows(pair3.at[1], right)
    left, right = pair3[0], pair3[1]
    before = (
        left, jnp.where(first_of_two, left, e2_in[0]), e2_in[1], jnp.where(first_of_two, e2_in[2], right), right
    )
    for k in range(5):
        third = jnp.clip(position + k - 1, 1, blocks)
        into_both_rows(pair3.at[k % 4], e3[third, body3])
        e2[k, :PAD] = edge
        e2[k, PAD + half:] = edge
        e2[k, body2] = before[k] + pair3[k % 4]
    for j in range(3):
        fzl2[j] = behind(fz2[j], 2, 1)
    for even in (True, False):
        fresh = []
        for j, sums in enumerate(neigh2(e2, fx2, fxl2, fy2, fz2, fzl2, first_of_two, (0, 1, 2))):
            value, here = (s2[j] + sums) * inv2[j], e2[j + 1, body2]
            fresh.append(jnp.where(even2, value, here) if even else jnp.where(even2, here, value))
        for j in range(3):
            e2[j + 1, body2] = fresh[j]

    body1, up1, down1 = pl.ds(PAD, height), pl.ds(PAD + 1, height), pl.ds(PAD - 1, height)
    rows, lane = rows_of((height, lanes)), lanes_of((height, lanes))
    even_sum = ((rows + lane) & 1) == 0
    count = e1.shape[0]
    for w in range(0, count, 2):
        coarse_layer = w // 2 - 1
        packed = e2[2 + coarse_layer // 2, body2]
        if coarse_layer % 2 == 0:
            plain = jnp.where(first_of_two, packed, behind(packed, 1, 1))
        else:
            plain = jnp.where(first_of_two, ahead(packed, 1, 1), packed)
        into_both_rows(cor.at[0], plain)
        fix = cor[0]
        for v in (w, w + 1):
            e1[v, :PAD] = edge
            e1[v, PAD + height:] = edge
            if v in (0, count - 1):
                into_both_rows(cor.at[1], (from_left if v == 0 else from_right)[4])
                e1[v, body1] = cor[1] + fix
            else:
                e1[v, body1] = field[v] + fix

    def smoothed1(w, even):
        here = e1[w, body1]
        face = fz_in[w]
        sums = fx_in[w] * e1[w + 1, body1] + fx_in[w - 1] * e1[w - 1, body1]
        sums = sums + fy_in[w, body1] * e1[w, up1] + fy_in[w, down1] * e1[w, down1]
        sums = sums + face * ahead(here, 1, 1) + behind(face, 1, 1) * behind(here, 1, 1)
        value = (source[w] + sums) * inv_in[w]
        keep = even_sum if (w + even) % 2 == 0 else ~even_sum
        return jnp.where(keep, here, value)

    for w in range(1, count - 1):
        e1[w, body1] = smoothed1(w, 1)
    for w in range(2, count - 2):
        solved[w - 2] = smoothed1(w, 0)


def f32(*shape):
    return jax.ShapeDtypeStruct(shape, jnp.float32)


def vmem(*shape):
    return pltpu.VMEM(shape, jnp.float32)


def call(kernel, outs, scratch, scalars, operands):
    def size(shape):
        count = 4
        for extent in shape:
            count *= extent
        return count

    asked = 8 * 2**20 + sum(size(s.shape) for s in scratch) + sum(size(o.shape) for o in outs)
    asked += sum(size(o.shape) for o in operands)
    return pl.pallas_call(
        kernel,
        out_shape=tuple(outs),
        in_specs=[pl.BlockSpec(memory_space=pltpu.SMEM)] * len(scalars)
        + [pl.BlockSpec(memory_space=pltpu.VMEM)] * len(operands),
        out_specs=tuple([pl.BlockSpec(memory_space=pltpu.VMEM)] * len(outs)),
        scratch_shapes=scratch,
        compiler_params=pltpu.CompilerParams(vmem_limit_bytes=asked),
    )(*scalars, *operands)


def on_device(iterate, source, phase_field, block_owner):
    layers, height, depth = iterate.shape
    half, quarter = height // 2, height // 4
    blocks = lax.axis_size("gx")
    window = layers + 4
    padded, padded2, padded3 = height + 2 * PAD, half + 2 * PAD, quarter + 2 * PAD
    to_left, to_right = call(
        edge_kernel, [f32(4 * height + half, depth)] * 2, [], (), (iterate, source, phase_field)
    )
    halos = from_behind(to_right, 1), from_behind(to_left, -1)
    position = lax.axis_index("gx")
    where = jnp.stack([position, jnp.full_like(position, blocks - 1), block_owner[position]]).astype(jnp.int32)
    plain = f32(window, height, depth)
    to_left, to_right, *fine = call(
        fine_down_kernel,
        [f32(5, half, depth)] * 2 + [plain, plain, plain, f32(window, padded, depth), plain, plain],
        [
            vmem(window, padded, depth), vmem(window, padded, depth), vmem(window, height, depth),
            vmem(layers, height, depth), vmem(2, height, depth),
        ],
        (where,), (iterate, source, phase_field, *halos),
    )
    halos = from_behind(to_right, 1), from_behind(to_left, -1)
    plain = f32(3, half, depth)
    slots, *middle = call(
        middle_down_kernel,
        [f32(blocks, 2, quarter, depth), plain, plain, plain, plain, f32(3, padded2, depth), plain, plain],
        [vmem(5, padded2, depth), vmem(3, half, depth), vmem(2, half, depth)],
        (where,), (to_left, to_right, *halos),
    )
    gathered = lax.all_to_all(slots, "gx", 0, 0, tiled=True)
    solved, owned = call(
        coarse_kernel,
        [f32(layers, height, depth), f32(1, quarter, depth // 4)],
        [
            vmem(blocks, quarter, depth), vmem(blocks + 1, quarter, depth), vmem(blocks, padded3, depth),
            vmem(blocks, quarter, depth), vmem(blocks, quarter, depth), vmem(blocks, quarter, depth),
            vmem(blocks + 2, padded3, depth), vmem(4, half, depth), vmem(4, blocks // 2, PAD, depth),
            vmem(5, padded2, depth), vmem(3, half, depth), vmem(window, padded, depth), vmem(2, height, depth),
        ],
        (where,), (gathered, *middle, *fine, *halos),
    )
    return solved, owned


def solution(mesh):
    split = P(("groups", "gx"), None, None)
    return jax.shard_map(
        on_device,
        mesh=mesh,
        in_specs=(split, split, split, P("groups")),
        out_specs=(split, split),
        check_vma=False,
    )
```

time: 85.3 us -> 48.6 us (0.57)
  waiting for transfers between devices: 47 us -> 2.99 us
  blocking collectives: 0 us -> 20.6 us
  between operations: 14.1 us -> 0.72 us
  starting transfers between devices: 4.38 us -> 11.2 us
  Pallas kernels: 12.4 us -> 8.11 us
  local copies, waits for them, and re-layouts: 6.39 us -> 3.95 us
    all_gather x1 -> x0, waiting for transfers between devices: 46.9 us -> none  [on_device(): gathered = lax.all_gather(coarse, 'gx', axis=0, tiled=False)]
    all_to_all x0 -> x1, blocking collectives: none -> 20.6 us  [on_device(): gathered = lax.all_to_all(slots, 'gx', 0, 0, tiled=True)]
    ppermute x2 -> x4, starting transfers between devices: 4.34 us -> 11.2 us  [from_behind(): return lax.ppermute(block, 'gx', route)]
    pallas_call x2 -> x4, Pallas kernels: 12.4 us -> 8.11 us  [call(): pl.pallas_call(kernel, out_shape=tuple(outs), in_specs=[pl.BlockSpec(memo...]
    ppermute x2 -> x4, waiting for transfers between devices: 0.01 us -> 2.99 us  [from_behind(): return lax.ppermute(block, 'gx', route)]
    unnamed x22 -> x14, local copies, waits for them, and re-layouts: 4.8 us -> 3.37 us
    slice x1 -> x0, local copies, waits for them, and re-layouts: 1.01 us -> none  [on_device(): to_left = jnp.concatenate([iterate, source[:-1], phase_field], 0)]
  transfers between devices with their start and end apart: 3 -> 4, of which waited for: 1 -> 2; matrix products, arithmetic and copies ran while one was open for 2% -> 3% of each run, Pallas kernels for 0% -> 0%
where the time goes in v2:
time: 48.6 us; the launch traced here: 48.3 us
  blocking collectives  20.6 us (42%)
  starting transfers between devices  11.2 us (23%)
  Pallas kernels  8.11 us (17%)
  local copies, waits for them, and re-layouts  3.95 us (8%)
  waiting for transfers between devices  2.99 us (6%)
  other arithmetic  0.72 us (1%)
  between operations  0.72 us (1%)
    all_to_all x1, blocking collectives, on_device(): gathered = lax.all_to_all(slots, 'gx', 0, 0, tiled=True)  20.6 us
    ppermute x4, starting transfers between devices, from_behind(): return lax.ppermute(block, 'gx', route)  11.2 us
    pallas_call x4, Pallas kernels, call(): pl.pallas_call(kernel, out_shape=tuple(outs), in_specs=[pl.BlockSpec(memo...  8.11 us
    unnamed x14, local copies, waits for them, and re-layouts  3.37 us
    ppermute x4, waiting for transfers between devices, from_behind(): return lax.ppermute(block, 'gx', route)  2.99 us
  transfers between devices with their start and end apart: 4, of which 2 were waited for; matrix products, arithmetic and copies ran while one was open for 3% of the time, Pallas kernels for 0%

profile of v2, /device:TPU:0, one launch (start us, length us, event | category | flops | bytes accessed | tf_op | source)
XLA Modules:
  0.0 48.3 jit_solution(16772256301392302186)
XLA Ops:
  0.6 0.0 copy-start
  0.6 0.9 %copy-done = f32[4,64,128]{2,1,0:T(8,128)S(1)} copy-done((f32[4,64,128]{2,1,0:T(8,128)S(1)}, f32[4,64,128]{2,1,0:T(8,128)}, u32[]{:S(2)}) %copy-start) | copy-done | bytes 131096
  1.5 0.0 copy-start.2
  1.5 0.9 %copy-done.2 = f32[4,64,128]{2,1,0:T(8,128)S(1)} copy-done((f32[4,64,128]{2,1,0:T(8,128)S(1)}, f32[4,64,128]{2,1,0:T(8,128)}, u32[]{:S(2)}) %copy-start.2) | copy-done | bytes 131096
  2.4 0.0 copy-start.4
  2.4 0.9 %copy-done.4 = f32[4,64,128]{2,1,0:T(8,128)S(1)} copy-done((f32[4,64,128]{2,1,0:T(8,128)S(1)}, f32[4,64,128]{2,1,0:T(8,128)}, u32[]{:S(2)}) %copy-start.4) | copy-done | bytes 131096
  3.3 0.0 copy-start.1
  3.3 0.0 copy-start.3
  3.3 0.0 copy-start.5
  3.4 0.2 shard_map.59
  3.5 2.4 %collective-permute-start = (f32[288,128]{1,0:T(8,128)S(1)}, f32[288,128]{1,0:T(8,128)S(1)}, u32[]{:S(2)}, u32[]{:S(2)}) collective-permute-start(f32[288,128]{1,0:T(8,128)S(1)} %get-tuple-element.20), channel_id=1, source_target_pairs={{0,1},{1,2},{2,3},{3,4},{4,5},{5,6},{6,7},{7,8},{8,9},{9,10},{10,1... | collective-permute-start | bytes 442376 | tf_op jit(solution)/shard_map/ppermute | solution.py:17
  5.9 1.3 %collective-permute-start.1 = (f32[288,128]{1,0:T(8,128)S(1)}, f32[288,128]{1,0:T(8,128)S(1)}, u32[]{:S(2)}, u32[]{:S(2)}) collective-permute-start(f32[288,128]{1,0:T(8,128)S(1)} %get-tuple-element.21), channel_id=1, source_target_pairs={{1,0},{2,1},{3,2},{4,3},{5,4},{6,5},{7,6},{8,7},{9,8},{10,9},{11,1... | collective-permute-start | bytes 442376 | tf_op jit(solution)/shard_map/ppermute | solution.py:17
  7.2 0.0 copy-start.6
  7.2 0.6 %copy-done.6 = s32[16]{0:T(128)S(1)} copy-done((s32[16]{0:T(128)S(1)}, s32[16]{0:T(128)}, u32[]{:S(2)}) %copy-start.6) | copy-done | bytes 88
  7.9 0.6 %dynamic_slice.3 = s32[1]{0:T(128)} dynamic-slice(s32[16]{0:T(128)S(1)} %copy-done.6, s32[]{:T(128)S(6)} %select_n.3), dynamic_slice_sizes={1} | dynamic-slice | bytes 12 | tf_op jit(solution)/shard_map/dynamic_slice | solution.py:592
  8.4 0.7 %pad_add_fusion.where_ref = s32[3]{0:T(128)S(1)} fusion(s32[1]{0:T(128)} %dynamic_slice.3, s32[1]{0:T(128)} %constant.1.clone.1, s32[1]{0:T(128)} %bitcast), kind=kLoop, calls=%fused_computation | loop fusion | flops 6 | bytes 24 | tf_op jit(solution)/shard_map/stack | solution.py:592
  9.2 0.0 collective-permute-done.from_left
  9.2 2.1 %collective-permute-done.1.from_right = f32[288,128]{1,0:T(8,128)S(1)} collective-permute-done((f32[288,128]{1,0:T(8,128)S(1)}, f32[288,128]{1,0:T(8,128)S(1)}, u32[]{:S(2)}, u32[]{:S(2)}) %collective-permute-start.1) | collective-permute-done | bytes 147488 | tf_op jit(solution)/shard_map/ppermute | solution.py:17
  11.3 0.0 copy-done.1
  11.3 0.0 copy-done.3
  11.3 0.0 copy-done.5
  11.3 1.4 %shard_map.60 = (f32[5,32,128]{2,1,0:T(8,128)S(1)}, f32[5,32,128]{2,1,0:T(8,128)S(1)}, f32[8,64,128]{2,1,0:T(8,128)S(1)}, f32[8,64,128]{2,1,0:T(8,128)S(1)}, f32...) custom-call(s32[3]{0:T(128)S(1)} %pad_add_fusion.where_ref, ...), custom_call_target="tpu_custom_call" | custom-call | tf_op jit(solution)/shard_map/pallas_call | solution.py:570
  12.7 1.3 %collective-permute-start.3 = (f32[5,32,128]{2,1,0:T(8,128)S(1)}, f32[5,32,128]{2,1,0:T(8,128)S(1)}, u32[]{:S(2)}, u32[]{:S(2)}) collective-permute-start(f32[5,32,128]{2,1,0:T(8,128)S(1)} %get-tuple-element.22.own_left), channel_id=1, source_target_pairs={{1,0},{2,1},{3,2},{4,3},{5,4},{6,5},{7,6},{8,7},{9,8},{10,9},{11,1... | collective-permute-start | bytes 245768 | tf_op jit(solution)/shard_map/ppermute | solution.py:17
  14.0 6.2 %collective-permute-start.2 = (f32[5,32,128]{2,1,0:T(8,128)S(1)}, f32[5,32,128]{2,1,0:T(8,128)S(1)}, u32[]{:S(2)}, u32[]{:S(2)}) collective-permute-start(f32[5,32,128]{2,1,0:T(8,128)S(1)} %get-tuple-element.23.own_right), channel_id=1, source_target_pairs={{0,1},{1,2},{2,3},{3,4},{4,5},{5,6},{6,7},{7,8},{8,9},{9,10},{10,1... | collective-permute-start | bytes 245768 | tf_op jit(solution)/shard_map/ppermute | solution.py:17
  20.2 0.0 collective-permute-done.3.from_right
  20.3 0.9 %collective-permute-done.2.from_left = f32[5,32,128]{2,1,0:T(8,128)S(1)} collective-permute-done((f32[5,32,128]{2,1,0:T(8,128)S(1)}, f32[5,32,128]{2,1,0:T(8,128)S(1)}, u32[]{:S(2)}, u32[]{:S(2)}) %collective-permute-start.2) | collective-permute-done | bytes 81952 | tf_op jit(solution)/shard_map/ppermute | solution.py:17
  21.1 1.0 %shard_map.61 = (f32[16,2,16,128]{3,2,1,0:T(8,128)S(1)}, f32[3,32,128]{2,1,0:T(8,128)S(1)}, f32[3,32,128]{2,1,0:T(8,128)S(1)}, f32[3,32,128]{2,1,0:T(8,128)S(1)}...) custom-call(s32[3]{0:T(128)S(1)} %pad_add_fusion.where_ref, ...), custom_call_target="tpu_custom_call" | custom-call | tf_op jit(solution)/shard_map/pallas_call | solution.py:570
  22.2 20.6 %all_to_all.5.gathered = f32[16,2,16,128]{3,2,1,0:T(8,128)S(1)} all-to-all(f32[16,2,16,128]{3,2,1,0:T(8,128)S(1)} %get-tuple-element.24), channel_id=1, replica_groups=mesh['groups'=2,'gx'=16] {'gx'}, dimensions={0} | all-to-all | bytes 524288 | tf_op jit(solution)/shard_map/all_to_all | solution.py:611
  42.8 5.5 %shard_map.62 = (f32[4,64,128]{2,1,0:T(8,128)}, f32[1,16,32]{2,1,0:T(8,128)}) custom-call(s32[3]{0:T(128)S(1)} %pad_add_fusion.where_ref, f32[16,2,16,128]{3,2,1,0:T(8,128)S(1)} %all_to_all.5.gathered, f32[3,32,128]{2,1,0:T(8,128)S(1)} %get-tuple-element.25.e2_in, f32[3,32,128]{2,1,0:T(8,128)S(1)} %get-tuple-element.26.s2, ...), custom_call_target="tpu_custom_call" | custom-call | tf_op jit(solution)/shard_map/pallas_call | solution.py:570
Async XLA Ops:
  0.6 0.9 %copy-start = (f32[4,64,128]{2,1,0:T(8,128)S(1)}, f32[4,64,128]{2,1,0:T(8,128)}, u32[]{:S(2)}) copy-start(f32[4,64,128]{2,1,0:T(8,128)} %iterate.3) | copy-start | bytes 393220
  1.5 0.9 %copy-start.2 = (f32[4,64,128]{2,1,0:T(8,128)S(1)}, f32[4,64,128]{2,1,0:T(8,128)}, u32[]{:S(2)}) copy-start(f32[4,64,128]{2,1,0:T(8,128)} %source.3) | copy-start | bytes 393220
  2.4 0.9 %copy-start.4 = (f32[4,64,128]{2,1,0:T(8,128)S(1)}, f32[4,64,128]{2,1,0:T(8,128)}, u32[]{:S(2)}) copy-start(f32[4,64,128]{2,1,0:T(8,128)} %phase.3) | copy-start | bytes 393220
  3.3 7.9 %copy-start.1 = (f32[4,64,128]{2,1,0:T(8,128)S(1)}, f32[4,64,128]{2,1,0:T(8,128)}, u32[]{:S(2)}) copy-start(f32[4,64,128]{2,1,0:T(8,128)} %iterate.3) | copy-start | bytes 393220
  3.3 7.9 %copy-start.3 = (f32[4,64,128]{2,1,0:T(8,128)S(1)}, f32[4,64,128]{2,1,0:T(8,128)}, u32[]{:S(2)}) copy-start(f32[4,64,128]{2,1,0:T(8,128)} %source.3) | copy-start | bytes 393220
  3.3 7.9 %copy-start.5 = (f32[4,64,128]{2,1,0:T(8,128)S(1)}, f32[4,64,128]{2,1,0:T(8,128)}, u32[]{:S(2)}) copy-start(f32[4,64,128]{2,1,0:T(8,128)} %phase.3) | copy-start | bytes 393220
  3.5 5.6 %collective-permute-start = (f32[288,128]{1,0:T(8,128)S(1)}, f32[288,128]{1,0:T(8,128)S(1)}, u32[]{:S(2)}, u32[]{:S(2)}) collective-permute-start(f32[288,128]{1,0:T(8,128)S(1)} %get-tuple-element.20), channel_id=1, source_target_pairs={{0,1},{1,2},{2,3},{3,4},{4,5},{5,6},{6,7},{7,8},{8,9},{9,10},{10,1... | collective-permute-start | bytes 442376 | tf_op jit(solution)/shard_map/ppermute | solution.py:17
  5.9 5.4 %collective-permute-start.1 = (f32[288,128]{1,0:T(8,128)S(1)}, f32[288,128]{1,0:T(8,128)S(1)}, u32[]{:S(2)}, u32[]{:S(2)}) collective-permute-start(f32[288,128]{1,0:T(8,128)S(1)} %get-tuple-element.21), channel_id=1, source_target_pairs={{1,0},{2,1},{3,2},{4,3},{5,4},{6,5},{7,6},{8,7},{9,8},{10,9},{11,1... | collective-permute-start | bytes 442376 | tf_op jit(solution)/shard_map/ppermute | solution.py:17
  7.2 0.7 %copy-start.6 = (s32[16]{0:T(128)S(1)}, s32[16]{0:T(128)}, u32[]{:S(2)}) copy-start(s32[16]{0:T(128)} %param.7) | copy-start | bytes 196
  12.7 7.5 %collective-permute-start.3 = (f32[5,32,128]{2,1,0:T(8,128)S(1)}, f32[5,32,128]{2,1,0:T(8,128)S(1)}, u32[]{:S(2)}, u32[]{:S(2)}) collective-permute-start(f32[5,32,128]{2,1,0:T(8,128)S(1)} %get-tuple-element.22.own_left), channel_id=1, source_target_pairs={{1,0},{2,1},{3,2},{4,3},{5,4},{6,5},{7,6},{8,7},{9,8},{10,9},{11,1... | collective-permute-start | bytes 245768 | tf_op jit(solution)/shard_map/ppermute | solution.py:17
  14.0 7.1 %collective-permute-start.2 = (f32[5,32,128]{2,1,0:T(8,128)S(1)}, f32[5,32,128]{2,1,0:T(8,128)S(1)}, u32[]{:S(2)}, u32[]{:S(2)}) collective-permute-start(f32[5,32,128]{2,1,0:T(8,128)S(1)} %get-tuple-element.23.own_right), channel_id=1, source_target_pairs={{0,1},{1,2},{2,3},{3,4},{4,5},{5,6},{6,7},{7,8},{8,9},{9,10},{10,1... | collective-permute-start | bytes 245768 | tf_op jit(solution)/shard_map/ppermute | solution.py:17

commit v3 on v2

--- a/solution.py
+++ b/solution.py
@@ -11,10 +11,32 @@
 PAD = 8
 
 
-def from_behind(block, distance):
-    devices = range(lax.axis_size("gx"))
-    route = [(i - distance, i) for i in devices if i - distance in devices]
-    return lax.ppermute(block, "gx", route)
+def swapped(across, within):
+    count = lax.axis_size("gx")
+    chips = [(i, i + 1 if i % 2 else i - 1) for i in range(1, count - 1)]
+    cores = [(i, i ^ 1) for i in range(count)]
+    return lax.ppermute(across, "gx", chips), lax.ppermute(within, "gx", cores)
+
+
+def by_side(across, within):
+    on_left = lax.axis_index("gx") % 2 == 0
+    return jnp.where(on_left, across, within), jnp.where(on_left, within, across)
+
+
+def store_by_side(across, within, pieces):
+    on_left = lax.axis_index("gx") % 2 == 0
+
+    @pl.when(on_left)
+    def _():
+        for index, left, right in pieces:
+            across[index] = left
+            within[index] = right
+
+    @pl.when(jnp.logical_not(on_left))
+    def _():
+        for index, left, right in pieces:
+            across[index] = right
+            within[index] = left
 
 
 def lanes_of(shape):
@@ -43,7 +65,13 @@
     return scratch[pl.ds(0, rows, 2), :] + scratch[pl.ds(1, rows, 2), :]
 
 
-def edge_kernel(iterate, source, phase, to_left, to_right):
+def three_parts(ref):
+    third = ref.shape[0] // 3
+    return [ref.at[pl.ds(k * third, third)] for k in range(3)]
+
+
+def edge_kernel(inputs, across, within):
+    iterate, source, phase = three_parts(inputs)
     layers, height, depth = iterate.shape
     row, lane = rows_of((height, depth)), lanes_of((height, depth))
     even_sum = ((row + lane) & 1) == 0
@@ -52,7 +80,8 @@
     for w in range(layers):
         value = phase[w]
         cell.append(STIFFNESS * (value * value + EPSILON))
-    for out, near, step in ((to_left, 0, 1), (to_right, layers - 1, -1)):
+    sides = []
+    for near, step in ((0, 1), (layers - 1, -1)):
         inner, far = near + step, near + 2 * step
         here, e = cell[inner], iterate[inner]
         face_near, face_far = 0.5 * (here + cell[near]), 0.5 * (here + cell[far])
@@ -64,11 +93,11 @@
         total = total + fz * ahead(e, 1, 1) + fzl * behind(e, 1, 1)
         weight = 1.0 + (face_near + face_far + fy + fyl + fz + fzl)
         even = even_sum if inner % 2 == 0 else ~even_sum
-        out[:height] = cell[near]
-        out[height:2 * height] = here
-        out[2 * height:3 * height] = source[near]
-        out[3 * height:4 * height] = jnp.where(even, (source[inner] + total) / weight, e)
-        out[4 * height:] = odd_cells(iterate.at[near], height // 2, odd_lane if near % 2 == 0 else ~odd_lane)
+        border = odd_cells(iterate.at[near], height // 2, odd_lane if near % 2 == 0 else ~odd_lane)
+        updated = jnp.where(even, (source[inner] + total) / weight, e)
+        sides.append((cell[near], here, source[near], updated, border))
+    places = [pl.ds(k * height, height) for k in range(4)] + [pl.ds(4 * height, height // 2)]
+    store_by_side(across, within, list(zip(places, *sides)))
 
 
 def odd_cells(ref, rows, first):
@@ -82,13 +111,14 @@
 
 
 def fine_down_kernel(
-    where_ref, iterate, source, phase, from_left, from_right,
-    to_left, to_right, field_out, source_out, fx, fy, fz, inv,
+    inputs, across_in, within_in,
+    across, within, fx2_out, field_out, source_out, fx, fy, fz, inv,
     cell, e, fzl, held, pair,
 ):
+    iterate, source, phase = three_parts(inputs)
     layers, height, depth = iterate.shape
     window = layers + 4
-    position, last = where_ref[0], where_ref[1]
+    position, last = lax.axis_index("gx"), lax.axis_size("gx") - 1
     body = pl.ds(PAD, height)
     up, down = pl.ds(PAD + 1, height), pl.ds(PAD - 1, height)
     row, lane = rows_of((height, depth)), lanes_of((height, depth))
@@ -104,13 +134,15 @@
             padded[w, :PAD] = edge
             padded[w, PAD + height:] = edge
         cell[w, PAD + height:] = edge
-    for ref, outer, inner in ((from_left, 0, 1), (from_right, window - 1, window - 2)):
-        cell[inner, body] = part(ref, 0)
-        cell[outer, body] = part(ref, 1)
-        source_out[inner] = part(ref, 2)
-        e[outer, body] = part(ref, 3)
-        into_both_rows(pair.at[0], ref[4 * height:])
-        e[inner, body] = pair[0]
+    halos = [by_side(part(across_in, k), part(within_in, k)) for k in range(4)]
+    borders = by_side(across_in[4 * height:], within_in[4 * height:])
+    for side, outer, inner in ((0, 0, 1), (1, window - 1, window - 2)):
+        cell[inner, body] = halos[0][side]
+        cell[outer, body] = halos[1][side]
+        source_out[inner] = halos[2][side]
+        e[outer, body] = halos[3][side]
+        into_both_rows(pair.at[side], borders[side])
+        e[inner, body] = pair[side]
     for w in range(layers):
         value = phase[w]
         cell[w + 2, body] = STIFFNESS * (value * value + EPSILON)
@@ -181,14 +213,16 @@
     coarse_source = slabs(lambda w: residual(w) + residual(w + 1), both_rows, both_lanes)
     coarse_fy = slabs(lambda w: fy[w, body] + fy[w + 1, body], odd_rows, both_lanes)
     coarse_fz = slabs(lambda w: fz[w] + fz[w + 1], both_rows, odd_lanes)
-    to_left[1] = slabs(lambda w: fx[w + 1], both_rows, both_lanes)
-    to_right[1] = slabs(lambda w: fx[w - 1], both_rows, both_lanes)
-    for out in (to_left, to_right):
-        out[0], out[2], out[3] = coarse_source, coarse_fy, coarse_fz
-    odd_lane = ~first_of_two
-    for out, w in ((to_left, 3), (to_right, window - 4)):
-        pair[0] = e[w, body]
-        out[4] = odd_cells(pair.at[0], half, odd_lane if w % 2 == 0 else ~odd_lane)
+    left_fx = slabs(lambda w: fx[w + 1], both_rows, both_lanes)
+    right_fx = slabs(lambda w: fx[w - 1], both_rows, both_lanes)
+    fx2_out[0], fx2_out[1] = left_fx, right_fx
+    borders = []
+    for t, w in enumerate((3, window - 4)):
+        pair[t] = e[w, body]
+        borders.append(odd_cells(pair.at[t], half, ~first_of_two if w % 2 == 0 else first_of_two))
+    pieces = [(0, coarse_source), (2, coarse_fy), (3, coarse_fz)]
+    pieces = [(k, value, value) for k, value in pieces]
+    store_by_side(across, within, pieces + [(1, left_fx, right_fx), (4, *borders)])
 
 
 def neigh2(e2, fx2, fxl2, fy2, fz2, fzl2, first_of_two, tiles):
@@ -220,31 +254,36 @@
 
 
 def middle_down_kernel(
-    where_ref, own_left, own_right, from_left, from_right,
+    own, own_fx, across_in, within_in,
     slots, e2_out, s2, fx2, fxl2, fy2, fz2, inv2,
     e2, fzl2, pair,
 ):
-    _, half, lanes = own_left.shape
+    _, half, lanes = own.shape
     quarter = half // 2
-    position = where_ref[0]
+    position = lax.axis_index("gx")
     first_of_two, even2 = parities2(half, lanes)
     body, down = pl.ds(PAD, half), pl.ds(PAD - 1, half)
     edge = jnp.zeros((PAD, lanes), jnp.float32)
     for j in range(5):
         e2[j] = jnp.zeros((half + 2 * PAD, lanes), jnp.float32)
-    for j, ref in enumerate((from_left, own_left, from_right)):
-        s2[j] = ref[0]
+    def three(k):
+        left, right = by_side(across_in[k], within_in[k])
+        return left, own[k], right
+
+    for j, (source, fy, fz) in enumerate(zip(three(0), three(2), three(3))):
+        s2[j] = source
         fy2[j, :PAD] = edge
-        fy2[j, body] = ref[2]
+        fy2[j, body] = fy
         fy2[j, PAD + half:] = edge
-        fz2[j] = ref[3]
-        fzl2[j] = behind(ref[3], 2, 1)
-    fx2[0] = jnp.where(first_of_two, ahead(from_left[1], 1, 1), behind(own_right[1], 1, 1))
-    fx2[1] = own_left[1]
-    fx2[2] = from_right[1]
-    fxl2[0] = from_left[1]
-    fxl2[1] = own_right[1]
-    fxl2[2] = jnp.where(first_of_two, ahead(own_left[1], 1, 1), behind(from_right[1], 1, 1))
+        fz2[j] = fz
+        fzl2[j] = behind(fz, 2, 1)
+    left_fx, _, right_fx = three(1)
+    fx2[0] = jnp.where(first_of_two, ahead(left_fx, 1, 1), behind(own_fx[1], 1, 1))
+    fx2[1] = own_fx[0]
+    fx2[2] = right_fx
+    fxl2[0] = left_fx
+    fxl2[1] = own_fx[1]
+    fxl2[2] = jnp.where(first_of_two, ahead(own_fx[0], 1, 1), behind(right_fx, 1, 1))
     for j in range(3):
         weight = fx2[j] + fxl2[j] + fy2[j, body] + fy2[j, down] + fz2[j] + fzl2[j]
         inverse = 1.0 / (8.0 + weight)
@@ -365,14 +404,15 @@
 
 
 def coarse_kernel(
-    where_ref, gathered, e2_in, s2, fx2, fxl2, fy2, fz2, inv2,
-    field, source, fx_in, fy_in, fz_in, inv_in, from_left, from_right,
+    owner_of, gathered, e2_in, s2, fx2, fxl2, fy2, fz2, inv2,
+    field, source, fx_in, fy_in, fz_in, inv_in, across_in, within_in,
     solved, owned,
     s3, fx3, fy3, fz3, fzl3, inv3, e3, pair3, small, e2, fzl2, e1, cor,
 ):
     blocks, _, quarter, lanes = gathered.shape
     half, height = 2 * quarter, 4 * quarter
-    position, last, owner = where_ref[0], where_ref[1], where_ref[2]
+    position, last = lax.axis_index("gx"), blocks - 1
+    owner = owner_of[position]
 
     body3, up3, down3 = pl.ds(PAD, quarter), pl.ds(PAD + 1, quarter), pl.ds(PAD - 1, quarter)
     row, lane = rows_of((quarter, lanes)), lanes_of((quarter, lanes))
@@ -516,6 +556,7 @@
     rows, lane = rows_of((height, lanes)), lanes_of((height, lanes))
     even_sum = ((rows + lane) & 1) == 0
     count = e1.shape[0]
+    borders = by_side(across_in[4], within_in[4])
     for w in range(0, count, 2):
         coarse_layer = w // 2 - 1
         packed = e2[2 + coarse_layer // 2, body2]
@@ -529,7 +570,7 @@
             e1[v, :PAD] = edge
             e1[v, PAD + height:] = edge
             if v in (0, count - 1):
-                into_both_rows(cor.at[1], (from_left if v == 0 else from_right)[4])
+                into_both_rows(cor.at[1], borders[0 if v == 0 else 1])
                 e1[v, body1] = cor[1] + fix
             else:
                 e1[v, body1] = field[v] + fix
@@ -558,7 +599,7 @@
     return pltpu.VMEM(shape, jnp.float32)
 
 
-def call(kernel, outs, scratch, scalars, operands):
+def call(kernel, outs, scratch, scalars, operands, space=pltpu.VMEM):
     def size(shape):
         count = 4
         for extent in shape:
@@ -571,7 +612,7 @@
         kernel,
         out_shape=tuple(outs),
         in_specs=[pl.BlockSpec(memory_space=pltpu.SMEM)] * len(scalars)
-        + [pl.BlockSpec(memory_space=pltpu.VMEM)] * len(operands),
+        + [pl.BlockSpec(memory_space=space)] * len(operands),
         out_specs=tuple([pl.BlockSpec(memory_space=pltpu.VMEM)] * len(outs)),
         scratch_shapes=scratch,
         compiler_params=pltpu.CompilerParams(vmem_limit_bytes=asked),
@@ -584,29 +625,26 @@
     blocks = lax.axis_size("gx")
     window = layers + 4
     padded, padded2, padded3 = height + 2 * PAD, half + 2 * PAD, quarter + 2 * PAD
-    to_left, to_right = call(
-        edge_kernel, [f32(4 * height + half, depth)] * 2, [], (), (iterate, source, phase_field)
-    )
-    halos = from_behind(to_right, 1), from_behind(to_left, -1)
-    position = lax.axis_index("gx")
-    where = jnp.stack([position, jnp.full_like(position, blocks - 1), block_owner[position]]).astype(jnp.int32)
+    inputs = jnp.concatenate([iterate, source, phase_field], 0)
+    sent = call(edge_kernel, [f32(4 * height + half, depth)] * 2, [], (), (inputs,))
     plain = f32(window, height, depth)
-    to_left, to_right, *fine = call(
+    across, within, fx2, *fine = call(
         fine_down_kernel,
-        [f32(5, half, depth)] * 2 + [plain, plain, plain, f32(window, padded, depth), plain, plain],
+        [f32(5, half, depth)] * 2
+        + [f32(2, half, depth), plain, plain, plain, f32(window, padded, depth), plain, plain],
         [
             vmem(window, padded, depth), vmem(window, padded, depth), vmem(window, height, depth),
             vmem(layers, height, depth), vmem(2, height, depth),
         ],
-        (where,), (iterate, source, phase_field, *halos),
+        (), (inputs, *swapped(*sent)),
     )
-    halos = from_behind(to_right, 1), from_behind(to_left, -1)
+    halos = swapped(across, within)
     plain = f32(3, half, depth)
     slots, *middle = call(
         middle_down_kernel,
         [f32(blocks, 2, quarter, depth), plain, plain, plain, plain, f32(3, padded2, depth), plain, plain],
         [vmem(5, padded2, depth), vmem(3, half, depth), vmem(2, half, depth)],
-        (where,), (to_left, to_right, *halos),
+        (), (across, fx2, *halos),
     )
     gathered = lax.all_to_all(slots, "gx", 0, 0, tiled=True)
     solved, owned = call(
@@ -618,7 +656,7 @@
             vmem(blocks + 2, padded3, depth), vmem(4, half, depth), vmem(4, blocks // 2, PAD, depth),
             vmem(5, padded2, depth), vmem(3, half, depth), vmem(window, padded, depth), vmem(2, height, depth),
         ],
-        (where,), (gathered, *middle, *fine, *halos),
+        (block_owner,), (gathered, *middle, *fine, *halos),
     )
     return solved, owned
 

time: 48.6 us -> 41.7 us (0.86)
  starting transfers between devices: 11.2 us -> 8.33 us
  waiting for transfers between devices: 2.99 us -> 1.27 us
  local copies, waits for them, and re-layouts: 3.95 us -> 2.51 us
  Pallas kernels: 8.11 us -> 7.18 us
  blocking collectives: 20.6 us -> 21.4 us
  other arithmetic: 0.72 us -> 0 us
    ppermute x4, starting transfers between devices: 11.2 us -> 8.33 us  [the longest x2 7.01 us: swapped(): lax.ppermute(within, 'gx', cores)]
    ppermute x4, waiting for transfers between devices: 2.99 us -> 1.27 us  [the longest x2 1.27 us: swapped(): lax.ppermute(within, 'gx', cores)]
    pallas_call x4, Pallas kernels: 8.11 us -> 7.18 us  [call(): pl.pallas_call(kernel, out_shape=tuple(outs), in_specs=[pl.BlockSpec(memo...]
    unnamed x14 -> x8, local copies, waits for them, and re-layouts: 3.37 us -> 2.5 us
    all_to_all x1, blocking collectives: 20.6 us -> 21.4 us  [on_device(): gathered = lax.all_to_all(slots, 'gx', 0, 0, tiled=True)]
    another operation x1 -> x0, other arithmetic: 0.72 us -> none  [on_device(): jnp.stack([position, jnp.full_like(position, blocks - 1), block_owner[pos...]
    dynamic_slice x1 -> x0, local copies, waits for them, and re-layouts: 0.58 us -> none  [on_device(): block_owner[position]]
  transfers between devices with their start and end apart: 4 -> 4, of which waited for: 2 -> 2; matrix products, arithmetic and copies ran while one was open for 3% -> 0% of each run, Pallas kernels for 0% -> 0%
where the time goes in v3:
time: 41.7 us; the launch traced here: 41.4 us
  blocking collectives  21.4 us (51%)
  starting transfers between devices  8.33 us (20%)
  Pallas kernels  7.18 us (17%)
  local copies, waits for them, and re-layouts  2.51 us (6%)
  waiting for transfers between devices  1.27 us (3%)
  between operations  0.71 us (2%)
    all_to_all x1, blocking collectives, on_device(): gathered = lax.all_to_all(slots, 'gx', 0, 0, tiled=True)  21.4 us
    pallas_call x4, Pallas kernels, call(): pl.pallas_call(kernel, out_shape=tuple(outs), in_specs=[pl.BlockSpec(memo...  7.18 us
    ppermute x2, starting transfers between devices, swapped(): lax.ppermute(within, 'gx', cores)  7.01 us
    unnamed x8, local copies, waits for them, and re-layouts  2.5 us
    ppermute x2, starting transfers between devices, swapped(): lax.ppermute(across, 'gx', chips)  1.32 us
    ppermute x2, waiting for transfers between devices, swapped(): lax.ppermute(within, 'gx', cores)  1.27 us
  transfers between devices with their start and end apart: 4, of which 2 were waited for; matrix products, arithmetic and copies ran while one was open for 0% of the time, Pallas kernels for 0%

profile of v3, /device:TPU:0, one launch (start us, length us, event | category | flops | bytes accessed | tf_op | source)
XLA Modules:
  0.0 41.4 jit_solution(13572149076631786557)
XLA Ops:
  0.6 0.0 copy-start.1
  0.6 0.9 %constant_dynamic-update-slice_fusion.2 = f32[12,64,128]{2,1,0:T(8,128)S(1)} fusion(f32[4,64,128]{2,1,0:T(8,128)} %param.4), kind=kLoop, calls=%fused_computation.2 | loop fusion | bytes 262144
  1.6 0.0 copy-done.1
  1.6 0.0 copy-start.2
  1.6 0.9 %copy-done.2 = f32[4,64,128]{2,1,0:T(8,128)S(1)} copy-done((f32[4,64,128]{2,1,0:T(8,128)S(1)}, f32[4,64,128]{2,1,0:T(8,128)}, u32[]{:S(2)}) %copy-start.2) | copy-done | bytes 131096
  2.5 0.2 shard_map.59
  2.7 0.7 %collective-permute-start = (f32[288,128]{1,0:T(8,128)S(1)}, f32[288,128]{1,0:T(8,128)S(1)}, u32[]{:S(2)}, u32[]{:S(2)}) collective-permute-start(f32[288,128]{1,0:T(8,128)S(1)} %get-tuple-element.21), channel_id=1, source_target_pairs={{1,2},{2,1},{3,4},{4,3},{5,6},{6,5},{7,8},{8,7},{9,10},{10,9},{11,... | collective-permute-start | bytes 442376 | tf_op jit(solution)/shard_map/ppermute | solution.py:18
  3.4 4.4 %collective-permute-start.1 = (f32[288,128]{1,0:T(8,128)S(1)}, f32[288,128]{1,0:T(8,128)S(1)}, u32[]{:S(2)}, u32[]{:S(2)}) collective-permute-start(f32[288,128]{1,0:T(8,128)S(1)} %get-tuple-element.22), channel_id=1, source_target_pairs={{0,1},{1,0},{2,3},{3,2},{4,5},{5,4},{6,7},{7,6},{8,9},{9,8},{10,11... | collective-permute-start | bytes 442376 | tf_op jit(solution)/shard_map/ppermute | solution.py:18
  7.8 0.0 collective-permute-done.across_in
  7.8 1.0 %collective-permute-done.1.within_in = f32[288,128]{1,0:T(8,128)S(1)} collective-permute-done((f32[288,128]{1,0:T(8,128)S(1)}, f32[288,128]{1,0:T(8,128)S(1)}, u32[]{:S(2)}, u32[]{:S(2)}) %collective-permute-start.1) | collective-permute-done | bytes 147488 | tf_op jit(solution)/shard_map/ppermute | solution.py:18
  8.8 1.0 %shard_map.60 = (f32[5,32,128]{2,1,0:T(8,128)S(1)}, f32[5,32,128]{2,1,0:T(8,128)S(1)}, f32[2,32,128]{2,1,0:T(8,128)S(1)}, f32[8,64,128]{2,1,0:T(8,128)S(1)}, f32...) custom-call(f32[12,64,128]{2,1,0:T(8,128)S(1)} %constant_dynamic-upd, ...), custom_call_target="tpu_custom_call" | custom-call | tf_op jit(solution)/shard_map/pallas_call | solution.py:611
  9.7 2.6 %collective-permute-start.3 = (f32[5,32,128]{2,1,0:T(8,128)S(1)}, f32[5,32,128]{2,1,0:T(8,128)S(1)}, u32[]{:S(2)}, u32[]{:S(2)}) collective-permute-start(f32[5,32,128]{2,1,0:T(8,128)S(1)} %get-tuple-element.25), channel_id=1, source_target_pairs={{0,1},{1,0},{2,3},{3,2},{4,5},{5,4},{6,7},{7,6},{8,9},{9,8},{10,11... | collective-permute-start | bytes 245768 | tf_op jit(solution)/shard_map/ppermute | solution.py:18
  12.4 0.7 %collective-permute-start.2 = (f32[5,32,128]{2,1,0:T(8,128)S(1)}, f32[5,32,128]{2,1,0:T(8,128)S(1)}, u32[]{:S(2)}, u32[]{:S(2)}) collective-permute-start(f32[5,32,128]{2,1,0:T(8,128)S(1)} %get-tuple-element.23.own), channel_id=1, source_target_pairs={{1,2},{2,1},{3,4},{4,3},{5,6},{6,5},{7,8},{8,7},{9,10},{10,9},{11,... | collective-permute-start | bytes 245768 | tf_op jit(solution)/shard_map/ppermute | solution.py:18
  13.0 0.3 collective-permute-done.3.within_in
  13.3 0.0 collective-permute-done.2.across_in
  13.3 0.5 %shard_map.61 = (f32[16,2,16,128]{3,2,1,0:T(8,128)S(1)}, f32[3,32,128]{2,1,0:T(8,128)S(1)}, f32[3,32,128]{2,1,0:T(8,128)S(1)}, f32[3,32,128]{2,1,0:T(8,128)S(1)}...) custom-call(f32[5,32,128]{2,1,0:T(8,128)S(1)} %get-tuple-element.23., ...), custom_call_target="tpu_custom_call" | custom-call | tf_op jit(solution)/shard_map/pallas_call | solution.py:611
  13.8 21.4 %all_to_all.5.gathered = f32[16,2,16,128]{3,2,1,0:T(8,128)S(1)} all-to-all(f32[16,2,16,128]{3,2,1,0:T(8,128)S(1)} %get-tuple-element.26), channel_id=1, replica_groups=mesh['groups'=2,'gx'=16] {'gx'}, dimensions={0} | all-to-all | bytes 524288 | tf_op jit(solution)/shard_map/all_to_all | solution.py:649
  35.2 0.0 copy-start
  35.2 0.7 %copy-done = s32[16]{0:T(128)S(1)} copy-done((s32[16]{0:T(128)S(1)}, s32[16]{0:T(128)}, u32[]{:S(2)}) %copy-start) | copy-done | bytes 88
  35.9 5.6 %shard_map.62 = (f32[4,64,128]{2,1,0:T(8,128)}, f32[1,16,32]{2,1,0:T(8,128)}) custom-call(s32[16]{0:T(128)S(1)} %copy-done, f32[16,2,16,128]{3,2,1,0:T(8,128)S(1)} %all_to_all.5.gathered, f32[3,32,128]{2,1,0:T(8,128)S(1)} %get-tuple-element.27.e2_in, f32[3,32,128]{2,1,0:T(8,128)S(1)} %get-tuple-element.28.s2, f32[3,32,128]{2,1,0:T(8,128)S(1)} %get-tuple-element.29.fx2, ...), custom_call_target="tpu_custom_call" | custom-call | tf_op jit(solution)/shard_map/pallas_call | solution.py:611
  (2 shorter events, 0.0 us)
Async XLA Ops:
  0.6 1.0 %copy-start.1 = (f32[4,64,128]{2,1,0:T(8,128)S(1)}, f32[4,64,128]{2,1,0:T(8,128)}, u32[]{:S(2)}) copy-start(f32[4,64,128]{2,1,0:T(8,128)} %param.5) | copy-start | bytes 393220
  1.6 0.9 %copy-start.2 = (f32[4,64,128]{2,1,0:T(8,128)S(1)}, f32[4,64,128]{2,1,0:T(8,128)}, u32[]{:S(2)}) copy-start(f32[4,64,128]{2,1,0:T(8,128)} %param.6) | copy-start | bytes 393220
  2.7 5.0 %collective-permute-start = (f32[288,128]{1,0:T(8,128)S(1)}, f32[288,128]{1,0:T(8,128)S(1)}, u32[]{:S(2)}, u32[]{:S(2)}) collective-permute-start(f32[288,128]{1,0:T(8,128)S(1)} %get-tuple-element.21), channel_id=1, source_target_pairs={{1,2},{2,1},{3,4},{4,3},{5,6},{6,5},{7,8},{8,7},{9,10},{10,9},{11,... | collective-permute-start | bytes 442376 | tf_op jit(solution)/shard_map/ppermute | solution.py:18
  3.4 5.4 %collective-permute-start.1 = (f32[288,128]{1,0:T(8,128)S(1)}, f32[288,128]{1,0:T(8,128)S(1)}, u32[]{:S(2)}, u32[]{:S(2)}) collective-permute-start(f32[288,128]{1,0:T(8,128)S(1)} %get-tuple-element.22), channel_id=1, source_target_pairs={{0,1},{1,0},{2,3},{3,2},{4,5},{5,4},{6,7},{7,6},{8,9},{9,8},{10,11... | collective-permute-start | bytes 442376 | tf_op jit(solution)/shard_map/ppermute | solution.py:18
  9.7 3.6 %collective-permute-start.3 = (f32[5,32,128]{2,1,0:T(8,128)S(1)}, f32[5,32,128]{2,1,0:T(8,128)S(1)}, u32[]{:S(2)}, u32[]{:S(2)}) collective-permute-start(f32[5,32,128]{2,1,0:T(8,128)S(1)} %get-tuple-element.25), channel_id=1, source_target_pairs={{0,1},{1,0},{2,3},{3,2},{4,5},{5,4},{6,7},{7,6},{8,9},{9,8},{10,11... | collective-permute-start | bytes 245768 | tf_op jit(solution)/shard_map/ppermute | solution.py:18
  12.4 0.9 %collective-permute-start.2 = (f32[5,32,128]{2,1,0:T(8,128)S(1)}, f32[5,32,128]{2,1,0:T(8,128)S(1)}, u32[]{:S(2)}, u32[]{:S(2)}) collective-permute-start(f32[5,32,128]{2,1,0:T(8,128)S(1)} %get-tuple-element.23.own), channel_id=1, source_target_pairs={{1,2},{2,1},{3,4},{4,3},{5,6},{6,5},{7,8},{8,7},{9,10},{10,9},{11,... | collective-permute-start | bytes 245768 | tf_op jit(solution)/shard_map/ppermute | solution.py:18
  35.2 0.7 %copy-start = (s32[16]{0:T(128)S(1)}, s32[16]{0:T(128)}, u32[]{:S(2)}) copy-start(s32[16]{0:T(128)} %owner_of.1) | copy-start | bytes 196

commit v4 on v3

--- a/solution.py
+++ b/solution.py
@@ -12,10 +12,12 @@
 
 
 def swapped(across, within):
-    count = lax.axis_size("gx")
-    chips = [(i, i + 1 if i % 2 else i - 1) for i in range(1, count - 1)]
-    cores = [(i, i ^ 1) for i in range(count)]
-    return lax.ppermute(across, "gx", chips), lax.ppermute(within, "gx", cores)
+    chips = [(i, i + 1 if i % 2 else i - 1) for i in range(1, lax.axis_size("gx") - 1)]
+    return lax.ppermute(across, "gx", chips), within_chip(within)
+
+
+def within_chip(block):
+    return lax.ppermute(block, "gx", [(i, i ^ 1) for i in range(lax.axis_size("gx"))])
 
 
 def by_side(across, within):
@@ -111,7 +113,7 @@
 
 
 def fine_down_kernel(
-    inputs, across_in, within_in,
+    owner_of, inputs, across_in, within_in,
     across, within, fx2_out, field_out, source_out, fx, fy, fz, inv,
     cell, e, fzl, held, pair,
 ):
@@ -312,9 +314,9 @@
     pair[1] = jnp.where(first_of_two, fresh[1], fresh[0])
     for_left = odd_cells(pair.at[0], quarter, first)
     for_right = odd_cells(pair.at[1], quarter, first)
-    for d in range(slots.shape[0]):
-        slots[d, 0] = tile
-        slots[d, 1] = jnp.where(position < d, for_right, for_left)
+    for c in range(slots.shape[0]):
+        slots[c, 0] = tile
+        slots[c, 1] = jnp.where(position < 2 * c + 1 - position % 2, for_right, for_left)
 
 
 class Level:
@@ -404,12 +406,13 @@
 
 
 def coarse_kernel(
-    owner_of, gathered, e2_in, s2, fx2, fxl2, fy2, fz2, inv2,
+    owner_of, same_cores, other_cores, e2_in, s2, fx2, fxl2, fy2, fz2, inv2,
     field, source, fx_in, fy_in, fz_in, inv_in, across_in, within_in,
     solved, owned,
     s3, fx3, fy3, fz3, fzl3, inv3, e3, pair3, small, e2, fzl2, e1, cor,
 ):
-    blocks, _, quarter, lanes = gathered.shape
+    chips, _, quarter, lanes = same_cores.shape
+    blocks = 2 * chips
     half, height = 2 * quarter, 4 * quarter
     position, last = lax.axis_index("gx"), blocks - 1
     owner = owner_of[position]
@@ -424,9 +427,12 @@
     fx3[0] = jnp.zeros((quarter, lanes), jnp.float32)
 
     def unpack(at):
-        for i in range(4):
+        tiles = []
+        for i in range(0, 4, 2):
+            chip = (at + i) // 2
+            tiles.extend(by_side(same_cores[chip, 0], other_cores[chip, 0]))
+        for i, tile in enumerate(tiles):
             j = at + i
-            tile = gathered[j, 0]
             moved = {0: tile}
             for step in (1, 2, 3):
                 moved[step] = ahead(tile, step, 1)
@@ -528,8 +534,8 @@
     first_of_two, even2 = parities2(half, lanes)
     body2 = pl.ds(PAD, half)
     edge = jnp.zeros((PAD, lanes), jnp.float32)
-    left = gathered[jnp.maximum(position - 1, 0), 1]
-    right = gathered[jnp.minimum(position + 1, last), 1]
+    left = other_cores[jnp.maximum(position - 1, 0) // 2, 1]
+    right = other_cores[jnp.minimum(position + 1, last) // 2, 1]
     into_both_rows(pair3.at[0], left)
     into_both_rows(pair3.at[1], right)
     left, right = pair3[0], pair3[1]
@@ -636,17 +642,19 @@
             vmem(window, padded, depth), vmem(window, padded, depth), vmem(window, height, depth),
             vmem(layers, height, depth), vmem(2, height, depth),
         ],
-        (), (inputs, *swapped(*sent)),
+        (block_owner,), (inputs, *swapped(*sent)),
     )
     halos = swapped(across, within)
     plain = f32(3, half, depth)
     slots, *middle = call(
         middle_down_kernel,
-        [f32(blocks, 2, quarter, depth), plain, plain, plain, plain, f32(3, padded2, depth), plain, plain],
+        [f32(blocks // 2, 2, quarter, depth), plain, plain, plain, plain, f32(3, padded2, depth), plain, plain],
         [vmem(5, padded2, depth), vmem(3, half, depth), vmem(2, half, depth)],
         (), (across, fx2, *halos),
     )
-    gathered = lax.all_to_all(slots, "gx", 0, 0, tiled=True)
+    kinds = [list(range(core, blocks, 2)) for core in range(2)]
+    same_cores = lax.all_to_all(slots, "gx", 0, 0, axis_index_groups=kinds, tiled=True)
+    other_cores = within_chip(same_cores)
     solved, owned = call(
         coarse_kernel,
         [f32(layers, height, depth), f32(1, quarter, depth // 4)],
@@ -656,7 +664,7 @@
             vmem(blocks + 2, padded3, depth), vmem(4, half, depth), vmem(4, blocks // 2, PAD, depth),
             vmem(5, padded2, depth), vmem(3, half, depth), vmem(window, padded, depth), vmem(2, height, depth),
         ],
-        (block_owner,), (gathered, *middle, *fine, *halos),
+        (block_owner,), (same_cores, other_cores, *middle, *fine, *halos),
     )
     return solved, owned
 

time: 41.7 us -> 40.2 us (0.964)
  blocking collectives: 21.4 us -> 18.8 us
  waiting for transfers between devices: 1.27 us -> 2.62 us
  local copies, waits for them, and re-layouts: 2.51 us -> 1.86 us
  Pallas kernels: 7.18 us -> 7.61 us
    all_to_all x1, blocking collectives: 21.4 us -> 18.8 us  [on_device(): lax.all_to_all(slots, 'gx', 0, 0, axis_index_groups=kinds, tiled=True)]
    ppermute x4 -> x5, waiting for transfers between devices: 1.27 us -> 2.62 us  [the longest x3 2.61 us: within_chip(): lax.ppermute(block, 'gx', [(i, i ^ 1) for i in range(lax.axis_size('gx'))])]
    unnamed x8, local copies, waits for them, and re-layouts: 2.5 us -> 1.85 us
    pallas_call x4, Pallas kernels: 7.18 us -> 7.61 us  [call(): pl.pallas_call(kernel, out_shape=tuple(outs), in_specs=[pl.BlockSpec(memo...]
    ppermute x4 -> x5, starting transfers between devices: 8.33 us -> 8.33 us  [the longest x3 7.01 us: within_chip(): lax.ppermute(block, 'gx', [(i, i ^ 1) for i in range(lax.axis_size('gx'))])]
  transfers between devices with their start and end apart: 4 -> 5, of which waited for: 2 -> 3; matrix products, arithmetic and copies ran while one was open for 0% -> 0% of each run, Pallas kernels for 0% -> 0%
where the time goes in v4:
time: 40.2 us; the launch traced here: 40 us
  blocking collectives  18.8 us (47%)
  starting transfers between devices  8.33 us (21%)
  Pallas kernels  7.61 us (19%)
  waiting for transfers between devices  2.62 us (7%)
  local copies, waits for them, and re-layouts  1.86 us (5%)
  between operations  0.71 us (2%)
    all_to_all x1, blocking collectives, on_device(): lax.all_to_all(slots, 'gx', 0, 0, axis_index_groups=kinds, tiled=True)  18.8 us
    pallas_call x4, Pallas kernels, call(): pl.pallas_call(kernel, out_shape=tuple(outs), in_specs=[pl.BlockSpec(memo...  7.61 us
    ppermute x3, starting transfers between devices, within_chip(): lax.ppermute(block, 'gx', [(i, i ^ 1) for i in range(lax.axis_size('gx'))])  7.01 us
    ppermute x3, waiting for transfers between devices, within_chip(): lax.ppermute(block, 'gx', [(i, i ^ 1) for i in range(lax.axis_size('gx'))])  2.61 us
    unnamed x8, local copies, waits for them, and re-layouts  1.85 us
    ppermute x2, starting transfers between devices, swapped(): return (lax.ppermute(across, 'gx', chips), within_chip(within))  1.32 us
  transfers between devices with their start and end apart: 5, of which 3 were waited for; matrix products, arithmetic and copies ran while one was open for 0% of the time, Pallas kernels for 0%

profile of v4, /device:TPU:0, one launch (start us, length us, event | category | flops | bytes accessed | tf_op | source)
XLA Modules:
  0.0 40.0 jit_solution(8840878860870903339)
XLA Ops:
  0.6 0.0 copy-start.1
  0.6 0.9 %constant_dynamic-update-slice_fusion.2 = f32[12,64,128]{2,1,0:T(8,128)S(1)} fusion(f32[4,64,128]{2,1,0:T(8,128)} %param.4), kind=kLoop, calls=%fused_computation.2 | loop fusion | bytes 262144
  1.6 0.0 copy-done.1
  1.6 0.0 copy-start.2
  1.6 0.9 %copy-done.2 = f32[4,64,128]{2,1,0:T(8,128)S(1)} copy-done((f32[4,64,128]{2,1,0:T(8,128)S(1)}, f32[4,64,128]{2,1,0:T(8,128)}, u32[]{:S(2)}) %copy-start.2) | copy-done | bytes 131096
  2.5 0.2 shard_map.59
  2.7 0.0 copy-start
  2.7 0.7 %collective-permute-start = (f32[288,128]{1,0:T(8,128)S(1)}, f32[288,128]{1,0:T(8,128)S(1)}, u32[]{:S(2)}, u32[]{:S(2)}) collective-permute-start(f32[288,128]{1,0:T(8,128)S(1)} %get-tuple-element.21), channel_id=1, source_target_pairs={{1,2},{2,1},{3,4},{4,3},{5,6},{6,5},{7,8},{8,7},{9,10},{10,9},{11,... | collective-permute-start | bytes 442376 | tf_op jit(solution)/shard_map/ppermute | solution.py:16
  3.4 4.4 %collective-permute-start.1 = (f32[288,128]{1,0:T(8,128)S(1)}, f32[288,128]{1,0:T(8,128)S(1)}, u32[]{:S(2)}, u32[]{:S(2)}) collective-permute-start(f32[288,128]{1,0:T(8,128)S(1)} %get-tuple-element.22), channel_id=1, source_target_pairs={{0,1},{1,0},{2,3},{3,2},{4,5},{5,4},{6,7},{7,6},{8,9},{9,8},{10,11... | collective-permute-start | bytes 442376 | tf_op jit(solution)/shard_map/ppermute | solution.py:20
  7.8 0.0 collective-permute-done.across_in
  7.8 1.0 %collective-permute-done.1.within_in = f32[288,128]{1,0:T(8,128)S(1)} collective-permute-done((f32[288,128]{1,0:T(8,128)S(1)}, f32[288,128]{1,0:T(8,128)S(1)}, u32[]{:S(2)}, u32[]{:S(2)}) %collective-permute-start.1) | collective-permute-done | bytes 147488 | tf_op jit(solution)/shard_map/ppermute | solution.py:20
  8.8 0.0 copy-done
  8.8 1.4 %shard_map.60 = (f32[5,32,128]{2,1,0:T(8,128)S(1)}, f32[5,32,128]{2,1,0:T(8,128)S(1)}, f32[2,32,128]{2,1,0:T(8,128)S(1)}, f32[8,64,128]{2,1,0:T(8,128)S(1)}, f32...) custom-call(s32[16]{0:T(128)S(1)} %copy-done, ...), custom_call_target="tpu_custom_call" | custom-call | tf_op jit(solution)/shard_map/pallas_call | solution.py:617
  10.2 2.7 %collective-permute-start.3 = (f32[5,32,128]{2,1,0:T(8,128)S(1)}, f32[5,32,128]{2,1,0:T(8,128)S(1)}, u32[]{:S(2)}, u32[]{:S(2)}) collective-permute-start(f32[5,32,128]{2,1,0:T(8,128)S(1)} %get-tuple-element.25), channel_id=1, source_target_pairs={{0,1},{1,0},{2,3},{3,2},{4,5},{5,4},{6,7},{7,6},{8,9},{9,8},{10,11... | collective-permute-start | bytes 245768 | tf_op jit(solution)/shard_map/ppermute | solution.py:20
  12.9 0.7 %collective-permute-start.2 = (f32[5,32,128]{2,1,0:T(8,128)S(1)}, f32[5,32,128]{2,1,0:T(8,128)S(1)}, u32[]{:S(2)}, u32[]{:S(2)}) collective-permute-start(f32[5,32,128]{2,1,0:T(8,128)S(1)} %get-tuple-element.23.own), channel_id=1, source_target_pairs={{1,2},{2,1},{3,4},{4,3},{5,6},{6,5},{7,8},{8,7},{9,10},{10,9},{11,... | collective-permute-start | bytes 245768 | tf_op jit(solution)/shard_map/ppermute | solution.py:16
  13.5 0.3 collective-permute-done.3.within_in
  13.8 0.0 collective-permute-done.2.across_in
  13.8 0.5 %shard_map.61 = (f32[8,2,16,128]{3,2,1,0:T(8,128)S(1)}, f32[3,32,128]{2,1,0:T(8,128)S(1)}, f32[3,32,128]{2,1,0:T(8,128)S(1)}, f32[3,32,128]{2,1,0:T(8,128)S(1)},...) custom-call(f32[5,32,128]{2,1,0:T(8,128)S(1)} %get-tuple-element.23., ...), custom_call_target="tpu_custom_call" | custom-call | tf_op jit(solution)/shard_map/pallas_call | solution.py:617
  14.3 18.8 %all_to_all.5.same_cores = f32[8,2,16,128]{3,2,1,0:T(8,128)S(1)} all-to-all(f32[8,2,16,128]{3,2,1,0:T(8,128)S(1)} %get-tuple-element.26), channel_id=1, replica_groups={{0,2,4,6,8,10,12,14},{1,3,5,7,9,11,13,15},{16,18,20,22,24,26,28,30},{17..., dimensions={0} | all-to-all | bytes 262144 | tf_op jit(solution)/shard_map/all_to_all | solution.py:656
  33.1 0.0 collective-permute-start.4
  33.1 1.3 %collective-permute-done.4.other_cores = f32[8,2,16,128]{3,2,1,0:T(8,128)S(1)} collective-permute-done((f32[8,2,16,128]{3,2,1,0:T(8,128)S(1)}, f32[8,2,16,128]{3,2,1,0:T(8,128)S(1)}, u32[]{:S(2)}, u32[]{:S(2)}) %collective-permute-start.4) | collective-permute-done | bytes 131104 | tf_op jit(solution)/shard_map/ppermute | solution.py:20
  34.4 5.5 %shard_map.62 = (f32[4,64,128]{2,1,0:T(8,128)}, f32[1,16,32]{2,1,0:T(8,128)}) custom-call(s32[16]{0:T(128)S(1)} %copy-done, f32[8,2,16,128]{3,2,1,0:T(8,128)S(1)} %all_to_all.5.same_cores, f32[8,2,16,128]{3,2,1,0:T(8,128)S(1)} %collective-permute-done.4.other_cores, f32[3,32,128]{2,1,0:T(8,128)S(1)} %get-tuple-element.27.e2_in, ...), custom_call_target="tpu_custom_call" | custom-call | tf_op jit(solution)/shard_map/pallas_call | solution.py:617
  (2 shorter events, 0.0 us)
Async XLA Ops:
  0.6 1.0 %copy-start.1 = (f32[4,64,128]{2,1,0:T(8,128)S(1)}, f32[4,64,128]{2,1,0:T(8,128)}, u32[]{:S(2)}) copy-start(f32[4,64,128]{2,1,0:T(8,128)} %param.5) | copy-start | bytes 393220
  1.6 0.9 %copy-start.2 = (f32[4,64,128]{2,1,0:T(8,128)S(1)}, f32[4,64,128]{2,1,0:T(8,128)}, u32[]{:S(2)}) copy-start(f32[4,64,128]{2,1,0:T(8,128)} %param.6) | copy-start | bytes 393220
  2.7 6.1 %copy-start = (s32[16]{0:T(128)S(1)}, s32[16]{0:T(128)}, u32[]{:S(2)}) copy-start(s32[16]{0:T(128)} %owner_of.3) | copy-start | bytes 196
  2.7 5.0 %collective-permute-start = (f32[288,128]{1,0:T(8,128)S(1)}, f32[288,128]{1,0:T(8,128)S(1)}, u32[]{:S(2)}, u32[]{:S(2)}) collective-permute-start(f32[288,128]{1,0:T(8,128)S(1)} %get-tuple-element.21), channel_id=1, source_target_pairs={{1,2},{2,1},{3,4},{4,3},{5,6},{6,5},{7,8},{8,7},{9,10},{10,9},{11,... | collective-permute-start | bytes 442376 | tf_op jit(solution)/shard_map/ppermute | solution.py:16
  3.4 5.4 %collective-permute-start.1 = (f32[288,128]{1,0:T(8,128)S(1)}, f32[288,128]{1,0:T(8,128)S(1)}, u32[]{:S(2)}, u32[]{:S(2)}) collective-permute-start(f32[288,128]{1,0:T(8,128)S(1)} %get-tuple-element.22), channel_id=1, source_target_pairs={{0,1},{1,0},{2,3},{3,2},{4,5},{5,4},{6,7},{7,6},{8,9},{9,8},{10,11... | collective-permute-start | bytes 442376 | tf_op jit(solution)/shard_map/ppermute | solution.py:20
  10.2 3.6 %collective-permute-start.3 = (f32[5,32,128]{2,1,0:T(8,128)S(1)}, f32[5,32,128]{2,1,0:T(8,128)S(1)}, u32[]{:S(2)}, u32[]{:S(2)}) collective-permute-start(f32[5,32,128]{2,1,0:T(8,128)S(1)} %get-tuple-element.25), channel_id=1, source_target_pairs={{0,1},{1,0},{2,3},{3,2},{4,5},{5,4},{6,7},{7,6},{8,9},{9,8},{10,11... | collective-permute-start | bytes 245768 | tf_op jit(solution)/shard_map/ppermute | solution.py:20
  12.9 0.9 %collective-permute-start.2 = (f32[5,32,128]{2,1,0:T(8,128)S(1)}, f32[5,32,128]{2,1,0:T(8,128)S(1)}, u32[]{:S(2)}, u32[]{:S(2)}) collective-permute-start(f32[5,32,128]{2,1,0:T(8,128)S(1)} %get-tuple-element.23.own), channel_id=1, source_target_pairs={{1,2},{2,1},{3,4},{4,3},{5,6},{6,5},{7,8},{8,7},{9,10},{10,9},{11,... | collective-permute-start | bytes 245768 | tf_op jit(solution)/shard_map/ppermute | solution.py:16
  33.1 1.3 %collective-permute-start.4 = (f32[8,2,16,128]{3,2,1,0:T(8,128)S(1)}, f32[8,2,16,128]{3,2,1,0:T(8,128)S(1)}, u32[]{:S(2)}, u32[]{:S(2)}) collective-permute-start(f32[8,2,16,128]{3,2,1,0:T(8,128)S(1)} %all_to_all.5.same_cores), channel_id=1, source_target_pairs={{0,1},{1,0},{2,3},{3,2},{4,5},{5,4},{6,7},{7,6},{8,9},{9,8},{10,11... | collective-permute-start | bytes 393224 | tf_op jit(solution)/shard_map/ppermute | solution.py:20

commit v5 on v4

--- a/solution.py
+++ b/solution.py
@@ -409,13 +409,14 @@
     owner_of, same_cores, other_cores, e2_in, s2, fx2, fxl2, fy2, fz2, inv2,
     field, source, fx_in, fy_in, fz_in, inv_in, across_in, within_in,
     solved, owned,
-    s3, fx3, fy3, fz3, fzl3, inv3, e3, pair3, small, e2, fzl2, e1, cor,
+    s3, fx3, fy3, fz3, fzl3, inv3, e3, pair3, small, e2, fzl2, e1, cor, owner_here, sem,
 ):
+    fetch = pltpu.make_async_copy(owner_of, owner_here, sem)
+    fetch.start()
     chips, _, quarter, lanes = same_cores.shape
     blocks = 2 * chips
     half, height = 2 * quarter, 4 * quarter
     position, last = lax.axis_index("gx"), blocks - 1
-    owner = owner_of[position]
 
     body3, up3, down3 = pl.ds(PAD, quarter), pl.ds(PAD + 1, quarter), pl.ds(PAD - 1, quarter)
     row, lane = rows_of((quarter, lanes)), lanes_of((quarter, lanes))
@@ -428,7 +429,7 @@
 
     def unpack(at):
         tiles = []
-        for i in range(0, 4, 2):
+        for i in range(0, min(16, blocks), 2):
             chip = (at + i) // 2
             tiles.extend(by_side(same_cores[chip, 0], other_cores[chip, 0]))
         for i, tile in enumerate(tiles):
@@ -450,13 +451,13 @@
             fz3[j] = spread[3]
             fzl3[j] = behind(spread[3], 4, 1)
 
-    chunked(blocks, 4, unpack)
+    chunked(blocks, 16, unpack)
 
     def is_even3(j):
         return ((parity3 + j) & 1) == 0
 
     def weights3(at):
-        for i in range(4):
+        for i in range(min(16, blocks)):
             j = at + i
             weight = fx3[j + 1] + fx3[j] + fy3[j, body3] + fy3[j, down3] + fz3[j] + fzl3[j]
             inverse = 1.0 / (64.0 + weight)
@@ -464,7 +465,7 @@
             e3[j + 1] = edge3
             e3[j + 1, body3] = jnp.where(is_even3(j), s3[j] * inverse, 0.0)
 
-    chunked(blocks, 4, weights3)
+    chunked(blocks, 16, weights3)
 
     def neigh3(j):
         here = e3[j + 1, body3]
@@ -483,10 +484,10 @@
         for i in range(count):
             e3[at + i + 1, body3] = fresh[i]
 
-    chunked(blocks, 8, lambda at: update3(at, 8, False))
+    chunked(blocks, 16, lambda at: update3(at, min(16, blocks), False))
 
     def restrict3(at):
-        for i in range(0, 4, 2):
+        for i in range(0, min(16, blocks), 2):
             j = at + i
             parts = []
             for k in (j, j + 1):
@@ -494,7 +495,7 @@
                 parts.append(jnp.where(is_even3(k), sums, 0.0))
             pair3[i, :quarter] = parts[0] + parts[1]
             pair3[i + 1, :quarter] = fz3[j] + fz3[j + 1]
-        for i in range(0, 4, 2):
+        for i in range(0, min(16, blocks), 2):
             j = at + i
             out = (at + i) // 2
             small[0, out] = with_partner(even_row_sum(pair3.at[i], PAD), 4, 1)
@@ -506,24 +507,26 @@
             odd = (lanes_of((PAD, lanes)) & 4) != 0
             small[3, out] = with_partner(jnp.where(odd, fzs, 0.0), 4, 1)
 
-    chunked(blocks, 4, restrict3)
+    chunked(blocks, 16, restrict3)
 
     small[0] = small_cycle(512.0, small[0], (small[1], small[2], small[3]), 1, 8, 2)
 
     def prolong3(at):
-        for i in range(4):
+        for i in range(min(16, blocks)):
             j = at + i
             fix = small[0, j // 2]
             pair3[i, pl.ds(0, PAD, 2), :] = fix
             pair3[i, pl.ds(1, PAD, 2), :] = fix
-        for i in range(4):
+        for i in range(min(16, blocks)):
             j = at + i
             e3[j + 1, body3] = e3[j + 1, body3] + pair3[i, :quarter]
 
-    chunked(blocks, 4, prolong3)
-    chunked(blocks, 8, lambda at: update3(at, 8, True))
-    chunked(blocks, 8, lambda at: update3(at, 8, False))
-
+    chunked(blocks, 16, prolong3)
+    chunked(blocks, 16, lambda at: update3(at, min(16, blocks), True))
+    chunked(blocks, 16, lambda at: update3(at, min(16, blocks), False))
+
+    fetch.wait()
+    owner = owner_here[position]
     wide, narrow = lanes_of((lanes, lanes)), rows_of((lanes, lanes))
     take = jnp.where(narrow == 4 * wide, 1.0, 0.0)
     block = jnp.dot(
@@ -605,24 +608,23 @@
     return pltpu.VMEM(shape, jnp.float32)
 
 
-def call(kernel, outs, scratch, scalars, operands, space=pltpu.VMEM):
+def call(kernel, outs, scratch, operands):
     def size(shape):
         count = 4
         for extent in shape:
             count *= extent
         return count
 
-    asked = 8 * 2**20 + sum(size(s.shape) for s in scratch) + sum(size(o.shape) for o in outs)
-    asked += sum(size(o.shape) for o in operands)
+    sized = [array for array in (*scratch, *outs, *operands) if hasattr(array, "shape")]
+    asked = 8 * 2**20 + sum(size(array.shape) for array in sized)
     return pl.pallas_call(
         kernel,
         out_shape=tuple(outs),
-        in_specs=[pl.BlockSpec(memory_space=pltpu.SMEM)] * len(scalars)
-        + [pl.BlockSpec(memory_space=space)] * len(operands),
+        in_specs=[pl.BlockSpec(memory_space=pltpu.VMEM)] * len(operands),
         out_specs=tuple([pl.BlockSpec(memory_space=pltpu.VMEM)] * len(outs)),
         scratch_shapes=scratch,
         compiler_params=pltpu.CompilerParams(vmem_limit_bytes=asked),
-    )(*scalars, *operands)
+    )(*operands)
 
 
 def on_device(iterate, source, phase_field, block_owner):
@@ -631,8 +633,11 @@
     blocks = lax.axis_size("gx")
     window = layers + 4
     padded, padded2, padded3 = height + 2 * PAD, half + 2 * PAD, quarter + 2 * PAD
-    inputs = jnp.concatenate([iterate, source, phase_field], 0)
-    sent = call(edge_kernel, [f32(4 * height + half, depth)] * 2, [], (), (inputs,))
+    inputs = sum(
+        jnp.pad(block, ((k * layers, (2 - k) * layers), (0, 0), (0, 0)))
+        for k, block in enumerate((iterate, source, phase_field))
+    )
+    sent = call(edge_kernel, [f32(4 * height + half, depth)] * 2, [], (inputs,))
     plain = f32(window, height, depth)
     across, within, fx2, *fine = call(
         fine_down_kernel,
@@ -642,7 +647,7 @@
             vmem(window, padded, depth), vmem(window, padded, depth), vmem(window, height, depth),
             vmem(layers, height, depth), vmem(2, height, depth),
         ],
-        (block_owner,), (inputs, *swapped(*sent)),
+        (block_owner, inputs, *swapped(*sent)),
     )
     halos = swapped(across, within)
     plain = f32(3, half, depth)
@@ -650,7 +655,7 @@
         middle_down_kernel,
         [f32(blocks // 2, 2, quarter, depth), plain, plain, plain, plain, f32(3, padded2, depth), plain, plain],
         [vmem(5, padded2, depth), vmem(3, half, depth), vmem(2, half, depth)],
-        (), (across, fx2, *halos),
+        (across, fx2, *halos),
     )
     kinds = [list(range(core, blocks, 2)) for core in range(2)]
     same_cores = lax.all_to_all(slots, "gx", 0, 0, axis_index_groups=kinds, tiled=True)
@@ -661,10 +666,11 @@
         [
             vmem(blocks, quarter, depth), vmem(blocks + 1, quarter, depth), vmem(blocks, padded3, depth),
             vmem(blocks, quarter, depth), vmem(blocks, quarter, depth), vmem(blocks, quarter, depth),
-            vmem(blocks + 2, padded3, depth), vmem(4, half, depth), vmem(4, blocks // 2, PAD, depth),
+            vmem(blocks + 2, padded3, depth), vmem(16, half, depth), vmem(4, blocks // 2, PAD, depth),
             vmem(5, padded2, depth), vmem(3, half, depth), vmem(window, padded, depth), vmem(2, height, depth),
+            pltpu.SMEM((blocks,), jnp.int32), pltpu.SemaphoreType.DMA,
         ],
-        (block_owner,), (same_cores, other_cores, *middle, *fine, *halos),
+        (block_owner, same_cores, other_cores, *middle, *fine, *halos),
     )
     return solved, owned
 

time: 40.2 us -> 37.3 us (0.928)
  Pallas kernels: 7.61 us -> 5.56 us
  local copies, waits for them, and re-layouts: 1.86 us -> 0.01 us
  other arithmetic: 0 us -> 1.06 us
    pallas_call x4, Pallas kernels: 7.61 us -> 5.56 us  [call(): pl.pallas_call(kernel, out_shape=tuple(outs), in_specs=[pl.BlockSpec(memo...]
    unnamed x8 -> x2, local copies, waits for them, and re-layouts: 1.85 us -> 0.01 us
    add x0 -> x1, other arithmetic: none -> 1.06 us  [on_device(): sum((jnp.pad(block, ((k * layers, (2 - k) * layers), (0, 0), (0, 0))) for...]
where the time goes in v5:
time: 37.3 us; the launch traced here: 37.1 us
  blocking collectives  18.8 us (50%)
  starting transfers between devices  8.33 us (22%)
  Pallas kernels  5.56 us (15%)
  waiting for transfers between devices  2.62 us (7%)
  other arithmetic  1.06 us (3%)
  between operations  0.68 us (2%)
    all_to_all x1, blocking collectives, on_device(): lax.all_to_all(slots, 'gx', 0, 0, axis_index_groups=kinds, tiled=True)  18.8 us
    ppermute x3, starting transfers between devices, within_chip(): lax.ppermute(block, 'gx', [(i, i ^ 1) for i in range(lax.axis_size('gx'))])  7.01 us
    pallas_call x4, Pallas kernels, call(): pl.pallas_call(kernel, out_shape=tuple(outs), in_specs=[pl.BlockSpec(memo...  5.56 us
    ppermute x3, waiting for transfers between devices, within_chip(): lax.ppermute(block, 'gx', [(i, i ^ 1) for i in range(lax.axis_size('gx'))])  2.61 us
    ppermute x2, starting transfers between devices, swapped(): return (lax.ppermute(across, 'gx', chips), within_chip(within))  1.32 us
    add x1, other arithmetic, on_device(): sum((jnp.pad(block, ((k * layers, (2 - k) * layers), (0, 0), (0, 0))) for...  1.06 us
  transfers between devices with their start and end apart: 5, of which 3 were waited for; matrix products, arithmetic and copies ran while one was open for 0% of the time, Pallas kernels for 0%

profile of v5, /device:TPU:0, one launch (start us, length us, event | category | flops | bytes accessed | tf_op | source)
XLA Modules:
  0.0 37.1 jit_solution(11648267549446444222)
XLA Ops:
  0.6 1.1 %pad_add_fusion.inputs = f32[12,64,128]{2,1,0:T(8,128)S(1)} fusion(f32[4,64,128]{2,1,0:T(8,128)} %param.6, f32[4,64,128]{2,1,0:T(8,128)} %param.5, f32[4,64,128]{2,1,0:T(8,128)} %param.4), kind=kLoop, calls=%fused_computation | loop fusion | flops 196608 | bytes 786432 | tf_op jit(solution)/shard_map/add | solution.py:636
  1.7 0.2 shard_map.59
  1.9 0.0 copy-start
  1.9 0.7 %collective-permute-start = (f32[288,128]{1,0:T(8,128)S(1)}, f32[288,128]{1,0:T(8,128)S(1)}, u32[]{:S(2)}, u32[]{:S(2)}) collective-permute-start(f32[288,128]{1,0:T(8,128)S(1)} %get-tuple-element.21), channel_id=1, source_target_pairs={{1,2},{2,1},{3,4},{4,3},{5,6},{6,5},{7,8},{8,7},{9,10},{10,9},{11,... | collective-permute-start | bytes 442376 | tf_op jit(solution)/shard_map/ppermute | solution.py:16
  2.6 4.4 %collective-permute-start.1 = (f32[288,128]{1,0:T(8,128)S(1)}, f32[288,128]{1,0:T(8,128)S(1)}, u32[]{:S(2)}, u32[]{:S(2)}) collective-permute-start(f32[288,128]{1,0:T(8,128)S(1)} %get-tuple-element.22), channel_id=1, source_target_pairs={{0,1},{1,0},{2,3},{3,2},{4,5},{5,4},{6,7},{7,6},{8,9},{9,8},{10,11... | collective-permute-start | bytes 442376 | tf_op jit(solution)/shard_map/ppermute | solution.py:20
  6.9 0.0 collective-permute-done.across_in
  6.9 1.0 %collective-permute-done.1.within_in = f32[288,128]{1,0:T(8,128)S(1)} collective-permute-done((f32[288,128]{1,0:T(8,128)S(1)}, f32[288,128]{1,0:T(8,128)S(1)}, u32[]{:S(2)}, u32[]{:S(2)}) %collective-permute-start.1) | collective-permute-done | bytes 147488 | tf_op jit(solution)/shard_map/ppermute | solution.py:20
  7.9 0.0 copy-done
  7.9 0.9 %shard_map.60 = (f32[5,32,128]{2,1,0:T(8,128)S(1)}, f32[5,32,128]{2,1,0:T(8,128)S(1)}, f32[2,32,128]{2,1,0:T(8,128)S(1)}, f32[8,64,128]{2,1,0:T(8,128)S(1)}, f32...) custom-call(s32[16]{0:T(128)S(1)} %copy-done, ...), custom_call_target="tpu_custom_call" | custom-call | tf_op jit(solution)/shard_map/pallas_call | solution.py:620
  8.9 2.6 %collective-permute-start.3 = (f32[5,32,128]{2,1,0:T(8,128)S(1)}, f32[5,32,128]{2,1,0:T(8,128)S(1)}, u32[]{:S(2)}, u32[]{:S(2)}) collective-permute-start(f32[5,32,128]{2,1,0:T(8,128)S(1)} %get-tuple-element.25), channel_id=1, source_target_pairs={{0,1},{1,0},{2,3},{3,2},{4,5},{5,4},{6,7},{7,6},{8,9},{9,8},{10,11... | collective-permute-start | bytes 245768 | tf_op jit(solution)/shard_map/ppermute | solution.py:20
  11.5 0.7 %collective-permute-start.2 = (f32[5,32,128]{2,1,0:T(8,128)S(1)}, f32[5,32,128]{2,1,0:T(8,128)S(1)}, u32[]{:S(2)}, u32[]{:S(2)}) collective-permute-start(f32[5,32,128]{2,1,0:T(8,128)S(1)} %get-tuple-element.23.own), channel_id=1, source_target_pairs={{1,2},{2,1},{3,4},{4,3},{5,6},{6,5},{7,8},{8,7},{9,10},{10,9},{11,... | collective-permute-start | bytes 245768 | tf_op jit(solution)/shard_map/ppermute | solution.py:16
  12.2 0.3 collective-permute-done.3.within_in
  12.4 0.0 collective-permute-done.2.across_in
  12.4 0.5 %shard_map.61 = (f32[8,2,16,128]{3,2,1,0:T(8,128)S(1)}, f32[3,32,128]{2,1,0:T(8,128)S(1)}, f32[3,32,128]{2,1,0:T(8,128)S(1)}, f32[3,32,128]{2,1,0:T(8,128)S(1)},...) custom-call(f32[5,32,128]{2,1,0:T(8,128)S(1)} %get-tuple-element.23., ...), custom_call_target="tpu_custom_call" | custom-call | tf_op jit(solution)/shard_map/pallas_call | solution.py:620
  12.9 18.8 %all_to_all.5.same_cores = f32[8,2,16,128]{3,2,1,0:T(8,128)S(1)} all-to-all(f32[8,2,16,128]{3,2,1,0:T(8,128)S(1)} %get-tuple-element.26), channel_id=1, replica_groups={{0,2,4,6,8,10,12,14},{1,3,5,7,9,11,13,15},{16,18,20,22,24,26,28,30},{17..., dimensions={0} | all-to-all | bytes 262144 | tf_op jit(solution)/shard_map/all_to_all | solution.py:661
  31.7 0.0 collective-permute-start.4
  31.7 1.3 %collective-permute-done.4.other_cores = f32[8,2,16,128]{3,2,1,0:T(8,128)S(1)} collective-permute-done((f32[8,2,16,128]{3,2,1,0:T(8,128)S(1)}, f32[8,2,16,128]{3,2,1,0:T(8,128)S(1)}, u32[]{:S(2)}, u32[]{:S(2)}) %collective-permute-start.4) | collective-permute-done | bytes 131104 | tf_op jit(solution)/shard_map/ppermute | solution.py:20
  33.1 4.0 %shard_map.62 = (f32[4,64,128]{2,1,0:T(8,128)}, f32[1,16,32]{2,1,0:T(8,128)}) custom-call(s32[16]{0:T(128)S(1)} %copy-done, f32[8,2,16,128]{3,2,1,0:T(8,128)S(1)} %all_to_all.5.same_cores, f32[8,2,16,128]{3,2,1,0:T(8,128)S(1)} %collective-permute-done.4.other_cores, f32[3,32,128]{2,1,0:T(8,128)S(1)} %get-tuple-element.27.e2_in, ...), custom_call_target="tpu_custom_call" | custom-call | tf_op jit(solution)/shard_map/pallas_call | solution.py:620
Async XLA Ops:
  1.9 6.1 %copy-start = (s32[16]{0:T(128)S(1)}, s32[16]{0:T(128)}, u32[]{:S(2)}) copy-start(s32[16]{0:T(128)} %owner_of.3) | copy-start | bytes 196
  1.9 5.0 %collective-permute-start = (f32[288,128]{1,0:T(8,128)S(1)}, f32[288,128]{1,0:T(8,128)S(1)}, u32[]{:S(2)}, u32[]{:S(2)}) collective-permute-start(f32[288,128]{1,0:T(8,128)S(1)} %get-tuple-element.21), channel_id=1, source_target_pairs={{1,2},{2,1},{3,4},{4,3},{5,6},{6,5},{7,8},{8,7},{9,10},{10,9},{11,... | collective-permute-start | bytes 442376 | tf_op jit(solution)/shard_map/ppermute | solution.py:16
  2.6 5.4 %collective-permute-start.1 = (f32[288,128]{1,0:T(8,128)S(1)}, f32[288,128]{1,0:T(8,128)S(1)}, u32[]{:S(2)}, u32[]{:S(2)}) collective-permute-start(f32[288,128]{1,0:T(8,128)S(1)} %get-tuple-element.22), channel_id=1, source_target_pairs={{0,1},{1,0},{2,3},{3,2},{4,5},{5,4},{6,7},{7,6},{8,9},{9,8},{10,11... | collective-permute-start | bytes 442376 | tf_op jit(solution)/shard_map/ppermute | solution.py:20
  8.9 3.6 %collective-permute-start.3 = (f32[5,32,128]{2,1,0:T(8,128)S(1)}, f32[5,32,128]{2,1,0:T(8,128)S(1)}, u32[]{:S(2)}, u32[]{:S(2)}) collective-permute-start(f32[5,32,128]{2,1,0:T(8,128)S(1)} %get-tuple-element.25), channel_id=1, source_target_pairs={{0,1},{1,0},{2,3},{3,2},{4,5},{5,4},{6,7},{7,6},{8,9},{9,8},{10,11... | collective-permute-start | bytes 245768 | tf_op jit(solution)/shard_map/ppermute | solution.py:20
  11.5 0.9 %collective-permute-start.2 = (f32[5,32,128]{2,1,0:T(8,128)S(1)}, f32[5,32,128]{2,1,0:T(8,128)S(1)}, u32[]{:S(2)}, u32[]{:S(2)}) collective-permute-start(f32[5,32,128]{2,1,0:T(8,128)S(1)} %get-tuple-element.23.own), channel_id=1, source_target_pairs={{1,2},{2,1},{3,4},{4,3},{5,6},{6,5},{7,8},{8,7},{9,10},{10,9},{11,... | collective-permute-start | bytes 245768 | tf_op jit(solution)/shard_map/ppermute | solution.py:16
  31.7 1.3 %collective-permute-start.4 = (f32[8,2,16,128]{3,2,1,0:T(8,128)S(1)}, f32[8,2,16,128]{3,2,1,0:T(8,128)S(1)}, u32[]{:S(2)}, u32[]{:S(2)}) collective-permute-start(f32[8,2,16,128]{3,2,1,0:T(8,128)S(1)} %all_to_all.5.same_cores), channel_id=1, source_target_pairs={{0,1},{1,0},{2,3},{3,2},{4,5},{5,4},{6,7},{7,6},{8,9},{9,8},{10,11... | collective-permute-start | bytes 393224 | tf_op jit(solution)/shard_map/ppermute | solution.py:20

commit v6 on v5

--- a/solution.py
+++ b/solution.py
@@ -75,30 +75,35 @@
 def edge_kernel(inputs, across, within):
     iterate, source, phase = three_parts(inputs)
     layers, height, depth = iterate.shape
+    half = height // 2
     row, lane = rows_of((height, depth)), lanes_of((height, depth))
     even_sum = ((row + lane) & 1) == 0
-    odd_lane = (lanes_of((height // 2, depth)) & 1) != 0
+    odd_lane = (lanes_of((half, depth)) & 1) != 0
     cell = []
     for w in range(layers):
         value = phase[w]
         cell.append(STIFFNESS * (value * value + EPSILON))
+
+    def in_layer(w):
+        here, e = cell[w], iterate[w]
+        fy = jnp.where(row < height - 1, 0.5 * (here + ahead(here, 1, 0)), 0.0)
+        fz = jnp.where(lane < depth - 1, 0.5 * (here + ahead(here, 1, 1)), 0.0)
+        fyl, fzl = behind(fy, 1, 0), behind(fz, 1, 1)
+        total = fy * ahead(e, 1, 0) + fyl * behind(e, 1, 0)
+        return total + fz * ahead(e, 1, 1) + fzl * behind(e, 1, 1), fy + fyl + fz + fzl
+
     sides = []
     for near, step in ((0, 1), (layers - 1, -1)):
         inner, far = near + step, near + 2 * step
-        here, e = cell[inner], iterate[inner]
-        face_near, face_far = 0.5 * (here + cell[near]), 0.5 * (here + cell[far])
-        fy = jnp.where(row < height - 1, 0.5 * (here + ahead(here, 1, 0)), 0.0)
-        fz = jnp.where(lane < depth - 1, 0.5 * (here + ahead(here, 1, 1)), 0.0)
-        fyl, fzl = behind(fy, 1, 0), behind(fz, 1, 1)
-        total = face_near * iterate[near] + face_far * iterate[far]
-        total = total + fy * ahead(e, 1, 0) + fyl * behind(e, 1, 0)
-        total = total + fz * ahead(e, 1, 1) + fzl * behind(e, 1, 1)
-        weight = 1.0 + (face_near + face_far + fy + fyl + fz + fzl)
-        even = even_sum if inner % 2 == 0 else ~even_sum
-        border = odd_cells(iterate.at[near], height // 2, odd_lane if near % 2 == 0 else ~odd_lane)
-        updated = jnp.where(even, (source[inner] + total) / weight, e)
-        sides.append((cell[near], here, source[near], updated, border))
-    places = [pl.ds(k * height, height) for k in range(4)] + [pl.ds(4 * height, height // 2)]
+        face_near, face_far = 0.5 * (cell[inner] + cell[near]), 0.5 * (cell[inner] + cell[far])
+        total, weight = in_layer(inner)
+        total = total + face_near * iterate[near] + face_far * iterate[far]
+        updated = (source[inner] + total) / (1.0 + (face_near + face_far + weight))
+        total, _ = in_layer(near)
+        even = even_sum if near % 2 == 0 else ~even_sum
+        known = source[near] + jnp.where(even, total + face_near * iterate[inner], face_near * updated)
+        sides.append((cell[near], cell[inner], known, odd_cells(iterate.at[near], half, odd_lane ^ (near % 2 != 0))))
+    places = [pl.ds(k * height, height) for k in range(3)] + [pl.ds(3 * height, half)]
     store_by_side(across, within, list(zip(places, *sides)))
 
 
@@ -114,21 +119,26 @@
 
 def fine_down_kernel(
     owner_of, inputs, across_in, within_in,
-    across, within, fx2_out, field_out, source_out, fx, fy, fz, inv,
-    cell, e, fzl, held, pair,
+    across, within, fx2_out, e, fx, fx_outer, fy, fz, inv,
+    cell, fzl, held, pair,
 ):
     iterate, source, phase = three_parts(inputs)
     layers, height, depth = iterate.shape
-    window = layers + 4
+    window = layers + 2
     position, last = lax.axis_index("gx"), lax.axis_size("gx") - 1
     body = pl.ds(PAD, height)
     up, down = pl.ds(PAD + 1, height), pl.ds(PAD - 1, height)
     row, lane = rows_of((height, depth)), lanes_of((height, depth))
     even_sum = ((row + lane) & 1) == 0
     half = height // 2
+    own = range(1, layers + 1)
+    outer = ((0, 0), (1, window - 1))
 
     def part(ref, k):
         return ref[k * height:(k + 1) * height]
+
+    def mask(w, odd):
+        return even_sum if (w + odd) % 2 == 1 else ~even_sum
 
     edge = jnp.zeros((PAD, depth), jnp.float32)
     for w in range(window):
@@ -136,67 +146,71 @@
             padded[w, :PAD] = edge
             padded[w, PAD + height:] = edge
         cell[w, PAD + height:] = edge
-    halos = [by_side(part(across_in, k), part(within_in, k)) for k in range(4)]
-    borders = by_side(across_in[4 * height:], within_in[4 * height:])
-    for side, outer, inner in ((0, 0, 1), (1, window - 1, window - 2)):
-        cell[inner, body] = halos[0][side]
-        cell[outer, body] = halos[1][side]
-        source_out[inner] = halos[2][side]
-        e[outer, body] = halos[3][side]
+    halos = [by_side(part(across_in, k), part(within_in, k)) for k in range(3)]
+    borders = by_side(across_in[3 * height:], within_in[3 * height:])
+    for side, w in outer:
+        cell[w, body] = halos[0][side]
+        fx_outer[side] = 0.5 * (halos[0][side] + halos[1][side])
         into_both_rows(pair.at[side], borders[side])
-        e[inner, body] = pair[side]
-    for w in range(layers):
-        value = phase[w]
-        cell[w + 2, body] = STIFFNESS * (value * value + EPSILON)
-        e[w + 2, body] = iterate[w]
-        source_out[w + 2] = source[w]
+        e[w, body] = pair[side]
+    for w in own:
+        value = phase[w - 1]
+        cell[w, body] = STIFFNESS * (value * value + EPSILON)
+        e[w, body] = iterate[w - 1]
     for w in range(window):
         here = cell[w, body]
         if w < window - 1:
             face = 0.5 * (here + cell[w + 1, body])
-            if w == 1:
+            if w == 0:
                 face = jnp.where(position > 0, face, 0.0)
-            if w == window - 3:
+            if w == window - 2:
                 face = jnp.where(position < last, face, 0.0)
             fx[w] = face
-        if 0 < w < window - 1:
-            fy[w, body] = jnp.where(row < height - 1, 0.5 * (here + cell[w, up]), 0.0)
-            face = jnp.where(lane < depth - 1, 0.5 * (here + ahead(here, 1, 1)), 0.0)
-            fz[w] = face
-            fzl[w] = behind(face, 1, 1)
-    for w in range(1, window - 1):
-        weight = fx[w] + fx[w - 1] + fy[w, body] + fy[w, down] + fz[w] + fzl[w]
+        fy[w, body] = jnp.where(row < height - 1, 0.5 * (here + cell[w, up]), 0.0)
+        face = jnp.where(lane < depth - 1, 0.5 * (here + ahead(here, 1, 1)), 0.0)
+        fz[w] = face
+        fzl[w] = behind(face, 1, 1)
+    for w in range(window):
+        beyond = fx[w] if w < window - 1 else fx_outer[1]
+        before = fx[w - 1] if w > 0 else fx_outer[0]
+        weight = beyond + before + fy[w, body] + fy[w, down] + fz[w] + fzl[w]
         inv[w] = 1.0 / (1.0 + weight)
 
+    def in_layer(w):
+        here = e[w, body]
+        total = fy[w, body] * e[w, up] + fy[w, down] * e[w, down]
+        return total + fz[w] * ahead(here, 1, 1) + fzl[w] * behind(here, 1, 1)
+
     def neigh(w):
-        here = e[w, body]
-        total = fx[w] * e[w + 1, body] + fx[w - 1] * e[w - 1, body]
-        total = total + fy[w, body] * e[w, up] + fy[w, down] * e[w, down]
-        return total + fz[w] * ahead(here, 1, 1) + fzl[w] * behind(here, 1, 1)
-
-    def mask(w, odd):
-        return even_sum if (w + odd) % 2 == 0 else ~even_sum
-
-    for w in range(1, window - 1):
-        total = source_out[w] + neigh(w)
-        if 2 <= w < layers + 2:
-            held[w - 2] = total
+        return fx[w] * e[w + 1, body] + fx[w - 1] * e[w - 1, body] + in_layer(w)
+
+    def towards_own(side, w):
+        return fx[0] * e[1, body] if side == 0 else fx[w - 1] * e[w - 1, body]
+
+    for w in own:
+        total = source[w - 1] + neigh(w)
+        held[w - 1] = total
         e[w, body] = jnp.where(mask(w, 0), total * inv[w], e[w, body])
-    for w in range(1, window - 1):
-        total = (source_out[w] + neigh(w)) * inv[w]
+    for side, w in outer:
+        total = halos[2][side] + towards_own(side, w)
+        e[w, body] = jnp.where(mask(w, 0), total * inv[w], e[w, body])
+    for side, w in outer:
+        total = (halos[2][side] + in_layer(w) + towards_own(side, w)) * inv[w]
         e[w, body] = jnp.where(mask(w, 1), total, e[w, body])
-        field_out[w] = e[w, body]
+    for w in own:
+        total = (source[w - 1] + neigh(w)) * inv[w]
+        e[w, body] = jnp.where(mask(w, 1), total, e[w, body])
 
     lane = lanes_of((half, depth))
     first_of_two = (lane & 1) == 0
 
     def residual(w):
-        return jnp.where(mask(w, 0), source_out[w] + neigh(w) - held[w - 2], 0.0)
-
-    def slabs(make, reduce_rows, reduce_lanes, start=2):
+        return jnp.where(mask(w, 0), source[w - 1] + neigh(w) - held[w - 1], 0.0)
+
+    def slabs(make, reduce_rows, reduce_lanes):
         found = []
         for t in range(2):
-            pair[t] = make(start + 2 * t)
+            pair[t] = make(1 + 2 * t)
             found.append(reduce_lanes(reduce_rows(pair.at[t])))
         return jnp.where(first_of_two, found[0], found[1])
 
@@ -218,13 +232,13 @@
     left_fx = slabs(lambda w: fx[w + 1], both_rows, both_lanes)
     right_fx = slabs(lambda w: fx[w - 1], both_rows, both_lanes)
     fx2_out[0], fx2_out[1] = left_fx, right_fx
-    borders = []
-    for t, w in enumerate((3, window - 4)):
-        pair[t] = e[w, body]
-        borders.append(odd_cells(pair.at[t], half, ~first_of_two if w % 2 == 0 else first_of_two))
+    known = []
+    for t, (w, face, inner) in enumerate(((1, 1, 2), (layers, layers - 1, layers - 1))):
+        pair[t] = source[w - 1] + fx[face] * e[inner, body]
+        known.append(odd_cells(pair.at[t], half, first_of_two if w % 2 == 1 else ~first_of_two))
     pieces = [(0, coarse_source), (2, coarse_fy), (3, coarse_fz)]
     pieces = [(k, value, value) for k, value in pieces]
-    store_by_side(across, within, pieces + [(1, left_fx, right_fx), (4, *borders)])
+    store_by_side(across, within, pieces + [(1, left_fx, right_fx), (4, *known)])
 
 
 def neigh2(e2, fx2, fxl2, fy2, fz2, fzl2, first_of_two, tiles):
@@ -407,7 +421,7 @@
 
 def coarse_kernel(
     owner_of, same_cores, other_cores, e2_in, s2, fx2, fxl2, fy2, fz2, inv2,
-    field, source, fx_in, fy_in, fz_in, inv_in, across_in, within_in,
+    inputs, field, fx_in, fx_outer, fy_in, fz_in, inv_in, across_in, within_in,
     solved, owned,
     s3, fx3, fy3, fz3, fzl3, inv3, e3, pair3, small, e2, fzl2, e1, cor, owner_here, sem,
 ):
@@ -561,43 +575,46 @@
         for j in range(3):
             e2[j + 1, body2] = fresh[j]
 
+    _, source, _ = three_parts(inputs)
     body1, up1, down1 = pl.ds(PAD, height), pl.ds(PAD + 1, height), pl.ds(PAD - 1, height)
     rows, lane = rows_of((height, lanes)), lanes_of((height, lanes))
     even_sum = ((rows + lane) & 1) == 0
     count = e1.shape[0]
-    borders = by_side(across_in[4], within_in[4])
-    for w in range(0, count, 2):
-        coarse_layer = w // 2 - 1
-        packed = e2[2 + coarse_layer // 2, body2]
-        if coarse_layer % 2 == 0:
+    fixes = []
+    for w in range(count):
+        tile, t = divmod((w - 1) // 2, 2)
+        packed = e2[2 + tile, body2]
+        if t == 0:
             plain = jnp.where(first_of_two, packed, behind(packed, 1, 1))
         else:
             plain = jnp.where(first_of_two, ahead(packed, 1, 1), packed)
-        into_both_rows(cor.at[0], plain)
-        fix = cor[0]
-        for v in (w, w + 1):
-            e1[v, :PAD] = edge
-            e1[v, PAD + height:] = edge
-            if v in (0, count - 1):
-                into_both_rows(cor.at[1], borders[0 if v == 0 else 1])
-                e1[v, body1] = cor[1] + fix
-            else:
-                e1[v, body1] = field[v] + fix
-
-    def smoothed1(w, even):
-        here = e1[w, body1]
-        face = fz_in[w]
-        sums = fx_in[w] * e1[w + 1, body1] + fx_in[w - 1] * e1[w - 1, body1]
-        sums = sums + fy_in[w, body1] * e1[w, up1] + fy_in[w, down1] * e1[w, down1]
-        sums = sums + face * ahead(here, 1, 1) + behind(face, 1, 1) * behind(here, 1, 1)
-        value = (source[w] + sums) * inv_in[w]
-        keep = even_sum if (w + even) % 2 == 0 else ~even_sum
-        return jnp.where(keep, here, value)
+        if w % 2 == 1 or w == 0:
+            into_both_rows(cor.at[len(fixes) % 2], plain)
+            fixes.append(cor[len(fixes) % 2])
+        e1[w, :PAD] = edge
+        e1[w, PAD + height:] = edge
+        e1[w, body1] = field[w, body1] + fixes[-1]
+
+    def in_layer1(w):
+        here, face = e1[w, body1], fz_in[w]
+        sums = fy_in[w, body1] * e1[w, up1] + fy_in[w, down1] * e1[w, down1]
+        return sums + face * ahead(here, 1, 1) + behind(face, 1, 1) * behind(here, 1, 1)
+
+    def smoothed1(w, odd):
+        keep = even_sum if (w + odd) % 2 == 0 else ~even_sum
+        sums = fx_in[w] * e1[w + 1, body1] + fx_in[w - 1] * e1[w - 1, body1] + in_layer1(w)
+        return jnp.where(keep, e1[w, body1], (source[w - 1] + sums) * inv_in[w])
 
     for w in range(1, count - 1):
-        e1[w, body1] = smoothed1(w, 1)
-    for w in range(2, count - 2):
-        solved[w - 2] = smoothed1(w, 0)
+        e1[w, body1] = smoothed1(w, 0)
+    borders = by_side(across_in[4], within_in[4])
+    for side, w, near in ((0, 0, 1), (1, count - 1, count - 2)):
+        into_both_rows(cor.at[side], borders[side])
+        sums = cor[side] + fx_outer[side] * fixes[0 if side == 0 else -1]
+        sums = sums + fx_in[min(w, near)] * e1[near, body1] + in_layer1(w)
+        e1[w, body1] = sums * inv_in[w]
+    for w in range(1, count - 1):
+        solved[w - 1] = smoothed1(w, 1)
 
 
 def f32(*shape):
@@ -631,21 +648,21 @@
     layers, height, depth = iterate.shape
     half, quarter = height // 2, height // 4
     blocks = lax.axis_size("gx")
-    window = layers + 4
+    window = layers + 2
     padded, padded2, padded3 = height + 2 * PAD, half + 2 * PAD, quarter + 2 * PAD
     inputs = sum(
         jnp.pad(block, ((k * layers, (2 - k) * layers), (0, 0), (0, 0)))
         for k, block in enumerate((iterate, source, phase_field))
     )
-    sent = call(edge_kernel, [f32(4 * height + half, depth)] * 2, [], (inputs,))
-    plain = f32(window, height, depth)
+    sent = call(edge_kernel, [f32(3 * height + half, depth)] * 2, [], (inputs,))
+    plain, tall = f32(window, height, depth), f32(window, padded, depth)
     across, within, fx2, *fine = call(
         fine_down_kernel,
         [f32(5, half, depth)] * 2
-        + [f32(2, half, depth), plain, plain, plain, f32(window, padded, depth), plain, plain],
+        + [f32(2, half, depth), tall, f32(window - 1, height, depth), f32(2, height, depth), tall, plain, plain],
         [
-            vmem(window, padded, depth), vmem(window, padded, depth), vmem(window, height, depth),
-            vmem(layers, height, depth), vmem(2, height, depth),
+            vmem(window, padded, depth), vmem(window, height, depth), vmem(layers, height, depth),
+            vmem(2, height, depth),
         ],
         (block_owner, inputs, *swapped(*sent)),
     )
@@ -670,7 +687,7 @@
             vmem(5, padded2, depth), vmem(3, half, depth), vmem(window, padded, depth), vmem(2, height, depth),
             pltpu.SMEM((blocks,), jnp.int32), pltpu.SemaphoreType.DMA,
         ],
-        (block_owner, same_cores, other_cores, *middle, *fine, *halos),
+        (block_owner, same_cores, other_cores, *middle, inputs, *fine, *halos),
     )
     return solved, owned
 

time: 37.3 us -> 36.6 us (0.981)
  starting transfers between devices: 8.33 us -> 7.67 us
    ppermute x3, starting transfers between devices: 7.01 us -> 6.35 us  [within_chip(): lax.ppermute(block, 'gx', [(i, i ^ 1) for i in range(lax.axis_size('gx'))])]
where the time goes in v6:
time: 36.6 us; the launch traced here: 36.4 us
  blocking collectives  18.8 us (51%)
  starting transfers between devices  7.67 us (21%)
  Pallas kernels  5.57 us (15%)
  waiting for transfers between devices  2.57 us (7%)
  other arithmetic  1.06 us (3%)
  between operations  0.68 us (2%)
    all_to_all x1, blocking collectives, on_device(): lax.all_to_all(slots, 'gx', 0, 0, axis_index_groups=kinds, tiled=True)  18.8 us
    ppermute x3, starting transfers between devices, within_chip(): lax.ppermute(block, 'gx', [(i, i ^ 1) for i in range(lax.axis_size('gx'))])  6.35 us
    pallas_call x4, Pallas kernels, call(): pl.pallas_call(kernel, out_shape=tuple(outs), in_specs=[pl.BlockSpec(memo...  5.57 us
    ppermute x3, waiting for transfers between devices, within_chip(): lax.ppermute(block, 'gx', [(i, i ^ 1) for i in range(lax.axis_size('gx'))])  2.57 us
    ppermute x2, starting transfers between devices, swapped(): return (lax.ppermute(across, 'gx', chips), within_chip(within))  1.32 us
    add x1, other arithmetic, on_device(): sum((jnp.pad(block, ((k * layers, (2 - k) * layers), (0, 0), (0, 0))) for...  1.06 us
  transfers between devices with their start and end apart: 5, of which 3 were waited for; matrix products, arithmetic and copies ran while one was open for 0% of the time, Pallas kernels for 0%

profile of v6, /device:TPU:0, one launch (start us, length us, event | category | flops | bytes accessed | tf_op | source)
XLA Modules:
  0.0 36.4 jit_solution(13104044355225617361)
XLA Ops:
  0.6 1.1 %pad_add_fusion.inputs = f32[12,64,128]{2,1,0:T(8,128)S(1)} fusion(f32[4,64,128]{2,1,0:T(8,128)} %param.6, f32[4,64,128]{2,1,0:T(8,128)} %param.5, f32[4,64,128]{2,1,0:T(8,128)} %param.4), kind=kLoop, calls=%fused_computation | loop fusion | flops 196608 | bytes 786432 | tf_op jit(solution)/shard_map/add | solution.py:653
  1.7 0.3 shard_map.59
  2.0 0.0 copy-start
  2.0 0.7 %collective-permute-start = (f32[224,128]{1,0:T(8,128)S(1)}, f32[224,128]{1,0:T(8,128)S(1)}, u32[]{:S(2)}, u32[]{:S(2)}) collective-permute-start(f32[224,128]{1,0:T(8,128)S(1)} %get-tuple-element.21), channel_id=1, source_target_pairs={{1,2},{2,1},{3,4},{4,3},{5,6},{6,5},{7,8},{8,7},{9,10},{10,9},{11,... | collective-permute-start | bytes 344072 | tf_op jit(solution)/shard_map/ppermute | solution.py:16
  2.7 4.4 %collective-permute-start.1 = (f32[224,128]{1,0:T(8,128)S(1)}, f32[224,128]{1,0:T(8,128)S(1)}, u32[]{:S(2)}, u32[]{:S(2)}) collective-permute-start(f32[224,128]{1,0:T(8,128)S(1)} %get-tuple-element.22), channel_id=1, source_target_pairs={{0,1},{1,0},{2,3},{3,2},{4,5},{5,4},{6,7},{7,6},{8,9},{9,8},{10,11... | collective-permute-start | bytes 344072 | tf_op jit(solution)/shard_map/ppermute | solution.py:20
  7.0 0.0 collective-permute-done.across_in
  7.0 1.0 %collective-permute-done.1.within_in = f32[224,128]{1,0:T(8,128)S(1)} collective-permute-done((f32[224,128]{1,0:T(8,128)S(1)}, f32[224,128]{1,0:T(8,128)S(1)}, u32[]{:S(2)}, u32[]{:S(2)}) %collective-permute-start.1) | collective-permute-done | bytes 114720 | tf_op jit(solution)/shard_map/ppermute | solution.py:20
  8.0 0.0 copy-done
  8.0 0.8 %shard_map.60 = (f32[5,32,128]{2,1,0:T(8,128)S(1)}, f32[5,32,128]{2,1,0:T(8,128)S(1)}, f32[2,32,128]{2,1,0:T(8,128)S(1)}, f32[6,80,128]{2,1,0:T(8,128)S(1)}, f32...) custom-call(s32[16]{0:T(128)S(1)} %copy-done, ...), custom_call_target="tpu_custom_call" | custom-call | tf_op jit(solution)/shard_map/pallas_call | solution.py:637
  8.8 2.0 %collective-permute-start.3 = (f32[5,32,128]{2,1,0:T(8,128)S(1)}, f32[5,32,128]{2,1,0:T(8,128)S(1)}, u32[]{:S(2)}, u32[]{:S(2)}) collective-permute-start(f32[5,32,128]{2,1,0:T(8,128)S(1)} %get-tuple-element.25), channel_id=1, source_target_pairs={{0,1},{1,0},{2,3},{3,2},{4,5},{5,4},{6,7},{7,6},{8,9},{9,8},{10,11... | collective-permute-start | bytes 245768 | tf_op jit(solution)/shard_map/ppermute | solution.py:20
  10.8 0.7 %collective-permute-start.2 = (f32[5,32,128]{2,1,0:T(8,128)S(1)}, f32[5,32,128]{2,1,0:T(8,128)S(1)}, u32[]{:S(2)}, u32[]{:S(2)}) collective-permute-start(f32[5,32,128]{2,1,0:T(8,128)S(1)} %get-tuple-element.23.own), channel_id=1, source_target_pairs={{1,2},{2,1},{3,4},{4,3},{5,6},{6,5},{7,8},{8,7},{9,10},{10,9},{11,... | collective-permute-start | bytes 245768 | tf_op jit(solution)/shard_map/ppermute | solution.py:16
  11.5 0.3 collective-permute-done.3.within_in
  11.7 0.0 collective-permute-done.2.across_in
  11.7 0.5 %shard_map.61 = (f32[8,2,16,128]{3,2,1,0:T(8,128)S(1)}, f32[3,32,128]{2,1,0:T(8,128)S(1)}, f32[3,32,128]{2,1,0:T(8,128)S(1)}, f32[3,32,128]{2,1,0:T(8,128)S(1)},...) custom-call(f32[5,32,128]{2,1,0:T(8,128)S(1)} %get-tuple-element.23., ...), custom_call_target="tpu_custom_call" | custom-call | tf_op jit(solution)/shard_map/pallas_call | solution.py:637
  12.2 18.8 %all_to_all.5.same_cores = f32[8,2,16,128]{3,2,1,0:T(8,128)S(1)} all-to-all(f32[8,2,16,128]{3,2,1,0:T(8,128)S(1)} %get-tuple-element.26), channel_id=1, replica_groups={{0,2,4,6,8,10,12,14},{1,3,5,7,9,11,13,15},{16,18,20,22,24,26,28,30},{17..., dimensions={0} | all-to-all | bytes 262144 | tf_op jit(solution)/shard_map/all_to_all | solution.py:678
  31.0 0.0 collective-permute-start.4
  31.0 1.3 %collective-permute-done.4.other_cores = f32[8,2,16,128]{3,2,1,0:T(8,128)S(1)} collective-permute-done((f32[8,2,16,128]{3,2,1,0:T(8,128)S(1)}, f32[8,2,16,128]{3,2,1,0:T(8,128)S(1)}, u32[]{:S(2)}, u32[]{:S(2)}) %collective-permute-start.4) | collective-permute-done | bytes 131104 | tf_op jit(solution)/shard_map/ppermute | solution.py:20
  32.4 4.0 %shard_map.62 = (f32[4,64,128]{2,1,0:T(8,128)}, f32[1,16,32]{2,1,0:T(8,128)}) custom-call(s32[16]{0:T(128)S(1)} %copy-done, f32[8,2,16,128]{3,2,1,0:T(8,128)S(1)} %all_to_all.5.same_cores, f32[8,2,16,128]{3,2,1,0:T(8,128)S(1)} %collective-permute-done.4.other_cores, f32[3,32,128]{2,1,0:T(8,128)S(1)} %get-tuple-element.27.e2_in, ...), custom_call_target="tpu_custom_call" | custom-call | tf_op jit(solution)/shard_map/pallas_call | solution.py:637
Async XLA Ops:
  2.0 6.0 %copy-start = (s32[16]{0:T(128)S(1)}, s32[16]{0:T(128)}, u32[]{:S(2)}) copy-start(s32[16]{0:T(128)} %owner_of.3) | copy-start | bytes 196
  2.0 5.0 %collective-permute-start = (f32[224,128]{1,0:T(8,128)S(1)}, f32[224,128]{1,0:T(8,128)S(1)}, u32[]{:S(2)}, u32[]{:S(2)}) collective-permute-start(f32[224,128]{1,0:T(8,128)S(1)} %get-tuple-element.21), channel_id=1, source_target_pairs={{1,2},{2,1},{3,4},{4,3},{5,6},{6,5},{7,8},{8,7},{9,10},{10,9},{11,... | collective-permute-start | bytes 344072 | tf_op jit(solution)/shard_map/ppermute | solution.py:16
  2.7 5.3 %collective-permute-start.1 = (f32[224,128]{1,0:T(8,128)S(1)}, f32[224,128]{1,0:T(8,128)S(1)}, u32[]{:S(2)}, u32[]{:S(2)}) collective-permute-start(f32[224,128]{1,0:T(8,128)S(1)} %get-tuple-element.22), channel_id=1, source_target_pairs={{0,1},{1,0},{2,3},{3,2},{4,5},{5,4},{6,7},{7,6},{8,9},{9,8},{10,11... | collective-permute-start | bytes 344072 | tf_op jit(solution)/shard_map/ppermute | solution.py:20
  8.8 2.9 %collective-permute-start.3 = (f32[5,32,128]{2,1,0:T(8,128)S(1)}, f32[5,32,128]{2,1,0:T(8,128)S(1)}, u32[]{:S(2)}, u32[]{:S(2)}) collective-permute-start(f32[5,32,128]{2,1,0:T(8,128)S(1)} %get-tuple-element.25), channel_id=1, source_target_pairs={{0,1},{1,0},{2,3},{3,2},{4,5},{5,4},{6,7},{7,6},{8,9},{9,8},{10,11... | collective-permute-start | bytes 245768 | tf_op jit(solution)/shard_map/ppermute | solution.py:20
  10.8 0.9 %collective-permute-start.2 = (f32[5,32,128]{2,1,0:T(8,128)S(1)}, f32[5,32,128]{2,1,0:T(8,128)S(1)}, u32[]{:S(2)}, u32[]{:S(2)}) collective-permute-start(f32[5,32,128]{2,1,0:T(8,128)S(1)} %get-tuple-element.23.own), channel_id=1, source_target_pairs={{1,2},{2,1},{3,4},{4,3},{5,6},{6,5},{7,8},{8,7},{9,10},{10,9},{11,... | collective-permute-start | bytes 245768 | tf_op jit(solution)/shard_map/ppermute | solution.py:16
  31.0 1.3 %collective-permute-start.4 = (f32[8,2,16,128]{3,2,1,0:T(8,128)S(1)}, f32[8,2,16,128]{3,2,1,0:T(8,128)S(1)}, u32[]{:S(2)}, u32[]{:S(2)}) collective-permute-start(f32[8,2,16,128]{3,2,1,0:T(8,128)S(1)} %all_to_all.5.same_cores), channel_id=1, source_target_pairs={{0,1},{1,0},{2,3},{3,2},{4,5},{5,4},{6,7},{7,6},{8,9},{9,8},{10,11... | collective-permute-start | bytes 393224 | tf_op jit(solution)/shard_map/ppermute | solution.py:20

commit v7 on v6

--- a/solution.py
+++ b/solution.py
@@ -317,7 +317,7 @@
         e2_out[j] = fresh[j]
     pair[0] = jnp.where(even2, neigh((1,))[0], 0.0)
     lane = lanes_of((quarter, lanes))
-    odd_layer, odd_depth, item = (lane & 1) != 0, (lane & 2) != 0, lane & 3
+    odd_layer, odd_depth, item = (lane & 1) != 0, (lane & 2) != 0, (lane - position) & 3
     source = group(even_row_sum(pair.at[0], quarter))
     fx = group(jnp.where(odd_layer, even_row_sum(fx2.at[1], quarter), 0.0))
     fy = group(fy2[1, pl.ds(PAD + 1, quarter, 2), :])
@@ -337,243 +337,229 @@
     def __init__(self, mass, source, faces, row_step, lane_step):
         self.source, self.row_step, self.lane_step = source, row_step, lane_step
         self.fx, self.fy, self.fz = faces
-        self.layers, rows, lanes = source.shape
-        nothing = jnp.zeros_like(source[:1])
-        self.nothing = nothing
-        self.fxl = jnp.concatenate([nothing, self.fx[:-1]], 0)
+        self.layers = source.shape[0]
+        self.setup()
+        self.fxl = self.lower(self.fx)
         self.fyl = behind(self.fy, row_step, 1)
         self.fzl = behind(self.fz, lane_step, 2)
-        weight = self.fx + self.fxl + self.fy + self.fyl + self.fz + self.fzl
+        weight = (self.fx + self.fxl) + (self.fy + self.fyl) + (self.fz + self.fzl)
         self.inv = 1.0 / (mass + weight)
-        shape = source.shape
+
+    def setup(self):
+        shape = self.source.shape
         total = lax.broadcasted_iota(jnp.int32, shape, 0)
-        total = total + rows_of(shape) // row_step + lanes_of(shape) // lane_step
+        total = total + rows_of(shape) // self.row_step + lanes_of(shape) // self.lane_step
         self.even = (total & 1) == 0
 
+    def upper(self, e):
+        return jnp.concatenate([e[1:], jnp.zeros_like(e[:1])], 0)
+
+    def lower(self, e):
+        return jnp.concatenate([jnp.zeros_like(e[:1]), e[:-1]], 0)
+
     def neigh(self, e):
-        upper = jnp.concatenate([e[1:], self.nothing], 0)
-        lower = jnp.concatenate([self.nothing, e[:-1]], 0)
-        total = self.fx * upper + self.fxl * lower
+        total = self.fx * self.upper(e) + self.fxl * self.lower(e)
         total = total + self.fy * ahead(e, self.row_step, 1) + self.fyl * behind(e, self.row_step, 1)
         return total + self.fz * ahead(e, self.lane_step, 2) + self.fzl * behind(e, self.lane_step, 2)
 
-    def start(self):
-        e = jnp.where(self.even, self.source * self.inv, 0.0)
-        return self.odd_update(e)
-
-    def even_update(self, e):
-        return jnp.where(self.even, (self.source + self.neigh(e)) * self.inv, e)
-
-    def odd_update(self, e):
-        return jnp.where(self.even, e, (self.source + self.neigh(e)) * self.inv)
-
-    def residual(self, e):
-        return jnp.where(self.even, self.neigh(e), 0.0)
+    def update(self, e):
+        return (self.source + self.neigh(e)) * self.inv
+
+    def cycle(self, deeper):
+        odd = self.update(self.source * self.inv)
+        residual = jnp.where(self.even, self.neigh(odd), 0.0)
+        fix = deeper(self.restricted(residual), self.coarse_faces())
+        even = self.update(odd + self.prolonged(fix))
+        return jnp.where(self.even, even, self.update(even))
 
     def pairs(self, values):
         halves = values.reshape(self.layers // 2, 2, *values.shape[1:])
         return halves[:, 0] + halves[:, 1]
+
+    def in_plane(self, values):
+        return with_partner(with_partner(values, self.row_step, 1), self.lane_step, 2)
+
+    def restricted(self, values):
+        return self.in_plane(self.pairs(values))
 
     def coarse_faces(self):
         row_bit = (rows_of(self.fx.shape) & self.row_step) != 0
         lane_bit = (lanes_of(self.fx.shape) & self.lane_step) != 0
         odd_layers = self.fx.reshape(self.layers // 2, 2, *self.fx.shape[1:])[:, 1]
-        fx = self.in_plane(odd_layers)
-        fy = self.in_plane(self.pairs(jnp.where(row_bit, self.fy, 0.0)))
-        fz = self.in_plane(self.pairs(jnp.where(lane_bit, self.fz, 0.0)))
-        return fx, fy, fz
-
-    def in_plane(self, values):
-        return with_partner(with_partner(values, self.row_step, 1), self.lane_step, 2)
+        fy = self.restricted(jnp.where(row_bit, self.fy, 0.0))
+        fz = self.restricted(jnp.where(lane_bit, self.fz, 0.0))
+        return self.in_plane(odd_layers), fy, fz
+
+    def prolonged(self, fix):
+        both = jnp.concatenate([fix[:, None], fix[:, None]], 1)
+        return both.reshape(self.layers, *fix.shape[1:])
+
+
+class Packed(Level):
+    def __init__(self, mass, source, faces, scratch):
+        self.scratch = scratch
+        super().__init__(mass, source, faces, 1, 4)
+
+    def setup(self):
+        shape = self.source.shape
+        lane = lanes_of(shape)
+        self.slot = lane & 3
+        self.even = ((rows_of(shape) + self.slot + (lane >> 2)) & 1) == 0
+
+    def upper(self, e):
+        return jnp.where(self.slot == 3, super().upper(behind(e, 3, 2)), ahead(e, 1, 2))
+
+    def lower(self, e):
+        return jnp.where(self.slot == 0, super().lower(ahead(e, 3, 2)), behind(e, 1, 2))
+
+    def rows_once(self, ref, start):
+        rows = ref.shape[1] // 2
+        return jnp.concatenate([ref[j, pl.ds(start, rows, 2), :][None] for j in range(self.layers)], 0)
+
+    def opened(self, values):
+        values = with_partner(with_partner(values, 1, 2), 4, 2)
+        second = (lanes_of(values.shape) & 2) != 0
+        one, two = jnp.where(second, behind(values, 2, 2), values), jnp.where(second, values, ahead(values, 2, 2))
+        both = jnp.concatenate([one[:, None], two[:, None]], 1)
+        return both.reshape(2 * self.layers, *values.shape[1:])
 
     def restricted(self, values):
-        return self.in_plane(self.pairs(values))
-
-
-def doubled_layers(values):
-    layers = values.shape[0]
-    both = jnp.concatenate([values[:, None], values[:, None]], 1)
-    return both.reshape(2 * layers, *values.shape[1:])
-
-
-def small_cycle(mass, source, faces, row_step, lane_step, deeper):
+        self.scratch[0] = values
+        return self.opened(self.rows_once(self.scratch.at[0], 0) + self.rows_once(self.scratch.at[0], 1))
+
+    def coarse_faces(self):
+        lane_bit = (lanes_of(self.fx.shape) & 4) != 0
+        self.scratch[1] = jnp.where((self.slot & 1) != 0, self.fx, 0.0)
+        self.scratch[2] = self.fy
+        self.scratch[3] = jnp.where(lane_bit, self.fz, 0.0)
+        fx, fz = [self.rows_once(self.scratch.at[k], 0) + self.rows_once(self.scratch.at[k], 1) for k in (1, 3)]
+        return self.opened(fx), self.opened(self.rows_once(self.scratch.at[2], 1)), self.opened(fz)
+
+    def prolonged(self, fix):
+        halves = fix.reshape(self.layers, 2, *fix.shape[1:])
+        packed = jnp.where((lanes_of(halves[:, 0].shape) & 2) == 0, halves[:, 0], halves[:, 1])
+        for j in range(self.layers):
+            into_both_rows(self.scratch.at[0, j], packed[j])
+        return self.scratch[0]
+
+
+def coarsest(mass, source, faces, row_step, lane_step):
     level = Level(mass, source, faces, row_step, lane_step)
-    e = level.start()
-    if deeper == 0:
-        for turn in range(COARSE_SWEEPS - 1):
-            e = level.odd_update(level.even_update(e))
-        return e
-    fix = small_cycle(
-        8.0 * mass, level.restricted(level.residual(e)), level.coarse_faces(),
-        2 * row_step, 2 * lane_step, deeper - 1,
-    )
-    e = e + doubled_layers(fix)
-    return level.odd_update(level.even_update(e))
-
-
-def chunked(count, size, body):
-    size = min(size, count)
-    if count == size:
-        body(0)
-    else:
-        lax.fori_loop(0, count // size, lambda i, c: (body(i * size), c)[1], 0)
+    rows, lanes = source.shape[1] // row_step, source.shape[2] // lane_step
+    frames = [(m, k) for m in range(rows) for k in range(lanes)]
+
+    def spread(values):
+        copies = {}
+        for m in range(rows):
+            turned = behind(values, m * row_step, 1) if m else values
+            for k in range(lanes):
+                copies[m, k] = behind(turned, k * lane_step, 2) if k else turned
+        return copies
+
+    inv = level.inv
+    start, fx, fxl, fy, fyl, fz, fzl = [
+        spread(values * inv)
+        for values in (source, level.fx, level.fxl, level.fy, level.fyl, level.fz, level.fzl)
+    ]
+
+    def update(e):
+        fresh = {}
+        for m, k in frames:
+            here = e[m, k]
+            total = start[m, k] + fx[m, k] * level.upper(here) + fxl[m, k] * level.lower(here)
+            total = total + (fy[m, k] * e[(m - 1) % rows, k] + fyl[m, k] * e[(m + 1) % rows, k])
+            fresh[m, k] = total + (fz[m, k] * e[m, (k - 1) % lanes] + fzl[m, k] * e[m, (k + 1) % lanes])
+        return fresh
+
+    even = start
+    odd = update(even)
+    for turn in range(COARSE_SWEEPS - 1):
+        even = update(odd)
+        odd = update(even)
+    return jnp.where(level.even, even[0, 0], odd[0, 0])
+
+
+def small_cycle(mass, source, faces, row_step, lane_step, between):
+    if between == 0:
+        return coarsest(mass, source, faces, row_step, lane_step)
+    level = Level(mass, source, faces, row_step, lane_step)
+    return level.cycle(
+        lambda inner, inner_faces: small_cycle(
+            8.0 * mass, inner, inner_faces, 2 * row_step, 2 * lane_step, between - 1
+        )
+    )
 
 
 def coarse_kernel(
     owner_of, same_cores, other_cores, e2_in, s2, fx2, fxl2, fy2, fz2, inv2,
     inputs, field, fx_in, fx_outer, fy_in, fz_in, inv_in, across_in, within_in,
-    solved, owned,
-    s3, fx3, fy3, fz3, fzl3, inv3, e3, pair3, small, e2, fzl2, e1, cor, owner_here, sem,
+    solved_out, owned_out,
+    e3, turn3, pair, e2, fzl2, e1, cor, solved, owned, owner_here, fetch_sem, sems,
 ):
-    fetch = pltpu.make_async_copy(owner_of, owner_here, sem)
+    fetch = pltpu.make_async_copy(owner_of, owner_here, fetch_sem)
     fetch.start()
     chips, _, quarter, lanes = same_cores.shape
     blocks = 2 * chips
     half, height = 2 * quarter, 4 * quarter
     position, last = lax.axis_index("gx"), blocks - 1
 
-    body3, up3, down3 = pl.ds(PAD, quarter), pl.ds(PAD + 1, quarter), pl.ds(PAD - 1, quarter)
-    row, lane = rows_of((quarter, lanes)), lanes_of((quarter, lanes))
-    parity3 = row + (lane >> 2)
-    item = lane & 3
-    edge3 = jnp.zeros((quarter + 2 * PAD, lanes), jnp.float32)
-    for j in (0, blocks + 1):
-        e3[j] = edge3
-    fx3[0] = jnp.zeros((quarter, lanes), jnp.float32)
-
-    def unpack(at):
-        tiles = []
-        for i in range(0, min(16, blocks), 2):
-            chip = (at + i) // 2
-            tiles.extend(by_side(same_cores[chip, 0], other_cores[chip, 0]))
-        for i, tile in enumerate(tiles):
-            j = at + i
-            moved = {0: tile}
-            for step in (1, 2, 3):
-                moved[step] = ahead(tile, step, 1)
-                moved[-step] = behind(tile, step, 1)
-            spread = []
-            for k in range(4):
-                value = moved[k]
-                for slot in (1, 2, 3):
-                    value = jnp.where(item == slot, moved[k - slot], value)
-                spread.append(value)
-            s3[j] = spread[0]
-            fx3[j + 1] = spread[1]
-            fy3[j] = edge3
-            fy3[j, body3] = spread[2]
-            fz3[j] = spread[3]
-            fzl3[j] = behind(spread[3], 4, 1)
-
-    chunked(blocks, 16, unpack)
-
-    def is_even3(j):
-        return ((parity3 + j) & 1) == 0
-
-    def weights3(at):
-        for i in range(min(16, blocks)):
-            j = at + i
-            weight = fx3[j + 1] + fx3[j] + fy3[j, body3] + fy3[j, down3] + fz3[j] + fzl3[j]
-            inverse = 1.0 / (64.0 + weight)
-            inv3[j] = inverse
-            e3[j + 1] = edge3
-            e3[j + 1, body3] = jnp.where(is_even3(j), s3[j] * inverse, 0.0)
-
-    chunked(blocks, 16, weights3)
-
-    def neigh3(j):
-        here = e3[j + 1, body3]
-        sums = fx3[j + 1] * e3[j + 2, body3] + fx3[j] * e3[j, body3]
-        sums = sums + fy3[j, body3] * e3[j + 1, up3] + fy3[j, down3] * e3[j + 1, down3]
-        return here, sums + fz3[j] * ahead(here, 4, 1) + fzl3[j] * behind(here, 4, 1)
-
-    def update3(at, count, even):
-        fresh = []
-        for i in range(count):
-            j = at + i
-            here, sums = neigh3(j)
-            value = (s3[j] + sums) * inv3[j]
-            where = is_even3(j)
-            fresh.append(jnp.where(where, value, here) if even else jnp.where(where, here, value))
-        for i in range(count):
-            e3[at + i + 1, body3] = fresh[i]
-
-    chunked(blocks, 16, lambda at: update3(at, min(16, blocks), False))
-
-    def restrict3(at):
-        for i in range(0, min(16, blocks), 2):
-            j = at + i
-            parts = []
-            for k in (j, j + 1):
-                _, sums = neigh3(k)
-                parts.append(jnp.where(is_even3(k), sums, 0.0))
-            pair3[i, :quarter] = parts[0] + parts[1]
-            pair3[i + 1, :quarter] = fz3[j] + fz3[j + 1]
-        for i in range(0, min(16, blocks), 2):
-            j = at + i
-            out = (at + i) // 2
-            small[0, out] = with_partner(even_row_sum(pair3.at[i], PAD), 4, 1)
-            fxs = fx3[j + 2, pl.ds(0, PAD, 2), :] + fx3[j + 2, pl.ds(1, PAD, 2), :]
-            small[1, out] = with_partner(fxs, 4, 1)
-            fys = fy3[j, pl.ds(PAD + 1, PAD, 2), :] + fy3[j + 1, pl.ds(PAD + 1, PAD, 2), :]
-            small[2, out] = with_partner(fys, 4, 1)
-            fzs = even_row_sum(pair3.at[i + 1], PAD)
-            odd = (lanes_of((PAD, lanes)) & 4) != 0
-            small[3, out] = with_partner(jnp.where(odd, fzs, 0.0), 4, 1)
-
-    chunked(blocks, 16, restrict3)
-
-    small[0] = small_cycle(512.0, small[0], (small[1], small[2], small[3]), 1, 8, 2)
-
-    def prolong3(at):
-        for i in range(min(16, blocks)):
-            j = at + i
-            fix = small[0, j // 2]
-            pair3[i, pl.ds(0, PAD, 2), :] = fix
-            pair3[i, pl.ds(1, PAD, 2), :] = fix
-        for i in range(min(16, blocks)):
-            j = at + i
-            e3[j + 1, body3] = e3[j + 1, body3] + pair3[i, :quarter]
-
-    chunked(blocks, 16, prolong3)
-    chunked(blocks, 16, lambda at: update3(at, min(16, blocks), True))
-    chunked(blocks, 16, lambda at: update3(at, min(16, blocks), False))
+    slot = lanes_of((quarter, lanes)) & 3
+    tiles = []
+    for chip in range(chips):
+        tiles.extend(by_side(same_cores[chip, 0], other_cores[chip, 0]))
+    items = []
+    for k in range(4):
+        packs = []
+        for j in range(0, blocks, 4):
+            value = tiles[j + (3 - k) % 4]
+            for at in range(3):
+                value = jnp.where(slot == at, tiles[j + (at - k) % 4], value)
+            if k:
+                value = jnp.where(slot < 4 - k, ahead(value, k, 1), behind(value, 4 - k, 1))
+            packs.append(value[None])
+        items.append(jnp.concatenate(packs, 0))
+    third = Packed(64.0, items[0], items[1:], turn3)
+    e3[...] = third.cycle(lambda inner, faces: small_cycle(512.0, inner, faces, 1, 8, 2))
 
     fetch.wait()
     owner = owner_here[position]
     wide, narrow = lanes_of((lanes, lanes)), rows_of((lanes, lanes))
-    take = jnp.where(narrow == 4 * wide, 1.0, 0.0)
+    take = jnp.where(narrow == 4 * wide + owner % 4, 1.0, 0.0)
     block = jnp.dot(
-        e3[owner + 1, body3], take, precision=lax.Precision.HIGHEST, preferred_element_type=jnp.float32
+        e3[owner // 4], take, precision=lax.Precision.HIGHEST, preferred_element_type=jnp.float32
     )
     owned[0] = block[:, : lanes // 4]
+    copies = [pltpu.make_async_copy(owned, owned_out, sems.at[0])]
+    copies[0].start()
 
     first_of_two, even2 = parities2(half, lanes)
     body2 = pl.ds(PAD, half)
     edge = jnp.zeros((PAD, lanes), jnp.float32)
     left = other_cores[jnp.maximum(position - 1, 0) // 2, 1]
     right = other_cores[jnp.minimum(position + 1, last) // 2, 1]
-    into_both_rows(pair3.at[0], left)
-    into_both_rows(pair3.at[1], right)
-    left, right = pair3[0], pair3[1]
+    into_both_rows(pair.at[5], left)
+    into_both_rows(pair.at[6], right)
+    left, right = pair[5], pair[6]
     before = (
         left, jnp.where(first_of_two, left, e2_in[0]), e2_in[1], jnp.where(first_of_two, e2_in[2], right), right
     )
     for k in range(5):
-        third = jnp.clip(position + k - 1, 1, blocks)
-        into_both_rows(pair3.at[k % 4], e3[third, body3])
+        j = jnp.clip(position + k - 2, 0, last)
+        into_both_rows(pair.at[k], group(jnp.where(slot == j % 4, e3[j // 4], 0.0)))
         e2[k, :PAD] = edge
         e2[k, PAD + half:] = edge
-        e2[k, body2] = before[k] + pair3[k % 4]
+        e2[k, body2] = before[k] + pair[k]
     for j in range(3):
         fzl2[j] = behind(fz2[j], 2, 1)
-    for even in (True, False):
-        fresh = []
-        for j, sums in enumerate(neigh2(e2, fx2, fxl2, fy2, fz2, fzl2, first_of_two, (0, 1, 2))):
-            value, here = (s2[j] + sums) * inv2[j], e2[j + 1, body2]
-            fresh.append(jnp.where(even2, value, here) if even else jnp.where(even2, here, value))
-        for j in range(3):
-            e2[j + 1, body2] = fresh[j]
+
+    def update2():
+        sums = neigh2(e2, fx2, fxl2, fy2, fz2, fzl2, first_of_two, (0, 1, 2))
+        return [(s2[j] + sums[j]) * inv2[j] for j in range(3)]
+
+    fresh = update2()
+    for j in range(3):
+        e2[j + 1, body2] = fresh[j]
+    fixes2 = [jnp.where(even2, even, odd) for even, odd in zip(fresh, update2())]
 
     _, source, _ = three_parts(inputs)
     body1, up1, down1 = pl.ds(PAD, height), pl.ds(PAD + 1, height), pl.ds(PAD - 1, height)
@@ -583,14 +569,14 @@
     fixes = []
     for w in range(count):
         tile, t = divmod((w - 1) // 2, 2)
-        packed = e2[2 + tile, body2]
-        if t == 0:
-            plain = jnp.where(first_of_two, packed, behind(packed, 1, 1))
-        else:
-            plain = jnp.where(first_of_two, ahead(packed, 1, 1), packed)
+        packed = fixes2[1 + tile]
         if w % 2 == 1 or w == 0:
-            into_both_rows(cor.at[len(fixes) % 2], plain)
-            fixes.append(cor[len(fixes) % 2])
+            if t == 0:
+                plain = jnp.where(first_of_two, packed, behind(packed, 1, 1))
+            else:
+                plain = jnp.where(first_of_two, ahead(packed, 1, 1), packed)
+            into_both_rows(cor.at[len(fixes)], plain)
+            fixes.append(cor[len(fixes)])
         e1[w, :PAD] = edge
         e1[w, PAD + height:] = edge
         e1[w, body1] = field[w, body1] + fixes[-1]
@@ -605,16 +591,20 @@
         sums = fx_in[w] * e1[w + 1, body1] + fx_in[w - 1] * e1[w - 1, body1] + in_layer1(w)
         return jnp.where(keep, e1[w, body1], (source[w - 1] + sums) * inv_in[w])
 
+    borders = by_side(across_in[4], within_in[4])
     for w in range(1, count - 1):
         e1[w, body1] = smoothed1(w, 0)
-    borders = by_side(across_in[4], within_in[4])
     for side, w, near in ((0, 0, 1), (1, count - 1, count - 2)):
-        into_both_rows(cor.at[side], borders[side])
-        sums = cor[side] + fx_outer[side] * fixes[0 if side == 0 else -1]
+        into_both_rows(cor.at[4 + side], borders[side])
+        sums = cor[4 + side] + fx_outer[side] * fixes[0 if side == 0 else -1]
         sums = sums + fx_in[min(w, near)] * e1[near, body1] + in_layer1(w)
         e1[w, body1] = sums * inv_in[w]
     for w in range(1, count - 1):
         solved[w - 1] = smoothed1(w, 1)
+        copies.append(pltpu.make_async_copy(solved.at[w - 1], solved_out.at[w - 1], sems.at[w]))
+        copies[-1].start()
+    for copy in copies:
+        copy.wait()
 
 
 def f32(*shape):
@@ -625,7 +615,7 @@
     return pltpu.VMEM(shape, jnp.float32)
 
 
-def call(kernel, outs, scratch, operands):
+def call(kernel, outs, scratch, operands, out_space=pltpu.VMEM):
     def size(shape):
         count = 4
         for extent in shape:
@@ -638,7 +628,7 @@
         kernel,
         out_shape=tuple(outs),
         in_specs=[pl.BlockSpec(memory_space=pltpu.VMEM)] * len(operands),
-        out_specs=tuple([pl.BlockSpec(memory_space=pltpu.VMEM)] * len(outs)),
+        out_specs=tuple([pl.BlockSpec(memory_space=out_space)] * len(outs)),
         scratch_shapes=scratch,
         compiler_params=pltpu.CompilerParams(vmem_limit_bytes=asked),
     )(*operands)
@@ -649,7 +639,7 @@
     half, quarter = height // 2, height // 4
     blocks = lax.axis_size("gx")
     window = layers + 2
-    padded, padded2, padded3 = height + 2 * PAD, half + 2 * PAD, quarter + 2 * PAD
+    padded, padded2 = height + 2 * PAD, half + 2 * PAD
     inputs = sum(
         jnp.pad(block, ((k * layers, (2 - k) * layers), (0, 0), (0, 0)))
         for k, block in enumerate((iterate, source, phase_field))
@@ -681,13 +671,13 @@
         coarse_kernel,
         [f32(layers, height, depth), f32(1, quarter, depth // 4)],
         [
-            vmem(blocks, quarter, depth), vmem(blocks + 1, quarter, depth), vmem(blocks, padded3, depth),
-            vmem(blocks, quarter, depth), vmem(blocks, quarter, depth), vmem(blocks, quarter, depth),
-            vmem(blocks + 2, padded3, depth), vmem(16, half, depth), vmem(4, blocks // 2, PAD, depth),
-            vmem(5, padded2, depth), vmem(3, half, depth), vmem(window, padded, depth), vmem(2, height, depth),
-            pltpu.SMEM((blocks,), jnp.int32), pltpu.SemaphoreType.DMA,
+            vmem(blocks // 4, quarter, depth), vmem(4, blocks // 4, quarter, depth), vmem(7, half, depth),
+            vmem(5, padded2, depth), vmem(3, half, depth), vmem(window, padded, depth), vmem(6, height, depth),
+            vmem(layers, height, depth), vmem(1, quarter, depth // 4), pltpu.SMEM((blocks,), jnp.int32),
+            pltpu.SemaphoreType.DMA, pltpu.SemaphoreType.DMA((layers + 1,)),
         ],
         (block_owner, same_cores, other_cores, *middle, inputs, *fine, *halos),
+        pl.ANY,
     )
     return solved, owned
 

time: 36.6 us -> 36.6 us (level)
  no operation moved by 1% of the time
where the time goes in v7:
time: 36.6 us; the launch traced here: 36.4 us
  blocking collectives  18.8 us (51%)
  starting transfers between devices  7.67 us (21%)
  Pallas kernels  5.54 us (15%)
  waiting for transfers between devices  2.57 us (7%)
  other arithmetic  1.06 us (3%)
  between operations  0.68 us (2%)
    all_to_all x1, blocking collectives, on_device(): lax.all_to_all(slots, 'gx', 0, 0, axis_index_groups=kinds, tiled=True)  18.8 us
    ppermute x3, starting transfers between devices, within_chip(): lax.ppermute(block, 'gx', [(i, i ^ 1) for i in range(lax.axis_size('gx'))])  6.35 us
    pallas_call x4, Pallas kernels, call(): pl.pallas_call(kernel, out_shape=tuple(outs), in_specs=[pl.BlockSpec(memo...  5.54 us
    ppermute x3, waiting for transfers between devices, within_chip(): lax.ppermute(block, 'gx', [(i, i ^ 1) for i in range(lax.axis_size('gx'))])  2.57 us
    ppermute x2, starting transfers between devices, swapped(): return (lax.ppermute(across, 'gx', chips), within_chip(within))  1.32 us
    add x1, other arithmetic, on_device(): sum((jnp.pad(block, ((k * layers, (2 - k) * layers), (0, 0), (0, 0))) for...  1.06 us
  transfers between devices with their start and end apart: 5, of which 3 were waited for; matrix products, arithmetic and copies ran while one was open for 0% of the time, Pallas kernels for 0%

profile of v7, /device:TPU:0, one launch (start us, length us, event | category | flops | bytes accessed | tf_op | source)
XLA Modules:
  0.0 36.4 jit_solution(10578206645623435966)
XLA Ops:
  0.6 1.1 %pad_add_fusion.inputs = f32[12,64,128]{2,1,0:T(8,128)S(1)} fusion(f32[4,64,128]{2,1,0:T(8,128)} %param.6, f32[4,64,128]{2,1,0:T(8,128)} %param.5, f32[4,64,128]{2,1,0:T(8,128)} %param.4), kind=kLoop, calls=%fused_computation | loop fusion | flops 196608 | bytes 786432 | tf_op jit(solution)/shard_map/add | solution.py:643
  1.7 0.3 shard_map.59
  2.0 0.0 copy-start
  2.0 0.7 %collective-permute-start = (f32[224,128]{1,0:T(8,128)S(1)}, f32[224,128]{1,0:T(8,128)S(1)}, u32[]{:S(2)}, u32[]{:S(2)}) collective-permute-start(f32[224,128]{1,0:T(8,128)S(1)} %get-tuple-element.21), channel_id=1, source_target_pairs={{1,2},{2,1},{3,4},{4,3},{5,6},{6,5},{7,8},{8,7},{9,10},{10,9},{11,... | collective-permute-start | bytes 344072 | tf_op jit(solution)/shard_map/ppermute | solution.py:16
  2.7 4.4 %collective-permute-start.1 = (f32[224,128]{1,0:T(8,128)S(1)}, f32[224,128]{1,0:T(8,128)S(1)}, u32[]{:S(2)}, u32[]{:S(2)}) collective-permute-start(f32[224,128]{1,0:T(8,128)S(1)} %get-tuple-element.22), channel_id=1, source_target_pairs={{0,1},{1,0},{2,3},{3,2},{4,5},{5,4},{6,7},{7,6},{8,9},{9,8},{10,11... | collective-permute-start | bytes 344072 | tf_op jit(solution)/shard_map/ppermute | solution.py:20
  7.0 0.0 collective-permute-done.across_in
  7.0 1.0 %collective-permute-done.1.within_in = f32[224,128]{1,0:T(8,128)S(1)} collective-permute-done((f32[224,128]{1,0:T(8,128)S(1)}, f32[224,128]{1,0:T(8,128)S(1)}, u32[]{:S(2)}, u32[]{:S(2)}) %collective-permute-start.1) | collective-permute-done | bytes 114720 | tf_op jit(solution)/shard_map/ppermute | solution.py:20
  8.0 0.0 copy-done
  8.0 0.9 %shard_map.60 = (f32[5,32,128]{2,1,0:T(8,128)S(1)}, f32[5,32,128]{2,1,0:T(8,128)S(1)}, f32[2,32,128]{2,1,0:T(8,128)S(1)}, f32[6,80,128]{2,1,0:T(8,128)S(1)}, f32...) custom-call(s32[16]{0:T(128)S(1)} %copy-done, ...), custom_call_target="tpu_custom_call" | custom-call | tf_op jit(solution)/shard_map/pallas_call | solution.py:627
  8.9 2.0 %collective-permute-start.3 = (f32[5,32,128]{2,1,0:T(8,128)S(1)}, f32[5,32,128]{2,1,0:T(8,128)S(1)}, u32[]{:S(2)}, u32[]{:S(2)}) collective-permute-start(f32[5,32,128]{2,1,0:T(8,128)S(1)} %get-tuple-element.25), channel_id=1, source_target_pairs={{0,1},{1,0},{2,3},{3,2},{4,5},{5,4},{6,7},{7,6},{8,9},{9,8},{10,11... | collective-permute-start | bytes 245768 | tf_op jit(solution)/shard_map/ppermute | solution.py:20
  10.9 0.7 %collective-permute-start.2 = (f32[5,32,128]{2,1,0:T(8,128)S(1)}, f32[5,32,128]{2,1,0:T(8,128)S(1)}, u32[]{:S(2)}, u32[]{:S(2)}) collective-permute-start(f32[5,32,128]{2,1,0:T(8,128)S(1)} %get-tuple-element.23.own), channel_id=1, source_target_pairs={{1,2},{2,1},{3,4},{4,3},{5,6},{6,5},{7,8},{8,7},{9,10},{10,9},{11,... | collective-permute-start | bytes 245768 | tf_op jit(solution)/shard_map/ppermute | solution.py:16
  11.5 0.3 collective-permute-done.3.within_in
  11.8 0.0 collective-permute-done.2.across_in
  11.8 0.5 %shard_map.61 = (f32[8,2,16,128]{3,2,1,0:T(8,128)S(1)}, f32[3,32,128]{2,1,0:T(8,128)S(1)}, f32[3,32,128]{2,1,0:T(8,128)S(1)}, f32[3,32,128]{2,1,0:T(8,128)S(1)},...) custom-call(f32[5,32,128]{2,1,0:T(8,128)S(1)} %get-tuple-element.23., ...), custom_call_target="tpu_custom_call" | custom-call | tf_op jit(solution)/shard_map/pallas_call | solution.py:627
  12.3 18.8 %all_to_all.5.same_cores = f32[8,2,16,128]{3,2,1,0:T(8,128)S(1)} all-to-all(f32[8,2,16,128]{3,2,1,0:T(8,128)S(1)} %get-tuple-element.26), channel_id=1, replica_groups={{0,2,4,6,8,10,12,14},{1,3,5,7,9,11,13,15},{16,18,20,22,24,26,28,30},{17..., dimensions={0} | all-to-all | bytes 262144 | tf_op jit(solution)/shard_map/all_to_all | solution.py:668
  31.1 0.0 collective-permute-start.4
  31.1 1.3 %collective-permute-done.4.other_cores = f32[8,2,16,128]{3,2,1,0:T(8,128)S(1)} collective-permute-done((f32[8,2,16,128]{3,2,1,0:T(8,128)S(1)}, f32[8,2,16,128]{3,2,1,0:T(8,128)S(1)}, u32[]{:S(2)}, u32[]{:S(2)}) %collective-permute-start.4) | collective-permute-done | bytes 131104 | tf_op jit(solution)/shard_map/ppermute | solution.py:20
  32.5 3.9 %shard_map.62 = (f32[4,64,128]{2,1,0:T(8,128)}, f32[1,16,32]{2,1,0:T(8,128)}) custom-call(s32[16]{0:T(128)S(1)} %copy-done, f32[8,2,16,128]{3,2,1,0:T(8,128)S(1)} %all_to_all.5.same_cores, f32[8,2,16,128]{3,2,1,0:T(8,128)S(1)} %collective-permute-done.4.other_cores, f32[3,32,128]{2,1,0:T(8,128)S(1)} %get-tuple-element.27.e2_in, ...), custom_call_target="tpu_custom_call" | custom-call | tf_op jit(solution)/shard_map/pallas_call | solution.py:627
Async XLA Ops:
  2.0 6.0 %copy-start = (s32[16]{0:T(128)S(1)}, s32[16]{0:T(128)}, u32[]{:S(2)}) copy-start(s32[16]{0:T(128)} %owner_of.3) | copy-start | bytes 196
  2.0 5.0 %collective-permute-start = (f32[224,128]{1,0:T(8,128)S(1)}, f32[224,128]{1,0:T(8,128)S(1)}, u32[]{:S(2)}, u32[]{:S(2)}) collective-permute-start(f32[224,128]{1,0:T(8,128)S(1)} %get-tuple-element.21), channel_id=1, source_target_pairs={{1,2},{2,1},{3,4},{4,3},{5,6},{6,5},{7,8},{8,7},{9,10},{10,9},{11,... | collective-permute-start | bytes 344072 | tf_op jit(solution)/shard_map/ppermute | solution.py:16
  2.7 5.3 %collective-permute-start.1 = (f32[224,128]{1,0:T(8,128)S(1)}, f32[224,128]{1,0:T(8,128)S(1)}, u32[]{:S(2)}, u32[]{:S(2)}) collective-permute-start(f32[224,128]{1,0:T(8,128)S(1)} %get-tuple-element.22), channel_id=1, source_target_pairs={{0,1},{1,0},{2,3},{3,2},{4,5},{5,4},{6,7},{7,6},{8,9},{9,8},{10,11... | collective-permute-start | bytes 344072 | tf_op jit(solution)/shard_map/ppermute | solution.py:20
  8.9 2.9 %collective-permute-start.3 = (f32[5,32,128]{2,1,0:T(8,128)S(1)}, f32[5,32,128]{2,1,0:T(8,128)S(1)}, u32[]{:S(2)}, u32[]{:S(2)}) collective-permute-start(f32[5,32,128]{2,1,0:T(8,128)S(1)} %get-tuple-element.25), channel_id=1, source_target_pairs={{0,1},{1,0},{2,3},{3,2},{4,5},{5,4},{6,7},{7,6},{8,9},{9,8},{10,11... | collective-permute-start | bytes 245768 | tf_op jit(solution)/shard_map/ppermute | solution.py:20
  10.9 0.9 %collective-permute-start.2 = (f32[5,32,128]{2,1,0:T(8,128)S(1)}, f32[5,32,128]{2,1,0:T(8,128)S(1)}, u32[]{:S(2)}, u32[]{:S(2)}) collective-permute-start(f32[5,32,128]{2,1,0:T(8,128)S(1)} %get-tuple-element.23.own), channel_id=1, source_target_pairs={{1,2},{2,1},{3,4},{4,3},{5,6},{6,5},{7,8},{8,7},{9,10},{10,9},{11,... | collective-permute-start | bytes 245768 | tf_op jit(solution)/shard_map/ppermute | solution.py:16
  31.1 1.3 %collective-permute-start.4 = (f32[8,2,16,128]{3,2,1,0:T(8,128)S(1)}, f32[8,2,16,128]{3,2,1,0:T(8,128)S(1)}, u32[]{:S(2)}, u32[]{:S(2)}) collective-permute-start(f32[8,2,16,128]{3,2,1,0:T(8,128)S(1)} %all_to_all.5.same_cores), channel_id=1, source_target_pairs={{0,1},{1,0},{2,3},{3,2},{4,5},{5,4},{6,7},{7,6},{8,9},{9,8},{10,11... | collective-permute-start | bytes 393224 | tf_op jit(solution)/shard_map/ppermute | solution.py:20

commit v8 on v7

--- a/solution.py
+++ b/solution.py
@@ -119,8 +119,8 @@
 
 def fine_down_kernel(
     owner_of, inputs, across_in, within_in,
-    across, within, fx2_out, e, fx, fx_outer, fy, fz, inv,
-    cell, fzl, held, pair,
+    across, within, fx2_out, e, fx, fx_outer, fy, fz, fzl, inv,
+    cell, held, pair,
 ):
     iterate, source, phase = three_parts(inputs)
     layers, height, depth = iterate.shape
@@ -271,8 +271,8 @@
 
 def middle_down_kernel(
     own, own_fx, across_in, within_in,
-    slots, e2_out, s2, fx2, fxl2, fy2, fz2, inv2,
-    e2, fzl2, pair,
+    slots, e2_out, s2, fx2, fxl2, fy2, fz2, fzl2, inv2,
+    e2, pair,
 ):
     _, half, lanes = own.shape
     quarter = half // 2
@@ -317,7 +317,8 @@
         e2_out[j] = fresh[j]
     pair[0] = jnp.where(even2, neigh((1,))[0], 0.0)
     lane = lanes_of((quarter, lanes))
-    odd_layer, odd_depth, item = (lane & 1) != 0, (lane & 2) != 0, (lane - position) & 3
+    slot = position // (slots.shape[0] // 2)
+    odd_layer, odd_depth, item = (lane & 1) != 0, (lane & 2) != 0, (lane - slot) & 3
     source = group(even_row_sum(pair.at[0], quarter))
     fx = group(jnp.where(odd_layer, even_row_sum(fx2.at[1], quarter), 0.0))
     fy = group(fy2[1, pl.ds(PAD + 1, quarter, 2), :])
@@ -333,34 +334,38 @@
         slots[c, 1] = jnp.where(position < 2 * c + 1 - position % 2, for_right, for_left)
 
 
+def joined(one, two):
+    return jnp.concatenate([part for part in (one, two) if part.shape[0]], 0)
+
+
 class Level:
-    def __init__(self, mass, source, faces, row_step, lane_step):
-        self.source, self.row_step, self.lane_step = source, row_step, lane_step
+    def __init__(self, mass, source, faces, row_step, lane_step, slot_step):
+        self.source, self.row_step, self.lane_step, self.slot_step = source, row_step, lane_step, slot_step
         self.fx, self.fy, self.fz = faces
-        self.layers = source.shape[0]
-        self.setup()
+        self.tiles = source.shape[0]
+        shape = source.shape
+        self.lane = lanes_of(shape)
+        layer = lax.broadcasted_iota(jnp.int32, shape, 0) if self.tiles > 1 else self.lane // slot_step
+        self.even = ((layer + rows_of(shape) // row_step + self.lane // lane_step) & 1) == 0
         self.fxl = self.lower(self.fx)
-        self.fyl = behind(self.fy, row_step, 1)
+        self.fyl = self.row_shifts(self.fy)[1]
         self.fzl = behind(self.fz, lane_step, 2)
         weight = (self.fx + self.fxl) + (self.fy + self.fyl) + (self.fz + self.fzl)
         self.inv = 1.0 / (mass + weight)
 
-    def setup(self):
-        shape = self.source.shape
-        total = lax.broadcasted_iota(jnp.int32, shape, 0)
-        total = total + rows_of(shape) // self.row_step + lanes_of(shape) // self.lane_step
-        self.even = (total & 1) == 0
-
     def upper(self, e):
-        return jnp.concatenate([e[1:], jnp.zeros_like(e[:1])], 0)
+        return joined(e[1:], ahead(e[:1], self.slot_step, 2))
 
     def lower(self, e):
-        return jnp.concatenate([jnp.zeros_like(e[:1]), e[:-1]], 0)
+        return joined(behind(e[-1:], self.slot_step, 2), e[:-1])
+
+    def row_shifts(self, e):
+        return ahead(e, self.row_step, 1), behind(e, self.row_step, 1)
 
     def neigh(self, e):
-        total = self.fx * self.upper(e) + self.fxl * self.lower(e)
-        total = total + self.fy * ahead(e, self.row_step, 1) + self.fyl * behind(e, self.row_step, 1)
-        return total + self.fz * ahead(e, self.lane_step, 2) + self.fzl * behind(e, self.lane_step, 2)
+        above, below = self.row_shifts(e)
+        total = (self.fx * self.upper(e) + self.fxl * self.lower(e)) + (self.fy * above + self.fyl * below)
+        return total + (self.fz * ahead(e, self.lane_step, 2) + self.fzl * behind(e, self.lane_step, 2))
 
     def update(self, e):
         return (self.source + self.neigh(e)) * self.inv
@@ -372,103 +377,131 @@
         even = self.update(odd + self.prolonged(fix))
         return jnp.where(self.even, even, self.update(even))
 
+    def coarse_slot_step(self):
+        return self.slot_step if self.tiles > 1 else 2 * self.slot_step
+
     def pairs(self, values):
-        halves = values.reshape(self.layers // 2, 2, *values.shape[1:])
+        if self.tiles == 1:
+            return with_partner(values, self.slot_step, 2)
+        halves = values.reshape(self.tiles // 2, 2, *values.shape[1:])
         return halves[:, 0] + halves[:, 1]
 
-    def in_plane(self, values):
-        return with_partner(with_partner(values, self.row_step, 1), self.lane_step, 2)
+    def odd_layers(self, values):
+        if self.tiles == 1:
+            return with_partner(jnp.where((self.lane & self.slot_step) != 0, values, 0.0), self.slot_step, 2)
+        return values.reshape(self.tiles // 2, 2, *values.shape[1:])[:, 1]
+
+    def row_pairs(self, values):
+        return with_partner(values, self.row_step, 1)
+
+    def odd_rows(self, values):
+        odd = (rows_of(values.shape) & self.row_step) != 0
+        return with_partner(jnp.where(odd, values, 0.0), self.row_step, 1)
 
     def restricted(self, values):
-        return self.in_plane(self.pairs(values))
+        return with_partner(self.row_pairs(self.pairs(values)), self.lane_step, 2)
 
     def coarse_faces(self):
-        row_bit = (rows_of(self.fx.shape) & self.row_step) != 0
-        lane_bit = (lanes_of(self.fx.shape) & self.lane_step) != 0
-        odd_layers = self.fx.reshape(self.layers // 2, 2, *self.fx.shape[1:])[:, 1]
-        fy = self.restricted(jnp.where(row_bit, self.fy, 0.0))
-        fz = self.restricted(jnp.where(lane_bit, self.fz, 0.0))
-        return self.in_plane(odd_layers), fy, fz
+        fx = with_partner(self.row_pairs(self.odd_layers(self.fx)), self.lane_step, 2)
+        fy = with_partner(self.odd_rows(self.pairs(self.fy)), self.lane_step, 2)
+        return fx, fy, self.restricted(jnp.where((self.lane & self.lane_step) != 0, self.fz, 0.0))
 
     def prolonged(self, fix):
+        if self.tiles == 1:
+            return fix
         both = jnp.concatenate([fix[:, None], fix[:, None]], 1)
-        return both.reshape(self.layers, *fix.shape[1:])
-
-
-class Packed(Level):
+        return both.reshape(self.tiles, *fix.shape[1:])
+
+
+class Rows(Level):
     def __init__(self, mass, source, faces, scratch):
-        self.scratch = scratch
-        super().__init__(mass, source, faces, 1, 4)
-
-    def setup(self):
-        shape = self.source.shape
-        lane = lanes_of(shape)
-        self.slot = lane & 3
-        self.even = ((rows_of(shape) + self.slot + (lane >> 2)) & 1) == 0
-
-    def upper(self, e):
-        return jnp.where(self.slot == 3, super().upper(behind(e, 3, 2)), ahead(e, 1, 2))
-
-    def lower(self, e):
-        return jnp.where(self.slot == 0, super().lower(ahead(e, 3, 2)), behind(e, 1, 2))
-
-    def rows_once(self, ref, start):
-        rows = ref.shape[1] // 2
-        return jnp.concatenate([ref[j, pl.ds(start, rows, 2), :][None] for j in range(self.layers)], 0)
-
-    def opened(self, values):
-        values = with_partner(with_partner(values, 1, 2), 4, 2)
-        second = (lanes_of(values.shape) & 2) != 0
-        one, two = jnp.where(second, behind(values, 2, 2), values), jnp.where(second, values, ahead(values, 2, 2))
-        both = jnp.concatenate([one[:, None], two[:, None]], 1)
-        return both.reshape(2 * self.layers, *values.shape[1:])
-
-    def restricted(self, values):
-        self.scratch[0] = values
-        return self.opened(self.rows_once(self.scratch.at[0], 0) + self.rows_once(self.scratch.at[0], 1))
-
-    def coarse_faces(self):
-        lane_bit = (lanes_of(self.fx.shape) & 4) != 0
-        self.scratch[1] = jnp.where((self.slot & 1) != 0, self.fx, 0.0)
-        self.scratch[2] = self.fy
-        self.scratch[3] = jnp.where(lane_bit, self.fz, 0.0)
-        fx, fz = [self.rows_once(self.scratch.at[k], 0) + self.rows_once(self.scratch.at[k], 1) for k in (1, 3)]
-        return self.opened(fx), self.opened(self.rows_once(self.scratch.at[2], 1)), self.opened(fz)
+        self.scratch, self.used = scratch, 0
+        self.rows = source.shape[1]
+        super().__init__(mass, source, faces, 1, 4, 1)
+
+    def place(self):
+        self.used += 1
+        return self.scratch.at[self.used % self.scratch.shape[0]]
+
+    def row_shifts(self, e):
+        place = self.place()
+        edge = jnp.zeros((e.shape[0], PAD, e.shape[2]), jnp.float32)
+        place[:, :PAD] = edge
+        place[:, PAD + self.rows:] = edge
+        place[:, pl.ds(PAD, self.rows)] = e
+        return place[:, pl.ds(PAD + 1, self.rows)], place[:, pl.ds(PAD - 1, self.rows)]
+
+    def every_other(self, values, starts):
+        place, tiles = self.place(), values.shape[0]
+        place[:tiles, : self.rows] = values
+        found = 0.0
+        for start in starts:
+            found = found + jnp.concatenate(
+                [place[j, pl.ds(start, self.rows // 2, 2), :][None] for j in range(tiles)], 0
+            )
+        return found
+
+    def row_pairs(self, values):
+        return self.every_other(values, (0, 1))
+
+    def odd_rows(self, values):
+        return self.every_other(values, (1,))
 
     def prolonged(self, fix):
-        halves = fix.reshape(self.layers, 2, *fix.shape[1:])
-        packed = jnp.where((lanes_of(halves[:, 0].shape) & 2) == 0, halves[:, 0], halves[:, 1])
-        for j in range(self.layers):
-            into_both_rows(self.scratch.at[0, j], packed[j])
-        return self.scratch[0]
-
-
-def coarsest(mass, source, faces, row_step, lane_step):
-    level = Level(mass, source, faces, row_step, lane_step)
-    rows, lanes = source.shape[1] // row_step, source.shape[2] // lane_step
-    frames = [(m, k) for m in range(rows) for k in range(lanes)]
+        place, tiles = self.place(), fix.shape[0]
+        for j in range(tiles):
+            into_both_rows(place.at[j, pl.ds(0, self.rows)], fix[j])
+        return super().prolonged(place[:tiles, : self.rows])
+
+
+def coarsest(mass, source, faces, *steps):
+    row_step, lane_step, slot_step = steps
+    level = Level(mass, source, faces, *steps)
+    counts = source.shape[1] // row_step, source.shape[2] // lane_step, 4 // slot_step
+    frames = [(m, k, q) for m in range(counts[0]) for k in range(counts[1]) for q in range(counts[2])]
+    place = level.lane & 3
 
     def spread(values):
         copies = {}
-        for m in range(rows):
-            turned = behind(values, m * row_step, 1) if m else values
-            for k in range(lanes):
-                copies[m, k] = behind(turned, k * lane_step, 2) if k else turned
+        for m, k, q in frames:
+            if k:
+                copies[m, k, q] = behind(copies[m, 0, q], k * lane_step, 2)
+            elif q:
+                by = q * slot_step
+                one, two = behind(copies[m, 0, 0], by, 2), ahead(copies[m, 0, 0], 4 - by, 2)
+                copies[m, k, q] = jnp.where(place >= by, one, two)
+            else:
+                copies[m, k, q] = behind(values, m * row_step, 1) if m else values
         return copies
 
-    inv = level.inv
-    start, fx, fxl, fy, fyl, fz, fzl = [
-        spread(values * inv)
-        for values in (source, level.fx, level.fxl, level.fy, level.fyl, level.fz, level.fzl)
-    ]
+    start, inv, fx, fy, fz = [spread(values) for values in (source * level.inv, level.inv, level.fx, level.fy, level.fz)]
+
+    def shifted(copies, frame, axis, by):
+        moved = list(frame)
+        moved[axis] = (frame[axis] - by) % counts[axis]
+        return copies[tuple(moved)]
+
+    def along_x(copies, frame, by):
+        here, wrapped = copies[frame], shifted(copies, frame, 2, by)
+        return joined(here[1:], wrapped[:1]) if by > 0 else joined(wrapped[-1:], here[:-1])
+
+    weights = {}
+    for frame in frames:
+        pairs = [
+            (fx[frame], along_x(fx, frame, -1)),
+            (fy[frame], shifted(fy, frame, 0, -1)),
+            (fz[frame], shifted(fz, frame, 1, -1)),
+        ]
+        weights[frame] = [(up * inv[frame], low * inv[frame]) for up, low in pairs]
 
     def update(e):
         fresh = {}
-        for m, k in frames:
-            here = e[m, k]
-            total = start[m, k] + fx[m, k] * level.upper(here) + fxl[m, k] * level.lower(here)
-            total = total + (fy[m, k] * e[(m - 1) % rows, k] + fyl[m, k] * e[(m + 1) % rows, k])
-            fresh[m, k] = total + (fz[m, k] * e[m, (k - 1) % lanes] + fzl[m, k] * e[m, (k + 1) % lanes])
+        for frame in frames:
+            (x_up, x_low), (y_up, y_low), (z_up, z_low) = weights[frame]
+            total = x_up * along_x(e, frame, 1) + x_low * along_x(e, frame, -1)
+            total = total + (y_up * shifted(e, frame, 0, 1) + y_low * shifted(e, frame, 0, -1))
+            total = total + (z_up * shifted(e, frame, 1, 1) + z_low * shifted(e, frame, 1, -1))
+            fresh[frame] = start[frame] + total
         return fresh
 
     even = start
@@ -476,25 +509,25 @@
     for turn in range(COARSE_SWEEPS - 1):
         even = update(odd)
         odd = update(even)
-    return jnp.where(level.even, even[0, 0], odd[0, 0])
-
-
-def small_cycle(mass, source, faces, row_step, lane_step, between):
+    return jnp.where(level.even, even[0, 0, 0], odd[0, 0, 0])
+
+
+def small_cycle(mass, source, faces, row_step, lane_step, slot_step, between):
     if between == 0:
-        return coarsest(mass, source, faces, row_step, lane_step)
-    level = Level(mass, source, faces, row_step, lane_step)
+        return coarsest(mass, source, faces, row_step, lane_step, slot_step)
+    level = Level(mass, source, faces, row_step, lane_step, slot_step)
     return level.cycle(
         lambda inner, inner_faces: small_cycle(
-            8.0 * mass, inner, inner_faces, 2 * row_step, 2 * lane_step, between - 1
+            8.0 * mass, inner, inner_faces, 2 * row_step, 2 * lane_step, level.coarse_slot_step(), between - 1
         )
     )
 
 
 def coarse_kernel(
-    owner_of, same_cores, other_cores, e2_in, s2, fx2, fxl2, fy2, fz2, inv2,
-    inputs, field, fx_in, fx_outer, fy_in, fz_in, inv_in, across_in, within_in,
+    owner_of, same_cores, other_cores, e2_in, s2, fx2, fxl2, fy2, fz2, fzl2, inv2,
+    inputs, field, fx_in, fx_outer, fy_in, fz_in, fzl_in, inv_in, across_in, within_in,
     solved_out, owned_out,
-    e3, turn3, pair, e2, fzl2, e1, cor, solved, owned, owner_here, fetch_sem, sems,
+    e3, rows3, pair, e2, e1, cor, solved, owned, owner_here, fetch_sem, sems,
 ):
     fetch = pltpu.make_async_copy(owner_of, owner_here, fetch_sem)
     fetch.start()
@@ -504,29 +537,32 @@
     position, last = lax.axis_index("gx"), blocks - 1
 
     slot = lanes_of((quarter, lanes)) & 3
+    spread = blocks // 4
     tiles = []
     for chip in range(chips):
         tiles.extend(by_side(same_cores[chip, 0], other_cores[chip, 0]))
     items = []
     for k in range(4):
         packs = []
-        for j in range(0, blocks, 4):
-            value = tiles[j + (3 - k) % 4]
+        for j in range(spread):
+            value = tiles[j + (3 - k) % 4 * spread]
             for at in range(3):
-                value = jnp.where(slot == at, tiles[j + (at - k) % 4], value)
+                value = jnp.where(slot == at, tiles[j + (at - k) % 4 * spread], value)
             if k:
                 value = jnp.where(slot < 4 - k, ahead(value, k, 1), behind(value, 4 - k, 1))
             packs.append(value[None])
         items.append(jnp.concatenate(packs, 0))
-    third = Packed(64.0, items[0], items[1:], turn3)
-    e3[...] = third.cycle(lambda inner, faces: small_cycle(512.0, inner, faces, 1, 8, 2))
+    third = Rows(64.0, items[0], items[1:], rows3)
+    e3[...] = third.cycle(
+        lambda inner, faces: small_cycle(512.0, inner, faces, 1, 8, third.coarse_slot_step(), 2)
+    )
 
     fetch.wait()
     owner = owner_here[position]
     wide, narrow = lanes_of((lanes, lanes)), rows_of((lanes, lanes))
-    take = jnp.where(narrow == 4 * wide + owner % 4, 1.0, 0.0)
+    take = jnp.where(narrow == 4 * wide + owner // spread, 1.0, 0.0)
     block = jnp.dot(
-        e3[owner // 4], take, precision=lax.Precision.HIGHEST, preferred_element_type=jnp.float32
+        e3[owner % spread], take, precision=lax.Precision.HIGHEST, preferred_element_type=jnp.float32
     )
     owned[0] = block[:, : lanes // 4]
     copies = [pltpu.make_async_copy(owned, owned_out, sems.at[0])]
@@ -545,12 +581,10 @@
     )
     for k in range(5):
         j = jnp.clip(position + k - 2, 0, last)
-        into_both_rows(pair.at[k], group(jnp.where(slot == j % 4, e3[j // 4], 0.0)))
+        into_both_rows(pair.at[k], group(jnp.where(slot == j // spread, e3[j % spread], 0.0)))
         e2[k, :PAD] = edge
         e2[k, PAD + half:] = edge
         e2[k, body2] = before[k] + pair[k]
-    for j in range(3):
-        fzl2[j] = behind(fz2[j], 2, 1)
 
     def update2():
         sums = neigh2(e2, fx2, fxl2, fy2, fz2, fzl2, first_of_two, (0, 1, 2))
@@ -582,9 +616,9 @@
         e1[w, body1] = field[w, body1] + fixes[-1]
 
     def in_layer1(w):
-        here, face = e1[w, body1], fz_in[w]
+        here = e1[w, body1]
         sums = fy_in[w, body1] * e1[w, up1] + fy_in[w, down1] * e1[w, down1]
-        return sums + face * ahead(here, 1, 1) + behind(face, 1, 1) * behind(here, 1, 1)
+        return sums + fz_in[w] * ahead(here, 1, 1) + fzl_in[w] * behind(here, 1, 1)
 
     def smoothed1(w, odd):
         keep = even_sum if (w + odd) % 2 == 0 else ~even_sum
@@ -649,19 +683,17 @@
     across, within, fx2, *fine = call(
         fine_down_kernel,
         [f32(5, half, depth)] * 2
-        + [f32(2, half, depth), tall, f32(window - 1, height, depth), f32(2, height, depth), tall, plain, plain],
-        [
-            vmem(window, padded, depth), vmem(window, height, depth), vmem(layers, height, depth),
-            vmem(2, height, depth),
-        ],
+        + [f32(2, half, depth), tall, f32(window - 1, height, depth), f32(2, height, depth), tall]
+        + [plain] * 3,
+        [vmem(window, padded, depth), vmem(layers, height, depth), vmem(2, height, depth)],
         (block_owner, inputs, *swapped(*sent)),
     )
     halos = swapped(across, within)
     plain = f32(3, half, depth)
     slots, *middle = call(
         middle_down_kernel,
-        [f32(blocks // 2, 2, quarter, depth), plain, plain, plain, plain, f32(3, padded2, depth), plain, plain],
-        [vmem(5, padded2, depth), vmem(3, half, depth), vmem(2, half, depth)],
+        [f32(blocks // 2, 2, quarter, depth), plain, plain, plain, plain, f32(3, padded2, depth)] + [plain] * 3,
+        [vmem(5, padded2, depth), vmem(2, half, depth)],
         (across, fx2, *halos),
     )
     kinds = [list(range(core, blocks, 2)) for core in range(2)]
@@ -671,8 +703,8 @@
         coarse_kernel,
         [f32(layers, height, depth), f32(1, quarter, depth // 4)],
         [
-            vmem(blocks // 4, quarter, depth), vmem(4, blocks // 4, quarter, depth), vmem(7, half, depth),
-            vmem(5, padded2, depth), vmem(3, half, depth), vmem(window, padded, depth), vmem(6, height, depth),
+            vmem(blocks // 4, quarter, depth), vmem(4, blocks // 4, quarter + 2 * PAD, depth), vmem(7, half, depth),
+            vmem(5, padded2, depth), vmem(window, padded, depth), vmem(6, height, depth),
             vmem(layers, height, depth), vmem(1, quarter, depth // 4), pltpu.SMEM((blocks,), jnp.int32),
             pltpu.SemaphoreType.DMA, pltpu.SemaphoreType.DMA((layers + 1,)),
         ],

time: 36.6 us -> 36.2 us (0.989)
  no operation moved by 1% of the time
where the time goes in v8:
time: 36.2 us; the launch traced here: 36 us
  blocking collectives  18.8 us (52%)
  starting transfers between devices  7.67 us (21%)
  Pallas kernels  5.18 us (14%)
  waiting for transfers between devices  2.57 us (7%)
  other arithmetic  1.06 us (3%)
  between operations  0.68 us (2%)
    all_to_all x1, blocking collectives, on_device(): lax.all_to_all(slots, 'gx', 0, 0, axis_index_groups=kinds, tiled=True)  18.8 us
    ppermute x3, starting transfers between devices, within_chip(): lax.ppermute(block, 'gx', [(i, i ^ 1) for i in range(lax.axis_size('gx'))])  6.35 us
    pallas_call x4, Pallas kernels, call(): pl.pallas_call(kernel, out_shape=tuple(outs), in_specs=[pl.BlockSpec(memo...  5.18 us
    ppermute x3, waiting for transfers between devices, within_chip(): lax.ppermute(block, 'gx', [(i, i ^ 1) for i in range(lax.axis_size('gx'))])  2.57 us
    ppermute x2, starting transfers between devices, swapped(): return (lax.ppermute(across, 'gx', chips), within_chip(within))  1.32 us
    add x1, other arithmetic, on_device(): sum((jnp.pad(block, ((k * layers, (2 - k) * layers), (0, 0), (0, 0))) for...  1.06 us
  transfers between devices with their start and end apart: 5, of which 3 were waited for; matrix products, arithmetic and copies ran while one was open for 0% of the time, Pallas kernels for 0%

profile of v8, /device:TPU:0, one launch (start us, length us, event | category | flops | bytes accessed | tf_op | source)
XLA Modules:
  0.0 36.0 jit_solution(5888622236300527004)
XLA Ops:
  0.6 1.1 %pad_add_fusion.inputs = f32[12,64,128]{2,1,0:T(8,128)S(1)} fusion(f32[4,64,128]{2,1,0:T(8,128)} %param.6, f32[4,64,128]{2,1,0:T(8,128)} %param.5, f32[4,64,128]{2,1,0:T(8,128)} %param.4), kind=kLoop, calls=%fused_computation | loop fusion | flops 196608 | bytes 786432 | tf_op jit(solution)/shard_map/add | solution.py:677
  1.7 0.3 shard_map.59
  2.0 0.0 copy-start
  2.0 0.7 %collective-permute-start = (f32[224,128]{1,0:T(8,128)S(1)}, f32[224,128]{1,0:T(8,128)S(1)}, u32[]{:S(2)}, u32[]{:S(2)}) collective-permute-start(f32[224,128]{1,0:T(8,128)S(1)} %get-tuple-element.23), channel_id=1, source_target_pairs={{1,2},{2,1},{3,4},{4,3},{5,6},{6,5},{7,8},{8,7},{9,10},{10,9},{11,... | collective-permute-start | bytes 344072 | tf_op jit(solution)/shard_map/ppermute | solution.py:16
  2.7 4.4 %collective-permute-start.1 = (f32[224,128]{1,0:T(8,128)S(1)}, f32[224,128]{1,0:T(8,128)S(1)}, u32[]{:S(2)}, u32[]{:S(2)}) collective-permute-start(f32[224,128]{1,0:T(8,128)S(1)} %get-tuple-element.24), channel_id=1, source_target_pairs={{0,1},{1,0},{2,3},{3,2},{4,5},{5,4},{6,7},{7,6},{8,9},{9,8},{10,11... | collective-permute-start | bytes 344072 | tf_op jit(solution)/shard_map/ppermute | solution.py:20
  7.0 0.0 collective-permute-done.across_in
  7.0 1.0 %collective-permute-done.1.within_in = f32[224,128]{1,0:T(8,128)S(1)} collective-permute-done((f32[224,128]{1,0:T(8,128)S(1)}, f32[224,128]{1,0:T(8,128)S(1)}, u32[]{:S(2)}, u32[]{:S(2)}) %collective-permute-start.1) | collective-permute-done | bytes 114720 | tf_op jit(solution)/shard_map/ppermute | solution.py:20
  8.0 0.0 copy-done
  8.0 0.9 %shard_map.60 = (f32[5,32,128]{2,1,0:T(8,128)S(1)}, f32[5,32,128]{2,1,0:T(8,128)S(1)}, f32[2,32,128]{2,1,0:T(8,128)S(1)}, f32[6,80,128]{2,1,0:T(8,128)S(1)}, f32...) custom-call(s32[16]{0:T(128)S(1)} %copy-done, ...), custom_call_target="tpu_custom_call" | custom-call | tf_op jit(solution)/shard_map/pallas_call | solution.py:661
  8.9 2.0 %collective-permute-start.3 = (f32[5,32,128]{2,1,0:T(8,128)S(1)}, f32[5,32,128]{2,1,0:T(8,128)S(1)}, u32[]{:S(2)}, u32[]{:S(2)}) collective-permute-start(f32[5,32,128]{2,1,0:T(8,128)S(1)} %get-tuple-element.27), channel_id=1, source_target_pairs={{0,1},{1,0},{2,3},{3,2},{4,5},{5,4},{6,7},{7,6},{8,9},{9,8},{10,11... | collective-permute-start | bytes 245768 | tf_op jit(solution)/shard_map/ppermute | solution.py:20
  10.9 0.7 %collective-permute-start.2 = (f32[5,32,128]{2,1,0:T(8,128)S(1)}, f32[5,32,128]{2,1,0:T(8,128)S(1)}, u32[]{:S(2)}, u32[]{:S(2)}) collective-permute-start(f32[5,32,128]{2,1,0:T(8,128)S(1)} %get-tuple-element.25.own), channel_id=1, source_target_pairs={{1,2},{2,1},{3,4},{4,3},{5,6},{6,5},{7,8},{8,7},{9,10},{10,9},{11,... | collective-permute-start | bytes 245768 | tf_op jit(solution)/shard_map/ppermute | solution.py:16
  11.5 0.3 collective-permute-done.3.within_in
  11.8 0.0 collective-permute-done.2.across_in
  11.8 0.5 %shard_map.61 = (f32[8,2,16,128]{3,2,1,0:T(8,128)S(1)}, f32[3,32,128]{2,1,0:T(8,128)S(1)}, f32[3,32,128]{2,1,0:T(8,128)S(1)}, f32[3,32,128]{2,1,0:T(8,128)S(1)},...) custom-call(f32[5,32,128]{2,1,0:T(8,128)S(1)} %get-tuple-element.25., ...), custom_call_target="tpu_custom_call" | custom-call | tf_op jit(solution)/shard_map/pallas_call | solution.py:661
  12.3 18.8 %all_to_all.5.same_cores = f32[8,2,16,128]{3,2,1,0:T(8,128)S(1)} all-to-all(f32[8,2,16,128]{3,2,1,0:T(8,128)S(1)} %get-tuple-element.28), channel_id=1, replica_groups={{0,2,4,6,8,10,12,14},{1,3,5,7,9,11,13,15},{16,18,20,22,24,26,28,30},{17..., dimensions={0} | all-to-all | bytes 262144 | tf_op jit(solution)/shard_map/all_to_all | solution.py:700
  31.1 0.0 collective-permute-start.4
  31.1 1.3 %collective-permute-done.4.other_cores = f32[8,2,16,128]{3,2,1,0:T(8,128)S(1)} collective-permute-done((f32[8,2,16,128]{3,2,1,0:T(8,128)S(1)}, f32[8,2,16,128]{3,2,1,0:T(8,128)S(1)}, u32[]{:S(2)}, u32[]{:S(2)}) %collective-permute-start.4) | collective-permute-done | bytes 131104 | tf_op jit(solution)/shard_map/ppermute | solution.py:20
  32.5 3.5 %shard_map.62 = (f32[4,64,128]{2,1,0:T(8,128)}, f32[1,16,32]{2,1,0:T(8,128)}) custom-call(s32[16]{0:T(128)S(1)} %copy-done, f32[8,2,16,128]{3,2,1,0:T(8,128)S(1)} %all_to_all.5.same_cores, f32[8,2,16,128]{3,2,1,0:T(8,128)S(1)} %collective-permute-done.4.other_cores, f32[3,32,128]{2,1,0:T(8,128)S(1)} %get-tuple-element.29.e2_in, ...), custom_call_target="tpu_custom_call" | custom-call | tf_op jit(solution)/shard_map/pallas_call | solution.py:661
Async XLA Ops:
  2.0 6.0 %copy-start = (s32[16]{0:T(128)S(1)}, s32[16]{0:T(128)}, u32[]{:S(2)}) copy-start(s32[16]{0:T(128)} %owner_of.3) | copy-start | bytes 196
  2.0 5.0 %collective-permute-start = (f32[224,128]{1,0:T(8,128)S(1)}, f32[224,128]{1,0:T(8,128)S(1)}, u32[]{:S(2)}, u32[]{:S(2)}) collective-permute-start(f32[224,128]{1,0:T(8,128)S(1)} %get-tuple-element.23), channel_id=1, source_target_pairs={{1,2},{2,1},{3,4},{4,3},{5,6},{6,5},{7,8},{8,7},{9,10},{10,9},{11,... | collective-permute-start | bytes 344072 | tf_op jit(solution)/shard_map/ppermute | solution.py:16
  2.7 5.3 %collective-permute-start.1 = (f32[224,128]{1,0:T(8,128)S(1)}, f32[224,128]{1,0:T(8,128)S(1)}, u32[]{:S(2)}, u32[]{:S(2)}) collective-permute-start(f32[224,128]{1,0:T(8,128)S(1)} %get-tuple-element.24), channel_id=1, source_target_pairs={{0,1},{1,0},{2,3},{3,2},{4,5},{5,4},{6,7},{7,6},{8,9},{9,8},{10,11... | collective-permute-start | bytes 344072 | tf_op jit(solution)/shard_map/ppermute | solution.py:20
  8.9 2.9 %collective-permute-start.3 = (f32[5,32,128]{2,1,0:T(8,128)S(1)}, f32[5,32,128]{2,1,0:T(8,128)S(1)}, u32[]{:S(2)}, u32[]{:S(2)}) collective-permute-start(f32[5,32,128]{2,1,0:T(8,128)S(1)} %get-tuple-element.27), channel_id=1, source_target_pairs={{0,1},{1,0},{2,3},{3,2},{4,5},{5,4},{6,7},{7,6},{8,9},{9,8},{10,11... | collective-permute-start | bytes 245768 | tf_op jit(solution)/shard_map/ppermute | solution.py:20
  10.9 0.9 %collective-permute-start.2 = (f32[5,32,128]{2,1,0:T(8,128)S(1)}, f32[5,32,128]{2,1,0:T(8,128)S(1)}, u32[]{:S(2)}, u32[]{:S(2)}) collective-permute-start(f32[5,32,128]{2,1,0:T(8,128)S(1)} %get-tuple-element.25.own), channel_id=1, source_target_pairs={{1,2},{2,1},{3,4},{4,3},{5,6},{6,5},{7,8},{8,7},{9,10},{10,9},{11,... | collective-permute-start | bytes 245768 | tf_op jit(solution)/shard_map/ppermute | solution.py:16
  31.1 1.3 %collective-permute-start.4 = (f32[8,2,16,128]{3,2,1,0:T(8,128)S(1)}, f32[8,2,16,128]{3,2,1,0:T(8,128)S(1)}, u32[]{:S(2)}, u32[]{:S(2)}) collective-permute-start(f32[8,2,16,128]{3,2,1,0:T(8,128)S(1)} %all_to_all.5.same_cores), channel_id=1, source_target_pairs={{0,1},{1,0},{2,3},{3,2},{4,5},{5,4},{6,7},{7,6},{8,9},{9,8},{10,11... | collective-permute-start | bytes 393224 | tf_op jit(solution)/shard_map/ppermute | solution.py:20

commit v9 on v8

--- a/solution.py
+++ b/solution.py
@@ -11,9 +11,8 @@
 PAD = 8
 
 
-def swapped(across, within):
-    chips = [(i, i + 1 if i % 2 else i - 1) for i in range(1, lax.axis_size("gx") - 1)]
-    return lax.ppermute(across, "gx", chips), within_chip(within)
+def between_chips(block):
+    return lax.ppermute(block, "gx", [(i, i + 1 if i % 2 else i - 1) for i in range(1, lax.axis_size("gx") - 1)])
 
 
 def within_chip(block):
@@ -269,9 +268,48 @@
     return with_partner(with_partner(values, 1, 1), 2, 1)
 
 
+def packed_odd(values, pair):
+    half, lanes = values.shape
+    lane = lanes_of((half // 2, lanes))
+    pair[...] = values
+    return odd_cells(pair, half // 2, (((lane & 1) + (lane >> 1)) & 1) != 0)
+
+
+def chip_kernel(outer, own_fx, within_in, across, fx2, fxl2, fy2, fz2, fzl2, e2, pair):
+    _, half, lanes = outer.shape
+    first_of_two, even2 = parities2(half, lanes)
+    body, down = pl.ds(PAD, half), pl.ds(PAD - 1, half)
+    edge = jnp.zeros((PAD, lanes), jnp.float32)
+    for j in range(4):
+        e2[j] = jnp.zeros((half + 2 * PAD, lanes), jnp.float32)
+    sources = by_side(outer[0], within_in[0])
+    for j, (fy, fz) in enumerate(zip(by_side(outer[2], within_in[2]), by_side(outer[3], within_in[3]))):
+        fy2[j, :PAD] = edge
+        fy2[j, body] = fy
+        fy2[j, PAD + half:] = edge
+        fz2[j] = fz
+        fzl2[j] = behind(fz, 2, 1)
+    fx_own, fxl_own = own_fx[0], own_fx[1]
+    fxl_left, _ = by_side(fxl_own, within_in[1])
+    fx_right, _ = by_side(within_in[1], fx_own)
+    fx2[0], _ = by_side(fx_own, jnp.where(first_of_two, ahead(fxl_left, 1, 1), behind(fxl_own, 1, 1)))
+    fxl2[1], _ = by_side(jnp.where(first_of_two, ahead(fx_own, 1, 1), behind(fx_right, 1, 1)), fxl_own)
+    fxl2[0], fx2[1] = fxl_left, fx_right
+    inverse = []
+    for j in range(2):
+        weight = fx2[j] + fxl2[j] + fy2[j, body] + fy2[j, down] + fz2[j] + fzl2[j]
+        inverse.append(1.0 / (8.0 + weight))
+        e2[j + 1, body] = sources[j] * inverse[j]
+    sums = neigh2(e2, fx2, fxl2, fy2, fz2, fzl2, first_of_two, (0, 1))
+    left, right = [(sources[j] + sums[j]) * inverse[j] for j in range(2)]
+    for k in range(5):
+        across[k * half:(k + 1) * half] = outer[k]
+    across[5 * half:] = packed_odd(jnp.where(first_of_two, right, left), pair)
+
+
 def middle_down_kernel(
     own, own_fx, across_in, within_in,
-    slots, e2_out, s2, fx2, fxl2, fy2, fz2, fzl2, inv2,
+    slots, halo, e2_out, s2, fx2, fxl2, fy2, fz2, fzl2, inv2,
     e2, pair,
 ):
     _, half, lanes = own.shape
@@ -282,8 +320,9 @@
     edge = jnp.zeros((PAD, lanes), jnp.float32)
     for j in range(5):
         e2[j] = jnp.zeros((half + 2 * PAD, lanes), jnp.float32)
+
     def three(k):
-        left, right = by_side(across_in[k], within_in[k])
+        left, right = by_side(across_in[k * half:(k + 1) * half], within_in[k])
         return left, own[k], right
 
     for j, (source, fy, fz) in enumerate(zip(three(0), three(2), three(3))):
@@ -304,14 +343,12 @@
         weight = fx2[j] + fxl2[j] + fy2[j, body] + fy2[j, down] + fz2[j] + fzl2[j]
         inverse = 1.0 / (8.0 + weight)
         inv2[j] = inverse
-        e2[j + 1, body] = jnp.where(even2, s2[j] * inverse, 0.0)
+        e2[j + 1, body] = s2[j] * inverse
 
     def neigh(tiles):
         return neigh2(e2, fx2, fxl2, fy2, fz2, fzl2, first_of_two, tiles)
 
-    fresh = [
-        jnp.where(even2, e2[j + 1, body], (s2[j] + sums) * inv2[j]) for j, sums in enumerate(neigh((0, 1, 2)))
-    ]
+    fresh = [(s2[j] + sums) * inv2[j] for j, sums in enumerate(neigh((0, 1, 2)))]
     for j in range(3):
         e2[j + 1, body] = fresh[j]
         e2_out[j] = fresh[j]
@@ -324,14 +361,12 @@
     fy = group(fy2[1, pl.ds(PAD + 1, quarter, 2), :])
     fz = group(jnp.where(odd_depth, even_row_sum(fz2.at[1], quarter), 0.0))
     tile = jnp.where(item == 0, source, jnp.where(item == 1, fx, jnp.where(item == 2, fy, fz)))
-    first = (((lane & 1) + (lane >> 1)) & 1) != 0
-    pair[0] = jnp.where(first_of_two, fresh[2], fresh[1])
-    pair[1] = jnp.where(first_of_two, fresh[1], fresh[0])
-    for_left = odd_cells(pair.at[0], quarter, first)
-    for_right = odd_cells(pair.at[1], quarter, first)
     for c in range(slots.shape[0]):
-        slots[c, 0] = tile
-        slots[c, 1] = jnp.where(position < 2 * c + 1 - position % 2, for_right, for_left)
+        slots[c] = tile
+    for_right, _ = by_side(
+        jnp.where(first_of_two, fresh[1], fresh[0]), jnp.where(first_of_two, fresh[2], fresh[1])
+    )
+    halo[...] = packed_odd(for_right, pair.at[1])
 
 
 def joined(one, two):
@@ -525,13 +560,13 @@
 
 def coarse_kernel(
     owner_of, same_cores, other_cores, e2_in, s2, fx2, fxl2, fy2, fz2, fzl2, inv2,
-    inputs, field, fx_in, fx_outer, fy_in, fz_in, fzl_in, inv_in, across_in, within_in,
+    inputs, field, fx_in, fx_outer, fy_in, fz_in, fzl_in, inv_in, across_in, within_in, halo_in,
     solved_out, owned_out,
     e3, rows3, pair, e2, e1, cor, solved, owned, owner_here, fetch_sem, sems,
 ):
     fetch = pltpu.make_async_copy(owner_of, owner_here, fetch_sem)
     fetch.start()
-    chips, _, quarter, lanes = same_cores.shape
+    chips, quarter, lanes = same_cores.shape
     blocks = 2 * chips
     half, height = 2 * quarter, 4 * quarter
     position, last = lax.axis_index("gx"), blocks - 1
@@ -540,7 +575,7 @@
     spread = blocks // 4
     tiles = []
     for chip in range(chips):
-        tiles.extend(by_side(same_cores[chip, 0], other_cores[chip, 0]))
+        tiles.extend(by_side(same_cores[chip], other_cores[chip]))
     items = []
     for k in range(4):
         packs = []
@@ -571,8 +606,7 @@
     first_of_two, even2 = parities2(half, lanes)
     body2 = pl.ds(PAD, half)
     edge = jnp.zeros((PAD, lanes), jnp.float32)
-    left = other_cores[jnp.maximum(position - 1, 0) // 2, 1]
-    right = other_cores[jnp.minimum(position + 1, last) // 2, 1]
+    left, right = by_side(across_in[5 * half:], halo_in[...])
     into_both_rows(pair.at[5], left)
     into_both_rows(pair.at[6], right)
     left, right = pair[5], pair[6]
@@ -625,7 +659,7 @@
         sums = fx_in[w] * e1[w + 1, body1] + fx_in[w - 1] * e1[w - 1, body1] + in_layer1(w)
         return jnp.where(keep, e1[w, body1], (source[w - 1] + sums) * inv_in[w])
 
-    borders = by_side(across_in[4], within_in[4])
+    borders = by_side(across_in[4 * half:5 * half], within_in[4])
     for w in range(1, count - 1):
         e1[w, body1] = smoothed1(w, 0)
     for side, w, near in ((0, 0, 1), (1, count - 1, count - 2)):
@@ -680,22 +714,33 @@
     )
     sent = call(edge_kernel, [f32(3 * height + half, depth)] * 2, [], (inputs,))
     plain, tall = f32(window, height, depth), f32(window, padded, depth)
-    across, within, fx2, *fine = call(
+    outer, within, fx2, *fine = call(
         fine_down_kernel,
         [f32(5, half, depth)] * 2
         + [f32(2, half, depth), tall, f32(window - 1, height, depth), f32(2, height, depth), tall]
         + [plain] * 3,
         [vmem(window, padded, depth), vmem(layers, height, depth), vmem(2, height, depth)],
-        (block_owner, inputs, *swapped(*sent)),
-    )
-    halos = swapped(across, within)
-    plain = f32(3, half, depth)
-    slots, *middle = call(
+        (block_owner, inputs, between_chips(sent[0]), within_chip(sent[1])),
+    )
+    within_in = within_chip(within)
+    plain, tall = f32(3, half, depth), f32(3, padded2, depth)
+    across, = call(
+        chip_kernel,
+        [f32(5 * half + quarter, depth)],
+        [
+            vmem(2, half, depth), vmem(2, half, depth), vmem(2, padded2, depth), vmem(2, half, depth),
+            vmem(2, half, depth), vmem(4, padded2, depth), vmem(half, depth),
+        ],
+        (outer, fx2, within_in),
+    )
+    across_in = between_chips(across)
+    slots, halo, *middle = call(
         middle_down_kernel,
-        [f32(blocks // 2, 2, quarter, depth), plain, plain, plain, plain, f32(3, padded2, depth)] + [plain] * 3,
+        [f32(blocks // 2, quarter, depth), f32(quarter, depth)] + [plain] * 4 + [tall] + [plain] * 3,
         [vmem(5, padded2, depth), vmem(2, half, depth)],
-        (across, fx2, *halos),
-    )
+        (outer, fx2, across_in, within_in),
+    )
+    halo_in = within_chip(halo)
     kinds = [list(range(core, blocks, 2)) for core in range(2)]
     same_cores = lax.all_to_all(slots, "gx", 0, 0, axis_index_groups=kinds, tiled=True)
     other_cores = within_chip(same_cores)
@@ -708,7 +753,7 @@
             vmem(layers, height, depth), vmem(1, quarter, depth // 4), pltpu.SMEM((blocks,), jnp.int32),
             pltpu.SemaphoreType.DMA, pltpu.SemaphoreType.DMA((layers + 1,)),
         ],
-        (block_owner, same_cores, other_cores, *middle, inputs, *fine, *halos),
+        (block_owner, same_cores, other_cores, *middle, inputs, *fine, across_in, within_in, halo_in),
         pl.ANY,
     )
     return solved, owned

time: 36.2 us -> 37 us (1.022)
  starting transfers between devices: 7.67 us -> 8.19 us
    ppermute x3 -> x4, starting transfers between devices: 6.35 us -> 6.86 us  [within_chip(): lax.ppermute(block, 'gx', [(i, i ^ 1) for i in range(lax.axis_size('gx'))])]
    pallas_call x4 -> x5, Pallas kernels: 5.18 us -> 5.38 us  [call(): pl.pallas_call(kernel, out_shape=tuple(outs), in_specs=[pl.BlockSpec(memo...]
    ppermute x3 -> x4, waiting for transfers between devices: 2.57 us -> 2.72 us  [within_chip(): lax.ppermute(block, 'gx', [(i, i ^ 1) for i in range(lax.axis_size('gx'))])]
  transfers between devices with their start and end apart: 5 -> 6, of which waited for: 3 -> 3; matrix products, arithmetic and copies ran while one was open for 0% -> 0% of each run, Pallas kernels for 0% -> 0%
where the time goes in v9:
time: 37 us; the launch traced here: 36.8 us
  blocking collectives  18.7 us (51%)
  starting transfers between devices  8.19 us (22%)
  Pallas kernels  5.38 us (15%)
  waiting for transfers between devices  2.72 us (7%)
  other arithmetic  1.06 us (3%)
  between operations  0.69 us (2%)
    all_to_all x1, blocking collectives, on_device(): lax.all_to_all(slots, 'gx', 0, 0, axis_index_groups=kinds, tiled=True)  18.7 us
    ppermute x4, starting transfers between devices, within_chip(): lax.ppermute(block, 'gx', [(i, i ^ 1) for i in range(lax.axis_size('gx'))])  6.86 us
    pallas_call x5, Pallas kernels, call(): pl.pallas_call(kernel, out_shape=tuple(outs), in_specs=[pl.BlockSpec(memo...  5.38 us
    ppermute x4, waiting for transfers between devices, within_chip(): lax.ppermute(block, 'gx', [(i, i ^ 1) for i in range(lax.axis_size('gx'))])  2.72 us
    ppermute x2, starting transfers between devices, between_chips(): lax.ppermute(block, 'gx', [(i, i + 1 if i % 2 else i - 1) for i in range(...  1.33 us
    add x1, other arithmetic, on_device(): sum((jnp.pad(block, ((k * layers, (2 - k) * layers), (0, 0), (0, 0))) for...  1.06 us
  transfers between devices with their start and end apart: 6, of which 3 were waited for; matrix products, arithmetic and copies ran while one was open for 0% of the time, Pallas kernels for 0%

profile of v9, /device:TPU:0, one launch (start us, length us, event | category | flops | bytes accessed | tf_op | source)
XLA Modules:
  0.0 36.8 jit_solution(1096831799902311073)
XLA Ops:
  0.6 1.1 %pad_add_fusion.inputs = f32[12,64,128]{2,1,0:T(8,128)S(1)} fusion(f32[4,64,128]{2,1,0:T(8,128)} %param.6, f32[4,64,128]{2,1,0:T(8,128)} %param.5, f32[4,64,128]{2,1,0:T(8,128)} %param.4), kind=kLoop, calls=%fused_computation | loop fusion | flops 196608 | bytes 786432 | tf_op jit(solution)/shard_map/add | solution.py:711
  1.7 0.3 shard_map.59
  2.0 0.0 copy-start
  2.0 0.7 %collective-permute-start = (f32[224,128]{1,0:T(8,128)S(1)}, f32[224,128]{1,0:T(8,128)S(1)}, u32[]{:S(2)}, u32[]{:S(2)}) collective-permute-start(f32[224,128]{1,0:T(8,128)S(1)} %get-tuple-element.24), channel_id=1, source_target_pairs={{1,2},{2,1},{3,4},{4,3},{5,6},{6,5},{7,8},{8,7},{9,10},{10,9},{11,... | collective-permute-start | bytes 344072 | tf_op jit(solution)/shard_map/ppermute | solution.py:15
  2.7 4.4 %collective-permute-start.1 = (f32[224,128]{1,0:T(8,128)S(1)}, f32[224,128]{1,0:T(8,128)S(1)}, u32[]{:S(2)}, u32[]{:S(2)}) collective-permute-start(f32[224,128]{1,0:T(8,128)S(1)} %get-tuple-element.25), channel_id=1, source_target_pairs={{0,1},{1,0},{2,3},{3,2},{4,5},{5,4},{6,7},{7,6},{8,9},{9,8},{10,11... | collective-permute-start | bytes 344072 | tf_op jit(solution)/shard_map/ppermute | solution.py:19
  7.0 0.0 collective-permute-done.across_in
  7.0 1.0 %collective-permute-done.1.within_in = f32[224,128]{1,0:T(8,128)S(1)} collective-permute-done((f32[224,128]{1,0:T(8,128)S(1)}, f32[224,128]{1,0:T(8,128)S(1)}, u32[]{:S(2)}, u32[]{:S(2)}) %collective-permute-start.1) | collective-permute-done | bytes 114720 | tf_op jit(solution)/shard_map/ppermute | solution.py:19
  8.0 0.0 copy-done
  8.0 0.9 %shard_map.60 = (f32[5,32,128]{2,1,0:T(8,128)S(1)}, f32[5,32,128]{2,1,0:T(8,128)S(1)}, f32[2,32,128]{2,1,0:T(8,128)S(1)}, f32[6,80,128]{2,1,0:T(8,128)S(1)}, f32...) custom-call(s32[16]{0:T(128)S(1)} %copy-done, ...), custom_call_target="tpu_custom_call" | custom-call | tf_op jit(solution)/shard_map/pallas_call | solution.py:695
  8.9 2.0 %collective-permute-start.2 = (f32[5,32,128]{2,1,0:T(8,128)S(1)}, f32[5,32,128]{2,1,0:T(8,128)S(1)}, u32[]{:S(2)}, u32[]{:S(2)}) collective-permute-start(f32[5,32,128]{2,1,0:T(8,128)S(1)} %get-tuple-element.28), channel_id=1, source_target_pairs={{0,1},{1,0},{2,3},{3,2},{4,5},{5,4},{6,7},{7,6},{8,9},{9,8},{10,11... | collective-permute-start | bytes 245768 | tf_op jit(solution)/shard_map/ppermute | solution.py:19
  10.9 0.9 %collective-permute-done.2.within_in = f32[5,32,128]{2,1,0:T(8,128)S(1)} collective-permute-done((f32[5,32,128]{2,1,0:T(8,128)S(1)}, f32[5,32,128]{2,1,0:T(8,128)S(1)}, u32[]{:S(2)}, u32[]{:S(2)}) %collective-permute-start.2) | collective-permute-done | bytes 81952 | tf_op jit(solution)/shard_map/ppermute | solution.py:19
  11.8 0.2 shard_map.61
  12.0 0.7 %collective-permute-start.3 = (f32[176,128]{1,0:T(8,128)S(1)}, f32[176,128]{1,0:T(8,128)S(1)}, u32[]{:S(2)}, u32[]{:S(2)}) collective-permute-start(f32[176,128]{1,0:T(8,128)S(1)} %shard_map.61), channel_id=1, source_target_pairs={{1,2},{2,1},{3,4},{4,3},{5,6},{6,5},{7,8},{8,7},{9,10},{10,9},{11,... | collective-permute-start | bytes 270344 | tf_op jit(solution)/shard_map/ppermute | solution.py:15
  12.7 0.0 collective-permute-done.3.across_in
  12.7 0.5 %shard_map.62 = (f32[8,16,128]{2,1,0:T(8,128)S(1)}, f32[16,128]{1,0:T(8,128)S(1)}, f32[3,32,128]{2,1,0:T(8,128)S(1)}, f32[3,32,128]{2,1,0:T(8,128)S(1)}, f32[3,3...) custom-call(f32[5,32,128]{2,1,0:T(8,128)S(1)} %get-tuple-element.26., ...), custom_call_target="tpu_custom_call" | custom-call | tf_op jit(solution)/shard_map/pallas_call | solution.py:695
  13.2 18.7 %all_to_all.5.same_cores = f32[8,16,128]{2,1,0:T(8,128)S(1)} all-to-all(f32[8,16,128]{2,1,0:T(8,128)S(1)} %get-tuple-element.29), channel_id=1, replica_groups={{0,2,4,6,8,10,12,14},{1,3,5,7,9,11,13,15},{16,18,20,22,24,26,28,30},{17..., dimensions={0} | all-to-all | bytes 131072 | tf_op jit(solution)/shard_map/all_to_all | solution.py:745
  31.9 0.0 collective-permute-start.4
  31.9 0.5 %collective-permute-start.5 = (f32[16,128]{1,0:T(8,128)S(1)}, f32[16,128]{1,0:T(8,128)S(1)}, u32[]{:S(2)}, u32[]{:S(2)}) collective-permute-start(f32[16,128]{1,0:T(8,128)S(1)} %get-tuple-element.45), channel_id=1, source_target_pairs={{0,1},{1,0},{2,3},{3,2},{4,5},{5,4},{6,7},{7,6},{8,9},{9,8},{10,11... | collective-permute-start | bytes 24584 | tf_op jit(solution)/shard_map/ppermute | solution.py:19
  32.4 0.8 %collective-permute-done.5.halo_in = f32[16,128]{1,0:T(8,128)S(1)} collective-permute-done((f32[16,128]{1,0:T(8,128)S(1)}, f32[16,128]{1,0:T(8,128)S(1)}, u32[]{:S(2)}, u32[]{:S(2)}) %collective-permute-start.5) | collective-permute-done | bytes 8224 | tf_op jit(solution)/shard_map/ppermute | solution.py:19
  33.3 0.0 collective-permute-done.4.other_cores
  33.3 3.5 %shard_map.63 = (f32[4,64,128]{2,1,0:T(8,128)}, f32[1,16,32]{2,1,0:T(8,128)}) custom-call(s32[16]{0:T(128)S(1)} %copy-done, f32[8,16,128]{2,1,0:T(8,128)S(1)} %all_to_all.5.same_cores, f32[8,16,128]{2,1,0:T(8,128)S(1)} %collective-permute-done.4.other_cores, f32[3,32,128]{2,1,0:T(8,128)S(1)} %get-tuple-element.30.e2_in, ...), custom_call_target="tpu_custom_call" | custom-call | tf_op jit(solution)/shard_map/pallas_call | solution.py:695
Async XLA Ops:
  2.0 6.0 %copy-start = (s32[16]{0:T(128)S(1)}, s32[16]{0:T(128)}, u32[]{:S(2)}) copy-start(s32[16]{0:T(128)} %owner_of.3) | copy-start | bytes 196
  2.0 5.0 %collective-permute-start = (f32[224,128]{1,0:T(8,128)S(1)}, f32[224,128]{1,0:T(8,128)S(1)}, u32[]{:S(2)}, u32[]{:S(2)}) collective-permute-start(f32[224,128]{1,0:T(8,128)S(1)} %get-tuple-element.24), channel_id=1, source_target_pairs={{1,2},{2,1},{3,4},{4,3},{5,6},{6,5},{7,8},{8,7},{9,10},{10,9},{11,... | collective-permute-start | bytes 344072 | tf_op jit(solution)/shard_map/ppermute | solution.py:15
  2.7 5.3 %collective-permute-start.1 = (f32[224,128]{1,0:T(8,128)S(1)}, f32[224,128]{1,0:T(8,128)S(1)}, u32[]{:S(2)}, u32[]{:S(2)}) collective-permute-start(f32[224,128]{1,0:T(8,128)S(1)} %get-tuple-element.25), channel_id=1, source_target_pairs={{0,1},{1,0},{2,3},{3,2},{4,5},{5,4},{6,7},{7,6},{8,9},{9,8},{10,11... | collective-permute-start | bytes 344072 | tf_op jit(solution)/shard_map/ppermute | solution.py:19
  8.9 2.9 %collective-permute-start.2 = (f32[5,32,128]{2,1,0:T(8,128)S(1)}, f32[5,32,128]{2,1,0:T(8,128)S(1)}, u32[]{:S(2)}, u32[]{:S(2)}) collective-permute-start(f32[5,32,128]{2,1,0:T(8,128)S(1)} %get-tuple-element.28), channel_id=1, source_target_pairs={{0,1},{1,0},{2,3},{3,2},{4,5},{5,4},{6,7},{7,6},{8,9},{9,8},{10,11... | collective-permute-start | bytes 245768 | tf_op jit(solution)/shard_map/ppermute | solution.py:19
  12.0 0.7 %collective-permute-start.3 = (f32[176,128]{1,0:T(8,128)S(1)}, f32[176,128]{1,0:T(8,128)S(1)}, u32[]{:S(2)}, u32[]{:S(2)}) collective-permute-start(f32[176,128]{1,0:T(8,128)S(1)} %shard_map.61), channel_id=1, source_target_pairs={{1,2},{2,1},{3,4},{4,3},{5,6},{6,5},{7,8},{8,7},{9,10},{10,9},{11,... | collective-permute-start | bytes 270344 | tf_op jit(solution)/shard_map/ppermute | solution.py:15
  31.9 1.3 %collective-permute-start.4 = (f32[8,16,128]{2,1,0:T(8,128)S(1)}, f32[8,16,128]{2,1,0:T(8,128)S(1)}, u32[]{:S(2)}, u32[]{:S(2)}) collective-permute-start(f32[8,16,128]{2,1,0:T(8,128)S(1)} %all_to_all.5.same_cores), channel_id=1, source_target_pairs={{0,1},{1,0},{2,3},{3,2},{4,5},{5,4},{6,7},{7,6},{8,9},{9,8},{10,11... | collective-permute-start | bytes 196616 | tf_op jit(solution)/shard_map/ppermute | solution.py:19
  31.9 1.3 %collective-permute-start.5 = (f32[16,128]{1,0:T(8,128)S(1)}, f32[16,128]{1,0:T(8,128)S(1)}, u32[]{:S(2)}, u32[]{:S(2)}) collective-permute-start(f32[16,128]{1,0:T(8,128)S(1)} %get-tuple-element.45), channel_id=1, source_target_pairs={{0,1},{1,0},{2,3},{3,2},{4,5},{5,4},{6,7},{7,6},{8,9},{9,8},{10,11... | collective-permute-start | bytes 24584 | tf_op jit(solution)/shard_map/ppermute | solution.py:19

commit v10 on v8

--- a/solution.py
+++ b/solution.py
@@ -11,9 +11,8 @@
 PAD = 8
 
 
-def swapped(across, within):
-    chips = [(i, i + 1 if i % 2 else i - 1) for i in range(1, lax.axis_size("gx") - 1)]
-    return lax.ppermute(across, "gx", chips), within_chip(within)
+def between_chips(block):
+    return lax.ppermute(block, "gx", [(i, i + 1 if i % 2 else i - 1) for i in range(1, lax.axis_size("gx") - 1)])
 
 
 def within_chip(block):
@@ -23,22 +22,6 @@
 def by_side(across, within):
     on_left = lax.axis_index("gx") % 2 == 0
     return jnp.where(on_left, across, within), jnp.where(on_left, within, across)
-
-
-def store_by_side(across, within, pieces):
-    on_left = lax.axis_index("gx") % 2 == 0
-
-    @pl.when(on_left)
-    def _():
-        for index, left, right in pieces:
-            across[index] = left
-            within[index] = right
-
-    @pl.when(jnp.logical_not(on_left))
-    def _():
-        for index, left, right in pieces:
-            across[index] = right
-            within[index] = left
 
 
 def lanes_of(shape):
@@ -67,44 +50,17 @@
     return scratch[pl.ds(0, rows, 2), :] + scratch[pl.ds(1, rows, 2), :]
 
 
+def core_of():
+    return lax.axis_index("gx") % 2
+
+
+def own_layer(u, layers):
+    return u + core_of() * (layers - 1 - 2 * u)
+
+
 def three_parts(ref):
     third = ref.shape[0] // 3
     return [ref.at[pl.ds(k * third, third)] for k in range(3)]
-
-
-def edge_kernel(inputs, across, within):
-    iterate, source, phase = three_parts(inputs)
-    layers, height, depth = iterate.shape
-    half = height // 2
-    row, lane = rows_of((height, depth)), lanes_of((height, depth))
-    even_sum = ((row + lane) & 1) == 0
-    odd_lane = (lanes_of((half, depth)) & 1) != 0
-    cell = []
-    for w in range(layers):
-        value = phase[w]
-        cell.append(STIFFNESS * (value * value + EPSILON))
-
-    def in_layer(w):
-        here, e = cell[w], iterate[w]
-        fy = jnp.where(row < height - 1, 0.5 * (here + ahead(here, 1, 0)), 0.0)
-        fz = jnp.where(lane < depth - 1, 0.5 * (here + ahead(here, 1, 1)), 0.0)
-        fyl, fzl = behind(fy, 1, 0), behind(fz, 1, 1)
-        total = fy * ahead(e, 1, 0) + fyl * behind(e, 1, 0)
-        return total + fz * ahead(e, 1, 1) + fzl * behind(e, 1, 1), fy + fyl + fz + fzl
-
-    sides = []
-    for near, step in ((0, 1), (layers - 1, -1)):
-        inner, far = near + step, near + 2 * step
-        face_near, face_far = 0.5 * (cell[inner] + cell[near]), 0.5 * (cell[inner] + cell[far])
-        total, weight = in_layer(inner)
-        total = total + face_near * iterate[near] + face_far * iterate[far]
-        updated = (source[inner] + total) / (1.0 + (face_near + face_far + weight))
-        total, _ = in_layer(near)
-        even = even_sum if near % 2 == 0 else ~even_sum
-        known = source[near] + jnp.where(even, total + face_near * iterate[inner], face_near * updated)
-        sides.append((cell[near], cell[inner], known, odd_cells(iterate.at[near], half, odd_lane ^ (near % 2 != 0))))
-    places = [pl.ds(k * height, height) for k in range(3)] + [pl.ds(3 * height, half)]
-    store_by_side(across, within, list(zip(places, *sides)))
 
 
 def odd_cells(ref, rows, first):
@@ -117,128 +73,266 @@
     ref[pl.ds(1, rows, 2), :] = values
 
 
-def fine_down_kernel(
-    owner_of, inputs, across_in, within_in,
-    across, within, fx2_out, e, fx, fx_outer, fy, fz, fzl, inv,
-    cell, held, pair,
+def cell_coef(value):
+    return STIFFNESS * (value * value + EPSILON)
+
+
+class Plane:
+    def __init__(self, height, depth):
+        self.height, self.half, self.depth = height, height // 2, depth
+        self.row, self.lane = rows_of((height, depth)), lanes_of((height, depth))
+        self.parity = self.row + self.lane + core_of()
+        self.half_lane = lanes_of((self.half, depth))
+        self.body = pl.ds(PAD, height)
+        self.up, self.down = pl.ds(PAD + 1, height), pl.ds(PAD - 1, height)
+
+    def even(self, u):
+        return ((self.parity + u) & 1) == 0
+
+    def odd_first(self, u):
+        return ((self.half_lane + core_of() + u) & 1) != 0
+
+    def put(self, ref, values):
+        edge = jnp.zeros((PAD, self.depth), jnp.float32)
+        ref[:PAD] = edge
+        ref[PAD + self.height:] = edge
+        ref[self.body] = values
+
+    def face_y(self, here):
+        return jnp.where(self.row < self.height - 1, 0.5 * (here + ahead(here, 1, 0)), 0.0)
+
+    def face_z(self, here):
+        return jnp.where(self.lane < self.depth - 1, 0.5 * (here + ahead(here, 1, 1)), 0.0)
+
+    def packed(self, outer, inner, core):
+        return jnp.where((self.half_lane & 1) == core, outer, inner)
+
+    def both_rows(self, ref):
+        return even_row_sum(ref, self.half)
+
+    def summed(self, values, ref):
+        ref[...] = values
+        return with_partner(self.both_rows(ref), 1, 1)
+
+    def odd_rows(self, values, ref):
+        ref[...] = values
+        return with_partner(ref[pl.ds(1, self.half, 2), :], 1, 1)
+
+    def odd_lanes(self, values, ref):
+        ref[...] = values
+        sums = self.both_rows(ref)
+        return jnp.where((self.half_lane & 1) == 0, ahead(sums, 1, 1), sums)
+
+
+def in_layer(plane, fy, fz, fzl, padded):
+    here = padded[plane.body]
+    total = fy[plane.body] * padded[plane.up] + fy[plane.down] * padded[plane.down]
+    return total + (fz[...] * ahead(here, 1, 1) + fzl[...] * behind(here, 1, 1))
+
+
+def edge_kernel(inputs, out):
+    iterate, source, phase = three_parts(inputs)
+    layers, height, depth = iterate.shape
+    plane = Plane(height, depth)
+    near, inner, far = [own_layer(u, layers) for u in (layers - 1, layers - 2, layers - 3)]
+    coef_near, coef_inner, coef_far = [cell_coef(phase[k]) for k in (near, inner, far)]
+
+    def around(here, e):
+        fy, fz = plane.face_y(here), plane.face_z(here)
+        fyl, fzl = behind(fy, 1, 0), behind(fz, 1, 1)
+        total = fy * ahead(e, 1, 0) + fyl * behind(e, 1, 0)
+        return total + fz * ahead(e, 1, 1) + fzl * behind(e, 1, 1), fy + fyl + fz + fzl
+
+    face_near, face_far = 0.5 * (coef_inner + coef_near), 0.5 * (coef_inner + coef_far)
+    total, weight = around(coef_inner, iterate[inner])
+    total = total + face_near * iterate[near] + face_far * iterate[far]
+    updated = (source[inner] + total) / (1.0 + (face_near + face_far + weight))
+    total, _ = around(coef_near, iterate[near])
+    known = jnp.where(plane.even(layers - 1), total + face_near * iterate[inner], face_near * updated)
+    out[:height] = coef_near
+    out[height:2 * height] = coef_inner
+    out[2 * height:3 * height] = source[near] + known
+    out[3 * height:] = odd_cells(iterate.at[near], plane.half, plane.odd_first(layers - 1))
+
+
+def chip_rows(height):
+    half, at, places = height // 2, 0, {}
+    for name, size in (
+        ("coef0", height), ("coef1", height), ("coef2", height), ("known0", height),
+        ("old0", half), ("known1", half), ("old1", half), ("source2", half), ("fx2", half), ("fy2", half), ("fz2", half),
+    ):
+        places[name] = pl.ds(at, size)
+        at += size
+    return places, at
+
+
+def chip_kernel(
+    inputs, within_in,
+    message, known1, new, fx, fy, fz, fzl, inv,
+    cell, old, even, change, turn,
 ):
     iterate, source, phase = three_parts(inputs)
     layers, height, depth = iterate.shape
-    window = layers + 2
-    position, last = lax.axis_index("gx"), lax.axis_size("gx") - 1
-    body = pl.ds(PAD, height)
-    up, down = pl.ds(PAD + 1, height), pl.ds(PAD - 1, height)
-    row, lane = rows_of((height, depth)), lanes_of((height, depth))
-    even_sum = ((row + lane) & 1) == 0
-    half = height // 2
-    own = range(1, layers + 1)
-    outer = ((0, 0), (1, window - 1))
-
-    def part(ref, k):
-        return ref[k * height:(k + 1) * height]
-
-    def mask(w, odd):
-        return even_sum if (w + odd) % 2 == 1 else ~even_sum
-
-    edge = jnp.zeros((PAD, depth), jnp.float32)
-    for w in range(window):
-        for padded in (e, fy):
-            padded[w, :PAD] = edge
-            padded[w, PAD + height:] = edge
-        cell[w, PAD + height:] = edge
-    halos = [by_side(part(across_in, k), part(within_in, k)) for k in range(3)]
-    borders = by_side(across_in[3 * height:], within_in[3 * height:])
-    for side, w in outer:
-        cell[w, body] = halos[0][side]
-        fx_outer[side] = 0.5 * (halos[0][side] + halos[1][side])
-        into_both_rows(pair.at[side], borders[side])
-        e[w, body] = pair[side]
-    for w in own:
-        value = phase[w - 1]
-        cell[w, body] = STIFFNESS * (value * value + EPSILON)
-        e[w, body] = iterate[w - 1]
-    for w in range(window):
-        here = cell[w, body]
-        if w < window - 1:
-            face = 0.5 * (here + cell[w + 1, body])
-            if w == 0:
-                face = jnp.where(position > 0, face, 0.0)
-            if w == window - 2:
-                face = jnp.where(position < last, face, 0.0)
-            fx[w] = face
-        fy[w, body] = jnp.where(row < height - 1, 0.5 * (here + cell[w, up]), 0.0)
-        face = jnp.where(lane < depth - 1, 0.5 * (here + ahead(here, 1, 1)), 0.0)
-        fz[w] = face
-        fzl[w] = behind(face, 1, 1)
-    for w in range(window):
-        beyond = fx[w] if w < window - 1 else fx_outer[1]
-        before = fx[w - 1] if w > 0 else fx_outer[0]
-        weight = beyond + before + fy[w, body] + fy[w, down] + fz[w] + fzl[w]
-        inv[w] = 1.0 / (1.0 + weight)
-
-    def in_layer(w):
-        here = e[w, body]
-        total = fy[w, body] * e[w, up] + fy[w, down] * e[w, down]
-        return total + fz[w] * ahead(here, 1, 1) + fzl[w] * behind(here, 1, 1)
-
-    def neigh(w):
-        return fx[w] * e[w + 1, body] + fx[w - 1] * e[w - 1, body] + in_layer(w)
-
-    def towards_own(side, w):
-        return fx[0] * e[1, body] if side == 0 else fx[w - 1] * e[w - 1, body]
-
-    for w in own:
-        total = source[w - 1] + neigh(w)
-        held[w - 1] = total
-        e[w, body] = jnp.where(mask(w, 0), total * inv[w], e[w, body])
-    for side, w in outer:
-        total = halos[2][side] + towards_own(side, w)
-        e[w, body] = jnp.where(mask(w, 0), total * inv[w], e[w, body])
-    for side, w in outer:
-        total = (halos[2][side] + in_layer(w) + towards_own(side, w)) * inv[w]
-        e[w, body] = jnp.where(mask(w, 1), total, e[w, body])
-    for w in own:
-        total = (source[w - 1] + neigh(w)) * inv[w]
-        e[w, body] = jnp.where(mask(w, 1), total, e[w, body])
-
-    lane = lanes_of((half, depth))
-    first_of_two = (lane & 1) == 0
-
-    def residual(w):
-        return jnp.where(mask(w, 0), source[w - 1] + neigh(w) - held[w - 1], 0.0)
-
-    def slabs(make, reduce_rows, reduce_lanes):
-        found = []
-        for t in range(2):
-            pair[t] = make(1 + 2 * t)
-            found.append(reduce_lanes(reduce_rows(pair.at[t])))
-        return jnp.where(first_of_two, found[0], found[1])
-
-    def both_rows(scratch):
-        return even_row_sum(scratch, half)
-
-    def odd_rows(scratch):
-        return scratch[pl.ds(1, half, 2), :]
-
-    def both_lanes(values):
-        return with_partner(values, 1, 1)
-
-    def odd_lanes(values):
-        return jnp.where(first_of_two, ahead(values, 1, 1), values)
-
-    coarse_source = slabs(lambda w: residual(w) + residual(w + 1), both_rows, both_lanes)
-    coarse_fy = slabs(lambda w: fy[w, body] + fy[w + 1, body], odd_rows, both_lanes)
-    coarse_fz = slabs(lambda w: fz[w] + fz[w + 1], both_rows, odd_lanes)
-    left_fx = slabs(lambda w: fx[w + 1], both_rows, both_lanes)
-    right_fx = slabs(lambda w: fx[w - 1], both_rows, both_lanes)
-    fx2_out[0], fx2_out[1] = left_fx, right_fx
-    known = []
-    for t, (w, face, inner) in enumerate(((1, 1, 2), (layers, layers - 1, layers - 1))):
-        pair[t] = source[w - 1] + fx[face] * e[inner, body]
-        known.append(odd_cells(pair.at[t], half, first_of_two if w % 2 == 1 else ~first_of_two))
-    pieces = [(0, coarse_source), (2, coarse_fy), (3, coarse_fz)]
-    pieces = [(k, value, value) for k, value in pieces]
-    store_by_side(across, within, pieces + [(1, left_fx, right_fx), (4, *known)])
+    plane = Plane(height, depth)
+    body, half = plane.body, plane.half
+    places, _ = chip_rows(height)
+    margin = layers
+
+    def part(k):
+        return within_in[k * height:(k + 1) * height]
+
+    def s(u):
+        return source[own_layer(u, layers)]
+
+    for u in range(layers):
+        cell[u] = cell_coef(phase[own_layer(u, layers)])
+        plane.put(old.at[u], iterate[own_layer(u, layers)])
+    cell[margin] = part(0)
+    into_both_rows(turn.at[0], within_in[3 * height:])
+    plane.put(old.at[margin], turn[0])
+    for u in range(margin + 1):
+        here = cell[u]
+        fx[u] = 0.5 * (here + (cell[u + 1] if u < margin else part(1)))
+        plane.put(fy.at[u], plane.face_y(here))
+        face = plane.face_z(here)
+        fz[u] = face
+        fzl[u] = behind(face, 1, 1)
+    for u in range(1, margin + 1):
+        weight = (fx[u] + fx[u - 1]) + (fy[u, body] + fy[u, plane.down]) + (fz[u] + fzl[u])
+        inv[u - 1] = 1.0 / (1.0 + weight)
+
+    def around(ref, u):
+        return in_layer(plane, fy.at[u], fz.at[u], fzl.at[u], ref.at[u])
+
+    for u in range(1, margin):
+        total = s(u) + around(old, u) + (fx[u] * old[u + 1, body] + fx[u - 1] * old[u - 1, body])
+        plane.put(even.at[u], total * inv[u - 1])
+    plane.put(even.at[margin], (part(2) + fx[margin - 1] * old[margin - 1, body]) * inv[margin - 1])
+    for u in range(2, margin + 1):
+        if u < margin:
+            total = s(u) + around(even, u) + (fx[u] * even[u + 1, body] + fx[u - 1] * even[u - 1, body])
+        else:
+            total = part(2) + around(even, u) + fx[u - 1] * even[u - 1, body]
+        fresh = total * inv[u - 1]
+        new[u - 2] = fresh
+        plane.put(change.at[u], fresh - old[u, body])
+
+    one = fx[1] * change[2, body]
+    two = around(change, 2) + fx[2] * change[3, body]
+    three = around(change, 3) + (fx[2] * change[2, body] + fx[3] * change[4, body])
+    outer = jnp.where(plane.even(1), one, 0.0)
+    inner = jnp.where(plane.even(2), two, 0.0) + jnp.where(plane.even(3), three, 0.0)
+    core = core_of()
+
+    def tile(name, outer, inner):
+        message[places[name], :] = plane.packed(outer, inner, core)
+
+    tile("source2", plane.summed(outer, turn.at[1]), plane.summed(inner, turn.at[2]))
+    tile("fx2", plane.summed(fx[1], turn.at[3]), plane.summed(fx[3], turn.at[4]))
+    tile("fy2", *[plane.odd_rows(fy[u, body] + fy[u + 1, body], turn.at[5 + u // 2]) for u in (0, 2)])
+    tile("fz2", *[plane.odd_lanes(fz[u] + fz[u + 1], turn.at[7 + u // 2]) for u in (0, 2)])
+    for u in range(3):
+        message[places["coef%d" % u], :] = cell[u]
+    first = s(0) + around(old, 0) + fx[0] * old[1, body]
+    second = s(0) + fx[0] * even[1, body]
+    message[places["known0"], :] = jnp.where(plane.even(0), first, second)
+    total = s(1) + around(even, 1) + fx[1] * even[2, body]
+    known1[...] = total
+    turn[9] = total
+    message[places["known1"], :] = odd_cells(turn.at[9], half, plane.odd_first(1))
+    for u in range(2):
+        message[places["old%d" % u], :] = odd_cells(iterate.at[own_layer(u, layers)], half, plane.odd_first(u))
+
+
+def border_kernel(
+    owner_of, inputs, message, known1, new_in, fx_in, fy_in, fz_in, fzl_in, inv_in, across_in,
+    within, outer2, fx2_in, new, known, fx, fy, fz, fzl, inv,
+    old, even, change, turn, face_y, face_z, face_zl,
+):
+    iterate, source, _ = three_parts(inputs)
+    layers, height, depth = iterate.shape
+    plane = Plane(height, depth)
+    body, half = plane.body, plane.half
+    places, _ = chip_rows(height)
+    core, last = core_of(), lax.axis_size("gx") - 1
+    position = lax.axis_index("gx")
+
+    def mine(name):
+        return message[places[name], :]
+
+    def theirs(name):
+        return across_in[places[name], :]
+
+    def opened(name, k):
+        into_both_rows(turn.at[k], theirs(name))
+        return turn[k]
+
+    for k in range(2):
+        here = theirs("coef%d" % k)
+        plane.put(face_y.at[k], plane.face_y(here))
+        face = plane.face_z(here)
+        face_z[k] = face
+        face_zl[k] = behind(face, 1, 1)
+    fy[...], fz[...], fzl[...] = face_y[0], face_z[0], face_zl[0]
+    there = position - 1 + 2 * core
+    border = jnp.where((there >= 0) & (there <= last), 0.5 * (mine("coef0") + theirs("coef0")), 0.0)
+    face1 = 0.5 * (theirs("coef0") + theirs("coef1"))
+    face2 = 0.5 * (theirs("coef1") + theirs("coef2"))
+    fx[0], fx[1] = border, face1
+
+    def inverse(faces, fy, fz, fzl):
+        weight = faces + (fy[body] + fy[plane.down]) + (fz[...] + fzl[...])
+        return 1.0 / (1.0 + weight)
+
+    inv_own = inverse(fx_in[0] + border, fy_in.at[0], fz_in.at[0], fzl_in.at[0])
+    inv_near = inverse(border + face1, face_y.at[0], face_z.at[0], face_zl.at[0])
+    inv_far = inverse(face1 + face2, face_y.at[1], face_z.at[1], face_zl.at[1])
+    inv[0], inv[1] = inv_near, inv_own
+    old_own, old_next = iterate[own_layer(0, layers)], iterate[own_layer(1, layers)]
+    old_near, old_far = opened("old0", 0), opened("old1", 1)
+    even_own = (mine("known0") + border * old_near) * inv_own
+    even_near = (theirs("known0") + border * old_own) * inv_near
+    plane.put(even.at[0], even_near)
+    plane.put(even.at[1], even_own)
+
+    def near(ref, k):
+        return in_layer(plane, face_y.at[k], face_z.at[k], face_zl.at[k], ref)
+
+    def own(ref, u):
+        return in_layer(plane, fy_in.at[u], fz_in.at[u], fzl_in.at[u], ref)
+
+    odd_own = (mine("known0") + own(even.at[1], 0) + border * even_near) * inv_own
+    odd_near = (theirs("known0") + near(even.at[0], 0) + border * even_own) * inv_near
+    odd_next = (known1[...] + fx_in[0] * even_own) * inv_in[0]
+    odd_far = (opened("known1", 2) + face1 * even_near) * inv_far
+    new[0], new[1], new[2] = odd_near, odd_own, odd_next
+    moved = odd_far - old_far, odd_near - old_near, odd_own - old_own, odd_next - old_next
+    for k, values in enumerate(moved):
+        plane.put(change.at[k], values)
+    far, near_by, here, following = moved
+    plane.put(old.at[0], old_near)
+    known[...] = theirs("known0") + face1 * far - near(old.at[0], 0)
+
+    def residual(u, values):
+        return jnp.where(plane.even(u), values, 0.0)
+
+    own_outer = residual(1, own(change.at[3], 1) + fx_in[0] * here)
+    own_outer = own_outer + residual(0, own(change.at[2], 0) + (fx_in[0] * following + border * near_by))
+    own_inner = residual(2, fx_in[1] * following)
+    its_outer = residual(-1, near(change.at[1], 0) + (face1 * far + border * here))
+    its_outer = its_outer + residual(-2, near(change.at[0], 1) + face1 * near_by)
+    its_inner = residual(-3, face2 * far)
+    sums = [plane.summed(values, turn.at[3 + k]) for k, values in enumerate((own_outer, own_inner, its_outer, its_inner))]
+    within[0] = mine("source2") + plane.packed(sums[0], sums[1], core)
+    outer2[0] = theirs("source2") + plane.packed(sums[2], sums[3], 1 - core)
+    for k, name in ((1, "fx2"), (2, "fy2"), (3, "fz2")):
+        outer2[k] = theirs(name)
+    fx2_in[...] = mine("fx2")
+    middle = jnp.where((plane.half_lane & 1) == 0, ahead(mine("fx2"), 1, 1), behind(mine("fx2"), 1, 1))
+    within[1] = plane.packed(plane.summed(border, turn.at[7]), middle, core)
+    within[2], within[3] = mine("fy2"), mine("fz2")
+    turn[0] = source[own_layer(layers - 1, layers)] + fx_in[layers - 2] * new_in[layers - 4]
+    within[4] = odd_cells(turn.at[0], half, jnp.logical_not(plane.odd_first(layers - 1)))
 
 
 def neigh2(e2, fx2, fxl2, fy2, fz2, fzl2, first_of_two, tiles):
@@ -270,7 +364,7 @@
 
 
 def middle_down_kernel(
-    own, own_fx, across_in, within_in,
+    own, fx2_in, outer, within_in,
     slots, e2_out, s2, fx2, fxl2, fy2, fz2, fzl2, inv2,
     e2, pair,
 ):
@@ -283,7 +377,7 @@
     for j in range(5):
         e2[j] = jnp.zeros((half + 2 * PAD, lanes), jnp.float32)
     def three(k):
-        left, right = by_side(across_in[k], within_in[k])
+        left, right = by_side(outer[k], within_in[k])
         return left, own[k], right
 
     for j, (source, fy, fz) in enumerate(zip(three(0), three(2), three(3))):
@@ -294,6 +388,7 @@
         fz2[j] = fz
         fzl2[j] = behind(fz, 2, 1)
     left_fx, _, right_fx = three(1)
+    own_fx = by_side(fx2_in[...], own[1])
     fx2[0] = jnp.where(first_of_two, ahead(left_fx, 1, 1), behind(own_fx[1], 1, 1))
     fx2[1] = own_fx[0]
     fx2[2] = right_fx
@@ -525,7 +620,8 @@
 
 def coarse_kernel(
     owner_of, same_cores, other_cores, e2_in, s2, fx2, fxl2, fy2, fz2, fzl2, inv2,
-    inputs, field, fx_in, fx_outer, fy_in, fz_in, fzl_in, inv_in, across_in, within_in,
+    inputs, new_in, fx_in, fy_in, fz_in, fzl_in, inv_in,
+    new_out, known_out, fx_out, fy_out, fz_out, fzl_out, inv_out, within_in,
     solved_out, owned_out,
     e3, rows3, pair, e2, e1, cor, solved, owned, owner_here, fetch_sem, sems,
 ):
@@ -596,46 +692,52 @@
     fixes2 = [jnp.where(even2, even, odd) for even, odd in zip(fresh, update2())]
 
     _, source, _ = three_parts(inputs)
-    body1, up1, down1 = pl.ds(PAD, height), pl.ds(PAD + 1, height), pl.ds(PAD - 1, height)
-    rows, lane = rows_of((height, lanes)), lanes_of((height, lanes))
-    even_sum = ((rows + lane) & 1) == 0
-    count = e1.shape[0]
+    layers = source.shape[0]
+    plane = Plane(height, lanes)
+    body1 = plane.body
+    core = core_of()
+    near_lane = (lanes_of((half, lanes)) & 1) == core
+    swaps = [jnp.where(first_of_two, ahead(v, 1, 1), behind(v, 1, 1)) for v in fixes2]
+    outer, inner = by_side(fixes2[0], fixes2[2])
+    outer_swap, inner_swap = by_side(swaps[0], swaps[2])
+    coarse = (
+        jnp.where(near_lane, outer_swap, outer), jnp.where(near_lane, fixes2[1], swaps[1]),
+        jnp.where(near_lane, swaps[1], fixes2[1]), jnp.where(near_lane, inner, inner_swap),
+    )
     fixes = []
-    for w in range(count):
-        tile, t = divmod((w - 1) // 2, 2)
-        packed = fixes2[1 + tile]
-        if w % 2 == 1 or w == 0:
-            if t == 0:
-                plain = jnp.where(first_of_two, packed, behind(packed, 1, 1))
-            else:
-                plain = jnp.where(first_of_two, ahead(packed, 1, 1), packed)
-            into_both_rows(cor.at[len(fixes)], plain)
-            fixes.append(cor[len(fixes)])
-        e1[w, :PAD] = edge
-        e1[w, PAD + height:] = edge
-        e1[w, body1] = field[w, body1] + fixes[-1]
-
-    def in_layer1(w):
-        here = e1[w, body1]
-        sums = fy_in[w, body1] * e1[w, up1] + fy_in[w, down1] * e1[w, down1]
-        return sums + fz_in[w] * ahead(here, 1, 1) + fzl_in[w] * behind(here, 1, 1)
-
-    def smoothed1(w, odd):
-        keep = even_sum if (w + odd) % 2 == 0 else ~even_sum
-        sums = fx_in[w] * e1[w + 1, body1] + fx_in[w - 1] * e1[w - 1, body1] + in_layer1(w)
-        return jnp.where(keep, e1[w, body1], (source[w - 1] + sums) * inv_in[w])
-
-    borders = by_side(across_in[4], within_in[4])
-    for w in range(1, count - 1):
-        e1[w, body1] = smoothed1(w, 0)
-    for side, w, near in ((0, 0, 1), (1, count - 1, count - 2)):
-        into_both_rows(cor.at[4 + side], borders[side])
-        sums = cor[4 + side] + fx_outer[side] * fixes[0 if side == 0 else -1]
-        sums = sums + fx_in[min(w, near)] * e1[near, body1] + in_layer1(w)
-        e1[w, body1] = sums * inv_in[w]
-    for w in range(1, count - 1):
-        solved[w - 1] = smoothed1(w, 1)
-        copies.append(pltpu.make_async_copy(solved.at[w - 1], solved_out.at[w - 1], sems.at[w]))
+    for k in range(4):
+        into_both_rows(cor.at[k], coarse[k])
+        fixes.append(cor[k])
+    for u in range(-1, layers + 1):
+        before = new_out[u + 1] if u < 2 else new_in[u - 2]
+        plane.put(e1.at[u + 1], before + fixes[(u + 2) // 2])
+
+    def fx1(u):
+        return fx_in[u] if u >= 0 else fx_out[-1 - u]
+
+    def inv1(u):
+        return inv_in[u - 1] if u > 0 else inv_out[u + 1]
+
+    def around1(u):
+        if u < 0:
+            return in_layer(plane, fy_out, fz_out, fzl_out, e1.at[0])
+        return in_layer(plane, fy_in.at[u], fz_in.at[u], fzl_in.at[u], e1.at[u + 1])
+
+    def updated1(u):
+        sums = around1(u) + (fx1(u) * e1[u + 2, body1] + fx1(u - 1) * e1[u, body1])
+        return (source[own_layer(u, layers)] + sums) * inv1(u)
+
+    for u in range(layers):
+        e1[u + 1, body1] = jnp.where(plane.even(u), updated1(u), e1[u + 1, body1])
+    e1[0, body1] = (known_out[...] + fx1(-2) * fixes[0] + (around1(-1) + fx1(-1) * e1[1, body1])) * inv1(-1)
+    into_both_rows(cor.at[4], within_in[4])
+    sums = cor[4] + fx1(layers) * fixes[3] + (around1(layers) + fx1(layers - 1) * e1[layers, body1])
+    e1[layers + 1, body1] = sums * inv1(layers)
+    for u in range(layers):
+        solved[u] = jnp.where(plane.even(u), e1[u + 1, body1], updated1(u))
+        copies.append(
+            pltpu.make_async_copy(solved.at[u], solved_out.at[own_layer(u, layers)], sems.at[u + 1])
+        )
         copies[-1].start()
     for copy in copies:
         copy.wait()
@@ -672,43 +774,55 @@
     layers, height, depth = iterate.shape
     half, quarter = height // 2, height // 4
     blocks = lax.axis_size("gx")
-    window = layers + 2
     padded, padded2 = height + 2 * PAD, half + 2 * PAD
     inputs = sum(
         jnp.pad(block, ((k * layers, (2 - k) * layers), (0, 0), (0, 0)))
         for k, block in enumerate((iterate, source, phase_field))
     )
-    sent = call(edge_kernel, [f32(3 * height + half, depth)] * 2, [], (inputs,))
-    plain, tall = f32(window, height, depth), f32(window, padded, depth)
-    across, within, fx2, *fine = call(
-        fine_down_kernel,
-        [f32(5, half, depth)] * 2
-        + [f32(2, half, depth), tall, f32(window - 1, height, depth), f32(2, height, depth), tall]
-        + [plain] * 3,
-        [vmem(window, padded, depth), vmem(layers, height, depth), vmem(2, height, depth)],
-        (block_owner, inputs, *swapped(*sent)),
-    )
-    halos = swapped(across, within)
-    plain = f32(3, half, depth)
+    edge, = call(edge_kernel, [f32(3 * height + half, depth)], [], (inputs,))
+    layer, tile, five = (height, depth), (half, depth), layers + 1
+    message, known1, *fine = call(
+        chip_kernel,
+        [
+            f32(chip_rows(height)[1], depth), f32(*layer), f32(3, *layer), f32(five, *layer),
+            f32(five, padded, depth), f32(five, *layer), f32(five, *layer), f32(layers, *layer),
+        ],
+        [vmem(five, *layer)] + [vmem(five, padded, depth)] * 3 + [vmem(10, *layer)],
+        (inputs, within_chip(edge)),
+    )
+    within, outer, fx2, *border = call(
+        border_kernel,
+        [
+            f32(5, *tile), f32(4, *tile), f32(*tile), f32(3, *layer), f32(*layer), f32(2, *layer),
+            f32(padded, depth), f32(*layer), f32(*layer), f32(2, *layer),
+        ],
+        [
+            vmem(1, padded, depth), vmem(2, padded, depth), vmem(4, padded, depth), vmem(8, *layer),
+            vmem(2, padded, depth), vmem(2, *layer), vmem(2, *layer),
+        ],
+        (block_owner, inputs, message, known1, *fine, between_chips(message)),
+    )
+    within_in = within_chip(within)
+    plain = f32(3, *tile)
     slots, *middle = call(
         middle_down_kernel,
         [f32(blocks // 2, 2, quarter, depth), plain, plain, plain, plain, f32(3, padded2, depth)] + [plain] * 3,
-        [vmem(5, padded2, depth), vmem(2, half, depth)],
-        (across, fx2, *halos),
+        [vmem(5, padded2, depth), vmem(2, *tile)],
+        (within, fx2, outer, within_in),
     )
     kinds = [list(range(core, blocks, 2)) for core in range(2)]
     same_cores = lax.all_to_all(slots, "gx", 0, 0, axis_index_groups=kinds, tiled=True)
     other_cores = within_chip(same_cores)
     solved, owned = call(
         coarse_kernel,
-        [f32(layers, height, depth), f32(1, quarter, depth // 4)],
+        [f32(layers, *layer), f32(1, quarter, depth // 4)],
         [
-            vmem(blocks // 4, quarter, depth), vmem(4, blocks // 4, quarter + 2 * PAD, depth), vmem(7, half, depth),
-            vmem(5, padded2, depth), vmem(window, padded, depth), vmem(6, height, depth),
-            vmem(layers, height, depth), vmem(1, quarter, depth // 4), pltpu.SMEM((blocks,), jnp.int32),
+            vmem(blocks // 4, quarter, depth), vmem(4, blocks // 4, quarter + 2 * PAD, depth), vmem(7, *tile),
+            vmem(5, padded2, depth), vmem(layers + 2, padded, depth), vmem(5, *layer), vmem(layers, *layer),
+            vmem(1, quarter, depth // 4), pltpu.SMEM((blocks,), jnp.int32),
             pltpu.SemaphoreType.DMA, pltpu.SemaphoreType.DMA((layers + 1,)),
         ],
-        (block_owner, same_cores, other_cores, *middle, inputs, *fine, *halos),
+        (block_owner, same_cores, other_cores, *middle, inputs, *fine, *border, within_in),
         pl.ANY,
     )
     return solved, owned

time: 36.2 us -> 35.4 us (0.978)
  blocking collectives: 18.8 us -> 13.2 us
  starting transfers between devices: 7.67 us -> 11.2 us
  waiting for transfers between devices: 2.57 us -> 3.24 us
  local copies, waits for them, and re-layouts: 0.01 us -> 0.65 us
    all_to_all x1, blocking collectives: 18.8 us -> 13.2 us  [on_device(): lax.all_to_all(slots, 'gx', 0, 0, axis_index_groups=kinds, tiled=True)]
    ppermute x3, starting transfers between devices: 6.35 us -> 10.5 us  [within_chip(): lax.ppermute(block, 'gx', [(i, i ^ 1) for i in range(lax.axis_size('gx'))])]
    ppermute x3, waiting for transfers between devices: 2.57 us -> 3.23 us  [within_chip(): lax.ppermute(block, 'gx', [(i, i ^ 1) for i in range(lax.axis_size('gx'))])]
    unnamed x2, local copies, waits for them, and re-layouts: 0.01 us -> 0.65 us
    ppermute x2 -> x1, starting transfers between devices: 1.32 us -> 0.68 us  [between_chips(): lax.ppermute(block, 'gx', [(i, i + 1 if i % 2 else i - 1) for i in range(...]
    pallas_call x4 -> x5, Pallas kernels: 5.18 us -> 5.16 us  [call(): pl.pallas_call(kernel, out_shape=tuple(outs), in_specs=[pl.BlockSpec(memo...]
  transfers between devices with their start and end apart: 5 -> 4, of which waited for: 3 -> 3; matrix products, arithmetic and copies ran while one was open for 0% -> 0% of each run, Pallas kernels for 0% -> 0%
where the time goes in v10:
time: 35.4 us; the launch traced here: 35.2 us
  blocking collectives  13.2 us (37%)
  starting transfers between devices  11.2 us (32%)
  Pallas kernels  5.16 us (15%)
  waiting for transfers between devices  3.24 us (9%)
  other arithmetic  1.06 us (3%)
  between operations  0.68 us (2%)
  local copies, waits for them, and re-layouts  0.65 us (2%)
    all_to_all x1, blocking collectives, on_device(): lax.all_to_all(slots, 'gx', 0, 0, axis_index_groups=kinds, tiled=True)  13.2 us
    ppermute x3, starting transfers between devices, within_chip(): lax.ppermute(block, 'gx', [(i, i ^ 1) for i in range(lax.axis_size('gx'))])  10.5 us
    pallas_call x5, Pallas kernels, call(): pl.pallas_call(kernel, out_shape=tuple(outs), in_specs=[pl.BlockSpec(memo...  5.16 us
    ppermute x3, waiting for transfers between devices, within_chip(): lax.ppermute(block, 'gx', [(i, i ^ 1) for i in range(lax.axis_size('gx'))])  3.23 us
    add x1, other arithmetic, on_device(): sum((jnp.pad(block, ((k * layers, (2 - k) * layers), (0, 0), (0, 0))) for...  1.06 us
  transfers between devices with their start and end apart: 4, of which 3 were waited for; matrix products, arithmetic and copies ran while one was open for 0% of the time, Pallas kernels for 0%

profile of v10, /device:TPU:0, one launch (start us, length us, event | category | flops | bytes accessed | tf_op | source)
XLA Modules:
  0.0 35.2 jit_solution(6508270694891973336)
XLA Ops:
  0.6 1.1 %pad_add_fusion.inputs = f32[12,64,128]{2,1,0:T(8,128)S(1)} fusion(f32[4,64,128]{2,1,0:T(8,128)} %param.6, f32[4,64,128]{2,1,0:T(8,128)} %param.5, f32[4,64,128]{2,1,0:T(8,128)} %param.4), kind=kLoop, calls=%fused_computation | loop fusion | flops 196608 | bytes 786432 | tf_op jit(solution)/shard_map/add | solution.py:778
  1.7 0.2 shard_map.59
  1.9 0.5 %collective-permute-start = (f32[224,128]{1,0:T(8,128)S(1)}, f32[224,128]{1,0:T(8,128)S(1)}, u32[]{:S(2)}, u32[]{:S(2)}) collective-permute-start(f32[224,128]{1,0:T(8,128)S(1)} %shard_map.59), channel_id=1, source_target_pairs={{0,1},{1,0},{2,3},{3,2},{4,5},{5,4},{6,7},{7,6},{8,9},{9,8},{10,11... | collective-permute-start | bytes 344072 | tf_op jit(solution)/shard_map/ppermute | solution.py:19
  2.4 1.0 %collective-permute-done.within_in = f32[224,128]{1,0:T(8,128)S(1)} collective-permute-done((f32[224,128]{1,0:T(8,128)S(1)}, f32[224,128]{1,0:T(8,128)S(1)}, u32[]{:S(2)}, u32[]{:S(2)}) %collective-permute-start) | collective-permute-done | bytes 114720 | tf_op jit(solution)/shard_map/ppermute | solution.py:19
  3.4 0.6 %shard_map.60 = (f32[480,128]{1,0:T(8,128)S(1)}, f32[64,128]{1,0:T(8,128)S(1)}, f32[3,64,128]{2,1,0:T(8,128)S(1)}, f32[5,64,128]{2,1,0:T(8,128)S(1)}, f32[5,80,1...) custom-call(f32[12,64,128]{2,1,0:T(8,128)S(1)} %pad_add_fusion.inputs, ...), custom_call_target="tpu_custom_call" | custom-call | tf_op jit(solution)/shard_map/pallas_call | solution.py:763
  4.0 0.7 %collective-permute-start.1 = (f32[480,128]{1,0:T(8,128)S(1)}, f32[480,128]{1,0:T(8,128)S(1)}, u32[]{:S(2)}, u32[]{:S(2)}) collective-permute-start(f32[480,128]{1,0:T(8,128)S(1)} %get-tuple-element.29.message), channel_id=1, source_target_pairs={{1,2},{2,1},{3,4},{4,3},{5,6},{6,5},{7,8},{8,7},{9,10},{10,9},{11,... | collective-permute-start | bytes 737288 | tf_op jit(solution)/shard_map/ppermute | solution.py:15
  4.7 0.0 collective-permute-done.1.across_in
  4.7 0.0 copy-start
  4.7 0.6 %copy-done = s32[16]{0:T(128)S(1)} copy-done((s32[16]{0:T(128)S(1)}, s32[16]{0:T(128)}, u32[]{:S(2)}) %copy-start) | copy-done | bytes 88
  5.4 0.5 %shard_map.61 = (f32[5,32,128]{2,1,0:T(8,128)S(1)}, f32[4,32,128]{2,1,0:T(8,128)S(1)}, f32[32,128]{1,0:T(8,128)S(1)}, f32[3,64,128]{2,1,0:T(8,128)S(1)}, f32[64,...) custom-call(s32[16]{0:T(128)S(1)} %copy-done, ...), custom_call_target="tpu_custom_call" | custom-call | tf_op jit(solution)/shard_map/pallas_call | solution.py:763
  5.8 10.0 %collective-permute-start.2 = (f32[5,32,128]{2,1,0:T(8,128)S(1)}, f32[5,32,128]{2,1,0:T(8,128)S(1)}, u32[]{:S(2)}, u32[]{:S(2)}) collective-permute-start(f32[5,32,128]{2,1,0:T(8,128)S(1)} %get-tuple-element.37.own), channel_id=1, source_target_pairs={{0,1},{1,0},{2,3},{3,2},{4,5},{5,4},{6,7},{7,6},{8,9},{9,8},{10,11... | collective-permute-start | bytes 245768 | tf_op jit(solution)/shard_map/ppermute | solution.py:19
  15.8 0.9 %collective-permute-done.2.within_in = f32[5,32,128]{2,1,0:T(8,128)S(1)} collective-permute-done((f32[5,32,128]{2,1,0:T(8,128)S(1)}, f32[5,32,128]{2,1,0:T(8,128)S(1)}, u32[]{:S(2)}, u32[]{:S(2)}) %collective-permute-start.2) | collective-permute-done | bytes 81952 | tf_op jit(solution)/shard_map/ppermute | solution.py:19
  16.7 0.5 %shard_map.62 = (f32[8,2,16,128]{3,2,1,0:T(8,128)S(1)}, f32[3,32,128]{2,1,0:T(8,128)S(1)}, f32[3,32,128]{2,1,0:T(8,128)S(1)}, f32[3,32,128]{2,1,0:T(8,128)S(1)},...) custom-call(f32[5,32,128]{2,1,0:T(8,128)S(1)} %get-tuple-element.37., ...), custom_call_target="tpu_custom_call" | custom-call | tf_op jit(solution)/shard_map/pallas_call | solution.py:763
  17.2 13.2 %all_to_all.5.same_cores = f32[8,2,16,128]{3,2,1,0:T(8,128)S(1)} all-to-all(f32[8,2,16,128]{3,2,1,0:T(8,128)S(1)} %get-tuple-element.40), channel_id=1, replica_groups={{0,2,4,6,8,10,12,14},{1,3,5,7,9,11,13,15},{16,18,20,22,24,26,28,30},{17..., dimensions={0} | all-to-all | bytes 262144 | tf_op jit(solution)/shard_map/all_to_all | solution.py:814
  30.4 0.0 collective-permute-start.3
  30.4 1.3 %collective-permute-done.3.other_cores = f32[8,2,16,128]{3,2,1,0:T(8,128)S(1)} collective-permute-done((f32[8,2,16,128]{3,2,1,0:T(8,128)S(1)}, f32[8,2,16,128]{3,2,1,0:T(8,128)S(1)}, u32[]{:S(2)}, u32[]{:S(2)}) %collective-permute-start.3) | collective-permute-done | bytes 131104 | tf_op jit(solution)/shard_map/ppermute | solution.py:19
  31.8 3.4 %shard_map.63 = (f32[4,64,128]{2,1,0:T(8,128)}, f32[1,16,32]{2,1,0:T(8,128)}) custom-call(s32[16]{0:T(128)S(1)} %copy-done, f32[8,2,16,128]{3,2,1,0:T(8,128)S(1)} %all_to_all.5.same_cores, f32[8,2,16,128]{3,2,1,0:T(8,128)S(1)} %collective-permute-done.3.other_cores, f32[3,32,128]{2,1,0:T(8,128)S(1)} %get-tuple-element.41.e2_in, ...), custom_call_target="tpu_custom_call" | custom-call | tf_op jit(solution)/shard_map/pallas_call | solution.py:763
Async XLA Ops:
  1.9 1.5 %collective-permute-start = (f32[224,128]{1,0:T(8,128)S(1)}, f32[224,128]{1,0:T(8,128)S(1)}, u32[]{:S(2)}, u32[]{:S(2)}) collective-permute-start(f32[224,128]{1,0:T(8,128)S(1)} %shard_map.59), channel_id=1, source_target_pairs={{0,1},{1,0},{2,3},{3,2},{4,5},{5,4},{6,7},{7,6},{8,9},{9,8},{10,11... | collective-permute-start | bytes 344072 | tf_op jit(solution)/shard_map/ppermute | solution.py:19
  4.0 0.7 %collective-permute-start.1 = (f32[480,128]{1,0:T(8,128)S(1)}, f32[480,128]{1,0:T(8,128)S(1)}, u32[]{:S(2)}, u32[]{:S(2)}) collective-permute-start(f32[480,128]{1,0:T(8,128)S(1)} %get-tuple-element.29.message), channel_id=1, source_target_pairs={{1,2},{2,1},{3,4},{4,3},{5,6},{6,5},{7,8},{8,7},{9,10},{10,9},{11,... | collective-permute-start | bytes 737288 | tf_op jit(solution)/shard_map/ppermute | solution.py:15
  4.7 0.7 %copy-start = (s32[16]{0:T(128)S(1)}, s32[16]{0:T(128)}, u32[]{:S(2)}) copy-start(s32[16]{0:T(128)} %owner_of.3) | copy-start | bytes 196
  5.8 10.9 %collective-permute-start.2 = (f32[5,32,128]{2,1,0:T(8,128)S(1)}, f32[5,32,128]{2,1,0:T(8,128)S(1)}, u32[]{:S(2)}, u32[]{:S(2)}) collective-permute-start(f32[5,32,128]{2,1,0:T(8,128)S(1)} %get-tuple-element.37.own), channel_id=1, source_target_pairs={{0,1},{1,0},{2,3},{3,2},{4,5},{5,4},{6,7},{7,6},{8,9},{9,8},{10,11... | collective-permute-start | bytes 245768 | tf_op jit(solution)/shard_map/ppermute | solution.py:19
  30.4 1.3 %collective-permute-start.3 = (f32[8,2,16,128]{3,2,1,0:T(8,128)S(1)}, f32[8,2,16,128]{3,2,1,0:T(8,128)S(1)}, u32[]{:S(2)}, u32[]{:S(2)}) collective-permute-start(f32[8,2,16,128]{3,2,1,0:T(8,128)S(1)} %all_to_all.5.same_cores), channel_id=1, source_target_pairs={{0,1},{1,0},{2,3},{3,2},{4,5},{5,4},{6,7},{7,6},{8,9},{9,8},{10,11... | collective-permute-start | bytes 393224 | tf_op jit(solution)/shard_map/ppermute | solution.py:19

commit v11 on v10

--- a/solution.py
+++ b/solution.py
@@ -158,8 +158,8 @@
 def chip_rows(height):
     half, at, places = height // 2, 0, {}
     for name, size in (
-        ("coef0", height), ("coef1", height), ("coef2", height), ("known0", height),
-        ("old0", half), ("known1", half), ("old1", half), ("source2", half), ("fx2", half), ("fy2", half), ("fz2", half),
+        ("coef0", height), ("coef1", height), ("known0", height), ("old0", half), ("moved1", half), ("face2", half),
+        ("source2", half), ("fx2", half), ("far2", half),
     ):
         places[name] = pl.ds(at, size)
         at += size
@@ -167,8 +167,8 @@
 
 
 def chip_kernel(
-    inputs, within_in,
-    message, known1, new, fx, fy, fz, fzl, inv,
+    owner_of, inputs, within_in,
+    message, own2, known1, new, fx, fy, fz, fzl, inv,
     cell, old, even, change, turn,
 ):
     iterate, source, phase = three_parts(inputs)
@@ -229,23 +229,25 @@
 
     tile("source2", plane.summed(outer, turn.at[1]), plane.summed(inner, turn.at[2]))
     tile("fx2", plane.summed(fx[1], turn.at[3]), plane.summed(fx[3], turn.at[4]))
-    tile("fy2", *[plane.odd_rows(fy[u, body] + fy[u + 1, body], turn.at[5 + u // 2]) for u in (0, 2)])
-    tile("fz2", *[plane.odd_lanes(fz[u] + fz[u + 1], turn.at[7 + u // 2]) for u in (0, 2)])
-    for u in range(3):
+    fy2 = [plane.odd_rows(fy[u, body] + fy[u + 1, body], turn.at[5 + u // 2]) for u in (0, 2)]
+    fz2 = [plane.odd_lanes(fz[u] + fz[u + 1], turn.at[7 + u // 2]) for u in (0, 2)]
+    own2[0], own2[1] = plane.packed(*fy2, core), plane.packed(*fz2, core)
+    tile("far2", fy2[1], fz2[1])
+    for u in range(2):
         message[places["coef%d" % u], :] = cell[u]
     first = s(0) + around(old, 0) + fx[0] * old[1, body]
     second = s(0) + fx[0] * even[1, body]
     message[places["known0"], :] = jnp.where(plane.even(0), first, second)
+    message[places["old0"], :] = odd_cells(iterate.at[own_layer(0, layers)], half, plane.odd_first(0))
     total = s(1) + around(even, 1) + fx[1] * even[2, body]
     known1[...] = total
-    turn[9] = total
-    message[places["known1"], :] = odd_cells(turn.at[9], half, plane.odd_first(1))
-    for u in range(2):
-        message[places["old%d" % u], :] = odd_cells(iterate.at[own_layer(u, layers)], half, plane.odd_first(u))
+    turn[9] = total * inv[0] - old[1, body]
+    message[places["moved1"], :] = odd_cells(turn.at[9], half, plane.odd_first(1))
+    message[places["face2"], :] = odd_cells(fx.at[1], half, plane.odd_first(1))
 
 
 def border_kernel(
-    owner_of, inputs, message, known1, new_in, fx_in, fy_in, fz_in, fzl_in, inv_in, across_in,
+    inputs, message, own2, known1, new_in, fx_in, fy_in, fz_in, fzl_in, inv_in, across_in,
     within, outer2, fx2_in, new, known, fx, fy, fz, fzl, inv,
     old, even, change, turn, face_y, face_z, face_zl,
 ):
@@ -277,7 +279,7 @@
     there = position - 1 + 2 * core
     border = jnp.where((there >= 0) & (there <= last), 0.5 * (mine("coef0") + theirs("coef0")), 0.0)
     face1 = 0.5 * (theirs("coef0") + theirs("coef1"))
-    face2 = 0.5 * (theirs("coef1") + theirs("coef2"))
+    face2 = opened("face2", 2)
     fx[0], fx[1] = border, face1
 
     def inverse(faces, fy, fz, fzl):
@@ -289,7 +291,7 @@
     inv_far = inverse(face1 + face2, face_y.at[1], face_z.at[1], face_zl.at[1])
     inv[0], inv[1] = inv_near, inv_own
     old_own, old_next = iterate[own_layer(0, layers)], iterate[own_layer(1, layers)]
-    old_near, old_far = opened("old0", 0), opened("old1", 1)
+    old_near, far = opened("old0", 0), opened("moved1", 1)
     even_own = (mine("known0") + border * old_near) * inv_own
     even_near = (theirs("known0") + border * old_own) * inv_near
     plane.put(even.at[0], even_near)
@@ -304,12 +306,11 @@
     odd_own = (mine("known0") + own(even.at[1], 0) + border * even_near) * inv_own
     odd_near = (theirs("known0") + near(even.at[0], 0) + border * even_own) * inv_near
     odd_next = (known1[...] + fx_in[0] * even_own) * inv_in[0]
-    odd_far = (opened("known1", 2) + face1 * even_near) * inv_far
+    far = far + face1 * even_near * inv_far
     new[0], new[1], new[2] = odd_near, odd_own, odd_next
-    moved = odd_far - old_far, odd_near - old_near, odd_own - old_own, odd_next - old_next
-    for k, values in enumerate(moved):
+    near_by, here, following = odd_near - old_near, odd_own - old_own, odd_next - old_next
+    for k, values in enumerate((far, near_by, here, following)):
         plane.put(change.at[k], values)
-    far, near_by, here, following = moved
     plane.put(old.at[0], old_near)
     known[...] = theirs("known0") + face1 * far - near(old.at[0], 0)
 
@@ -325,12 +326,17 @@
     sums = [plane.summed(values, turn.at[3 + k]) for k, values in enumerate((own_outer, own_inner, its_outer, its_inner))]
     within[0] = mine("source2") + plane.packed(sums[0], sums[1], core)
     outer2[0] = theirs("source2") + plane.packed(sums[2], sums[3], 1 - core)
-    for k, name in ((1, "fx2"), (2, "fy2"), (3, "fz2")):
-        outer2[k] = theirs(name)
+    outer2[1] = theirs("fx2")
+    far2 = theirs("far2")
+    far2_swap = jnp.where((plane.half_lane & 1) == 0, ahead(far2, 1, 1), behind(far2, 1, 1))
+    near_fy2 = plane.odd_rows(face_y[0, body] + face_y[1, body], turn.at[1])
+    near_fz2 = plane.odd_lanes(face_z[0] + face_z[1], turn.at[2])
+    outer2[2] = plane.packed(near_fy2, far2_swap, 1 - core)
+    outer2[3] = plane.packed(near_fz2, far2, 1 - core)
     fx2_in[...] = mine("fx2")
     middle = jnp.where((plane.half_lane & 1) == 0, ahead(mine("fx2"), 1, 1), behind(mine("fx2"), 1, 1))
     within[1] = plane.packed(plane.summed(border, turn.at[7]), middle, core)
-    within[2], within[3] = mine("fy2"), mine("fz2")
+    within[2], within[3] = own2[0], own2[1]
     turn[0] = source[own_layer(layers - 1, layers)] + fx_in[layers - 2] * new_in[layers - 4]
     within[4] = odd_cells(turn.at[0], half, jnp.logical_not(plane.odd_first(layers - 1)))
 
@@ -781,14 +787,14 @@
     )
     edge, = call(edge_kernel, [f32(3 * height + half, depth)], [], (inputs,))
     layer, tile, five = (height, depth), (half, depth), layers + 1
-    message, known1, *fine = call(
+    message, own2, known1, *fine = call(
         chip_kernel,
         [
-            f32(chip_rows(height)[1], depth), f32(*layer), f32(3, *layer), f32(five, *layer),
+            f32(chip_rows(height)[1], depth), f32(2, *tile), f32(*layer), f32(3, *layer), f32(five, *layer),
             f32(five, padded, depth), f32(five, *layer), f32(five, *layer), f32(layers, *layer),
         ],
         [vmem(five, *layer)] + [vmem(five, padded, depth)] * 3 + [vmem(10, *layer)],
-        (inputs, within_chip(edge)),
+        (block_owner, inputs, within_chip(edge)),
     )
     within, outer, fx2, *border = call(
         border_kernel,
@@ -800,7 +806,7 @@
             vmem(1, padded, depth), vmem(2, padded, depth), vmem(4, padded, depth), vmem(8, *layer),
             vmem(2, padded, depth), vmem(2, *layer), vmem(2, *layer),
         ],
-        (block_owner, inputs, message, known1, *fine, between_chips(message)),
+        (inputs, message, own2, known1, *fine, between_chips(message)),
     )
     within_in = within_chip(within)
     plain = f32(3, *tile)

time: 35.4 us -> 33.7 us (0.952)
  starting transfers between devices: 11.2 us -> 10.1 us
  local copies, waits for them, and re-layouts: 0.65 us -> 0.01 us
    ppermute x3, starting transfers between devices: 10.5 us -> 9.47 us  [within_chip(): lax.ppermute(block, 'gx', [(i, i ^ 1) for i in range(lax.axis_size('gx'))])]
    unnamed x2, local copies, waits for them, and re-layouts: 0.65 us -> 0.01 us
where the time goes in v11:
time: 33.7 us; the launch traced here: 33.5 us
  blocking collectives  13.2 us (39%)
  starting transfers between devices  10.1 us (30%)
  Pallas kernels  5.17 us (15%)
  waiting for transfers between devices  3.24 us (10%)
  other arithmetic  1.06 us (3%)
  between operations  0.67 us (2%)
    all_to_all x1, blocking collectives, on_device(): lax.all_to_all(slots, 'gx', 0, 0, axis_index_groups=kinds, tiled=True)  13.2 us
    ppermute x3, starting transfers between devices, within_chip(): lax.ppermute(block, 'gx', [(i, i ^ 1) for i in range(lax.axis_size('gx'))])  9.47 us
    pallas_call x5, Pallas kernels, call(): pl.pallas_call(kernel, out_shape=tuple(outs), in_specs=[pl.BlockSpec(memo...  5.17 us
    ppermute x3, waiting for transfers between devices, within_chip(): lax.ppermute(block, 'gx', [(i, i ^ 1) for i in range(lax.axis_size('gx'))])  3.23 us
    add x1, other arithmetic, on_device(): sum((jnp.pad(block, ((k * layers, (2 - k) * layers), (0, 0), (0, 0))) for...  1.06 us
  transfers between devices with their start and end apart: 4, of which 3 were waited for; matrix products, arithmetic and copies ran while one was open for 0% of the time, Pallas kernels for 0%

profile of v11, /device:TPU:0, one launch (start us, length us, event | category | flops | bytes accessed | tf_op | source)
XLA Modules:
  0.0 33.5 jit_solution(17497586172865433255)
XLA Ops:
  0.6 1.1 %pad_add_fusion.inputs = f32[12,64,128]{2,1,0:T(8,128)S(1)} fusion(f32[4,64,128]{2,1,0:T(8,128)} %param.6, f32[4,64,128]{2,1,0:T(8,128)} %param.5, f32[4,64,128]{2,1,0:T(8,128)} %param.4), kind=kLoop, calls=%fused_computation | loop fusion | flops 196608 | bytes 786432 | tf_op jit(solution)/shard_map/add | solution.py:784
  1.7 0.0 copy-start
  1.7 0.2 shard_map.59
  1.9 0.5 %collective-permute-start = (f32[224,128]{1,0:T(8,128)S(1)}, f32[224,128]{1,0:T(8,128)S(1)}, u32[]{:S(2)}, u32[]{:S(2)}) collective-permute-start(f32[224,128]{1,0:T(8,128)S(1)} %shard_map.59), channel_id=1, source_target_pairs={{0,1},{1,0},{2,3},{3,2},{4,5},{5,4},{6,7},{7,6},{8,9},{9,8},{10,11... | collective-permute-start | bytes 344072 | tf_op jit(solution)/shard_map/ppermute | solution.py:19
  2.4 1.0 %collective-permute-done.within_in = f32[224,128]{1,0:T(8,128)S(1)} collective-permute-done((f32[224,128]{1,0:T(8,128)S(1)}, f32[224,128]{1,0:T(8,128)S(1)}, u32[]{:S(2)}, u32[]{:S(2)}) %collective-permute-start) | collective-permute-done | bytes 114720 | tf_op jit(solution)/shard_map/ppermute | solution.py:19
  3.4 0.0 copy-done
  3.4 0.6 %shard_map.60 = (f32[384,128]{1,0:T(8,128)S(1)}, f32[2,32,128]{2,1,0:T(8,128)S(1)}, f32[64,128]{1,0:T(8,128)S(1)}, f32[3,64,128]{2,1,0:T(8,128)S(1)}, f32[5,64,1...) custom-call(s32[16]{0:T(128)S(1)} %copy-done, ...), custom_call_target="tpu_custom_call" | custom-call | tf_op jit(solution)/shard_map/pallas_call | solution.py:769
  4.0 0.7 %collective-permute-start.1 = (f32[384,128]{1,0:T(8,128)S(1)}, f32[384,128]{1,0:T(8,128)S(1)}, u32[]{:S(2)}, u32[]{:S(2)}) collective-permute-start(f32[384,128]{1,0:T(8,128)S(1)} %get-tuple-element.30.message), channel_id=1, source_target_pairs={{1,2},{2,1},{3,4},{4,3},{5,6},{6,5},{7,8},{8,7},{9,10},{10,9},{11,... | collective-permute-start | bytes 589832 | tf_op jit(solution)/shard_map/ppermute | solution.py:15
  4.7 0.0 collective-permute-done.1.across_in
  4.7 0.5 %shard_map.61 = (f32[5,32,128]{2,1,0:T(8,128)S(1)}, f32[4,32,128]{2,1,0:T(8,128)S(1)}, f32[32,128]{1,0:T(8,128)S(1)}, f32[3,64,128]{2,1,0:T(8,128)S(1)}, f32[64,...) custom-call(f32[12,64,128]{2,1,0:T(8,128)S(1)} %pad_add_fusion.input, ...), custom_call_target="tpu_custom_call" | custom-call | tf_op jit(solution)/shard_map/pallas_call | solution.py:769
  5.2 8.9 %collective-permute-start.2 = (f32[5,32,128]{2,1,0:T(8,128)S(1)}, f32[5,32,128]{2,1,0:T(8,128)S(1)}, u32[]{:S(2)}, u32[]{:S(2)}) collective-permute-start(f32[5,32,128]{2,1,0:T(8,128)S(1)} %get-tuple-element.39.own), channel_id=1, source_target_pairs={{0,1},{1,0},{2,3},{3,2},{4,5},{5,4},{6,7},{7,6},{8,9},{9,8},{10,11... | collective-permute-start | bytes 245768 | tf_op jit(solution)/shard_map/ppermute | solution.py:19
  14.1 0.9 %collective-permute-done.2.within_in = f32[5,32,128]{2,1,0:T(8,128)S(1)} collective-permute-done((f32[5,32,128]{2,1,0:T(8,128)S(1)}, f32[5,32,128]{2,1,0:T(8,128)S(1)}, u32[]{:S(2)}, u32[]{:S(2)}) %collective-permute-start.2) | collective-permute-done | bytes 81952 | tf_op jit(solution)/shard_map/ppermute | solution.py:19
  15.0 0.5 %shard_map.62 = (f32[8,2,16,128]{3,2,1,0:T(8,128)S(1)}, f32[3,32,128]{2,1,0:T(8,128)S(1)}, f32[3,32,128]{2,1,0:T(8,128)S(1)}, f32[3,32,128]{2,1,0:T(8,128)S(1)},...) custom-call(f32[5,32,128]{2,1,0:T(8,128)S(1)} %get-tuple-element.39., ...), custom_call_target="tpu_custom_call" | custom-call | tf_op jit(solution)/shard_map/pallas_call | solution.py:769
  15.5 13.2 %all_to_all.5.same_cores = f32[8,2,16,128]{3,2,1,0:T(8,128)S(1)} all-to-all(f32[8,2,16,128]{3,2,1,0:T(8,128)S(1)} %get-tuple-element.42), channel_id=1, replica_groups={{0,2,4,6,8,10,12,14},{1,3,5,7,9,11,13,15},{16,18,20,22,24,26,28,30},{17..., dimensions={0} | all-to-all | bytes 262144 | tf_op jit(solution)/shard_map/all_to_all | solution.py:820
  28.7 0.0 collective-permute-start.3
  28.7 1.3 %collective-permute-done.3.other_cores = f32[8,2,16,128]{3,2,1,0:T(8,128)S(1)} collective-permute-done((f32[8,2,16,128]{3,2,1,0:T(8,128)S(1)}, f32[8,2,16,128]{3,2,1,0:T(8,128)S(1)}, u32[]{:S(2)}, u32[]{:S(2)}) %collective-permute-start.3) | collective-permute-done | bytes 131104 | tf_op jit(solution)/shard_map/ppermute | solution.py:19
  30.1 3.4 %shard_map.63 = (f32[4,64,128]{2,1,0:T(8,128)}, f32[1,16,32]{2,1,0:T(8,128)}) custom-call(s32[16]{0:T(128)S(1)} %copy-done, f32[8,2,16,128]{3,2,1,0:T(8,128)S(1)} %all_to_all.5.same_cores, f32[8,2,16,128]{3,2,1,0:T(8,128)S(1)} %collective-permute-done.3.other_cores, f32[3,32,128]{2,1,0:T(8,128)S(1)} %get-tuple-element.43.e2_in, ...), custom_call_target="tpu_custom_call" | custom-call | tf_op jit(solution)/shard_map/pallas_call | solution.py:769
Async XLA Ops:
  1.7 1.7 %copy-start = (s32[16]{0:T(128)S(1)}, s32[16]{0:T(128)}, u32[]{:S(2)}) copy-start(s32[16]{0:T(128)} %owner_of.3) | copy-start | bytes 196
  1.9 1.5 %collective-permute-start = (f32[224,128]{1,0:T(8,128)S(1)}, f32[224,128]{1,0:T(8,128)S(1)}, u32[]{:S(2)}, u32[]{:S(2)}) collective-permute-start(f32[224,128]{1,0:T(8,128)S(1)} %shard_map.59), channel_id=1, source_target_pairs={{0,1},{1,0},{2,3},{3,2},{4,5},{5,4},{6,7},{7,6},{8,9},{9,8},{10,11... | collective-permute-start | bytes 344072 | tf_op jit(solution)/shard_map/ppermute | solution.py:19
  4.0 0.7 %collective-permute-start.1 = (f32[384,128]{1,0:T(8,128)S(1)}, f32[384,128]{1,0:T(8,128)S(1)}, u32[]{:S(2)}, u32[]{:S(2)}) collective-permute-start(f32[384,128]{1,0:T(8,128)S(1)} %get-tuple-element.30.message), channel_id=1, source_target_pairs={{1,2},{2,1},{3,4},{4,3},{5,6},{6,5},{7,8},{8,7},{9,10},{10,9},{11,... | collective-permute-start | bytes 589832 | tf_op jit(solution)/shard_map/ppermute | solution.py:15
  5.2 9.9 %collective-permute-start.2 = (f32[5,32,128]{2,1,0:T(8,128)S(1)}, f32[5,32,128]{2,1,0:T(8,128)S(1)}, u32[]{:S(2)}, u32[]{:S(2)}) collective-permute-start(f32[5,32,128]{2,1,0:T(8,128)S(1)} %get-tuple-element.39.own), channel_id=1, source_target_pairs={{0,1},{1,0},{2,3},{3,2},{4,5},{5,4},{6,7},{7,6},{8,9},{9,8},{10,11... | collective-permute-start | bytes 245768 | tf_op jit(solution)/shard_map/ppermute | solution.py:19
  28.7 1.3 %collective-permute-start.3 = (f32[8,2,16,128]{3,2,1,0:T(8,128)S(1)}, f32[8,2,16,128]{3,2,1,0:T(8,128)S(1)}, u32[]{:S(2)}, u32[]{:S(2)}) collective-permute-start(f32[8,2,16,128]{3,2,1,0:T(8,128)S(1)} %all_to_all.5.same_cores), channel_id=1, source_target_pairs={{0,1},{1,0},{2,3},{3,2},{4,5},{5,4},{6,7},{7,6},{8,9},{9,8},{10,11... | collective-permute-start | bytes 393224 | tf_op jit(solution)/shard_map/ppermute | solution.py:19

commit v12 on v11

--- a/solution.py
+++ b/solution.py
@@ -166,10 +166,35 @@
     return places, at
 
 
+def own_kernel(owner_of, inputs, cell, old, fx, fy, fz, fzl, inv, even):
+    iterate, source, phase = three_parts(inputs)
+    layers, height, depth = iterate.shape
+    plane = Plane(height, depth)
+    body = plane.body
+    for u in range(layers):
+        cell[u] = cell_coef(phase[own_layer(u, layers)])
+        plane.put(old.at[u], iterate[own_layer(u, layers)])
+    for u in range(layers):
+        here = cell[u]
+        if u < layers - 1:
+            fx[u] = 0.5 * (here + cell[u + 1])
+        plane.put(fy.at[u], plane.face_y(here))
+        face = plane.face_z(here)
+        fz[u] = face
+        fzl[u] = behind(face, 1, 1)
+    for u in (1, 2):
+        weight = (fx[u] + fx[u - 1]) + (fy[u, body] + fy[u, plane.down]) + (fz[u] + fzl[u])
+        inverse = 1.0 / (1.0 + weight)
+        inv[u - 1] = inverse
+        around = in_layer(plane, fy.at[u], fz.at[u], fzl.at[u], old.at[u])
+        total = source[own_layer(u, layers)] + around + (fx[u] * old[u + 1, body] + fx[u - 1] * old[u - 1, body])
+        plane.put(even.at[u - 1], total * inverse)
+
+
 def chip_kernel(
-    owner_of, inputs, within_in,
-    message, own2, known1, new, fx, fy, fz, fzl, inv,
-    cell, old, even, change, turn,
+    inputs, cell, old_own, fx_own, fy_own, fz_own, fzl_own, inv_own, even_own, within_in,
+    message, own2, known1, new, fx_more, fy_margin, fz_margin, fzl_margin, inv_more,
+    old_margin, even_more, change, turn,
 ):
     iterate, source, phase = three_parts(inputs)
     layers, height, depth = iterate.shape
@@ -184,42 +209,45 @@
     def s(u):
         return source[own_layer(u, layers)]
 
-    for u in range(layers):
-        cell[u] = cell_coef(phase[own_layer(u, layers)])
-        plane.put(old.at[u], iterate[own_layer(u, layers)])
-    cell[margin] = part(0)
     into_both_rows(turn.at[0], within_in[3 * height:])
-    plane.put(old.at[margin], turn[0])
-    for u in range(margin + 1):
-        here = cell[u]
-        fx[u] = 0.5 * (here + (cell[u + 1] if u < margin else part(1)))
-        plane.put(fy.at[u], plane.face_y(here))
-        face = plane.face_z(here)
-        fz[u] = face
-        fzl[u] = behind(face, 1, 1)
-    for u in range(1, margin + 1):
-        weight = (fx[u] + fx[u - 1]) + (fy[u, body] + fy[u, plane.down]) + (fz[u] + fzl[u])
-        inv[u - 1] = 1.0 / (1.0 + weight)
+    plane.put(old_margin, turn[0])
+    fx_more[0] = 0.5 * (cell[layers - 1] + part(0))
+    fx_more[1] = 0.5 * (part(0) + part(1))
+    plane.put(fy_margin, plane.face_y(part(0)))
+    face = plane.face_z(part(0))
+    fz_margin[...] = face
+    fzl_margin[...] = behind(face, 1, 1)
+    fx = [fx_own.at[u] for u in range(3)] + [fx_more.at[0], fx_more.at[1]]
+    fy = [fy_own.at[u] for u in range(layers)] + [fy_margin]
+    fz = [fz_own.at[u] for u in range(layers)] + [fz_margin]
+    fzl = [fzl_own.at[u] for u in range(layers)] + [fzl_margin]
+    old = [old_own.at[u] for u in range(layers)] + [old_margin]
+    inv = [None, inv_own.at[0], inv_own.at[1], inv_more.at[0], inv_more.at[1]]
+    even = [None, even_own.at[0], even_own.at[1], even_more.at[0], even_more.at[1]]
+    for u in (margin - 1, margin):
+        weight = (fx[u][...] + fx[u - 1][...]) + (fy[u][body] + fy[u][plane.down]) + (fz[u][...] + fzl[u][...])
+        inv[u][...] = 1.0 / (1.0 + weight)
 
     def around(ref, u):
-        return in_layer(plane, fy.at[u], fz.at[u], fzl.at[u], ref.at[u])
-
-    for u in range(1, margin):
-        total = s(u) + around(old, u) + (fx[u] * old[u + 1, body] + fx[u - 1] * old[u - 1, body])
-        plane.put(even.at[u], total * inv[u - 1])
-    plane.put(even.at[margin], (part(2) + fx[margin - 1] * old[margin - 1, body]) * inv[margin - 1])
+        return in_layer(plane, fy[u], fz[u], fzl[u], ref[u])
+
+    u = margin - 1
+    total = s(u) + around(old, u) + (fx[u][...] * old[u + 1][body] + fx[u - 1][...] * old[u - 1][body])
+    plane.put(even[u], total * inv[u][...])
+    plane.put(even[margin], (part(2) + fx[u][...] * old[u][body]) * inv[margin][...])
     for u in range(2, margin + 1):
         if u < margin:
-            total = s(u) + around(even, u) + (fx[u] * even[u + 1, body] + fx[u - 1] * even[u - 1, body])
+            total = s(u) + around(even, u) + (fx[u][...] * even[u + 1][body] + fx[u - 1][...] * even[u - 1][body])
         else:
-            total = part(2) + around(even, u) + fx[u - 1] * even[u - 1, body]
-        fresh = total * inv[u - 1]
+            total = part(2) + around(even, u) + fx[u - 1][...] * even[u - 1][body]
+        fresh = total * inv[u][...]
         new[u - 2] = fresh
-        plane.put(change.at[u], fresh - old[u, body])
-
-    one = fx[1] * change[2, body]
-    two = around(change, 2) + fx[2] * change[3, body]
-    three = around(change, 3) + (fx[2] * change[2, body] + fx[3] * change[4, body])
+        plane.put(change.at[u - 2], fresh - old[u][body])
+    change = {u: change.at[u - 2] for u in range(2, margin + 1)}
+
+    one = fx[1][...] * change[2][body]
+    two = around(change, 2) + fx[2][...] * change[3][body]
+    three = around(change, 3) + (fx[2][...] * change[2][body] + fx[3][...] * change[4][body])
     outer = jnp.where(plane.even(1), one, 0.0)
     inner = jnp.where(plane.even(2), two, 0.0) + jnp.where(plane.even(3), three, 0.0)
     core = core_of()
@@ -228,22 +256,22 @@
         message[places[name], :] = plane.packed(outer, inner, core)
 
     tile("source2", plane.summed(outer, turn.at[1]), plane.summed(inner, turn.at[2]))
-    tile("fx2", plane.summed(fx[1], turn.at[3]), plane.summed(fx[3], turn.at[4]))
-    fy2 = [plane.odd_rows(fy[u, body] + fy[u + 1, body], turn.at[5 + u // 2]) for u in (0, 2)]
-    fz2 = [plane.odd_lanes(fz[u] + fz[u + 1], turn.at[7 + u // 2]) for u in (0, 2)]
+    tile("fx2", plane.summed(fx[1][...], turn.at[3]), plane.summed(fx[3][...], turn.at[4]))
+    fy2 = [plane.odd_rows(fy[u][body] + fy[u + 1][body], turn.at[5 + u // 2]) for u in (0, 2)]
+    fz2 = [plane.odd_lanes(fz[u][...] + fz[u + 1][...], turn.at[7 + u // 2]) for u in (0, 2)]
     own2[0], own2[1] = plane.packed(*fy2, core), plane.packed(*fz2, core)
     tile("far2", fy2[1], fz2[1])
     for u in range(2):
         message[places["coef%d" % u], :] = cell[u]
-    first = s(0) + around(old, 0) + fx[0] * old[1, body]
-    second = s(0) + fx[0] * even[1, body]
+    first = s(0) + around(old, 0) + fx[0][...] * old[1][body]
+    second = s(0) + fx[0][...] * even[1][body]
     message[places["known0"], :] = jnp.where(plane.even(0), first, second)
     message[places["old0"], :] = odd_cells(iterate.at[own_layer(0, layers)], half, plane.odd_first(0))
-    total = s(1) + around(even, 1) + fx[1] * even[2, body]
+    total = s(1) + around(even, 1) + fx[1][...] * even[2][body]
     known1[...] = total
-    turn[9] = total * inv[0] - old[1, body]
+    turn[9] = total * inv[1][...] - old[1][body]
     message[places["moved1"], :] = odd_cells(turn.at[9], half, plane.odd_first(1))
-    message[places["face2"], :] = odd_cells(fx.at[1], half, plane.odd_first(1))
+    message[places["face2"], :] = odd_cells(fx[1], half, plane.odd_first(1))
 
 
 def border_kernel(
@@ -424,7 +452,10 @@
     fx = group(jnp.where(odd_layer, even_row_sum(fx2.at[1], quarter), 0.0))
     fy = group(fy2[1, pl.ds(PAD + 1, quarter, 2), :])
     fz = group(jnp.where(odd_depth, even_row_sum(fz2.at[1], quarter), 0.0))
-    tile = jnp.where(item == 0, source, jnp.where(item == 1, fx, jnp.where(item == 2, fy, fz)))
+    fxl = group(jnp.where(odd_layer, 0.0, even_row_sum(fxl2.at[1], quarter)))
+    weight = (fx + fxl) + (fy + behind(fy, 1, 0)) + (fz + behind(fz, 4, 1))
+    start = source / (64.0 + weight)
+    tile = jnp.where(item == 0, start, jnp.where(item == 1, fx, jnp.where(item == 2, fy, fz)))
     first = (((lane & 1) + (lane >> 1)) & 1) != 0
     pair[0] = jnp.where(first_of_two, fresh[2], fresh[1])
     pair[1] = jnp.where(first_of_two, fresh[1], fresh[0])
@@ -468,11 +499,14 @@
         total = (self.fx * self.upper(e) + self.fxl * self.lower(e)) + (self.fy * above + self.fyl * below)
         return total + (self.fz * ahead(e, self.lane_step, 2) + self.fzl * behind(e, self.lane_step, 2))
 
+    def start(self):
+        return self.source * self.inv
+
     def update(self, e):
-        return (self.source + self.neigh(e)) * self.inv
+        return self.start() + self.neigh(e) * self.inv
 
     def cycle(self, deeper):
-        odd = self.update(self.source * self.inv)
+        odd = self.update(self.start())
         residual = jnp.where(self.even, self.neigh(odd), 0.0)
         fix = deeper(self.restricted(residual), self.coarse_faces())
         even = self.update(odd + self.prolonged(fix))
@@ -519,6 +553,9 @@
         self.scratch, self.used = scratch, 0
         self.rows = source.shape[1]
         super().__init__(mass, source, faces, 1, 4, 1)
+
+    def start(self):
+        return self.source
 
     def place(self):
         self.used += 1
@@ -626,7 +663,7 @@
 
 def coarse_kernel(
     owner_of, same_cores, other_cores, e2_in, s2, fx2, fxl2, fy2, fz2, fzl2, inv2,
-    inputs, new_in, fx_in, fy_in, fz_in, fzl_in, inv_in,
+    inputs, new_in, fx_more, fy_margin, fz_margin, fzl_margin, inv_more, fx_in, fy_in, fz_in, fzl_in, inv_in,
     new_out, known_out, fx_out, fy_out, fz_out, fzl_out, inv_out, within_in,
     solved_out, owned_out,
     e3, rows3, pair, e2, e1, cor, solved, owned, owner_here, fetch_sem, sems,
@@ -683,7 +720,12 @@
     )
     for k in range(5):
         j = jnp.clip(position + k - 2, 0, last)
-        into_both_rows(pair.at[k], group(jnp.where(slot == j // spread, e3[j % spread], 0.0)))
+        here = e3[j % spread]
+        turned = [pltpu.roll(here, (at - j // spread) % lanes, 1) for at in range(4)]
+        value = turned[3]
+        for at in range(3):
+            value = jnp.where(slot == at, turned[at], value)
+        into_both_rows(pair.at[k], value)
         e2[k, :PAD] = edge
         e2[k, PAD + half:] = edge
         e2[k, body2] = before[k] + pair[k]
@@ -719,14 +761,20 @@
         plane.put(e1.at[u + 1], before + fixes[(u + 2) // 2])
 
     def fx1(u):
-        return fx_in[u] if u >= 0 else fx_out[-1 - u]
+        if u < 0:
+            return fx_out[-1 - u]
+        return fx_in[u] if u < layers - 1 else fx_more[u - layers + 1]
 
     def inv1(u):
-        return inv_in[u - 1] if u > 0 else inv_out[u + 1]
+        if u <= 0:
+            return inv_out[u + 1]
+        return inv_in[u - 1] if u < layers - 1 else inv_more[u - layers + 1]
 
     def around1(u):
         if u < 0:
             return in_layer(plane, fy_out, fz_out, fzl_out, e1.at[0])
+        if u == layers:
+            return in_layer(plane, fy_margin, fz_margin, fzl_margin, e1.at[u + 1])
         return in_layer(plane, fy_in.at[u], fz_in.at[u], fzl_in.at[u], e1.at[u + 1])
 
     def updated1(u):
@@ -786,15 +834,24 @@
         for k, block in enumerate((iterate, source, phase_field))
     )
     edge, = call(edge_kernel, [f32(3 * height + half, depth)], [], (inputs,))
-    layer, tile, five = (height, depth), (half, depth), layers + 1
-    message, own2, known1, *fine = call(
+    edge_in = within_chip(edge)
+    layer, tile, tall = (height, depth), (half, depth), (padded, depth)
+    cell, old, *fine, even = call(
+        own_kernel,
+        [
+            f32(layers, *layer), f32(layers, *tall), f32(layers - 1, *layer), f32(layers, *tall),
+            f32(layers, *layer), f32(layers, *layer), f32(2, *layer), f32(2, *tall),
+        ],
+        [], (block_owner, inputs),
+    )
+    message, own2, known1, new, *margin = call(
         chip_kernel,
         [
-            f32(chip_rows(height)[1], depth), f32(2, *tile), f32(*layer), f32(3, *layer), f32(five, *layer),
-            f32(five, padded, depth), f32(five, *layer), f32(five, *layer), f32(layers, *layer),
+            f32(chip_rows(height)[1], depth), f32(2, *tile), f32(*layer), f32(3, *layer),
+            f32(2, *layer), f32(*tall), f32(*layer), f32(*layer), f32(2, *layer),
         ],
-        [vmem(five, *layer)] + [vmem(five, padded, depth)] * 3 + [vmem(10, *layer)],
-        (block_owner, inputs, within_chip(edge)),
+        [vmem(*tall), vmem(2, *tall), vmem(3, *tall), vmem(10, *layer)],
+        (inputs, cell, old, *fine, even, edge_in),
     )
     within, outer, fx2, *border = call(
         border_kernel,
@@ -806,7 +863,7 @@
             vmem(1, padded, depth), vmem(2, padded, depth), vmem(4, padded, depth), vmem(8, *layer),
             vmem(2, padded, depth), vmem(2, *layer), vmem(2, *layer),
         ],
-        (inputs, message, own2, known1, *fine, between_chips(message)),
+        (inputs, message, own2, known1, new, *fine, between_chips(message)),
     )
     within_in = within_chip(within)
     plain = f32(3, *tile)
@@ -828,7 +885,7 @@
             vmem(1, quarter, depth // 4), pltpu.SMEM((blocks,), jnp.int32),
             pltpu.SemaphoreType.DMA, pltpu.SemaphoreType.DMA((layers + 1,)),
         ],
-        (block_owner, same_cores, other_cores, *middle, inputs, *fine, *border, within_in),
+        (block_owner, same_cores, other_cores, *middle, inputs, new, *margin, *fine, *border, within_in),
         pl.ANY,
     )
     return solved, owned

time: 33.7 us -> 33.7 us (level)
    pallas_call x5 -> x6, Pallas kernels: 5.17 us -> 5.36 us  [call(): pl.pallas_call(kernel, out_shape=tuple(outs), in_specs=[pl.BlockSpec(memo...]
  transfers between devices with their start and end apart: 4 -> 4, of which waited for: 3 -> 3; matrix products, arithmetic and copies ran while one was open for 0% -> 0% of each run, Pallas kernels for 0% -> 1%
where the time goes in v12:
time: 33.7 us; the launch traced here: 33.5 us
  blocking collectives  13.2 us (39%)
  starting transfers between devices  10.1 us (30%)
  Pallas kernels  5.36 us (16%)
  waiting for transfers between devices  3.04 us (9%)
  other arithmetic  1.06 us (3%)
  between operations  0.68 us (2%)
    all_to_all x1, blocking collectives, on_device(): lax.all_to_all(slots, 'gx', 0, 0, axis_index_groups=kinds, tiled=True)  13.2 us
    ppermute x3, starting transfers between devices, within_chip(): lax.ppermute(block, 'gx', [(i, i ^ 1) for i in range(lax.axis_size('gx'))])  9.47 us
    pallas_call x6, Pallas kernels, call(): pl.pallas_call(kernel, out_shape=tuple(outs), in_specs=[pl.BlockSpec(memo...  5.36 us
    ppermute x3, waiting for transfers between devices, within_chip(): lax.ppermute(block, 'gx', [(i, i ^ 1) for i in range(lax.axis_size('gx'))])  3.04 us
    add x1, other arithmetic, on_device(): sum((jnp.pad(block, ((k * layers, (2 - k) * layers), (0, 0), (0, 0))) for...  1.06 us
    ppermute x1, starting transfers between devices, between_chips(): lax.ppermute(block, 'gx', [(i, i + 1 if i % 2 else i - 1) for i in range(...  0.68 us
  transfers between devices with their start and end apart: 4, of which 3 were waited for; matrix products, arithmetic and copies ran while one was open for 0% of the time, Pallas kernels for 1%

profile of v12, /device:TPU:0, one launch (start us, length us, event | category | flops | bytes accessed | tf_op | source)
XLA Modules:
  0.0 33.5 jit_solution(3853446530189321514)
XLA Ops:
  0.6 1.1 %pad_add_fusion.inputs = f32[12,64,128]{2,1,0:T(8,128)S(1)} fusion(f32[4,64,128]{2,1,0:T(8,128)} %param.6, f32[4,64,128]{2,1,0:T(8,128)} %param.5, f32[4,64,128]{2,1,0:T(8,128)} %param.4), kind=kLoop, calls=%fused_computation | loop fusion | flops 196608 | bytes 786432 | tf_op jit(solution)/shard_map/add | solution.py:832
  1.7 0.0 copy-start
  1.7 0.2 shard_map.60
  1.9 0.5 %collective-permute-start = (f32[224,128]{1,0:T(8,128)S(1)}, f32[224,128]{1,0:T(8,128)S(1)}, u32[]{:S(2)}, u32[]{:S(2)}) collective-permute-start(f32[224,128]{1,0:T(8,128)S(1)} %shard_map.60), channel_id=1, source_target_pairs={{0,1},{1,0},{2,3},{3,2},{4,5},{5,4},{6,7},{7,6},{8,9},{9,8},{10,11... | collective-permute-start | bytes 344072 | tf_op jit(solution)/shard_map/ppermute | solution.py:19
  2.4 0.0 copy-done
  2.4 0.2 shard_map.59
  2.6 0.8 %collective-permute-done.within_in = f32[224,128]{1,0:T(8,128)S(1)} collective-permute-done((f32[224,128]{1,0:T(8,128)S(1)}, f32[224,128]{1,0:T(8,128)S(1)}, u32[]{:S(2)}, u32[]{:S(2)}) %collective-permute-start) | collective-permute-done | bytes 114720 | tf_op jit(solution)/shard_map/ppermute | solution.py:19
  3.4 0.4 %shard_map.61 = (f32[384,128]{1,0:T(8,128)S(1)}, f32[2,32,128]{2,1,0:T(8,128)S(1)}, f32[64,128]{1,0:T(8,128)S(1)}, f32[3,64,128]{2,1,0:T(8,128)S(1)}, f32[2,64,1...) custom-call(f32[12,64,128]{2,1,0:T(8,128)S(1)} %pad_add_fusion.input, ...), custom_call_target="tpu_custom_call" | custom-call | tf_op jit(solution)/shard_map/pallas_call | solution.py:817
  3.8 0.7 %collective-permute-start.1 = (f32[384,128]{1,0:T(8,128)S(1)}, f32[384,128]{1,0:T(8,128)S(1)}, u32[]{:S(2)}, u32[]{:S(2)}) collective-permute-start(f32[384,128]{1,0:T(8,128)S(1)} %get-tuple-element.46.message), channel_id=1, source_target_pairs={{1,2},{2,1},{3,4},{4,3},{5,6},{6,5},{7,8},{8,7},{9,10},{10,9},{11,... | collective-permute-start | bytes 589832 | tf_op jit(solution)/shard_map/ppermute | solution.py:15
  4.5 0.0 collective-permute-done.1.across_in
  4.5 0.5 %shard_map.62 = (f32[5,32,128]{2,1,0:T(8,128)S(1)}, f32[4,32,128]{2,1,0:T(8,128)S(1)}, f32[32,128]{1,0:T(8,128)S(1)}, f32[3,64,128]{2,1,0:T(8,128)S(1)}, f32[64,...) custom-call(f32[12,64,128]{2,1,0:T(8,128)S(1)} %pad_add_fusion.input, ...), custom_call_target="tpu_custom_call" | custom-call | tf_op jit(solution)/shard_map/pallas_call | solution.py:817
  5.0 8.9 %collective-permute-start.2 = (f32[5,32,128]{2,1,0:T(8,128)S(1)}, f32[5,32,128]{2,1,0:T(8,128)S(1)}, u32[]{:S(2)}, u32[]{:S(2)}) collective-permute-start(f32[5,32,128]{2,1,0:T(8,128)S(1)} %get-tuple-element.50.own), channel_id=1, source_target_pairs={{0,1},{1,0},{2,3},{3,2},{4,5},{5,4},{6,7},{7,6},{8,9},{9,8},{10,11... | collective-permute-start | bytes 245768 | tf_op jit(solution)/shard_map/ppermute | solution.py:19
  13.9 0.9 %collective-permute-done.2.within_in = f32[5,32,128]{2,1,0:T(8,128)S(1)} collective-permute-done((f32[5,32,128]{2,1,0:T(8,128)S(1)}, f32[5,32,128]{2,1,0:T(8,128)S(1)}, u32[]{:S(2)}, u32[]{:S(2)}) %collective-permute-start.2) | collective-permute-done | bytes 81952 | tf_op jit(solution)/shard_map/ppermute | solution.py:19
  14.8 0.5 %shard_map.63 = (f32[8,2,16,128]{3,2,1,0:T(8,128)S(1)}, f32[3,32,128]{2,1,0:T(8,128)S(1)}, f32[3,32,128]{2,1,0:T(8,128)S(1)}, f32[3,32,128]{2,1,0:T(8,128)S(1)},...) custom-call(f32[5,32,128]{2,1,0:T(8,128)S(1)} %get-tuple-element.50., ...), custom_call_target="tpu_custom_call" | custom-call | tf_op jit(solution)/shard_map/pallas_call | solution.py:817
  15.3 13.2 %all_to_all.5.same_cores = f32[8,2,16,128]{3,2,1,0:T(8,128)S(1)} all-to-all(f32[8,2,16,128]{3,2,1,0:T(8,128)S(1)} %get-tuple-element.53), channel_id=1, replica_groups={{0,2,4,6,8,10,12,14},{1,3,5,7,9,11,13,15},{16,18,20,22,24,26,28,30},{17..., dimensions={0} | all-to-all | bytes 262144 | tf_op jit(solution)/shard_map/all_to_all | solution.py:877
  28.5 0.0 collective-permute-start.3
  28.5 1.3 %collective-permute-done.3.other_cores = f32[8,2,16,128]{3,2,1,0:T(8,128)S(1)} collective-permute-done((f32[8,2,16,128]{3,2,1,0:T(8,128)S(1)}, f32[8,2,16,128]{3,2,1,0:T(8,128)S(1)}, u32[]{:S(2)}, u32[]{:S(2)}) %collective-permute-start.3) | collective-permute-done | bytes 131104 | tf_op jit(solution)/shard_map/ppermute | solution.py:19
  29.9 3.6 %shard_map.64 = (f32[4,64,128]{2,1,0:T(8,128)}, f32[1,16,32]{2,1,0:T(8,128)}) custom-call(s32[16]{0:T(128)S(1)} %copy-done, f32[8,2,16,128]{3,2,1,0:T(8,128)S(1)} %all_to_all.5.same_cores, f32[8,2,16,128]{3,2,1,0:T(8,128)S(1)} %collective-permute-done.3.other_cores, f32[3,32,128]{2,1,0:T(8,128)S(1)} %get-tuple-element.54.e2_in, ...), custom_call_target="tpu_custom_call" | custom-call | tf_op jit(solution)/shard_map/pallas_call | solution.py:817
Async XLA Ops:
  1.7 0.7 %copy-start = (s32[16]{0:T(128)S(1)}, s32[16]{0:T(128)}, u32[]{:S(2)}) copy-start(s32[16]{0:T(128)} %owner_of.3) | copy-start | bytes 196
  1.9 1.5 %collective-permute-start = (f32[224,128]{1,0:T(8,128)S(1)}, f32[224,128]{1,0:T(8,128)S(1)}, u32[]{:S(2)}, u32[]{:S(2)}) collective-permute-start(f32[224,128]{1,0:T(8,128)S(1)} %shard_map.60), channel_id=1, source_target_pairs={{0,1},{1,0},{2,3},{3,2},{4,5},{5,4},{6,7},{7,6},{8,9},{9,8},{10,11... | collective-permute-start | bytes 344072 | tf_op jit(solution)/shard_map/ppermute | solution.py:19
  3.8 0.7 %collective-permute-start.1 = (f32[384,128]{1,0:T(8,128)S(1)}, f32[384,128]{1,0:T(8,128)S(1)}, u32[]{:S(2)}, u32[]{:S(2)}) collective-permute-start(f32[384,128]{1,0:T(8,128)S(1)} %get-tuple-element.46.message), channel_id=1, source_target_pairs={{1,2},{2,1},{3,4},{4,3},{5,6},{6,5},{7,8},{8,7},{9,10},{10,9},{11,... | collective-permute-start | bytes 589832 | tf_op jit(solution)/shard_map/ppermute | solution.py:15
  5.0 9.9 %collective-permute-start.2 = (f32[5,32,128]{2,1,0:T(8,128)S(1)}, f32[5,32,128]{2,1,0:T(8,128)S(1)}, u32[]{:S(2)}, u32[]{:S(2)}) collective-permute-start(f32[5,32,128]{2,1,0:T(8,128)S(1)} %get-tuple-element.50.own), channel_id=1, source_target_pairs={{0,1},{1,0},{2,3},{3,2},{4,5},{5,4},{6,7},{7,6},{8,9},{9,8},{10,11... | collective-permute-start | bytes 245768 | tf_op jit(solution)/shard_map/ppermute | solution.py:19
  28.5 1.3 %collective-permute-start.3 = (f32[8,2,16,128]{3,2,1,0:T(8,128)S(1)}, f32[8,2,16,128]{3,2,1,0:T(8,128)S(1)}, u32[]{:S(2)}, u32[]{:S(2)}) collective-permute-start(f32[8,2,16,128]{3,2,1,0:T(8,128)S(1)} %all_to_all.5.same_cores), channel_id=1, source_target_pairs={{0,1},{1,0},{2,3},{3,2},{4,5},{5,4},{6,7},{7,6},{8,9},{9,8},{10,11... | collective-permute-start | bytes 393224 | tf_op jit(solution)/shard_map/ppermute | solution.py:19

commit v13 on v12

--- a/solution.py
+++ b/solution.py
@@ -276,7 +276,7 @@
 
 def border_kernel(
     inputs, message, own2, known1, new_in, fx_in, fy_in, fz_in, fzl_in, inv_in, across_in,
-    within, outer2, fx2_in, new, known, fx, fy, fz, fzl, inv,
+    within, fx2_in, new, known, fx, fy, fz, fzl, inv,
     old, even, change, turn, face_y, face_z, face_zl,
 ):
     iterate, source, _ = three_parts(inputs)
@@ -353,14 +353,14 @@
     its_inner = residual(-3, face2 * far)
     sums = [plane.summed(values, turn.at[3 + k]) for k, values in enumerate((own_outer, own_inner, its_outer, its_inner))]
     within[0] = mine("source2") + plane.packed(sums[0], sums[1], core)
-    outer2[0] = theirs("source2") + plane.packed(sums[2], sums[3], 1 - core)
-    outer2[1] = theirs("fx2")
+    within[5] = theirs("source2") + plane.packed(sums[2], sums[3], 1 - core)
+    within[6] = theirs("fx2")
     far2 = theirs("far2")
     far2_swap = jnp.where((plane.half_lane & 1) == 0, ahead(far2, 1, 1), behind(far2, 1, 1))
     near_fy2 = plane.odd_rows(face_y[0, body] + face_y[1, body], turn.at[1])
     near_fz2 = plane.odd_lanes(face_z[0] + face_z[1], turn.at[2])
-    outer2[2] = plane.packed(near_fy2, far2_swap, 1 - core)
-    outer2[3] = plane.packed(near_fz2, far2, 1 - core)
+    within[7] = plane.packed(near_fy2, far2_swap, 1 - core)
+    within[8] = plane.packed(near_fz2, far2, 1 - core)
     fx2_in[...] = mine("fx2")
     middle = jnp.where((plane.half_lane & 1) == 0, ahead(mine("fx2"), 1, 1), behind(mine("fx2"), 1, 1))
     within[1] = plane.packed(plane.summed(border, turn.at[7]), middle, core)
@@ -397,73 +397,86 @@
     return with_partner(with_partner(values, 1, 1), 2, 1)
 
 
+def packed_odd(values, pair):
+    half, lanes = values.shape
+    lane = lanes_of((half // 2, lanes))
+    pair[...] = values
+    return odd_cells(pair, half // 2, (((lane & 1) + (lane >> 1)) & 1) != 0)
+
+
 def middle_down_kernel(
-    own, fx2_in, outer, within_in,
+    own, fx2_in, within_in,
     slots, e2_out, s2, fx2, fxl2, fy2, fz2, fzl2, inv2,
     e2, pair,
 ):
     _, half, lanes = own.shape
     quarter = half // 2
-    position = lax.axis_index("gx")
     first_of_two, even2 = parities2(half, lanes)
     body, down = pl.ds(PAD, half), pl.ds(PAD - 1, half)
     edge = jnp.zeros((PAD, lanes), jnp.float32)
-    for j in range(5):
+    for j in (0, 5):
         e2[j] = jnp.zeros((half + 2 * PAD, lanes), jnp.float32)
-    def three(k):
-        left, right = by_side(outer[k], within_in[k])
-        return left, own[k], right
-
-    for j, (source, fy, fz) in enumerate(zip(three(0), three(2), three(3))):
+
+    def pair_of(k):
+        return by_side(own[k], within_in[k])
+
+    def four(k):
+        (left, right), (far_left, far_right) = pair_of(k), pair_of(5 + k)
+        return far_left, left, right, far_right
+
+    for j, (source, fy, fz) in enumerate(zip(four(0), four(2), four(3))):
         s2[j] = source
         fy2[j, :PAD] = edge
         fy2[j, body] = fy
         fy2[j, PAD + half:] = edge
         fz2[j] = fz
         fzl2[j] = behind(fz, 2, 1)
-    left_fx, _, right_fx = three(1)
-    own_fx = by_side(fx2_in[...], own[1])
-    fx2[0] = jnp.where(first_of_two, ahead(left_fx, 1, 1), behind(own_fx[1], 1, 1))
-    fx2[1] = own_fx[0]
-    fx2[2] = right_fx
-    fxl2[0] = left_fx
-    fxl2[1] = own_fx[1]
-    fxl2[2] = jnp.where(first_of_two, ahead(own_fx[0], 1, 1), behind(right_fx, 1, 1))
-    for j in range(3):
-        weight = fx2[j] + fxl2[j] + fy2[j, body] + fy2[j, down] + fz2[j] + fzl2[j]
+
+    def between(left, right):
+        return jnp.where(first_of_two, ahead(left, 1, 1), behind(right, 1, 1))
+
+    fxl0, fxl1, fxr2, fxr3 = four(1)
+    inner = fx2_in[...]
+    fxr1, _ = by_side(inner, between(fxl1, inner))
+    fxl2_, _ = by_side(between(inner, fxr2), inner)
+    for j, (face, low) in enumerate(
+        ((between(fxl0, fxl1), fxl0), (fxr1, fxl1), (fxr2, fxl2_), (fxr3, between(fxr2, fxr3)))
+    ):
+        fx2[j], fxl2[j] = face, low
+        weight = face + low + fy2[j, body] + fy2[j, down] + fz2[j] + fzl2[j]
         inverse = 1.0 / (8.0 + weight)
         inv2[j] = inverse
-        e2[j + 1, body] = jnp.where(even2, s2[j] * inverse, 0.0)
+        e2[j + 1, :PAD] = edge
+        e2[j + 1, PAD + half:] = edge
+        e2[j + 1, body] = s2[j] * inverse
 
     def neigh(tiles):
         return neigh2(e2, fx2, fxl2, fy2, fz2, fzl2, first_of_two, tiles)
 
-    fresh = [
-        jnp.where(even2, e2[j + 1, body], (s2[j] + sums) * inv2[j]) for j, sums in enumerate(neigh((0, 1, 2)))
-    ]
-    for j in range(3):
+    fresh = [(s2[j] + sums) * inv2[j] for j, sums in enumerate(neigh((0, 1, 2, 3)))]
+    for j in range(4):
         e2[j + 1, body] = fresh[j]
         e2_out[j] = fresh[j]
-    pair[0] = jnp.where(even2, neigh((1,))[0], 0.0)
     lane = lanes_of((quarter, lanes))
-    slot = position // (slots.shape[0] // 2)
-    odd_layer, odd_depth, item = (lane & 1) != 0, (lane & 2) != 0, (lane - slot) & 3
-    source = group(even_row_sum(pair.at[0], quarter))
-    fx = group(jnp.where(odd_layer, even_row_sum(fx2.at[1], quarter), 0.0))
-    fy = group(fy2[1, pl.ds(PAD + 1, quarter, 2), :])
-    fz = group(jnp.where(odd_depth, even_row_sum(fz2.at[1], quarter), 0.0))
-    fxl = group(jnp.where(odd_layer, 0.0, even_row_sum(fxl2.at[1], quarter)))
-    weight = (fx + fxl) + (fy + behind(fy, 1, 0)) + (fz + behind(fz, 4, 1))
-    start = source / (64.0 + weight)
-    tile = jnp.where(item == 0, start, jnp.where(item == 1, fx, jnp.where(item == 2, fy, fz)))
-    first = (((lane & 1) + (lane >> 1)) & 1) != 0
-    pair[0] = jnp.where(first_of_two, fresh[2], fresh[1])
-    pair[1] = jnp.where(first_of_two, fresh[1], fresh[0])
-    for_left = odd_cells(pair.at[0], quarter, first)
-    for_right = odd_cells(pair.at[1], quarter, first)
-    for c in range(slots.shape[0]):
-        slots[c, 0] = tile
-        slots[c, 1] = jnp.where(position < 2 * c + 1 - position % 2, for_right, for_left)
+    odd_layer, odd_depth = (lane & 1) != 0, (lane & 2) != 0
+    chips = slots.shape[0]
+    for k, sums in enumerate(neigh((1, 2))):
+        j = k + 1
+        pair[k] = jnp.where(even2, sums, 0.0)
+        item = (lane - (lax.axis_index("gx") // 2 * 2 + k) // (chips // 2)) & 3
+        source = group(even_row_sum(pair.at[k], quarter))
+        fx = group(jnp.where(odd_layer, even_row_sum(fx2.at[j], quarter), 0.0))
+        fxl = group(jnp.where(odd_layer, 0.0, even_row_sum(fxl2.at[j], quarter)))
+        fy = group(fy2[j, pl.ds(PAD + 1, quarter, 2), :])
+        fz = group(jnp.where(odd_depth, even_row_sum(fz2.at[j], quarter), 0.0))
+        weight = (fx + fxl) + (fy + behind(fy, 1, 0)) + (fz + behind(fz, 4, 1))
+        start = source / (64.0 + weight)
+        tile = jnp.where(item == 0, start, jnp.where(item == 1, fx, jnp.where(item == 2, fy, fz)))
+        for c in range(chips):
+            slots[c, k] = tile
+    halo = packed_odd(jnp.where(first_of_two, fresh[2], fresh[1]), pair.at[2])
+    for c in range(chips):
+        slots[c, 2] = halo
 
 
 def joined(one, two):
@@ -662,7 +675,7 @@
 
 
 def coarse_kernel(
-    owner_of, same_cores, other_cores, e2_in, s2, fx2, fxl2, fy2, fz2, fzl2, inv2,
+    owner_of, gathered, e2_in, s2_in, fx2_in, fxl2_in, fy2_in, fz2_in, fzl2_in, inv2_in,
     inputs, new_in, fx_more, fy_margin, fz_margin, fzl_margin, inv_more, fx_in, fy_in, fz_in, fzl_in, inv_in,
     new_out, known_out, fx_out, fy_out, fz_out, fzl_out, inv_out, within_in,
     solved_out, owned_out,
@@ -670,16 +683,14 @@
 ):
     fetch = pltpu.make_async_copy(owner_of, owner_here, fetch_sem)
     fetch.start()
-    chips, _, quarter, lanes = same_cores.shape
+    chips, _, quarter, lanes = gathered.shape
     blocks = 2 * chips
     half, height = 2 * quarter, 4 * quarter
     position, last = lax.axis_index("gx"), blocks - 1
 
     slot = lanes_of((quarter, lanes)) & 3
     spread = blocks // 4
-    tiles = []
-    for chip in range(chips):
-        tiles.extend(by_side(same_cores[chip, 0], other_cores[chip, 0]))
+    tiles = [gathered[chip, k] for chip in range(chips) for k in range(2)]
     items = []
     for k in range(4):
         packs = []
@@ -710,22 +721,21 @@
     first_of_two, even2 = parities2(half, lanes)
     body2 = pl.ds(PAD, half)
     edge = jnp.zeros((PAD, lanes), jnp.float32)
-    left = other_cores[jnp.maximum(position - 1, 0) // 2, 1]
-    right = other_cores[jnp.minimum(position + 1, last) // 2, 1]
-    into_both_rows(pair.at[5], left)
-    into_both_rows(pair.at[6], right)
-    left, right = pair[5], pair[6]
+    core = core_of()
+    s2, fx2, fxl2, fy2, fz2, fzl2, inv2 = [
+        ref.at[pl.ds(core, 3)] for ref in (s2_in, fx2_in, fxl2_in, fy2_in, fz2_in, fzl2_in, inv2_in)
+    ]
+    next_chip = jnp.clip(position // 2 - 1 + 2 * core, 0, chips - 1)
+    into_both_rows(pair.at[5], gathered[next_chip, 2])
+    halo = pair[5]
     before = (
-        left, jnp.where(first_of_two, left, e2_in[0]), e2_in[1], jnp.where(first_of_two, e2_in[2], right), right
+        by_side(halo, e2_in[0])[0], by_side(jnp.where(first_of_two, halo, e2_in[0]), e2_in[1])[0],
+        by_side(e2_in[1], e2_in[2])[0],
+        by_side(e2_in[2], jnp.where(first_of_two, e2_in[3], halo))[0], by_side(e2_in[3], halo)[0],
     )
     for k in range(5):
         j = jnp.clip(position + k - 2, 0, last)
-        here = e3[j % spread]
-        turned = [pltpu.roll(here, (at - j // spread) % lanes, 1) for at in range(4)]
-        value = turned[3]
-        for at in range(3):
-            value = jnp.where(slot == at, turned[at], value)
-        into_both_rows(pair.at[k], value)
+        into_both_rows(pair.at[k], group(jnp.where(slot == j // spread, e3[j % spread], 0.0)))
         e2[k, :PAD] = edge
         e2[k, PAD + half:] = edge
         e2[k, body2] = before[k] + pair[k]
@@ -743,7 +753,6 @@
     layers = source.shape[0]
     plane = Plane(height, lanes)
     body1 = plane.body
-    core = core_of()
     near_lane = (lanes_of((half, lanes)) & 1) == core
     swaps = [jnp.where(first_of_two, ahead(v, 1, 1), behind(v, 1, 1)) for v in fixes2]
     outer, inner = by_side(fixes2[0], fixes2[2])
@@ -853,10 +862,10 @@
         [vmem(*tall), vmem(2, *tall), vmem(3, *tall), vmem(10, *layer)],
         (inputs, cell, old, *fine, even, edge_in),
     )
-    within, outer, fx2, *border = call(
+    within, fx2, *border = call(
         border_kernel,
         [
-            f32(5, *tile), f32(4, *tile), f32(*tile), f32(3, *layer), f32(*layer), f32(2, *layer),
+            f32(9, *tile), f32(*tile), f32(3, *layer), f32(*layer), f32(2, *layer),
             f32(padded, depth), f32(*layer), f32(*layer), f32(2, *layer),
         ],
         [
@@ -866,16 +875,15 @@
         (inputs, message, own2, known1, new, *fine, between_chips(message)),
     )
     within_in = within_chip(within)
-    plain = f32(3, *tile)
+    plain = f32(4, *tile)
     slots, *middle = call(
         middle_down_kernel,
-        [f32(blocks // 2, 2, quarter, depth), plain, plain, plain, plain, f32(3, padded2, depth)] + [plain] * 3,
-        [vmem(5, padded2, depth), vmem(2, *tile)],
-        (within, fx2, outer, within_in),
+        [f32(blocks // 2, 3, quarter, depth), plain, plain, plain, plain, f32(4, padded2, depth)] + [plain] * 3,
+        [vmem(6, padded2, depth), vmem(3, *tile)],
+        (within, fx2, within_in),
     )
     kinds = [list(range(core, blocks, 2)) for core in range(2)]
-    same_cores = lax.all_to_all(slots, "gx", 0, 0, axis_index_groups=kinds, tiled=True)
-    other_cores = within_chip(same_cores)
+    gathered = lax.all_to_all(slots, "gx", 0, 0, axis_index_groups=kinds, tiled=True)
     solved, owned = call(
         coarse_kernel,
         [f32(layers, *layer), f32(1, quarter, depth // 4)],
@@ -885,7 +893,7 @@
             vmem(1, quarter, depth // 4), pltpu.SMEM((blocks,), jnp.int32),
             pltpu.SemaphoreType.DMA, pltpu.SemaphoreType.DMA((layers + 1,)),
         ],
-        (block_owner, same_cores, other_cores, *middle, inputs, new, *margin, *fine, *border, within_in),
+        (block_owner, gathered, *middle, inputs, new, *margin, *fine, *border, within_in),
         pl.ANY,
     )
     return solved, owned

time: 33.7 us -> 33 us (0.979)
  waiting for transfers between devices: 3.04 us -> 1.77 us
  blocking collectives: 13.2 us -> 14.2 us
  Pallas kernels: 5.36 us -> 4.97 us
    ppermute x3 -> x2, waiting for transfers between devices: 3.04 us -> 1.77 us  [within_chip(): lax.ppermute(block, 'gx', [(i, i ^ 1) for i in range(lax.axis_size('gx'))])]
    all_to_all x1, blocking collectives: 13.2 us -> 14.2 us  [on_device(): lax.all_to_all(slots, 'gx', 0, 0, axis_index_groups=kinds, tiled=True)]
    pallas_call x6, Pallas kernels: 5.36 us -> 4.97 us  [call(): pl.pallas_call(kernel, out_shape=tuple(outs), in_specs=[pl.BlockSpec(memo...]
    ppermute x3 -> x2, starting transfers between devices: 9.47 us -> 9.46 us  [within_chip(): lax.ppermute(block, 'gx', [(i, i ^ 1) for i in range(lax.axis_size('gx'))])]
  transfers between devices with their start and end apart: 4 -> 3, of which waited for: 3 -> 2; matrix products, arithmetic and copies ran while one was open for 0% -> 0% of each run, Pallas kernels for 1% -> 1%
where the time goes in v13:
time: 33 us; the launch traced here: 32.8 us
  blocking collectives  14.2 us (43%)
  starting transfers between devices  10.1 us (31%)
  Pallas kernels  4.97 us (15%)
  waiting for transfers between devices  1.77 us (5%)
  other arithmetic  1.06 us (3%)
  between operations  0.69 us (2%)
    all_to_all x1, blocking collectives, on_device(): lax.all_to_all(slots, 'gx', 0, 0, axis_index_groups=kinds, tiled=True)  14.2 us
    ppermute x2, starting transfers between devices, within_chip(): lax.ppermute(block, 'gx', [(i, i ^ 1) for i in range(lax.axis_size('gx'))])  9.46 us
    pallas_call x6, Pallas kernels, call(): pl.pallas_call(kernel, out_shape=tuple(outs), in_specs=[pl.BlockSpec(memo...  4.97 us
    ppermute x2, waiting for transfers between devices, within_chip(): lax.ppermute(block, 'gx', [(i, i ^ 1) for i in range(lax.axis_size('gx'))])  1.77 us
    add x1, other arithmetic, on_device(): sum((jnp.pad(block, ((k * layers, (2 - k) * layers), (0, 0), (0, 0))) for...  1.06 us
    ppermute x1, starting transfers between devices, between_chips(): lax.ppermute(block, 'gx', [(i, i + 1 if i % 2 else i - 1) for i in range(...  0.68 us
  transfers between devices with their start and end apart: 3, of which 2 were waited for; matrix products, arithmetic and copies ran while one was open for 0% of the time, Pallas kernels for 1%

profile of v13, /device:TPU:0, one launch (start us, length us, event | category | flops | bytes accessed | tf_op | source)
XLA Modules:
  0.0 32.8 jit_solution(7038809029342253390)
XLA Ops:
  0.6 1.1 %pad_add_fusion.inputs = f32[12,64,128]{2,1,0:T(8,128)S(1)} fusion(f32[4,64,128]{2,1,0:T(8,128)} %param.6, f32[4,64,128]{2,1,0:T(8,128)} %param.5, f32[4,64,128]{2,1,0:T(8,128)} %param.4), kind=kLoop, calls=%fused_computation | loop fusion | flops 196608 | bytes 786432 | tf_op jit(solution)/shard_map/add | solution.py:841
  1.7 0.0 copy-start
  1.7 0.2 shard_map.60
  1.9 0.5 %collective-permute-start = (f32[224,128]{1,0:T(8,128)S(1)}, f32[224,128]{1,0:T(8,128)S(1)}, u32[]{:S(2)}, u32[]{:S(2)}) collective-permute-start(f32[224,128]{1,0:T(8,128)S(1)} %shard_map.60), channel_id=1, source_target_pairs={{0,1},{1,0},{2,3},{3,2},{4,5},{5,4},{6,7},{7,6},{8,9},{9,8},{10,11... | collective-permute-start | bytes 344072 | tf_op jit(solution)/shard_map/ppermute | solution.py:19
  2.4 0.0 copy-done
  2.4 0.2 shard_map.59
  2.6 0.8 %collective-permute-done.within_in = f32[224,128]{1,0:T(8,128)S(1)} collective-permute-done((f32[224,128]{1,0:T(8,128)S(1)}, f32[224,128]{1,0:T(8,128)S(1)}, u32[]{:S(2)}, u32[]{:S(2)}) %collective-permute-start) | collective-permute-done | bytes 114720 | tf_op jit(solution)/shard_map/ppermute | solution.py:19
  3.4 0.4 %shard_map.61 = (f32[384,128]{1,0:T(8,128)S(1)}, f32[2,32,128]{2,1,0:T(8,128)S(1)}, f32[64,128]{1,0:T(8,128)S(1)}, f32[3,64,128]{2,1,0:T(8,128)S(1)}, f32[2,64,1...) custom-call(f32[12,64,128]{2,1,0:T(8,128)S(1)} %pad_add_fusion.input, ...), custom_call_target="tpu_custom_call" | custom-call | tf_op jit(solution)/shard_map/pallas_call | solution.py:826
  3.8 0.7 %collective-permute-start.1 = (f32[384,128]{1,0:T(8,128)S(1)}, f32[384,128]{1,0:T(8,128)S(1)}, u32[]{:S(2)}, u32[]{:S(2)}) collective-permute-start(f32[384,128]{1,0:T(8,128)S(1)} %get-tuple-element.45.message), channel_id=1, source_target_pairs={{1,2},{2,1},{3,4},{4,3},{5,6},{6,5},{7,8},{8,7},{9,10},{10,9},{11,... | collective-permute-start | bytes 589832 | tf_op jit(solution)/shard_map/ppermute | solution.py:15
  4.5 0.0 collective-permute-done.1.across_in
  4.5 0.5 %shard_map.62 = (f32[9,32,128]{2,1,0:T(8,128)S(1)}, f32[32,128]{1,0:T(8,128)S(1)}, f32[3,64,128]{2,1,0:T(8,128)S(1)}, f32[64,128]{1,0:T(8,128)S(1)}, f32[2,64,12...) custom-call(f32[12,64,128]{2,1,0:T(8,128)S(1)} %pad_add_fusion.input, ...), custom_call_target="tpu_custom_call" | custom-call | tf_op jit(solution)/shard_map/pallas_call | solution.py:826
  5.0 8.9 %collective-permute-start.2 = (f32[9,32,128]{2,1,0:T(8,128)S(1)}, f32[9,32,128]{2,1,0:T(8,128)S(1)}, u32[]{:S(2)}, u32[]{:S(2)}) collective-permute-start(f32[9,32,128]{2,1,0:T(8,128)S(1)} %get-tuple-element.49.own), channel_id=1, source_target_pairs={{0,1},{1,0},{2,3},{3,2},{4,5},{5,4},{6,7},{7,6},{8,9},{9,8},{10,11... | collective-permute-start | bytes 442376 | tf_op jit(solution)/shard_map/ppermute | solution.py:19
  13.9 1.0 %collective-permute-done.2.within_in = f32[9,32,128]{2,1,0:T(8,128)S(1)} collective-permute-done((f32[9,32,128]{2,1,0:T(8,128)S(1)}, f32[9,32,128]{2,1,0:T(8,128)S(1)}, u32[]{:S(2)}, u32[]{:S(2)}) %collective-permute-start.2) | collective-permute-done | bytes 147488 | tf_op jit(solution)/shard_map/ppermute | solution.py:19
  14.9 0.5 %shard_map.63 = (f32[8,3,16,128]{3,2,1,0:T(8,128)S(1)}, f32[4,32,128]{2,1,0:T(8,128)S(1)}, f32[4,32,128]{2,1,0:T(8,128)S(1)}, f32[4,32,128]{2,1,0:T(8,128)S(1)},...) custom-call(f32[9,32,128]{2,1,0:T(8,128)S(1)} %get-tuple-element.49., ...), custom_call_target="tpu_custom_call" | custom-call | tf_op jit(solution)/shard_map/pallas_call | solution.py:826
  15.5 14.2 %all_to_all.5.gathered = f32[8,3,16,128]{3,2,1,0:T(8,128)S(1)} all-to-all(f32[8,3,16,128]{3,2,1,0:T(8,128)S(1)} %get-tuple-element.51), channel_id=1, replica_groups={{0,2,4,6,8,10,12,14},{1,3,5,7,9,11,13,15},{16,18,20,22,24,26,28,30},{17..., dimensions={0} | all-to-all | bytes 393216 | tf_op jit(solution)/shard_map/all_to_all | solution.py:886
  29.6 3.2 %shard_map.64 = (f32[4,64,128]{2,1,0:T(8,128)}, f32[1,16,32]{2,1,0:T(8,128)}) custom-call(s32[16]{0:T(128)S(1)} %copy-done, f32[8,3,16,128]{3,2,1,0:T(8,128)S(1)} %all_to_all.5.gathered, f32[4,32,128]{2,1,0:T(8,128)S(1)} %get-tuple-element.52.e2_in, f32[4,32,128]{2,1,0:T(8,128)S(1)} %get-tuple-element.53.s2_in, f32[4,32,128]{2,1,0:T(8,128)S(1)} %get-tuple-element.54.fx2_in, ...), custom_call_target="tpu_custom_call" | custom-call | tf_op jit(solution)/shard_map/pallas_call | solution.py:826
Async XLA Ops:
  1.7 0.7 %copy-start = (s32[16]{0:T(128)S(1)}, s32[16]{0:T(128)}, u32[]{:S(2)}) copy-start(s32[16]{0:T(128)} %owner_of.3) | copy-start | bytes 196
  1.9 1.5 %collective-permute-start = (f32[224,128]{1,0:T(8,128)S(1)}, f32[224,128]{1,0:T(8,128)S(1)}, u32[]{:S(2)}, u32[]{:S(2)}) collective-permute-start(f32[224,128]{1,0:T(8,128)S(1)} %shard_map.60), channel_id=1, source_target_pairs={{0,1},{1,0},{2,3},{3,2},{4,5},{5,4},{6,7},{7,6},{8,9},{9,8},{10,11... | collective-permute-start | bytes 344072 | tf_op jit(solution)/shard_map/ppermute | solution.py:19
  3.8 0.7 %collective-permute-start.1 = (f32[384,128]{1,0:T(8,128)S(1)}, f32[384,128]{1,0:T(8,128)S(1)}, u32[]{:S(2)}, u32[]{:S(2)}) collective-permute-start(f32[384,128]{1,0:T(8,128)S(1)} %get-tuple-element.45.message), channel_id=1, source_target_pairs={{1,2},{2,1},{3,4},{4,3},{5,6},{6,5},{7,8},{8,7},{9,10},{10,9},{11,... | collective-permute-start | bytes 589832 | tf_op jit(solution)/shard_map/ppermute | solution.py:15
  5.0 10.0 %collective-permute-start.2 = (f32[9,32,128]{2,1,0:T(8,128)S(1)}, f32[9,32,128]{2,1,0:T(8,128)S(1)}, u32[]{:S(2)}, u32[]{:S(2)}) collective-permute-start(f32[9,32,128]{2,1,0:T(8,128)S(1)} %get-tuple-element.49.own), channel_id=1, source_target_pairs={{0,1},{1,0},{2,3},{3,2},{4,5},{5,4},{6,7},{7,6},{8,9},{9,8},{10,11... | collective-permute-start | bytes 442376 | tf_op jit(solution)/shard_map/ppermute | solution.py:19

commit v14 on v13

--- a/solution.py
+++ b/solution.py
@@ -882,7 +882,7 @@
         [vmem(6, padded2, depth), vmem(3, *tile)],
         (within, fx2, within_in),
     )
-    kinds = [list(range(core, blocks, 2)) for core in range(2)]
+    kinds = [[2 * chip + (chip + core) % 2 for chip in range(blocks // 2)] for core in range(2)]
     gathered = lax.all_to_all(slots, "gx", 0, 0, axis_index_groups=kinds, tiled=True)
     solved, owned = call(
         coarse_kernel,

time: 33 us -> 32.8 us (level)
  no operation moved by 1% of the time
where the time goes in v14:
time: 32.8 us; the launch traced here: 32.6 us
  blocking collectives  13.9 us (42%)
  starting transfers between devices  10.1 us (31%)
  Pallas kernels  4.97 us (15%)
  waiting for transfers between devices  1.77 us (5%)
  other arithmetic  1.06 us (3%)
  between operations  0.69 us (2%)
    all_to_all x1, blocking collectives, on_device(): lax.all_to_all(slots, 'gx', 0, 0, axis_index_groups=kinds, tiled=True)  13.9 us
    ppermute x2, starting transfers between devices, within_chip(): lax.ppermute(block, 'gx', [(i, i ^ 1) for i in range(lax.axis_size('gx'))])  9.46 us
    pallas_call x6, Pallas kernels, call(): pl.pallas_call(kernel, out_shape=tuple(outs), in_specs=[pl.BlockSpec(memo...  4.97 us
    ppermute x2, waiting for transfers between devices, within_chip(): lax.ppermute(block, 'gx', [(i, i ^ 1) for i in range(lax.axis_size('gx'))])  1.77 us
    add x1, other arithmetic, on_device(): sum((jnp.pad(block, ((k * layers, (2 - k) * layers), (0, 0), (0, 0))) for...  1.06 us
    ppermute x1, starting transfers between devices, between_chips(): lax.ppermute(block, 'gx', [(i, i + 1 if i % 2 else i - 1) for i in range(...  0.68 us
  transfers between devices with their start and end apart: 3, of which 2 were waited for; matrix products, arithmetic and copies ran while one was open for 0% of the time, Pallas kernels for 1%

profile of v14, /device:TPU:0, one launch (start us, length us, event | category | flops | bytes accessed | tf_op | source)
XLA Modules:
  0.0 32.6 jit_solution(2655923529490091563)
XLA Ops:
  0.6 1.1 %pad_add_fusion.inputs = f32[12,64,128]{2,1,0:T(8,128)S(1)} fusion(f32[4,64,128]{2,1,0:T(8,128)} %param.6, f32[4,64,128]{2,1,0:T(8,128)} %param.5, f32[4,64,128]{2,1,0:T(8,128)} %param.4), kind=kLoop, calls=%fused_computation | loop fusion | flops 196608 | bytes 786432 | tf_op jit(solution)/shard_map/add | solution.py:841
  1.7 0.0 copy-start
  1.7 0.2 shard_map.60
  1.9 0.5 %collective-permute-start = (f32[224,128]{1,0:T(8,128)S(1)}, f32[224,128]{1,0:T(8,128)S(1)}, u32[]{:S(2)}, u32[]{:S(2)}) collective-permute-start(f32[224,128]{1,0:T(8,128)S(1)} %shard_map.60), channel_id=1, source_target_pairs={{0,1},{1,0},{2,3},{3,2},{4,5},{5,4},{6,7},{7,6},{8,9},{9,8},{10,11... | collective-permute-start | bytes 344072 | tf_op jit(solution)/shard_map/ppermute | solution.py:19
  2.4 0.0 copy-done
  2.4 0.2 shard_map.59
  2.6 0.8 %collective-permute-done.within_in = f32[224,128]{1,0:T(8,128)S(1)} collective-permute-done((f32[224,128]{1,0:T(8,128)S(1)}, f32[224,128]{1,0:T(8,128)S(1)}, u32[]{:S(2)}, u32[]{:S(2)}) %collective-permute-start) | collective-permute-done | bytes 114720 | tf_op jit(solution)/shard_map/ppermute | solution.py:19
  3.4 0.4 %shard_map.61 = (f32[384,128]{1,0:T(8,128)S(1)}, f32[2,32,128]{2,1,0:T(8,128)S(1)}, f32[64,128]{1,0:T(8,128)S(1)}, f32[3,64,128]{2,1,0:T(8,128)S(1)}, f32[2,64,1...) custom-call(f32[12,64,128]{2,1,0:T(8,128)S(1)} %pad_add_fusion.input, ...), custom_call_target="tpu_custom_call" | custom-call | tf_op jit(solution)/shard_map/pallas_call | solution.py:826
  3.8 0.7 %collective-permute-start.1 = (f32[384,128]{1,0:T(8,128)S(1)}, f32[384,128]{1,0:T(8,128)S(1)}, u32[]{:S(2)}, u32[]{:S(2)}) collective-permute-start(f32[384,128]{1,0:T(8,128)S(1)} %get-tuple-element.45.message), channel_id=1, source_target_pairs={{1,2},{2,1},{3,4},{4,3},{5,6},{6,5},{7,8},{8,7},{9,10},{10,9},{11,... | collective-permute-start | bytes 589832 | tf_op jit(solution)/shard_map/ppermute | solution.py:15
  4.5 0.0 collective-permute-done.1.across_in
  4.5 0.5 %shard_map.62 = (f32[9,32,128]{2,1,0:T(8,128)S(1)}, f32[32,128]{1,0:T(8,128)S(1)}, f32[3,64,128]{2,1,0:T(8,128)S(1)}, f32[64,128]{1,0:T(8,128)S(1)}, f32[2,64,12...) custom-call(f32[12,64,128]{2,1,0:T(8,128)S(1)} %pad_add_fusion.input, ...), custom_call_target="tpu_custom_call" | custom-call | tf_op jit(solution)/shard_map/pallas_call | solution.py:826
  5.0 8.9 %collective-permute-start.2 = (f32[9,32,128]{2,1,0:T(8,128)S(1)}, f32[9,32,128]{2,1,0:T(8,128)S(1)}, u32[]{:S(2)}, u32[]{:S(2)}) collective-permute-start(f32[9,32,128]{2,1,0:T(8,128)S(1)} %get-tuple-element.49.own), channel_id=1, source_target_pairs={{0,1},{1,0},{2,3},{3,2},{4,5},{5,4},{6,7},{7,6},{8,9},{9,8},{10,11... | collective-permute-start | bytes 442376 | tf_op jit(solution)/shard_map/ppermute | solution.py:19
  13.9 1.0 %collective-permute-done.2.within_in = f32[9,32,128]{2,1,0:T(8,128)S(1)} collective-permute-done((f32[9,32,128]{2,1,0:T(8,128)S(1)}, f32[9,32,128]{2,1,0:T(8,128)S(1)}, u32[]{:S(2)}, u32[]{:S(2)}) %collective-permute-start.2) | collective-permute-done | bytes 147488 | tf_op jit(solution)/shard_map/ppermute | solution.py:19
  14.9 0.5 %shard_map.63 = (f32[8,3,16,128]{3,2,1,0:T(8,128)S(1)}, f32[4,32,128]{2,1,0:T(8,128)S(1)}, f32[4,32,128]{2,1,0:T(8,128)S(1)}, f32[4,32,128]{2,1,0:T(8,128)S(1)},...) custom-call(f32[9,32,128]{2,1,0:T(8,128)S(1)} %get-tuple-element.49., ...), custom_call_target="tpu_custom_call" | custom-call | tf_op jit(solution)/shard_map/pallas_call | solution.py:826
  15.5 13.9 %all_to_all.5.gathered = f32[8,3,16,128]{3,2,1,0:T(8,128)S(1)} all-to-all(f32[8,3,16,128]{3,2,1,0:T(8,128)S(1)} %get-tuple-element.51), channel_id=1, replica_groups={{0,3,4,7,8,11,12,15},{1,2,5,6,9,10,13,14},{16,19,20,23,24,27,28,31},{17..., dimensions={0} | all-to-all | bytes 393216 | tf_op jit(solution)/shard_map/all_to_all | solution.py:886
  29.4 3.2 %shard_map.64 = (f32[4,64,128]{2,1,0:T(8,128)}, f32[1,16,32]{2,1,0:T(8,128)}) custom-call(s32[16]{0:T(128)S(1)} %copy-done, f32[8,3,16,128]{3,2,1,0:T(8,128)S(1)} %all_to_all.5.gathered, f32[4,32,128]{2,1,0:T(8,128)S(1)} %get-tuple-element.52.e2_in, f32[4,32,128]{2,1,0:T(8,128)S(1)} %get-tuple-element.53.s2_in, f32[4,32,128]{2,1,0:T(8,128)S(1)} %get-tuple-element.54.fx2_in, ...), custom_call_target="tpu_custom_call" | custom-call | tf_op jit(solution)/shard_map/pallas_call | solution.py:826
Async XLA Ops:
  1.7 0.7 %copy-start = (s32[16]{0:T(128)S(1)}, s32[16]{0:T(128)}, u32[]{:S(2)}) copy-start(s32[16]{0:T(128)} %owner_of.3) | copy-start | bytes 196
  1.9 1.5 %collective-permute-start = (f32[224,128]{1,0:T(8,128)S(1)}, f32[224,128]{1,0:T(8,128)S(1)}, u32[]{:S(2)}, u32[]{:S(2)}) collective-permute-start(f32[224,128]{1,0:T(8,128)S(1)} %shard_map.60), channel_id=1, source_target_pairs={{0,1},{1,0},{2,3},{3,2},{4,5},{5,4},{6,7},{7,6},{8,9},{9,8},{10,11... | collective-permute-start | bytes 344072 | tf_op jit(solution)/shard_map/ppermute | solution.py:19
  3.8 0.7 %collective-permute-start.1 = (f32[384,128]{1,0:T(8,128)S(1)}, f32[384,128]{1,0:T(8,128)S(1)}, u32[]{:S(2)}, u32[]{:S(2)}) collective-permute-start(f32[384,128]{1,0:T(8,128)S(1)} %get-tuple-element.45.message), channel_id=1, source_target_pairs={{1,2},{2,1},{3,4},{4,3},{5,6},{6,5},{7,8},{8,7},{9,10},{10,9},{11,... | collective-permute-start | bytes 589832 | tf_op jit(solution)/shard_map/ppermute | solution.py:15
  5.0 10.0 %collective-permute-start.2 = (f32[9,32,128]{2,1,0:T(8,128)S(1)}, f32[9,32,128]{2,1,0:T(8,128)S(1)}, u32[]{:S(2)}, u32[]{:S(2)}) collective-permute-start(f32[9,32,128]{2,1,0:T(8,128)S(1)} %get-tuple-element.49.own), channel_id=1, source_target_pairs={{0,1},{1,0},{2,3},{3,2},{4,5},{5,4},{6,7},{7,6},{8,9},{9,8},{10,11... | collective-permute-start | bytes 442376 | tf_op jit(solution)/shard_map/ppermute | solution.py:19

commit v15 on v14

--- a/solution.py
+++ b/solution.py
@@ -690,7 +690,7 @@
 
     slot = lanes_of((quarter, lanes)) & 3
     spread = blocks // 4
-    tiles = [gathered[chip, k] for chip in range(chips) for k in range(2)]
+    tiles = [gathered[chip, k] for chip in reversed(range(chips)) for k in range(2)]
     items = []
     for k in range(4):
         packs = []
@@ -726,7 +726,7 @@
         ref.at[pl.ds(core, 3)] for ref in (s2_in, fx2_in, fxl2_in, fy2_in, fz2_in, fzl2_in, inv2_in)
     ]
     next_chip = jnp.clip(position // 2 - 1 + 2 * core, 0, chips - 1)
-    into_both_rows(pair.at[5], gathered[next_chip, 2])
+    into_both_rows(pair.at[5], gathered[chips - 1 - next_chip, 2])
     halo = pair[5]
     before = (
         by_side(halo, e2_in[0])[0], by_side(jnp.where(first_of_two, halo, e2_in[0]), e2_in[1])[0],
@@ -882,7 +882,7 @@
         [vmem(6, padded2, depth), vmem(3, *tile)],
         (within, fx2, within_in),
     )
-    kinds = [[2 * chip + (chip + core) % 2 for chip in range(blocks // 2)] for core in range(2)]
+    kinds = [[2 * chip + (chip + core) % 2 for chip in reversed(range(blocks // 2))] for core in range(2)]
     gathered = lax.all_to_all(slots, "gx", 0, 0, axis_index_groups=kinds, tiled=True)
     solved, owned = call(
         coarse_kernel,

time: 32.8 us -> 32.1 us (0.979)
  blocking collectives: 13.9 us -> 13.2 us
    all_to_all x1, blocking collectives: 13.9 us -> 13.2 us  [on_device(): lax.all_to_all(slots, 'gx', 0, 0, axis_index_groups=kinds, tiled=True)]
where the time goes in v15:
time: 32.1 us; the launch traced here: 31.9 us
  blocking collectives  13.2 us (41%)
  starting transfers between devices  10.1 us (31%)
  Pallas kernels  4.97 us (15%)
  waiting for transfers between devices  1.77 us (6%)
  other arithmetic  1.06 us (3%)
  between operations  0.69 us (2%)
    all_to_all x1, blocking collectives, on_device(): lax.all_to_all(slots, 'gx', 0, 0, axis_index_groups=kinds, tiled=True)  13.2 us
    ppermute x2, starting transfers between devices, within_chip(): lax.ppermute(block, 'gx', [(i, i ^ 1) for i in range(lax.axis_size('gx'))])  9.46 us
    pallas_call x6, Pallas kernels, call(): pl.pallas_call(kernel, out_shape=tuple(outs), in_specs=[pl.BlockSpec(memo...  4.97 us
    ppermute x2, waiting for transfers between devices, within_chip(): lax.ppermute(block, 'gx', [(i, i ^ 1) for i in range(lax.axis_size('gx'))])  1.77 us
    add x1, other arithmetic, on_device(): sum((jnp.pad(block, ((k * layers, (2 - k) * layers), (0, 0), (0, 0))) for...  1.06 us
    ppermute x1, starting transfers between devices, between_chips(): lax.ppermute(block, 'gx', [(i, i + 1 if i % 2 else i - 1) for i in range(...  0.68 us
  transfers between devices with their start and end apart: 3, of which 2 were waited for; matrix products, arithmetic and copies ran while one was open for 0% of the time, Pallas kernels for 1%

profile of v15, /device:TPU:0, one launch (start us, length us, event | category | flops | bytes accessed | tf_op | source)
XLA Modules:
  0.0 31.9 jit_solution(2229207348561096331)
XLA Ops:
  0.6 1.1 %pad_add_fusion.inputs = f32[12,64,128]{2,1,0:T(8,128)S(1)} fusion(f32[4,64,128]{2,1,0:T(8,128)} %param.6, f32[4,64,128]{2,1,0:T(8,128)} %param.5, f32[4,64,128]{2,1,0:T(8,128)} %param.4), kind=kLoop, calls=%fused_computation | loop fusion | flops 196608 | bytes 786432 | tf_op jit(solution)/shard_map/add | solution.py:841
  1.7 0.0 copy-start
  1.7 0.2 shard_map.60
  1.9 0.5 %collective-permute-start = (f32[224,128]{1,0:T(8,128)S(1)}, f32[224,128]{1,0:T(8,128)S(1)}, u32[]{:S(2)}, u32[]{:S(2)}) collective-permute-start(f32[224,128]{1,0:T(8,128)S(1)} %shard_map.60), channel_id=1, source_target_pairs={{0,1},{1,0},{2,3},{3,2},{4,5},{5,4},{6,7},{7,6},{8,9},{9,8},{10,11... | collective-permute-start | bytes 344072 | tf_op jit(solution)/shard_map/ppermute | solution.py:19
  2.4 0.0 copy-done
  2.4 0.2 shard_map.59
  2.6 0.8 %collective-permute-done.within_in = f32[224,128]{1,0:T(8,128)S(1)} collective-permute-done((f32[224,128]{1,0:T(8,128)S(1)}, f32[224,128]{1,0:T(8,128)S(1)}, u32[]{:S(2)}, u32[]{:S(2)}) %collective-permute-start) | collective-permute-done | bytes 114720 | tf_op jit(solution)/shard_map/ppermute | solution.py:19
  3.4 0.4 %shard_map.61 = (f32[384,128]{1,0:T(8,128)S(1)}, f32[2,32,128]{2,1,0:T(8,128)S(1)}, f32[64,128]{1,0:T(8,128)S(1)}, f32[3,64,128]{2,1,0:T(8,128)S(1)}, f32[2,64,1...) custom-call(f32[12,64,128]{2,1,0:T(8,128)S(1)} %pad_add_fusion.input, ...), custom_call_target="tpu_custom_call" | custom-call | tf_op jit(solution)/shard_map/pallas_call | solution.py:826
  3.8 0.7 %collective-permute-start.1 = (f32[384,128]{1,0:T(8,128)S(1)}, f32[384,128]{1,0:T(8,128)S(1)}, u32[]{:S(2)}, u32[]{:S(2)}) collective-permute-start(f32[384,128]{1,0:T(8,128)S(1)} %get-tuple-element.45.message), channel_id=1, source_target_pairs={{1,2},{2,1},{3,4},{4,3},{5,6},{6,5},{7,8},{8,7},{9,10},{10,9},{11,... | collective-permute-start | bytes 589832 | tf_op jit(solution)/shard_map/ppermute | solution.py:15
  4.5 0.0 collective-permute-done.1.across_in
  4.5 0.5 %shard_map.62 = (f32[9,32,128]{2,1,0:T(8,128)S(1)}, f32[32,128]{1,0:T(8,128)S(1)}, f32[3,64,128]{2,1,0:T(8,128)S(1)}, f32[64,128]{1,0:T(8,128)S(1)}, f32[2,64,12...) custom-call(f32[12,64,128]{2,1,0:T(8,128)S(1)} %pad_add_fusion.input, ...), custom_call_target="tpu_custom_call" | custom-call | tf_op jit(solution)/shard_map/pallas_call | solution.py:826
  5.0 8.9 %collective-permute-start.2 = (f32[9,32,128]{2,1,0:T(8,128)S(1)}, f32[9,32,128]{2,1,0:T(8,128)S(1)}, u32[]{:S(2)}, u32[]{:S(2)}) collective-permute-start(f32[9,32,128]{2,1,0:T(8,128)S(1)} %get-tuple-element.49.own), channel_id=1, source_target_pairs={{0,1},{1,0},{2,3},{3,2},{4,5},{5,4},{6,7},{7,6},{8,9},{9,8},{10,11... | collective-permute-start | bytes 442376 | tf_op jit(solution)/shard_map/ppermute | solution.py:19
  13.9 1.0 %collective-permute-done.2.within_in = f32[9,32,128]{2,1,0:T(8,128)S(1)} collective-permute-done((f32[9,32,128]{2,1,0:T(8,128)S(1)}, f32[9,32,128]{2,1,0:T(8,128)S(1)}, u32[]{:S(2)}, u32[]{:S(2)}) %collective-permute-start.2) | collective-permute-done | bytes 147488 | tf_op jit(solution)/shard_map/ppermute | solution.py:19
  14.9 0.5 %shard_map.63 = (f32[8,3,16,128]{3,2,1,0:T(8,128)S(1)}, f32[4,32,128]{2,1,0:T(8,128)S(1)}, f32[4,32,128]{2,1,0:T(8,128)S(1)}, f32[4,32,128]{2,1,0:T(8,128)S(1)},...) custom-call(f32[9,32,128]{2,1,0:T(8,128)S(1)} %get-tuple-element.49., ...), custom_call_target="tpu_custom_call" | custom-call | tf_op jit(solution)/shard_map/pallas_call | solution.py:826
  15.5 13.2 %all_to_all.5.gathered = f32[8,3,16,128]{3,2,1,0:T(8,128)S(1)} all-to-all(f32[8,3,16,128]{3,2,1,0:T(8,128)S(1)} %get-tuple-element.51), channel_id=1, replica_groups={{15,12,11,8,7,4,3,0},{14,13,10,9,6,5,2,1},{31,28,27,24,23,20,19,16},{30..., dimensions={0} | all-to-all | bytes 393216 | tf_op jit(solution)/shard_map/all_to_all | solution.py:886
  28.7 3.2 %shard_map.64 = (f32[4,64,128]{2,1,0:T(8,128)}, f32[1,16,32]{2,1,0:T(8,128)}) custom-call(s32[16]{0:T(128)S(1)} %copy-done, f32[8,3,16,128]{3,2,1,0:T(8,128)S(1)} %all_to_all.5.gathered, f32[4,32,128]{2,1,0:T(8,128)S(1)} %get-tuple-element.52.e2_in, f32[4,32,128]{2,1,0:T(8,128)S(1)} %get-tuple-element.53.s2_in, f32[4,32,128]{2,1,0:T(8,128)S(1)} %get-tuple-element.54.fx2_in, ...), custom_call_target="tpu_custom_call" | custom-call | tf_op jit(solution)/shard_map/pallas_call | solution.py:826
Async XLA Ops:
  1.7 0.7 %copy-start = (s32[16]{0:T(128)S(1)}, s32[16]{0:T(128)}, u32[]{:S(2)}) copy-start(s32[16]{0:T(128)} %owner_of.3) | copy-start | bytes 196
  1.9 1.5 %collective-permute-start = (f32[224,128]{1,0:T(8,128)S(1)}, f32[224,128]{1,0:T(8,128)S(1)}, u32[]{:S(2)}, u32[]{:S(2)}) collective-permute-start(f32[224,128]{1,0:T(8,128)S(1)} %shard_map.60), channel_id=1, source_target_pairs={{0,1},{1,0},{2,3},{3,2},{4,5},{5,4},{6,7},{7,6},{8,9},{9,8},{10,11... | collective-permute-start | bytes 344072 | tf_op jit(solution)/shard_map/ppermute | solution.py:19
  3.8 0.7 %collective-permute-start.1 = (f32[384,128]{1,0:T(8,128)S(1)}, f32[384,128]{1,0:T(8,128)S(1)}, u32[]{:S(2)}, u32[]{:S(2)}) collective-permute-start(f32[384,128]{1,0:T(8,128)S(1)} %get-tuple-element.45.message), channel_id=1, source_target_pairs={{1,2},{2,1},{3,4},{4,3},{5,6},{6,5},{7,8},{8,7},{9,10},{10,9},{11,... | collective-permute-start | bytes 589832 | tf_op jit(solution)/shard_map/ppermute | solution.py:15
  5.0 10.0 %collective-permute-start.2 = (f32[9,32,128]{2,1,0:T(8,128)S(1)}, f32[9,32,128]{2,1,0:T(8,128)S(1)}, u32[]{:S(2)}, u32[]{:S(2)}) collective-permute-start(f32[9,32,128]{2,1,0:T(8,128)S(1)} %get-tuple-element.49.own), channel_id=1, source_target_pairs={{0,1},{1,0},{2,3},{3,2},{4,5},{5,4},{6,7},{7,6},{8,9},{9,8},{10,11... | collective-permute-start | bytes 442376 | tf_op jit(solution)/shard_map/ppermute | solution.py:19

commit v16 on v15

--- a/solution.py
+++ b/solution.py
@@ -17,6 +17,16 @@
 
 def within_chip(block):
     return lax.ppermute(block, "gx", [(i, i ^ 1) for i in range(lax.axis_size("gx"))])
+
+
+def chip_order(chips):
+    half = chips // 2
+    return [0, *range(chips - 2, half - 1, -1), chips - 1, *range(half - 1, 0, -1)]
+
+
+def place_of(chip, chips):
+    late = jnp.where(chip == chips - 1, chips // 2, chips - 1 - chip)
+    return jnp.where(chip >= chips // 2, late, (chips - chip) % chips)
 
 
 def by_side(across, within):
@@ -690,7 +700,8 @@
 
     slot = lanes_of((quarter, lanes)) & 3
     spread = blocks // 4
-    tiles = [gathered[chip, k] for chip in reversed(range(chips)) for k in range(2)]
+    order = chip_order(chips)
+    tiles = [gathered[order.index(chip), k] for chip in range(chips) for k in range(2)]
     items = []
     for k in range(4):
         packs = []
@@ -726,7 +737,7 @@
         ref.at[pl.ds(core, 3)] for ref in (s2_in, fx2_in, fxl2_in, fy2_in, fz2_in, fzl2_in, inv2_in)
     ]
     next_chip = jnp.clip(position // 2 - 1 + 2 * core, 0, chips - 1)
-    into_both_rows(pair.at[5], gathered[chips - 1 - next_chip, 2])
+    into_both_rows(pair.at[5], gathered[place_of(next_chip, chips), 2])
     halo = pair[5]
     before = (
         by_side(halo, e2_in[0])[0], by_side(jnp.where(first_of_two, halo, e2_in[0]), e2_in[1])[0],
@@ -882,7 +893,7 @@
         [vmem(6, padded2, depth), vmem(3, *tile)],
         (within, fx2, within_in),
     )
-    kinds = [[2 * chip + (chip + core) % 2 for chip in reversed(range(blocks // 2))] for core in range(2)]
+    kinds = [[2 * chip + (chip + core) % 2 for chip in chip_order(blocks // 2)] for core in range(2)]
     gathered = lax.all_to_all(slots, "gx", 0, 0, axis_index_groups=kinds, tiled=True)
     solved, owned = call(
         coarse_kernel,

time: 32.1 us -> 33.3 us (1.037)
  blocking collectives: 13.2 us -> 14.4 us
    all_to_all x1, blocking collectives: 13.2 us -> 14.4 us  [on_device(): lax.all_to_all(slots, 'gx', 0, 0, axis_index_groups=kinds, tiled=True)]
where the time goes in v16:
time: 33.3 us; the launch traced here: 33.1 us
  blocking collectives  14.4 us (43%)
  starting transfers between devices  10.1 us (30%)
  Pallas kernels  4.97 us (15%)
  waiting for transfers between devices  1.77 us (5%)
  other arithmetic  1.06 us (3%)
  between operations  0.69 us (2%)
    all_to_all x1, blocking collectives, on_device(): lax.all_to_all(slots, 'gx', 0, 0, axis_index_groups=kinds, tiled=True)  14.4 us
    ppermute x2, starting transfers between devices, within_chip(): lax.ppermute(block, 'gx', [(i, i ^ 1) for i in range(lax.axis_size('gx'))])  9.46 us
    pallas_call x6, Pallas kernels, call(): pl.pallas_call(kernel, out_shape=tuple(outs), in_specs=[pl.BlockSpec(memo...  4.97 us
    ppermute x2, waiting for transfers between devices, within_chip(): lax.ppermute(block, 'gx', [(i, i ^ 1) for i in range(lax.axis_size('gx'))])  1.77 us
    add x1, other arithmetic, on_device(): sum((jnp.pad(block, ((k * layers, (2 - k) * layers), (0, 0), (0, 0))) for...  1.06 us
    ppermute x1, starting transfers between devices, between_chips(): lax.ppermute(block, 'gx', [(i, i + 1 if i % 2 else i - 1) for i in range(...  0.68 us
  transfers between devices with their start and end apart: 3, of which 2 were waited for; matrix products, arithmetic and copies ran while one was open for 0% of the time, Pallas kernels for 1%

profile of v16, /device:TPU:0, one launch (start us, length us, event | category | flops | bytes accessed | tf_op | source)
XLA Modules:
  0.0 33.1 jit_solution(452871452005934233)
XLA Ops:
  0.6 1.1 %pad_add_fusion.inputs = f32[12,64,128]{2,1,0:T(8,128)S(1)} fusion(f32[4,64,128]{2,1,0:T(8,128)} %param.6, f32[4,64,128]{2,1,0:T(8,128)} %param.5, f32[4,64,128]{2,1,0:T(8,128)} %param.4), kind=kLoop, calls=%fused_computation | loop fusion | flops 196608 | bytes 786432 | tf_op jit(solution)/shard_map/add | solution.py:852
  1.7 0.0 copy-start
  1.7 0.2 shard_map.60
  1.9 0.5 %collective-permute-start = (f32[224,128]{1,0:T(8,128)S(1)}, f32[224,128]{1,0:T(8,128)S(1)}, u32[]{:S(2)}, u32[]{:S(2)}) collective-permute-start(f32[224,128]{1,0:T(8,128)S(1)} %shard_map.60), channel_id=1, source_target_pairs={{0,1},{1,0},{2,3},{3,2},{4,5},{5,4},{6,7},{7,6},{8,9},{9,8},{10,11... | collective-permute-start | bytes 344072 | tf_op jit(solution)/shard_map/ppermute | solution.py:19
  2.4 0.0 copy-done
  2.4 0.2 shard_map.59
  2.6 0.8 %collective-permute-done.within_in = f32[224,128]{1,0:T(8,128)S(1)} collective-permute-done((f32[224,128]{1,0:T(8,128)S(1)}, f32[224,128]{1,0:T(8,128)S(1)}, u32[]{:S(2)}, u32[]{:S(2)}) %collective-permute-start) | collective-permute-done | bytes 114720 | tf_op jit(solution)/shard_map/ppermute | solution.py:19
  3.4 0.4 %shard_map.61 = (f32[384,128]{1,0:T(8,128)S(1)}, f32[2,32,128]{2,1,0:T(8,128)S(1)}, f32[64,128]{1,0:T(8,128)S(1)}, f32[3,64,128]{2,1,0:T(8,128)S(1)}, f32[2,64,1...) custom-call(f32[12,64,128]{2,1,0:T(8,128)S(1)} %pad_add_fusion.input, ...), custom_call_target="tpu_custom_call" | custom-call | tf_op jit(solution)/shard_map/pallas_call | solution.py:837
  3.8 0.7 %collective-permute-start.1 = (f32[384,128]{1,0:T(8,128)S(1)}, f32[384,128]{1,0:T(8,128)S(1)}, u32[]{:S(2)}, u32[]{:S(2)}) collective-permute-start(f32[384,128]{1,0:T(8,128)S(1)} %get-tuple-element.45.message), channel_id=1, source_target_pairs={{1,2},{2,1},{3,4},{4,3},{5,6},{6,5},{7,8},{8,7},{9,10},{10,9},{11,... | collective-permute-start | bytes 589832 | tf_op jit(solution)/shard_map/ppermute | solution.py:15
  4.5 0.0 collective-permute-done.1.across_in
  4.5 0.5 %shard_map.62 = (f32[9,32,128]{2,1,0:T(8,128)S(1)}, f32[32,128]{1,0:T(8,128)S(1)}, f32[3,64,128]{2,1,0:T(8,128)S(1)}, f32[64,128]{1,0:T(8,128)S(1)}, f32[2,64,12...) custom-call(f32[12,64,128]{2,1,0:T(8,128)S(1)} %pad_add_fusion.input, ...), custom_call_target="tpu_custom_call" | custom-call | tf_op jit(solution)/shard_map/pallas_call | solution.py:837
  5.0 8.9 %collective-permute-start.2 = (f32[9,32,128]{2,1,0:T(8,128)S(1)}, f32[9,32,128]{2,1,0:T(8,128)S(1)}, u32[]{:S(2)}, u32[]{:S(2)}) collective-permute-start(f32[9,32,128]{2,1,0:T(8,128)S(1)} %get-tuple-element.49.own), channel_id=1, source_target_pairs={{0,1},{1,0},{2,3},{3,2},{4,5},{5,4},{6,7},{7,6},{8,9},{9,8},{10,11... | collective-permute-start | bytes 442376 | tf_op jit(solution)/shard_map/ppermute | solution.py:19
  13.9 1.0 %collective-permute-done.2.within_in = f32[9,32,128]{2,1,0:T(8,128)S(1)} collective-permute-done((f32[9,32,128]{2,1,0:T(8,128)S(1)}, f32[9,32,128]{2,1,0:T(8,128)S(1)}, u32[]{:S(2)}, u32[]{:S(2)}) %collective-permute-start.2) | collective-permute-done | bytes 147488 | tf_op jit(solution)/shard_map/ppermute | solution.py:19
  14.9 0.5 %shard_map.63 = (f32[8,3,16,128]{3,2,1,0:T(8,128)S(1)}, f32[4,32,128]{2,1,0:T(8,128)S(1)}, f32[4,32,128]{2,1,0:T(8,128)S(1)}, f32[4,32,128]{2,1,0:T(8,128)S(1)},...) custom-call(f32[9,32,128]{2,1,0:T(8,128)S(1)} %get-tuple-element.49., ...), custom_call_target="tpu_custom_call" | custom-call | tf_op jit(solution)/shard_map/pallas_call | solution.py:837
  15.5 14.4 %all_to_all.5.gathered = f32[8,3,16,128]{3,2,1,0:T(8,128)S(1)} all-to-all(f32[8,3,16,128]{3,2,1,0:T(8,128)S(1)} %get-tuple-element.51), channel_id=1, replica_groups={{0,12,11,8,15,7,4,3},{1,13,10,9,14,6,5,2},{16,28,27,24,31,23,20,19},{17..., dimensions={0} | all-to-all | bytes 393216 | tf_op jit(solution)/shard_map/all_to_all | solution.py:897
  29.9 3.2 %shard_map.64 = (f32[4,64,128]{2,1,0:T(8,128)}, f32[1,16,32]{2,1,0:T(8,128)}) custom-call(s32[16]{0:T(128)S(1)} %copy-done, f32[8,3,16,128]{3,2,1,0:T(8,128)S(1)} %all_to_all.5.gathered, f32[4,32,128]{2,1,0:T(8,128)S(1)} %get-tuple-element.52.e2_in, f32[4,32,128]{2,1,0:T(8,128)S(1)} %get-tuple-element.53.s2_in, f32[4,32,128]{2,1,0:T(8,128)S(1)} %get-tuple-element.54.fx2_in, ...), custom_call_target="tpu_custom_call" | custom-call | tf_op jit(solution)/shard_map/pallas_call | solution.py:837
Async XLA Ops:
  1.7 0.7 %copy-start = (s32[16]{0:T(128)S(1)}, s32[16]{0:T(128)}, u32[]{:S(2)}) copy-start(s32[16]{0:T(128)} %owner_of.3) | copy-start | bytes 196
  1.9 1.5 %collective-permute-start = (f32[224,128]{1,0:T(8,128)S(1)}, f32[224,128]{1,0:T(8,128)S(1)}, u32[]{:S(2)}, u32[]{:S(2)}) collective-permute-start(f32[224,128]{1,0:T(8,128)S(1)} %shard_map.60), channel_id=1, source_target_pairs={{0,1},{1,0},{2,3},{3,2},{4,5},{5,4},{6,7},{7,6},{8,9},{9,8},{10,11... | collective-permute-start | bytes 344072 | tf_op jit(solution)/shard_map/ppermute | solution.py:19
  3.8 0.7 %collective-permute-start.1 = (f32[384,128]{1,0:T(8,128)S(1)}, f32[384,128]{1,0:T(8,128)S(1)}, u32[]{:S(2)}, u32[]{:S(2)}) collective-permute-start(f32[384,128]{1,0:T(8,128)S(1)} %get-tuple-element.45.message), channel_id=1, source_target_pairs={{1,2},{2,1},{3,4},{4,3},{5,6},{6,5},{7,8},{8,7},{9,10},{10,9},{11,... | collective-permute-start | bytes 589832 | tf_op jit(solution)/shard_map/ppermute | solution.py:15
  5.0 10.0 %collective-permute-start.2 = (f32[9,32,128]{2,1,0:T(8,128)S(1)}, f32[9,32,128]{2,1,0:T(8,128)S(1)}, u32[]{:S(2)}, u32[]{:S(2)}) collective-permute-start(f32[9,32,128]{2,1,0:T(8,128)S(1)} %get-tuple-element.49.own), channel_id=1, source_target_pairs={{0,1},{1,0},{2,3},{3,2},{4,5},{5,4},{6,7},{7,6},{8,9},{9,8},{10,11... | collective-permute-start | bytes 442376 | tf_op jit(solution)/shard_map/ppermute | solution.py:19

commit v17 on v15

--- a/solution.py
+++ b/solution.py
@@ -690,7 +690,12 @@
 
     slot = lanes_of((quarter, lanes)) & 3
     spread = blocks // 4
-    tiles = [gathered[chip, k] for chip in reversed(range(chips)) for k in range(2)]
+    downwards = (position // 2 + position) % 2
+
+    def place(chip):
+        return chip + downwards * (chips - 1 - 2 * chip)
+
+    tiles = [gathered[place(chip), k] for chip in range(chips) for k in range(2)]
     items = []
     for k in range(4):
         packs = []
@@ -726,7 +731,7 @@
         ref.at[pl.ds(core, 3)] for ref in (s2_in, fx2_in, fxl2_in, fy2_in, fz2_in, fzl2_in, inv2_in)
     ]
     next_chip = jnp.clip(position // 2 - 1 + 2 * core, 0, chips - 1)
-    into_both_rows(pair.at[5], gathered[chips - 1 - next_chip, 2])
+    into_both_rows(pair.at[5], gathered[place(next_chip), 2])
     halo = pair[5]
     before = (
         by_side(halo, e2_in[0])[0], by_side(jnp.where(first_of_two, halo, e2_in[0]), e2_in[1])[0],
@@ -882,7 +887,9 @@
         [vmem(6, padded2, depth), vmem(3, *tile)],
         (within, fx2, within_in),
     )
-    kinds = [[2 * chip + (chip + core) % 2 for chip in reversed(range(blocks // 2))] for core in range(2)]
+    up = [2 * chip + chip % 2 for chip in range(blocks // 2)]
+    down = [device ^ 1 for device in reversed(up)]
+    kinds = [up, down]
     gathered = lax.all_to_all(slots, "gx", 0, 0, axis_index_groups=kinds, tiled=True)
     solved, owned = call(
         coarse_kernel,

time: 32.1 us -> 32.5 us (1.012)
  Pallas kernels: 4.97 us -> 5.42 us
    pallas_call x6, Pallas kernels: 4.97 us -> 5.42 us  [call(): pl.pallas_call(kernel, out_shape=tuple(outs), in_specs=[pl.BlockSpec(memo...]
where the time goes in v17:
time: 32.5 us; the launch traced here: 32.3 us
  blocking collectives  13.2 us (41%)
  starting transfers between devices  10.1 us (31%)
  Pallas kernels  5.42 us (17%)
  waiting for transfers between devices  1.77 us (5%)
  other arithmetic  1.06 us (3%)
  between operations  0.69 us (2%)
    all_to_all x1, blocking collectives, on_device(): lax.all_to_all(slots, 'gx', 0, 0, axis_index_groups=kinds, tiled=True)  13.2 us
    ppermute x2, starting transfers between devices, within_chip(): lax.ppermute(block, 'gx', [(i, i ^ 1) for i in range(lax.axis_size('gx'))])  9.46 us
    pallas_call x6, Pallas kernels, call(): pl.pallas_call(kernel, out_shape=tuple(outs), in_specs=[pl.BlockSpec(memo...  5.42 us
    ppermute x2, waiting for transfers between devices, within_chip(): lax.ppermute(block, 'gx', [(i, i ^ 1) for i in range(lax.axis_size('gx'))])  1.77 us
    add x1, other arithmetic, on_device(): sum((jnp.pad(block, ((k * layers, (2 - k) * layers), (0, 0), (0, 0))) for...  1.06 us
    ppermute x1, starting transfers between devices, between_chips(): lax.ppermute(block, 'gx', [(i, i + 1 if i % 2 else i - 1) for i in range(...  0.68 us
  transfers between devices with their start and end apart: 3, of which 2 were waited for; matrix products, arithmetic and copies ran while one was open for 0% of the time, Pallas kernels for 1%

profile of v17, /device:TPU:0, one launch (start us, length us, event | category | flops | bytes accessed | tf_op | source)
XLA Modules:
  0.0 32.3 jit_solution(11842550247583213651)
XLA Ops:
  0.6 1.1 %pad_add_fusion.inputs = f32[12,64,128]{2,1,0:T(8,128)S(1)} fusion(f32[4,64,128]{2,1,0:T(8,128)} %param.6, f32[4,64,128]{2,1,0:T(8,128)} %param.5, f32[4,64,128]{2,1,0:T(8,128)} %param.4), kind=kLoop, calls=%fused_computation | loop fusion | flops 196608 | bytes 786432 | tf_op jit(solution)/shard_map/add | solution.py:846
  1.7 0.0 copy-start
  1.7 0.2 shard_map.60
  1.9 0.5 %collective-permute-start = (f32[224,128]{1,0:T(8,128)S(1)}, f32[224,128]{1,0:T(8,128)S(1)}, u32[]{:S(2)}, u32[]{:S(2)}) collective-permute-start(f32[224,128]{1,0:T(8,128)S(1)} %shard_map.60), channel_id=1, source_target_pairs={{0,1},{1,0},{2,3},{3,2},{4,5},{5,4},{6,7},{7,6},{8,9},{9,8},{10,11... | collective-permute-start | bytes 344072 | tf_op jit(solution)/shard_map/ppermute | solution.py:19
  2.4 0.0 copy-done
  2.4 0.2 shard_map.59
  2.6 0.8 %collective-permute-done.within_in = f32[224,128]{1,0:T(8,128)S(1)} collective-permute-done((f32[224,128]{1,0:T(8,128)S(1)}, f32[224,128]{1,0:T(8,128)S(1)}, u32[]{:S(2)}, u32[]{:S(2)}) %collective-permute-start) | collective-permute-done | bytes 114720 | tf_op jit(solution)/shard_map/ppermute | solution.py:19
  3.4 0.4 %shard_map.61 = (f32[384,128]{1,0:T(8,128)S(1)}, f32[2,32,128]{2,1,0:T(8,128)S(1)}, f32[64,128]{1,0:T(8,128)S(1)}, f32[3,64,128]{2,1,0:T(8,128)S(1)}, f32[2,64,1...) custom-call(f32[12,64,128]{2,1,0:T(8,128)S(1)} %pad_add_fusion.input, ...), custom_call_target="tpu_custom_call" | custom-call | tf_op jit(solution)/shard_map/pallas_call | solution.py:831
  3.8 0.7 %collective-permute-start.1 = (f32[384,128]{1,0:T(8,128)S(1)}, f32[384,128]{1,0:T(8,128)S(1)}, u32[]{:S(2)}, u32[]{:S(2)}) collective-permute-start(f32[384,128]{1,0:T(8,128)S(1)} %get-tuple-element.45.message), channel_id=1, source_target_pairs={{1,2},{2,1},{3,4},{4,3},{5,6},{6,5},{7,8},{8,7},{9,10},{10,9},{11,... | collective-permute-start | bytes 589832 | tf_op jit(solution)/shard_map/ppermute | solution.py:15
  4.5 0.0 collective-permute-done.1.across_in
  4.5 0.5 %shard_map.62 = (f32[9,32,128]{2,1,0:T(8,128)S(1)}, f32[32,128]{1,0:T(8,128)S(1)}, f32[3,64,128]{2,1,0:T(8,128)S(1)}, f32[64,128]{1,0:T(8,128)S(1)}, f32[2,64,12...) custom-call(f32[12,64,128]{2,1,0:T(8,128)S(1)} %pad_add_fusion.input, ...), custom_call_target="tpu_custom_call" | custom-call | tf_op jit(solution)/shard_map/pallas_call | solution.py:831
  5.0 8.9 %collective-permute-start.2 = (f32[9,32,128]{2,1,0:T(8,128)S(1)}, f32[9,32,128]{2,1,0:T(8,128)S(1)}, u32[]{:S(2)}, u32[]{:S(2)}) collective-permute-start(f32[9,32,128]{2,1,0:T(8,128)S(1)} %get-tuple-element.49.own), channel_id=1, source_target_pairs={{0,1},{1,0},{2,3},{3,2},{4,5},{5,4},{6,7},{7,6},{8,9},{9,8},{10,11... | collective-permute-start | bytes 442376 | tf_op jit(solution)/shard_map/ppermute | solution.py:19
  13.9 1.0 %collective-permute-done.2.within_in = f32[9,32,128]{2,1,0:T(8,128)S(1)} collective-permute-done((f32[9,32,128]{2,1,0:T(8,128)S(1)}, f32[9,32,128]{2,1,0:T(8,128)S(1)}, u32[]{:S(2)}, u32[]{:S(2)}) %collective-permute-start.2) | collective-permute-done | bytes 147488 | tf_op jit(solution)/shard_map/ppermute | solution.py:19
  14.9 0.5 %shard_map.63 = (f32[8,3,16,128]{3,2,1,0:T(8,128)S(1)}, f32[4,32,128]{2,1,0:T(8,128)S(1)}, f32[4,32,128]{2,1,0:T(8,128)S(1)}, f32[4,32,128]{2,1,0:T(8,128)S(1)},...) custom-call(f32[9,32,128]{2,1,0:T(8,128)S(1)} %get-tuple-element.49., ...), custom_call_target="tpu_custom_call" | custom-call | tf_op jit(solution)/shard_map/pallas_call | solution.py:831
  15.5 13.2 %all_to_all.5.gathered = f32[8,3,16,128]{3,2,1,0:T(8,128)S(1)} all-to-all(f32[8,3,16,128]{3,2,1,0:T(8,128)S(1)} %get-tuple-element.51), channel_id=1, replica_groups={{0,3,4,7,8,11,12,15},{14,13,10,9,6,5,2,1},{16,19,20,23,24,27,28,31},{30..., dimensions={0} | all-to-all | bytes 393216 | tf_op jit(solution)/shard_map/all_to_all | solution.py:893
  28.7 3.6 %shard_map.64 = (f32[4,64,128]{2,1,0:T(8,128)}, f32[1,16,32]{2,1,0:T(8,128)}) custom-call(s32[16]{0:T(128)S(1)} %copy-done, f32[8,3,16,128]{3,2,1,0:T(8,128)S(1)} %all_to_all.5.gathered, f32[4,32,128]{2,1,0:T(8,128)S(1)} %get-tuple-element.52.e2_in, f32[4,32,128]{2,1,0:T(8,128)S(1)} %get-tuple-element.53.s2_in, f32[4,32,128]{2,1,0:T(8,128)S(1)} %get-tuple-element.54.fx2_in, ...), custom_call_target="tpu_custom_call" | custom-call | tf_op jit(solution)/shard_map/pallas_call | solution.py:831
Async XLA Ops:
  1.7 0.7 %copy-start = (s32[16]{0:T(128)S(1)}, s32[16]{0:T(128)}, u32[]{:S(2)}) copy-start(s32[16]{0:T(128)} %owner_of.3) | copy-start | bytes 196
  1.9 1.5 %collective-permute-start = (f32[224,128]{1,0:T(8,128)S(1)}, f32[224,128]{1,0:T(8,128)S(1)}, u32[]{:S(2)}, u32[]{:S(2)}) collective-permute-start(f32[224,128]{1,0:T(8,128)S(1)} %shard_map.60), channel_id=1, source_target_pairs={{0,1},{1,0},{2,3},{3,2},{4,5},{5,4},{6,7},{7,6},{8,9},{9,8},{10,11... | collective-permute-start | bytes 344072 | tf_op jit(solution)/shard_map/ppermute | solution.py:19
  3.8 0.7 %collective-permute-start.1 = (f32[384,128]{1,0:T(8,128)S(1)}, f32[384,128]{1,0:T(8,128)S(1)}, u32[]{:S(2)}, u32[]{:S(2)}) collective-permute-start(f32[384,128]{1,0:T(8,128)S(1)} %get-tuple-element.45.message), channel_id=1, source_target_pairs={{1,2},{2,1},{3,4},{4,3},{5,6},{6,5},{7,8},{8,7},{9,10},{10,9},{11,... | collective-permute-start | bytes 589832 | tf_op jit(solution)/shard_map/ppermute | solution.py:15
  5.0 10.0 %collective-permute-start.2 = (f32[9,32,128]{2,1,0:T(8,128)S(1)}, f32[9,32,128]{2,1,0:T(8,128)S(1)}, u32[]{:S(2)}, u32[]{:S(2)}) collective-permute-start(f32[9,32,128]{2,1,0:T(8,128)S(1)} %get-tuple-element.49.own), channel_id=1, source_target_pairs={{0,1},{1,0},{2,3},{3,2},{4,5},{5,4},{6,7},{7,6},{8,9},{9,8},{10,11... | collective-permute-start | bytes 442376 | tf_op jit(solution)/shard_map/ppermute | solution.py:19

commit v18 on v15

--- a/solution.py
+++ b/solution.py
@@ -17,6 +17,10 @@
 
 def within_chip(block):
     return lax.ppermute(block, "gx", [(i, i ^ 1) for i in range(lax.axis_size("gx"))])
+
+
+def chip_order(chips, kind):
+    return [-(1, 3)[kind] * i % chips for i in range(chips)]
 
 
 def by_side(across, within):
@@ -690,7 +694,13 @@
 
     slot = lanes_of((quarter, lanes)) & 3
     spread = blocks // 4
-    tiles = [gathered[chip, k] for chip in reversed(range(chips)) for k in range(2)]
+    orders = [chip_order(chips, kind) for kind in range(2)]
+    kind = (position // 2 + position) % 2
+
+    def from_chip(chip, k):
+        return jnp.where(kind == 0, gathered[orders[0].index(chip), k], gathered[orders[1].index(chip), k])
+
+    tiles = [from_chip(chip, k) for chip in range(chips) for k in range(2)]
     items = []
     for k in range(4):
         packs = []
@@ -726,7 +736,7 @@
         ref.at[pl.ds(core, 3)] for ref in (s2_in, fx2_in, fxl2_in, fy2_in, fz2_in, fzl2_in, inv2_in)
     ]
     next_chip = jnp.clip(position // 2 - 1 + 2 * core, 0, chips - 1)
-    into_both_rows(pair.at[5], gathered[chips - 1 - next_chip, 2])
+    into_both_rows(pair.at[5], gathered[next_chip * jnp.where(kind == 0, chips - 1, pow(-3, -1, chips)) % chips, 2])
     halo = pair[5]
     before = (
         by_side(halo, e2_in[0])[0], by_side(jnp.where(first_of_two, halo, e2_in[0]), e2_in[1])[0],
@@ -882,7 +892,8 @@
         [vmem(6, padded2, depth), vmem(3, *tile)],
         (within, fx2, within_in),
     )
-    kinds = [[2 * chip + (chip + core) % 2 for chip in reversed(range(blocks // 2))] for core in range(2)]
+    chips = blocks // 2
+    kinds = [[2 * chip + (chip + core) % 2 for chip in chip_order(chips, core)] for core in range(2)]
     gathered = lax.all_to_all(slots, "gx", 0, 0, axis_index_groups=kinds, tiled=True)
     solved, owned = call(
         coarse_kernel,

time: 32.1 us -> 32.7 us (1.019)
  blocking collectives: 13.2 us -> 13.9 us
    all_to_all x1, blocking collectives: 13.2 us -> 13.9 us  [on_device(): lax.all_to_all(slots, 'gx', 0, 0, axis_index_groups=kinds, tiled=True)]
where the time goes in v18:
time: 32.7 us; the launch traced here: 32.5 us
  blocking collectives  13.9 us (43%)
  starting transfers between devices  10.1 us (31%)
  Pallas kernels  4.98 us (15%)
  waiting for transfers between devices  1.77 us (5%)
  other arithmetic  1.06 us (3%)
  between operations  0.69 us (2%)
    all_to_all x1, blocking collectives, on_device(): lax.all_to_all(slots, 'gx', 0, 0, axis_index_groups=kinds, tiled=True)  13.9 us
    ppermute x2, starting transfers between devices, within_chip(): lax.ppermute(block, 'gx', [(i, i ^ 1) for i in range(lax.axis_size('gx'))])  9.46 us
    pallas_call x6, Pallas kernels, call(): pl.pallas_call(kernel, out_shape=tuple(outs), in_specs=[pl.BlockSpec(memo...  4.98 us
    ppermute x2, waiting for transfers between devices, within_chip(): lax.ppermute(block, 'gx', [(i, i ^ 1) for i in range(lax.axis_size('gx'))])  1.77 us
    add x1, other arithmetic, on_device(): sum((jnp.pad(block, ((k * layers, (2 - k) * layers), (0, 0), (0, 0))) for...  1.06 us
    ppermute x1, starting transfers between devices, between_chips(): lax.ppermute(block, 'gx', [(i, i + 1 if i % 2 else i - 1) for i in range(...  0.68 us
  transfers between devices with their start and end apart: 3, of which 2 were waited for; matrix products, arithmetic and copies ran while one was open for 0% of the time, Pallas kernels for 1%

profile of v18, /device:TPU:0, one launch (start us, length us, event | category | flops | bytes accessed | tf_op | source)
XLA Modules:
  0.0 32.5 jit_solution(1376049165162237214)
XLA Ops:
  0.6 1.1 %pad_add_fusion.inputs = f32[12,64,128]{2,1,0:T(8,128)S(1)} fusion(f32[4,64,128]{2,1,0:T(8,128)} %param.6, f32[4,64,128]{2,1,0:T(8,128)} %param.5, f32[4,64,128]{2,1,0:T(8,128)} %param.4), kind=kLoop, calls=%fused_computation | loop fusion | flops 196608 | bytes 786432 | tf_op jit(solution)/shard_map/add | solution.py:851
  1.7 0.0 copy-start
  1.7 0.2 shard_map.60
  1.9 0.5 %collective-permute-start = (f32[224,128]{1,0:T(8,128)S(1)}, f32[224,128]{1,0:T(8,128)S(1)}, u32[]{:S(2)}, u32[]{:S(2)}) collective-permute-start(f32[224,128]{1,0:T(8,128)S(1)} %shard_map.60), channel_id=1, source_target_pairs={{0,1},{1,0},{2,3},{3,2},{4,5},{5,4},{6,7},{7,6},{8,9},{9,8},{10,11... | collective-permute-start | bytes 344072 | tf_op jit(solution)/shard_map/ppermute | solution.py:19
  2.4 0.0 copy-done
  2.4 0.2 shard_map.59
  2.6 0.8 %collective-permute-done.within_in = f32[224,128]{1,0:T(8,128)S(1)} collective-permute-done((f32[224,128]{1,0:T(8,128)S(1)}, f32[224,128]{1,0:T(8,128)S(1)}, u32[]{:S(2)}, u32[]{:S(2)}) %collective-permute-start) | collective-permute-done | bytes 114720 | tf_op jit(solution)/shard_map/ppermute | solution.py:19
  3.4 0.4 %shard_map.61 = (f32[384,128]{1,0:T(8,128)S(1)}, f32[2,32,128]{2,1,0:T(8,128)S(1)}, f32[64,128]{1,0:T(8,128)S(1)}, f32[3,64,128]{2,1,0:T(8,128)S(1)}, f32[2,64,1...) custom-call(f32[12,64,128]{2,1,0:T(8,128)S(1)} %pad_add_fusion.input, ...), custom_call_target="tpu_custom_call" | custom-call | tf_op jit(solution)/shard_map/pallas_call | solution.py:836
  3.8 0.7 %collective-permute-start.1 = (f32[384,128]{1,0:T(8,128)S(1)}, f32[384,128]{1,0:T(8,128)S(1)}, u32[]{:S(2)}, u32[]{:S(2)}) collective-permute-start(f32[384,128]{1,0:T(8,128)S(1)} %get-tuple-element.45.message), channel_id=1, source_target_pairs={{1,2},{2,1},{3,4},{4,3},{5,6},{6,5},{7,8},{8,7},{9,10},{10,9},{11,... | collective-permute-start | bytes 589832 | tf_op jit(solution)/shard_map/ppermute | solution.py:15
  4.5 0.0 collective-permute-done.1.across_in
  4.5 0.5 %shard_map.62 = (f32[9,32,128]{2,1,0:T(8,128)S(1)}, f32[32,128]{1,0:T(8,128)S(1)}, f32[3,64,128]{2,1,0:T(8,128)S(1)}, f32[64,128]{1,0:T(8,128)S(1)}, f32[2,64,12...) custom-call(f32[12,64,128]{2,1,0:T(8,128)S(1)} %pad_add_fusion.input, ...), custom_call_target="tpu_custom_call" | custom-call | tf_op jit(solution)/shard_map/pallas_call | solution.py:836
  5.0 8.9 %collective-permute-start.2 = (f32[9,32,128]{2,1,0:T(8,128)S(1)}, f32[9,32,128]{2,1,0:T(8,128)S(1)}, u32[]{:S(2)}, u32[]{:S(2)}) collective-permute-start(f32[9,32,128]{2,1,0:T(8,128)S(1)} %get-tuple-element.49.own), channel_id=1, source_target_pairs={{0,1},{1,0},{2,3},{3,2},{4,5},{5,4},{6,7},{7,6},{8,9},{9,8},{10,11... | collective-permute-start | bytes 442376 | tf_op jit(solution)/shard_map/ppermute | solution.py:19
  13.9 1.0 %collective-permute-done.2.within_in = f32[9,32,128]{2,1,0:T(8,128)S(1)} collective-permute-done((f32[9,32,128]{2,1,0:T(8,128)S(1)}, f32[9,32,128]{2,1,0:T(8,128)S(1)}, u32[]{:S(2)}, u32[]{:S(2)}) %collective-permute-start.2) | collective-permute-done | bytes 147488 | tf_op jit(solution)/shard_map/ppermute | solution.py:19
  14.9 0.5 %shard_map.63 = (f32[8,3,16,128]{3,2,1,0:T(8,128)S(1)}, f32[4,32,128]{2,1,0:T(8,128)S(1)}, f32[4,32,128]{2,1,0:T(8,128)S(1)}, f32[4,32,128]{2,1,0:T(8,128)S(1)},...) custom-call(f32[9,32,128]{2,1,0:T(8,128)S(1)} %get-tuple-element.49., ...), custom_call_target="tpu_custom_call" | custom-call | tf_op jit(solution)/shard_map/pallas_call | solution.py:836
  15.5 13.9 %all_to_all.5.gathered = f32[8,3,16,128]{3,2,1,0:T(8,128)S(1)} all-to-all(f32[8,3,16,128]{3,2,1,0:T(8,128)S(1)} %get-tuple-element.51), channel_id=1, replica_groups={{0,15,12,11,8,7,4,3},{1,10,5,14,9,2,13,6},{16,31,28,27,24,23,20,19},{17..., dimensions={0} | all-to-all | bytes 393216 | tf_op jit(solution)/shard_map/all_to_all | solution.py:897
  29.3 3.2 %shard_map.64 = (f32[4,64,128]{2,1,0:T(8,128)}, f32[1,16,32]{2,1,0:T(8,128)}) custom-call(s32[16]{0:T(128)S(1)} %copy-done, f32[8,3,16,128]{3,2,1,0:T(8,128)S(1)} %all_to_all.5.gathered, f32[4,32,128]{2,1,0:T(8,128)S(1)} %get-tuple-element.52.e2_in, f32[4,32,128]{2,1,0:T(8,128)S(1)} %get-tuple-element.53.s2_in, f32[4,32,128]{2,1,0:T(8,128)S(1)} %get-tuple-element.54.fx2_in, ...), custom_call_target="tpu_custom_call" | custom-call | tf_op jit(solution)/shard_map/pallas_call | solution.py:836
Async XLA Ops:
  1.7 0.7 %copy-start = (s32[16]{0:T(128)S(1)}, s32[16]{0:T(128)}, u32[]{:S(2)}) copy-start(s32[16]{0:T(128)} %owner_of.3) | copy-start | bytes 196
  1.9 1.5 %collective-permute-start = (f32[224,128]{1,0:T(8,128)S(1)}, f32[224,128]{1,0:T(8,128)S(1)}, u32[]{:S(2)}, u32[]{:S(2)}) collective-permute-start(f32[224,128]{1,0:T(8,128)S(1)} %shard_map.60), channel_id=1, source_target_pairs={{0,1},{1,0},{2,3},{3,2},{4,5},{5,4},{6,7},{7,6},{8,9},{9,8},{10,11... | collective-permute-start | bytes 344072 | tf_op jit(solution)/shard_map/ppermute | solution.py:19
  3.8 0.7 %collective-permute-start.1 = (f32[384,128]{1,0:T(8,128)S(1)}, f32[384,128]{1,0:T(8,128)S(1)}, u32[]{:S(2)}, u32[]{:S(2)}) collective-permute-start(f32[384,128]{1,0:T(8,128)S(1)} %get-tuple-element.45.message), channel_id=1, source_target_pairs={{1,2},{2,1},{3,4},{4,3},{5,6},{6,5},{7,8},{8,7},{9,10},{10,9},{11,... | collective-permute-start | bytes 589832 | tf_op jit(solution)/shard_map/ppermute | solution.py:15
  5.0 10.0 %collective-permute-start.2 = (f32[9,32,128]{2,1,0:T(8,128)S(1)}, f32[9,32,128]{2,1,0:T(8,128)S(1)}, u32[]{:S(2)}, u32[]{:S(2)}) collective-permute-start(f32[9,32,128]{2,1,0:T(8,128)S(1)} %get-tuple-element.49.own), channel_id=1, source_target_pairs={{0,1},{1,0},{2,3},{3,2},{4,5},{5,4},{6,7},{7,6},{8,9},{9,8},{10,11... | collective-permute-start | bytes 442376 | tf_op jit(solution)/shard_map/ppermute | solution.py:19

commit v19 on v18

--- a/solution.py
+++ b/solution.py
@@ -20,7 +20,7 @@
 
 
 def chip_order(chips, kind):
-    return [-(1, 3)[kind] * i % chips for i in range(chips)]
+    return list(reversed(range(chips))) if kind == 0 else list(range(chips))
 
 
 def by_side(across, within):
@@ -736,7 +736,7 @@
         ref.at[pl.ds(core, 3)] for ref in (s2_in, fx2_in, fxl2_in, fy2_in, fz2_in, fzl2_in, inv2_in)
     ]
     next_chip = jnp.clip(position // 2 - 1 + 2 * core, 0, chips - 1)
-    into_both_rows(pair.at[5], gathered[next_chip * jnp.where(kind == 0, chips - 1, pow(-3, -1, chips)) % chips, 2])
+    into_both_rows(pair.at[5], gathered[jnp.where(kind == 0, chips - 1 - next_chip, next_chip), 2])
     halo = pair[5]
     before = (
         by_side(halo, e2_in[0])[0], by_side(jnp.where(first_of_two, halo, e2_in[0]), e2_in[1])[0],

time: 32.7 us -> 32.2 us (0.985)
  blocking collectives: 13.9 us -> 13.4 us
    all_to_all x1, blocking collectives: 13.9 us -> 13.4 us  [on_device(): lax.all_to_all(slots, 'gx', 0, 0, axis_index_groups=kinds, tiled=True)]
where the time goes in v19:
time: 32.2 us; the launch traced here: 32 us
  blocking collectives  13.4 us (42%)
  starting transfers between devices  10.1 us (31%)
  Pallas kernels  4.98 us (15%)
  waiting for transfers between devices  1.77 us (5%)
  other arithmetic  1.06 us (3%)
  between operations  0.69 us (2%)
    all_to_all x1, blocking collectives, on_device(): lax.all_to_all(slots, 'gx', 0, 0, axis_index_groups=kinds, tiled=True)  13.4 us
    ppermute x2, starting transfers between devices, within_chip(): lax.ppermute(block, 'gx', [(i, i ^ 1) for i in range(lax.axis_size('gx'))])  9.46 us
    pallas_call x6, Pallas kernels, call(): pl.pallas_call(kernel, out_shape=tuple(outs), in_specs=[pl.BlockSpec(memo...  4.98 us
    ppermute x2, waiting for transfers between devices, within_chip(): lax.ppermute(block, 'gx', [(i, i ^ 1) for i in range(lax.axis_size('gx'))])  1.77 us
    add x1, other arithmetic, on_device(): sum((jnp.pad(block, ((k * layers, (2 - k) * layers), (0, 0), (0, 0))) for...  1.06 us
    ppermute x1, starting transfers between devices, between_chips(): lax.ppermute(block, 'gx', [(i, i + 1 if i % 2 else i - 1) for i in range(...  0.68 us
  transfers between devices with their start and end apart: 3, of which 2 were waited for; matrix products, arithmetic and copies ran while one was open for 0% of the time, Pallas kernels for 1%

profile of v19, /device:TPU:0, one launch (start us, length us, event | category | flops | bytes accessed | tf_op | source)
XLA Modules:
  0.0 32.0 jit_solution(11775283307155880944)
XLA Ops:
  0.6 1.1 %pad_add_fusion.inputs = f32[12,64,128]{2,1,0:T(8,128)S(1)} fusion(f32[4,64,128]{2,1,0:T(8,128)} %param.6, f32[4,64,128]{2,1,0:T(8,128)} %param.5, f32[4,64,128]{2,1,0:T(8,128)} %param.4), kind=kLoop, calls=%fused_computation | loop fusion | flops 196608 | bytes 786432 | tf_op jit(solution)/shard_map/add | solution.py:851
  1.7 0.0 copy-start
  1.7 0.2 shard_map.60
  1.9 0.5 %collective-permute-start = (f32[224,128]{1,0:T(8,128)S(1)}, f32[224,128]{1,0:T(8,128)S(1)}, u32[]{:S(2)}, u32[]{:S(2)}) collective-permute-start(f32[224,128]{1,0:T(8,128)S(1)} %shard_map.60), channel_id=1, source_target_pairs={{0,1},{1,0},{2,3},{3,2},{4,5},{5,4},{6,7},{7,6},{8,9},{9,8},{10,11... | collective-permute-start | bytes 344072 | tf_op jit(solution)/shard_map/ppermute | solution.py:19
  2.4 0.0 copy-done
  2.4 0.2 shard_map.59
  2.6 0.8 %collective-permute-done.within_in = f32[224,128]{1,0:T(8,128)S(1)} collective-permute-done((f32[224,128]{1,0:T(8,128)S(1)}, f32[224,128]{1,0:T(8,128)S(1)}, u32[]{:S(2)}, u32[]{:S(2)}) %collective-permute-start) | collective-permute-done | bytes 114720 | tf_op jit(solution)/shard_map/ppermute | solution.py:19
  3.4 0.4 %shard_map.61 = (f32[384,128]{1,0:T(8,128)S(1)}, f32[2,32,128]{2,1,0:T(8,128)S(1)}, f32[64,128]{1,0:T(8,128)S(1)}, f32[3,64,128]{2,1,0:T(8,128)S(1)}, f32[2,64,1...) custom-call(f32[12,64,128]{2,1,0:T(8,128)S(1)} %pad_add_fusion.input, ...), custom_call_target="tpu_custom_call" | custom-call | tf_op jit(solution)/shard_map/pallas_call | solution.py:836
  3.8 0.7 %collective-permute-start.1 = (f32[384,128]{1,0:T(8,128)S(1)}, f32[384,128]{1,0:T(8,128)S(1)}, u32[]{:S(2)}, u32[]{:S(2)}) collective-permute-start(f32[384,128]{1,0:T(8,128)S(1)} %get-tuple-element.45.message), channel_id=1, source_target_pairs={{1,2},{2,1},{3,4},{4,3},{5,6},{6,5},{7,8},{8,7},{9,10},{10,9},{11,... | collective-permute-start | bytes 589832 | tf_op jit(solution)/shard_map/ppermute | solution.py:15
  4.5 0.0 collective-permute-done.1.across_in
  4.5 0.5 %shard_map.62 = (f32[9,32,128]{2,1,0:T(8,128)S(1)}, f32[32,128]{1,0:T(8,128)S(1)}, f32[3,64,128]{2,1,0:T(8,128)S(1)}, f32[64,128]{1,0:T(8,128)S(1)}, f32[2,64,12...) custom-call(f32[12,64,128]{2,1,0:T(8,128)S(1)} %pad_add_fusion.input, ...), custom_call_target="tpu_custom_call" | custom-call | tf_op jit(solution)/shard_map/pallas_call | solution.py:836
  5.0 8.9 %collective-permute-start.2 = (f32[9,32,128]{2,1,0:T(8,128)S(1)}, f32[9,32,128]{2,1,0:T(8,128)S(1)}, u32[]{:S(2)}, u32[]{:S(2)}) collective-permute-start(f32[9,32,128]{2,1,0:T(8,128)S(1)} %get-tuple-element.49.own), channel_id=1, source_target_pairs={{0,1},{1,0},{2,3},{3,2},{4,5},{5,4},{6,7},{7,6},{8,9},{9,8},{10,11... | collective-permute-start | bytes 442376 | tf_op jit(solution)/shard_map/ppermute | solution.py:19
  13.9 1.0 %collective-permute-done.2.within_in = f32[9,32,128]{2,1,0:T(8,128)S(1)} collective-permute-done((f32[9,32,128]{2,1,0:T(8,128)S(1)}, f32[9,32,128]{2,1,0:T(8,128)S(1)}, u32[]{:S(2)}, u32[]{:S(2)}) %collective-permute-start.2) | collective-permute-done | bytes 147488 | tf_op jit(solution)/shard_map/ppermute | solution.py:19
  14.9 0.5 %shard_map.63 = (f32[8,3,16,128]{3,2,1,0:T(8,128)S(1)}, f32[4,32,128]{2,1,0:T(8,128)S(1)}, f32[4,32,128]{2,1,0:T(8,128)S(1)}, f32[4,32,128]{2,1,0:T(8,128)S(1)},...) custom-call(f32[9,32,128]{2,1,0:T(8,128)S(1)} %get-tuple-element.49., ...), custom_call_target="tpu_custom_call" | custom-call | tf_op jit(solution)/shard_map/pallas_call | solution.py:836
  15.5 13.4 %all_to_all.5.gathered = f32[8,3,16,128]{3,2,1,0:T(8,128)S(1)} all-to-all(f32[8,3,16,128]{3,2,1,0:T(8,128)S(1)} %get-tuple-element.51), channel_id=1, replica_groups={{15,12,11,8,7,4,3,0},{1,2,5,6,9,10,13,14},{31,28,27,24,23,20,19,16},{17..., dimensions={0} | all-to-all | bytes 393216 | tf_op jit(solution)/shard_map/all_to_all | solution.py:897
  28.8 3.2 %shard_map.64 = (f32[4,64,128]{2,1,0:T(8,128)}, f32[1,16,32]{2,1,0:T(8,128)}) custom-call(s32[16]{0:T(128)S(1)} %copy-done, f32[8,3,16,128]{3,2,1,0:T(8,128)S(1)} %all_to_all.5.gathered, f32[4,32,128]{2,1,0:T(8,128)S(1)} %get-tuple-element.52.e2_in, f32[4,32,128]{2,1,0:T(8,128)S(1)} %get-tuple-element.53.s2_in, f32[4,32,128]{2,1,0:T(8,128)S(1)} %get-tuple-element.54.fx2_in, ...), custom_call_target="tpu_custom_call" | custom-call | tf_op jit(solution)/shard_map/pallas_call | solution.py:836
Async XLA Ops:
  1.7 0.7 %copy-start = (s32[16]{0:T(128)S(1)}, s32[16]{0:T(128)}, u32[]{:S(2)}) copy-start(s32[16]{0:T(128)} %owner_of.3) | copy-start | bytes 196
  1.9 1.5 %collective-permute-start = (f32[224,128]{1,0:T(8,128)S(1)}, f32[224,128]{1,0:T(8,128)S(1)}, u32[]{:S(2)}, u32[]{:S(2)}) collective-permute-start(f32[224,128]{1,0:T(8,128)S(1)} %shard_map.60), channel_id=1, source_target_pairs={{0,1},{1,0},{2,3},{3,2},{4,5},{5,4},{6,7},{7,6},{8,9},{9,8},{10,11... | collective-permute-start | bytes 344072 | tf_op jit(solution)/shard_map/ppermute | solution.py:19
  3.8 0.7 %collective-permute-start.1 = (f32[384,128]{1,0:T(8,128)S(1)}, f32[384,128]{1,0:T(8,128)S(1)}, u32[]{:S(2)}, u32[]{:S(2)}) collective-permute-start(f32[384,128]{1,0:T(8,128)S(1)} %get-tuple-element.45.message), channel_id=1, source_target_pairs={{1,2},{2,1},{3,4},{4,3},{5,6},{6,5},{7,8},{8,7},{9,10},{10,9},{11,... | collective-permute-start | bytes 589832 | tf_op jit(solution)/shard_map/ppermute | solution.py:15
  5.0 10.0 %collective-permute-start.2 = (f32[9,32,128]{2,1,0:T(8,128)S(1)}, f32[9,32,128]{2,1,0:T(8,128)S(1)}, u32[]{:S(2)}, u32[]{:S(2)}) collective-permute-start(f32[9,32,128]{2,1,0:T(8,128)S(1)} %get-tuple-element.49.own), channel_id=1, source_target_pairs={{0,1},{1,0},{2,3},{3,2},{4,5},{5,4},{6,7},{7,6},{8,9},{9,8},{10,11... | collective-permute-start | bytes 442376 | tf_op jit(solution)/shard_map/ppermute | solution.py:19

commit v20 on v15

--- a/solution.py
+++ b/solution.py
@@ -636,6 +636,7 @@
         here, wrapped = copies[frame], shifted(copies, frame, 2, by)
         return joined(here[1:], wrapped[:1]) if by > 0 else joined(wrapped[-1:], here[:-1])
 
+    same = level.tiles == 1 and counts[2] == 2, counts[0] == 2, counts[1] == 2
     weights = {}
     for frame in frames:
         pairs = [
@@ -643,15 +644,19 @@
             (fy[frame], shifted(fy, frame, 0, -1)),
             (fz[frame], shifted(fz, frame, 1, -1)),
         ]
-        weights[frame] = [(up * inv[frame], low * inv[frame]) for up, low in pairs]
+        weights[frame] = [
+            ((up + low) * inv[frame], None) if merged else (up * inv[frame], low * inv[frame])
+            for (up, low), merged in zip(pairs, same)
+        ]
 
     def update(e):
         fresh = {}
         for frame in frames:
-            (x_up, x_low), (y_up, y_low), (z_up, z_low) = weights[frame]
-            total = x_up * along_x(e, frame, 1) + x_low * along_x(e, frame, -1)
-            total = total + (y_up * shifted(e, frame, 0, 1) + y_low * shifted(e, frame, 0, -1))
-            total = total + (z_up * shifted(e, frame, 1, 1) + z_low * shifted(e, frame, 1, -1))
+            moves = along_x, lambda c, f, by: shifted(c, f, 0, by), lambda c, f, by: shifted(c, f, 1, by)
+            total = 0.0
+            for (up, low), move in zip(weights[frame], moves):
+                part = up * move(e, frame, 1)
+                total = total + (part if low is None else part + low * move(e, frame, -1))
             fresh[frame] = start[frame] + total
         return fresh
 

time: 32.1 us -> 32 us (level)
  no operation moved by 1% of the time
where the time goes in v20:
time: 32 us; the launch traced here: 31.8 us
  blocking collectives  13.2 us (41%)
  starting transfers between devices  10.1 us (32%)
  Pallas kernels  4.91 us (15%)
  waiting for transfers between devices  1.77 us (6%)
  other arithmetic  1.06 us (3%)
  between operations  0.69 us (2%)
    all_to_all x1, blocking collectives, on_device(): lax.all_to_all(slots, 'gx', 0, 0, axis_index_groups=kinds, tiled=True)  13.2 us
    ppermute x2, starting transfers between devices, within_chip(): lax.ppermute(block, 'gx', [(i, i ^ 1) for i in range(lax.axis_size('gx'))])  9.46 us
    pallas_call x6, Pallas kernels, call(): pl.pallas_call(kernel, out_shape=tuple(outs), in_specs=[pl.BlockSpec(memo...  4.91 us
    ppermute x2, waiting for transfers between devices, within_chip(): lax.ppermute(block, 'gx', [(i, i ^ 1) for i in range(lax.axis_size('gx'))])  1.77 us
    add x1, other arithmetic, on_device(): sum((jnp.pad(block, ((k * layers, (2 - k) * layers), (0, 0), (0, 0))) for...  1.06 us
    ppermute x1, starting transfers between devices, between_chips(): lax.ppermute(block, 'gx', [(i, i + 1 if i % 2 else i - 1) for i in range(...  0.68 us
  transfers between devices with their start and end apart: 3, of which 2 were waited for; matrix products, arithmetic and copies ran while one was open for 0% of the time, Pallas kernels for 1%

profile of v20, /device:TPU:0, one launch (start us, length us, event | category | flops | bytes accessed | tf_op | source)
XLA Modules:
  0.0 31.8 jit_solution(14926440056440772756)
XLA Ops:
  0.6 1.1 %pad_add_fusion.inputs = f32[12,64,128]{2,1,0:T(8,128)S(1)} fusion(f32[4,64,128]{2,1,0:T(8,128)} %param.6, f32[4,64,128]{2,1,0:T(8,128)} %param.5, f32[4,64,128]{2,1,0:T(8,128)} %param.4), kind=kLoop, calls=%fused_computation | loop fusion | flops 196608 | bytes 786432 | tf_op jit(solution)/shard_map/add | solution.py:846
  1.7 0.0 copy-start
  1.7 0.2 shard_map.60
  1.9 0.5 %collective-permute-start = (f32[224,128]{1,0:T(8,128)S(1)}, f32[224,128]{1,0:T(8,128)S(1)}, u32[]{:S(2)}, u32[]{:S(2)}) collective-permute-start(f32[224,128]{1,0:T(8,128)S(1)} %shard_map.60), channel_id=1, source_target_pairs={{0,1},{1,0},{2,3},{3,2},{4,5},{5,4},{6,7},{7,6},{8,9},{9,8},{10,11... | collective-permute-start | bytes 344072 | tf_op jit(solution)/shard_map/ppermute | solution.py:19
  2.4 0.0 copy-done
  2.4 0.2 shard_map.59
  2.6 0.8 %collective-permute-done.within_in = f32[224,128]{1,0:T(8,128)S(1)} collective-permute-done((f32[224,128]{1,0:T(8,128)S(1)}, f32[224,128]{1,0:T(8,128)S(1)}, u32[]{:S(2)}, u32[]{:S(2)}) %collective-permute-start) | collective-permute-done | bytes 114720 | tf_op jit(solution)/shard_map/ppermute | solution.py:19
  3.4 0.4 %shard_map.61 = (f32[384,128]{1,0:T(8,128)S(1)}, f32[2,32,128]{2,1,0:T(8,128)S(1)}, f32[64,128]{1,0:T(8,128)S(1)}, f32[3,64,128]{2,1,0:T(8,128)S(1)}, f32[2,64,1...) custom-call(f32[12,64,128]{2,1,0:T(8,128)S(1)} %pad_add_fusion.input, ...), custom_call_target="tpu_custom_call" | custom-call | tf_op jit(solution)/shard_map/pallas_call | solution.py:831
  3.8 0.7 %collective-permute-start.1 = (f32[384,128]{1,0:T(8,128)S(1)}, f32[384,128]{1,0:T(8,128)S(1)}, u32[]{:S(2)}, u32[]{:S(2)}) collective-permute-start(f32[384,128]{1,0:T(8,128)S(1)} %get-tuple-element.45.message), channel_id=1, source_target_pairs={{1,2},{2,1},{3,4},{4,3},{5,6},{6,5},{7,8},{8,7},{9,10},{10,9},{11,... | collective-permute-start | bytes 589832 | tf_op jit(solution)/shard_map/ppermute | solution.py:15
  4.5 0.0 collective-permute-done.1.across_in
  4.5 0.5 %shard_map.62 = (f32[9,32,128]{2,1,0:T(8,128)S(1)}, f32[32,128]{1,0:T(8,128)S(1)}, f32[3,64,128]{2,1,0:T(8,128)S(1)}, f32[64,128]{1,0:T(8,128)S(1)}, f32[2,64,12...) custom-call(f32[12,64,128]{2,1,0:T(8,128)S(1)} %pad_add_fusion.input, ...), custom_call_target="tpu_custom_call" | custom-call | tf_op jit(solution)/shard_map/pallas_call | solution.py:831
  5.0 8.9 %collective-permute-start.2 = (f32[9,32,128]{2,1,0:T(8,128)S(1)}, f32[9,32,128]{2,1,0:T(8,128)S(1)}, u32[]{:S(2)}, u32[]{:S(2)}) collective-permute-start(f32[9,32,128]{2,1,0:T(8,128)S(1)} %get-tuple-element.49.own), channel_id=1, source_target_pairs={{0,1},{1,0},{2,3},{3,2},{4,5},{5,4},{6,7},{7,6},{8,9},{9,8},{10,11... | collective-permute-start | bytes 442376 | tf_op jit(solution)/shard_map/ppermute | solution.py:19
  13.9 1.0 %collective-permute-done.2.within_in = f32[9,32,128]{2,1,0:T(8,128)S(1)} collective-permute-done((f32[9,32,128]{2,1,0:T(8,128)S(1)}, f32[9,32,128]{2,1,0:T(8,128)S(1)}, u32[]{:S(2)}, u32[]{:S(2)}) %collective-permute-start.2) | collective-permute-done | bytes 147488 | tf_op jit(solution)/shard_map/ppermute | solution.py:19
  14.9 0.5 %shard_map.63 = (f32[8,3,16,128]{3,2,1,0:T(8,128)S(1)}, f32[4,32,128]{2,1,0:T(8,128)S(1)}, f32[4,32,128]{2,1,0:T(8,128)S(1)}, f32[4,32,128]{2,1,0:T(8,128)S(1)},...) custom-call(f32[9,32,128]{2,1,0:T(8,128)S(1)} %get-tuple-element.49., ...), custom_call_target="tpu_custom_call" | custom-call | tf_op jit(solution)/shard_map/pallas_call | solution.py:831
  15.5 13.2 %all_to_all.5.gathered = f32[8,3,16,128]{3,2,1,0:T(8,128)S(1)} all-to-all(f32[8,3,16,128]{3,2,1,0:T(8,128)S(1)} %get-tuple-element.51), channel_id=1, replica_groups={{15,12,11,8,7,4,3,0},{14,13,10,9,6,5,2,1},{31,28,27,24,23,20,19,16},{30..., dimensions={0} | all-to-all | bytes 393216 | tf_op jit(solution)/shard_map/all_to_all | solution.py:891
  28.7 3.1 %shard_map.64 = (f32[4,64,128]{2,1,0:T(8,128)}, f32[1,16,32]{2,1,0:T(8,128)}) custom-call(s32[16]{0:T(128)S(1)} %copy-done, f32[8,3,16,128]{3,2,1,0:T(8,128)S(1)} %all_to_all.5.gathered, f32[4,32,128]{2,1,0:T(8,128)S(1)} %get-tuple-element.52.e2_in, f32[4,32,128]{2,1,0:T(8,128)S(1)} %get-tuple-element.53.s2_in, f32[4,32,128]{2,1,0:T(8,128)S(1)} %get-tuple-element.54.fx2_in, ...), custom_call_target="tpu_custom_call" | custom-call | tf_op jit(solution)/shard_map/pallas_call | solution.py:831
Async XLA Ops:
  1.7 0.7 %copy-start = (s32[16]{0:T(128)S(1)}, s32[16]{0:T(128)}, u32[]{:S(2)}) copy-start(s32[16]{0:T(128)} %owner_of.3) | copy-start | bytes 196
  1.9 1.5 %collective-permute-start = (f32[224,128]{1,0:T(8,128)S(1)}, f32[224,128]{1,0:T(8,128)S(1)}, u32[]{:S(2)}, u32[]{:S(2)}) collective-permute-start(f32[224,128]{1,0:T(8,128)S(1)} %shard_map.60), channel_id=1, source_target_pairs={{0,1},{1,0},{2,3},{3,2},{4,5},{5,4},{6,7},{7,6},{8,9},{9,8},{10,11... | collective-permute-start | bytes 344072 | tf_op jit(solution)/shard_map/ppermute | solution.py:19
  3.8 0.7 %collective-permute-start.1 = (f32[384,128]{1,0:T(8,128)S(1)}, f32[384,128]{1,0:T(8,128)S(1)}, u32[]{:S(2)}, u32[]{:S(2)}) collective-permute-start(f32[384,128]{1,0:T(8,128)S(1)} %get-tuple-element.45.message), channel_id=1, source_target_pairs={{1,2},{2,1},{3,4},{4,3},{5,6},{6,5},{7,8},{8,7},{9,10},{10,9},{11,... | collective-permute-start | bytes 589832 | tf_op jit(solution)/shard_map/ppermute | solution.py:15
  5.0 10.0 %collective-permute-start.2 = (f32[9,32,128]{2,1,0:T(8,128)S(1)}, f32[9,32,128]{2,1,0:T(8,128)S(1)}, u32[]{:S(2)}, u32[]{:S(2)}) collective-permute-start(f32[9,32,128]{2,1,0:T(8,128)S(1)} %get-tuple-element.49.own), channel_id=1, source_target_pairs={{0,1},{1,0},{2,3},{3,2},{4,5},{5,4},{6,7},{7,6},{8,9},{9,8},{10,11... | collective-permute-start | bytes 442376 | tf_op jit(solution)/shard_map/ppermute | solution.py:19

commit v21 on v20

--- a/solution.py
+++ b/solution.py
@@ -887,7 +887,7 @@
         [vmem(6, padded2, depth), vmem(3, *tile)],
         (within, fx2, within_in),
     )
-    kinds = [[2 * chip + (chip + core) % 2 for chip in reversed(range(blocks // 2))] for core in range(2)]
+    kinds = [[2 * chip + (chip // 2 + core) % 2 for chip in reversed(range(blocks // 2))] for core in range(2)]
     gathered = lax.all_to_all(slots, "gx", 0, 0, axis_index_groups=kinds, tiled=True)
     solved, owned = call(
         coarse_kernel,

time: 32 us -> 31.7 us (level)
  no operation moved by 1% of the time
where the time goes in v21:
time: 31.7 us; the launch traced here: 31.5 us
  blocking collectives  13 us (41%)
  starting transfers between devices  10.1 us (32%)
  Pallas kernels  4.91 us (15%)
  waiting for transfers between devices  1.77 us (6%)
  other arithmetic  1.06 us (3%)
  between operations  0.69 us (2%)
    all_to_all x1, blocking collectives, on_device(): lax.all_to_all(slots, 'gx', 0, 0, axis_index_groups=kinds, tiled=True)  13 us
    ppermute x2, starting transfers between devices, within_chip(): lax.ppermute(block, 'gx', [(i, i ^ 1) for i in range(lax.axis_size('gx'))])  9.46 us
    pallas_call x6, Pallas kernels, call(): pl.pallas_call(kernel, out_shape=tuple(outs), in_specs=[pl.BlockSpec(memo...  4.91 us
    ppermute x2, waiting for transfers between devices, within_chip(): lax.ppermute(block, 'gx', [(i, i ^ 1) for i in range(lax.axis_size('gx'))])  1.77 us
    add x1, other arithmetic, on_device(): sum((jnp.pad(block, ((k * layers, (2 - k) * layers), (0, 0), (0, 0))) for...  1.06 us
    ppermute x1, starting transfers between devices, between_chips(): lax.ppermute(block, 'gx', [(i, i + 1 if i % 2 else i - 1) for i in range(...  0.68 us
  transfers between devices with their start and end apart: 3, of which 2 were waited for; matrix products, arithmetic and copies ran while one was open for 0% of the time, Pallas kernels for 1%

profile of v21, /device:TPU:0, one launch (start us, length us, event | category | flops | bytes accessed | tf_op | source)
XLA Modules:
  0.0 31.5 jit_solution(5369766029241982719)
XLA Ops:
  0.6 1.1 %pad_add_fusion.inputs = f32[12,64,128]{2,1,0:T(8,128)S(1)} fusion(f32[4,64,128]{2,1,0:T(8,128)} %param.6, f32[4,64,128]{2,1,0:T(8,128)} %param.5, f32[4,64,128]{2,1,0:T(8,128)} %param.4), kind=kLoop, calls=%fused_computation | loop fusion | flops 196608 | bytes 786432 | tf_op jit(solution)/shard_map/add | solution.py:846
  1.7 0.0 copy-start
  1.7 0.2 shard_map.60
  1.9 0.5 %collective-permute-start = (f32[224,128]{1,0:T(8,128)S(1)}, f32[224,128]{1,0:T(8,128)S(1)}, u32[]{:S(2)}, u32[]{:S(2)}) collective-permute-start(f32[224,128]{1,0:T(8,128)S(1)} %shard_map.60), channel_id=1, source_target_pairs={{0,1},{1,0},{2,3},{3,2},{4,5},{5,4},{6,7},{7,6},{8,9},{9,8},{10,11... | collective-permute-start | bytes 344072 | tf_op jit(solution)/shard_map/ppermute | solution.py:19
  2.4 0.0 copy-done
  2.4 0.2 shard_map.59
  2.6 0.8 %collective-permute-done.within_in = f32[224,128]{1,0:T(8,128)S(1)} collective-permute-done((f32[224,128]{1,0:T(8,128)S(1)}, f32[224,128]{1,0:T(8,128)S(1)}, u32[]{:S(2)}, u32[]{:S(2)}) %collective-permute-start) | collective-permute-done | bytes 114720 | tf_op jit(solution)/shard_map/ppermute | solution.py:19
  3.4 0.4 %shard_map.61 = (f32[384,128]{1,0:T(8,128)S(1)}, f32[2,32,128]{2,1,0:T(8,128)S(1)}, f32[64,128]{1,0:T(8,128)S(1)}, f32[3,64,128]{2,1,0:T(8,128)S(1)}, f32[2,64,1...) custom-call(f32[12,64,128]{2,1,0:T(8,128)S(1)} %pad_add_fusion.input, ...), custom_call_target="tpu_custom_call" | custom-call | tf_op jit(solution)/shard_map/pallas_call | solution.py:831
  3.8 0.7 %collective-permute-start.1 = (f32[384,128]{1,0:T(8,128)S(1)}, f32[384,128]{1,0:T(8,128)S(1)}, u32[]{:S(2)}, u32[]{:S(2)}) collective-permute-start(f32[384,128]{1,0:T(8,128)S(1)} %get-tuple-element.45.message), channel_id=1, source_target_pairs={{1,2},{2,1},{3,4},{4,3},{5,6},{6,5},{7,8},{8,7},{9,10},{10,9},{11,... | collective-permute-start | bytes 589832 | tf_op jit(solution)/shard_map/ppermute | solution.py:15
  4.5 0.0 collective-permute-done.1.across_in
  4.5 0.5 %shard_map.62 = (f32[9,32,128]{2,1,0:T(8,128)S(1)}, f32[32,128]{1,0:T(8,128)S(1)}, f32[3,64,128]{2,1,0:T(8,128)S(1)}, f32[64,128]{1,0:T(8,128)S(1)}, f32[2,64,12...) custom-call(f32[12,64,128]{2,1,0:T(8,128)S(1)} %pad_add_fusion.input, ...), custom_call_target="tpu_custom_call" | custom-call | tf_op jit(solution)/shard_map/pallas_call | solution.py:831
  5.0 8.9 %collective-permute-start.2 = (f32[9,32,128]{2,1,0:T(8,128)S(1)}, f32[9,32,128]{2,1,0:T(8,128)S(1)}, u32[]{:S(2)}, u32[]{:S(2)}) collective-permute-start(f32[9,32,128]{2,1,0:T(8,128)S(1)} %get-tuple-element.49.own), channel_id=1, source_target_pairs={{0,1},{1,0},{2,3},{3,2},{4,5},{5,4},{6,7},{7,6},{8,9},{9,8},{10,11... | collective-permute-start | bytes 442376 | tf_op jit(solution)/shard_map/ppermute | solution.py:19
  13.9 1.0 %collective-permute-done.2.within_in = f32[9,32,128]{2,1,0:T(8,128)S(1)} collective-permute-done((f32[9,32,128]{2,1,0:T(8,128)S(1)}, f32[9,32,128]{2,1,0:T(8,128)S(1)}, u32[]{:S(2)}, u32[]{:S(2)}) %collective-permute-start.2) | collective-permute-done | bytes 147488 | tf_op jit(solution)/shard_map/ppermute | solution.py:19
  14.9 0.5 %shard_map.63 = (f32[8,3,16,128]{3,2,1,0:T(8,128)S(1)}, f32[4,32,128]{2,1,0:T(8,128)S(1)}, f32[4,32,128]{2,1,0:T(8,128)S(1)}, f32[4,32,128]{2,1,0:T(8,128)S(1)},...) custom-call(f32[9,32,128]{2,1,0:T(8,128)S(1)} %get-tuple-element.49., ...), custom_call_target="tpu_custom_call" | custom-call | tf_op jit(solution)/shard_map/pallas_call | solution.py:831
  15.5 13.0 %all_to_all.5.gathered = f32[8,3,16,128]{3,2,1,0:T(8,128)S(1)} all-to-all(f32[8,3,16,128]{3,2,1,0:T(8,128)S(1)} %get-tuple-element.51), channel_id=1, replica_groups={{15,13,10,8,7,5,2,0},{14,12,11,9,6,4,3,1},{31,29,26,24,23,21,18,16},{30..., dimensions={0} | all-to-all | bytes 393216 | tf_op jit(solution)/shard_map/all_to_all | solution.py:891
  28.4 3.1 %shard_map.64 = (f32[4,64,128]{2,1,0:T(8,128)}, f32[1,16,32]{2,1,0:T(8,128)}) custom-call(s32[16]{0:T(128)S(1)} %copy-done, f32[8,3,16,128]{3,2,1,0:T(8,128)S(1)} %all_to_all.5.gathered, f32[4,32,128]{2,1,0:T(8,128)S(1)} %get-tuple-element.52.e2_in, f32[4,32,128]{2,1,0:T(8,128)S(1)} %get-tuple-element.53.s2_in, f32[4,32,128]{2,1,0:T(8,128)S(1)} %get-tuple-element.54.fx2_in, ...), custom_call_target="tpu_custom_call" | custom-call | tf_op jit(solution)/shard_map/pallas_call | solution.py:831
Async XLA Ops:
  1.7 0.7 %copy-start = (s32[16]{0:T(128)S(1)}, s32[16]{0:T(128)}, u32[]{:S(2)}) copy-start(s32[16]{0:T(128)} %owner_of.3) | copy-start | bytes 196
  1.9 1.5 %collective-permute-start = (f32[224,128]{1,0:T(8,128)S(1)}, f32[224,128]{1,0:T(8,128)S(1)}, u32[]{:S(2)}, u32[]{:S(2)}) collective-permute-start(f32[224,128]{1,0:T(8,128)S(1)} %shard_map.60), channel_id=1, source_target_pairs={{0,1},{1,0},{2,3},{3,2},{4,5},{5,4},{6,7},{7,6},{8,9},{9,8},{10,11... | collective-permute-start | bytes 344072 | tf_op jit(solution)/shard_map/ppermute | solution.py:19
  3.8 0.7 %collective-permute-start.1 = (f32[384,128]{1,0:T(8,128)S(1)}, f32[384,128]{1,0:T(8,128)S(1)}, u32[]{:S(2)}, u32[]{:S(2)}) collective-permute-start(f32[384,128]{1,0:T(8,128)S(1)} %get-tuple-element.45.message), channel_id=1, source_target_pairs={{1,2},{2,1},{3,4},{4,3},{5,6},{6,5},{7,8},{8,7},{9,10},{10,9},{11,... | collective-permute-start | bytes 589832 | tf_op jit(solution)/shard_map/ppermute | solution.py:15
  5.0 10.0 %collective-permute-start.2 = (f32[9,32,128]{2,1,0:T(8,128)S(1)}, f32[9,32,128]{2,1,0:T(8,128)S(1)}, u32[]{:S(2)}, u32[]{:S(2)}) collective-permute-start(f32[9,32,128]{2,1,0:T(8,128)S(1)} %get-tuple-element.49.own), channel_id=1, source_target_pairs={{0,1},{1,0},{2,3},{3,2},{4,5},{5,4},{6,7},{7,6},{8,9},{9,8},{10,11... | collective-permute-start | bytes 442376 | tf_op jit(solution)/shard_map/ppermute | solution.py:19

commit v22 on v21

--- a/solution.py
+++ b/solution.py
@@ -695,7 +695,7 @@
 
     slot = lanes_of((quarter, lanes)) & 3
     spread = blocks // 4
-    tiles = [gathered[chip, k] for chip in reversed(range(chips)) for k in range(2)]
+    tiles = [gathered[-chip % chips, k] for chip in range(chips) for k in range(2)]
     items = []
     for k in range(4):
         packs = []
@@ -731,7 +731,7 @@
         ref.at[pl.ds(core, 3)] for ref in (s2_in, fx2_in, fxl2_in, fy2_in, fz2_in, fzl2_in, inv2_in)
     ]
     next_chip = jnp.clip(position // 2 - 1 + 2 * core, 0, chips - 1)
-    into_both_rows(pair.at[5], gathered[chips - 1 - next_chip, 2])
+    into_both_rows(pair.at[5], gathered[(chips - next_chip) % chips, 2])
     halo = pair[5]
     before = (
         by_side(halo, e2_in[0])[0], by_side(jnp.where(first_of_two, halo, e2_in[0]), e2_in[1])[0],
@@ -887,7 +887,8 @@
         [vmem(6, padded2, depth), vmem(3, *tile)],
         (within, fx2, within_in),
     )
-    kinds = [[2 * chip + (chip // 2 + core) % 2 for chip in reversed(range(blocks // 2))] for core in range(2)]
+    downwards = [-place % (blocks // 2) for place in range(blocks // 2)]
+    kinds = [[2 * chip + (chip // 2 + core) % 2 for chip in downwards] for core in range(2)]
     gathered = lax.all_to_all(slots, "gx", 0, 0, axis_index_groups=kinds, tiled=True)
     solved, owned = call(
         coarse_kernel,

time: 31.7 us -> 32 us (level)
  no operation moved by 1% of the time
where the time goes in v22:
time: 32 us; the launch traced here: 31.8 us
  blocking collectives  13.2 us (41%)
  starting transfers between devices  10.1 us (32%)
  Pallas kernels  4.91 us (15%)
  waiting for transfers between devices  1.77 us (6%)
  other arithmetic  1.06 us (3%)
  between operations  0.69 us (2%)
    all_to_all x1, blocking collectives, on_device(): lax.all_to_all(slots, 'gx', 0, 0, axis_index_groups=kinds, tiled=True)  13.2 us
    ppermute x2, starting transfers between devices, within_chip(): lax.ppermute(block, 'gx', [(i, i ^ 1) for i in range(lax.axis_size('gx'))])  9.46 us
    pallas_call x6, Pallas kernels, call(): pl.pallas_call(kernel, out_shape=tuple(outs), in_specs=[pl.BlockSpec(memo...  4.91 us
    ppermute x2, waiting for transfers between devices, within_chip(): lax.ppermute(block, 'gx', [(i, i ^ 1) for i in range(lax.axis_size('gx'))])  1.77 us
    add x1, other arithmetic, on_device(): sum((jnp.pad(block, ((k * layers, (2 - k) * layers), (0, 0), (0, 0))) for...  1.06 us
    ppermute x1, starting transfers between devices, between_chips(): lax.ppermute(block, 'gx', [(i, i + 1 if i % 2 else i - 1) for i in range(...  0.68 us
  transfers between devices with their start and end apart: 3, of which 2 were waited for; matrix products, arithmetic and copies ran while one was open for 0% of the time, Pallas kernels for 1%

profile of v22, /device:TPU:0, one launch (start us, length us, event | category | flops | bytes accessed | tf_op | source)
XLA Modules:
  0.0 31.8 jit_solution(18095869967335490768)
XLA Ops:
  0.6 1.1 %pad_add_fusion.inputs = f32[12,64,128]{2,1,0:T(8,128)S(1)} fusion(f32[4,64,128]{2,1,0:T(8,128)} %param.6, f32[4,64,128]{2,1,0:T(8,128)} %param.5, f32[4,64,128]{2,1,0:T(8,128)} %param.4), kind=kLoop, calls=%fused_computation | loop fusion | flops 196608 | bytes 786432 | tf_op jit(solution)/shard_map/add | solution.py:846
  1.7 0.0 copy-start
  1.7 0.2 shard_map.60
  1.9 0.5 %collective-permute-start = (f32[224,128]{1,0:T(8,128)S(1)}, f32[224,128]{1,0:T(8,128)S(1)}, u32[]{:S(2)}, u32[]{:S(2)}) collective-permute-start(f32[224,128]{1,0:T(8,128)S(1)} %shard_map.60), channel_id=1, source_target_pairs={{0,1},{1,0},{2,3},{3,2},{4,5},{5,4},{6,7},{7,6},{8,9},{9,8},{10,11... | collective-permute-start | bytes 344072 | tf_op jit(solution)/shard_map/ppermute | solution.py:19
  2.4 0.0 copy-done
  2.4 0.2 shard_map.59
  2.6 0.8 %collective-permute-done.within_in = f32[224,128]{1,0:T(8,128)S(1)} collective-permute-done((f32[224,128]{1,0:T(8,128)S(1)}, f32[224,128]{1,0:T(8,128)S(1)}, u32[]{:S(2)}, u32[]{:S(2)}) %collective-permute-start) | collective-permute-done | bytes 114720 | tf_op jit(solution)/shard_map/ppermute | solution.py:19
  3.4 0.4 %shard_map.61 = (f32[384,128]{1,0:T(8,128)S(1)}, f32[2,32,128]{2,1,0:T(8,128)S(1)}, f32[64,128]{1,0:T(8,128)S(1)}, f32[3,64,128]{2,1,0:T(8,128)S(1)}, f32[2,64,1...) custom-call(f32[12,64,128]{2,1,0:T(8,128)S(1)} %pad_add_fusion.input, ...), custom_call_target="tpu_custom_call" | custom-call | tf_op jit(solution)/shard_map/pallas_call | solution.py:831
  3.8 0.7 %collective-permute-start.1 = (f32[384,128]{1,0:T(8,128)S(1)}, f32[384,128]{1,0:T(8,128)S(1)}, u32[]{:S(2)}, u32[]{:S(2)}) collective-permute-start(f32[384,128]{1,0:T(8,128)S(1)} %get-tuple-element.45.message), channel_id=1, source_target_pairs={{1,2},{2,1},{3,4},{4,3},{5,6},{6,5},{7,8},{8,7},{9,10},{10,9},{11,... | collective-permute-start | bytes 589832 | tf_op jit(solution)/shard_map/ppermute | solution.py:15
  4.5 0.0 collective-permute-done.1.across_in
  4.5 0.5 %shard_map.62 = (f32[9,32,128]{2,1,0:T(8,128)S(1)}, f32[32,128]{1,0:T(8,128)S(1)}, f32[3,64,128]{2,1,0:T(8,128)S(1)}, f32[64,128]{1,0:T(8,128)S(1)}, f32[2,64,12...) custom-call(f32[12,64,128]{2,1,0:T(8,128)S(1)} %pad_add_fusion.input, ...), custom_call_target="tpu_custom_call" | custom-call | tf_op jit(solution)/shard_map/pallas_call | solution.py:831
  5.0 8.9 %collective-permute-start.2 = (f32[9,32,128]{2,1,0:T(8,128)S(1)}, f32[9,32,128]{2,1,0:T(8,128)S(1)}, u32[]{:S(2)}, u32[]{:S(2)}) collective-permute-start(f32[9,32,128]{2,1,0:T(8,128)S(1)} %get-tuple-element.49.own), channel_id=1, source_target_pairs={{0,1},{1,0},{2,3},{3,2},{4,5},{5,4},{6,7},{7,6},{8,9},{9,8},{10,11... | collective-permute-start | bytes 442376 | tf_op jit(solution)/shard_map/ppermute | solution.py:19
  13.9 1.0 %collective-permute-done.2.within_in = f32[9,32,128]{2,1,0:T(8,128)S(1)} collective-permute-done((f32[9,32,128]{2,1,0:T(8,128)S(1)}, f32[9,32,128]{2,1,0:T(8,128)S(1)}, u32[]{:S(2)}, u32[]{:S(2)}) %collective-permute-start.2) | collective-permute-done | bytes 147488 | tf_op jit(solution)/shard_map/ppermute | solution.py:19
  14.9 0.5 %shard_map.63 = (f32[8,3,16,128]{3,2,1,0:T(8,128)S(1)}, f32[4,32,128]{2,1,0:T(8,128)S(1)}, f32[4,32,128]{2,1,0:T(8,128)S(1)}, f32[4,32,128]{2,1,0:T(8,128)S(1)},...) custom-call(f32[9,32,128]{2,1,0:T(8,128)S(1)} %get-tuple-element.49., ...), custom_call_target="tpu_custom_call" | custom-call | tf_op jit(solution)/shard_map/pallas_call | solution.py:831
  15.5 13.2 %all_to_all.5.gathered = f32[8,3,16,128]{3,2,1,0:T(8,128)S(1)} all-to-all(f32[8,3,16,128]{3,2,1,0:T(8,128)S(1)} %get-tuple-element.51), channel_id=1, replica_groups={{0,15,13,10,8,7,5,2},{1,14,12,11,9,6,4,3},{16,31,29,26,24,23,21,18},{17..., dimensions={0} | all-to-all | bytes 393216 | tf_op jit(solution)/shard_map/all_to_all | solution.py:892
  28.7 3.1 %shard_map.64 = (f32[4,64,128]{2,1,0:T(8,128)}, f32[1,16,32]{2,1,0:T(8,128)}) custom-call(s32[16]{0:T(128)S(1)} %copy-done, f32[8,3,16,128]{3,2,1,0:T(8,128)S(1)} %all_to_all.5.gathered, f32[4,32,128]{2,1,0:T(8,128)S(1)} %get-tuple-element.52.e2_in, f32[4,32,128]{2,1,0:T(8,128)S(1)} %get-tuple-element.53.s2_in, f32[4,32,128]{2,1,0:T(8,128)S(1)} %get-tuple-element.54.fx2_in, ...), custom_call_target="tpu_custom_call" | custom-call | tf_op jit(solution)/shard_map/pallas_call | solution.py:831
Async XLA Ops:
  1.7 0.7 %copy-start = (s32[16]{0:T(128)S(1)}, s32[16]{0:T(128)}, u32[]{:S(2)}) copy-start(s32[16]{0:T(128)} %owner_of.3) | copy-start | bytes 196
  1.9 1.5 %collective-permute-start = (f32[224,128]{1,0:T(8,128)S(1)}, f32[224,128]{1,0:T(8,128)S(1)}, u32[]{:S(2)}, u32[]{:S(2)}) collective-permute-start(f32[224,128]{1,0:T(8,128)S(1)} %shard_map.60), channel_id=1, source_target_pairs={{0,1},{1,0},{2,3},{3,2},{4,5},{5,4},{6,7},{7,6},{8,9},{9,8},{10,11... | collective-permute-start | bytes 344072 | tf_op jit(solution)/shard_map/ppermute | solution.py:19
  3.8 0.7 %collective-permute-start.1 = (f32[384,128]{1,0:T(8,128)S(1)}, f32[384,128]{1,0:T(8,128)S(1)}, u32[]{:S(2)}, u32[]{:S(2)}) collective-permute-start(f32[384,128]{1,0:T(8,128)S(1)} %get-tuple-element.45.message), channel_id=1, source_target_pairs={{1,2},{2,1},{3,4},{4,3},{5,6},{6,5},{7,8},{8,7},{9,10},{10,9},{11,... | collective-permute-start | bytes 589832 | tf_op jit(solution)/shard_map/ppermute | solution.py:15
  5.0 10.0 %collective-permute-start.2 = (f32[9,32,128]{2,1,0:T(8,128)S(1)}, f32[9,32,128]{2,1,0:T(8,128)S(1)}, u32[]{:S(2)}, u32[]{:S(2)}) collective-permute-start(f32[9,32,128]{2,1,0:T(8,128)S(1)} %get-tuple-element.49.own), channel_id=1, source_target_pairs={{0,1},{1,0},{2,3},{3,2},{4,5},{5,4},{6,7},{7,6},{8,9},{9,8},{10,11... | collective-permute-start | bytes 442376 | tf_op jit(solution)/shard_map/ppermute | solution.py:19

commit v23 on v21

--- a/solution.py
+++ b/solution.py
@@ -714,12 +714,12 @@
 
     fetch.wait()
     owner = owner_here[position]
-    wide, narrow = lanes_of((lanes, lanes)), rows_of((lanes, lanes))
-    take = jnp.where(narrow == 4 * wide + owner // spread, 1.0, 0.0)
-    block = jnp.dot(
-        e3[owner % spread], take, precision=lax.Precision.HIGHEST, preferred_element_type=jnp.float32
-    )
-    owned[0] = block[:, : lanes // 4]
+    shape = lanes // 4, lanes
+    take = jnp.where(lanes_of(shape) == 4 * rows_of(shape) + owner // spread, 1.0, 0.0)
+    owned[0] = lax.dot_general(
+        e3[owner % spread], take, (((1,), (1,)), ((), ())),
+        precision=lax.Precision.HIGHEST, preferred_element_type=jnp.float32,
+    )
     copies = [pltpu.make_async_copy(owned, owned_out, sems.at[0])]
     copies[0].start()
 

time: 31.7 us -> 31.7 us (level)
  no operation moved by 1% of the time
where the time goes in v23:
time: 31.7 us; the launch traced here: 31.5 us
  blocking collectives  13 us (41%)
  starting transfers between devices  10.1 us (32%)
  Pallas kernels  4.91 us (15%)
  waiting for transfers between devices  1.77 us (6%)
  other arithmetic  1.06 us (3%)
  between operations  0.69 us (2%)
    all_to_all x1, blocking collectives, on_device(): lax.all_to_all(slots, 'gx', 0, 0, axis_index_groups=kinds, tiled=True)  13 us
    ppermute x2, starting transfers between devices, within_chip(): lax.ppermute(block, 'gx', [(i, i ^ 1) for i in range(lax.axis_size('gx'))])  9.46 us
    pallas_call x6, Pallas kernels, call(): pl.pallas_call(kernel, out_shape=tuple(outs), in_specs=[pl.BlockSpec(memo...  4.91 us
    ppermute x2, waiting for transfers between devices, within_chip(): lax.ppermute(block, 'gx', [(i, i ^ 1) for i in range(lax.axis_size('gx'))])  1.77 us
    add x1, other arithmetic, on_device(): sum((jnp.pad(block, ((k * layers, (2 - k) * layers), (0, 0), (0, 0))) for...  1.06 us
    ppermute x1, starting transfers between devices, between_chips(): lax.ppermute(block, 'gx', [(i, i + 1 if i % 2 else i - 1) for i in range(...  0.68 us
  transfers between devices with their start and end apart: 3, of which 2 were waited for; matrix products, arithmetic and copies ran while one was open for 0% of the time, Pallas kernels for 1%

profile of v23, /device:TPU:0, one launch (start us, length us, event | category | flops | bytes accessed | tf_op | source)
XLA Modules:
  0.0 31.5 jit_solution(6781929493298378047)
XLA Ops:
  0.6 1.1 %pad_add_fusion.inputs = f32[12,64,128]{2,1,0:T(8,128)S(1)} fusion(f32[4,64,128]{2,1,0:T(8,128)} %param.6, f32[4,64,128]{2,1,0:T(8,128)} %param.5, f32[4,64,128]{2,1,0:T(8,128)} %param.4), kind=kLoop, calls=%fused_computation | loop fusion | flops 196608 | bytes 786432 | tf_op jit(solution)/shard_map/add | solution.py:846
  1.7 0.0 copy-start
  1.7 0.2 shard_map.60
  1.9 0.5 %collective-permute-start = (f32[224,128]{1,0:T(8,128)S(1)}, f32[224,128]{1,0:T(8,128)S(1)}, u32[]{:S(2)}, u32[]{:S(2)}) collective-permute-start(f32[224,128]{1,0:T(8,128)S(1)} %shard_map.60), channel_id=1, source_target_pairs={{0,1},{1,0},{2,3},{3,2},{4,5},{5,4},{6,7},{7,6},{8,9},{9,8},{10,11... | collective-permute-start | bytes 344072 | tf_op jit(solution)/shard_map/ppermute | solution.py:19
  2.4 0.0 copy-done
  2.4 0.2 shard_map.59
  2.6 0.8 %collective-permute-done.within_in = f32[224,128]{1,0:T(8,128)S(1)} collective-permute-done((f32[224,128]{1,0:T(8,128)S(1)}, f32[224,128]{1,0:T(8,128)S(1)}, u32[]{:S(2)}, u32[]{:S(2)}) %collective-permute-start) | collective-permute-done | bytes 114720 | tf_op jit(solution)/shard_map/ppermute | solution.py:19
  3.4 0.4 %shard_map.61 = (f32[384,128]{1,0:T(8,128)S(1)}, f32[2,32,128]{2,1,0:T(8,128)S(1)}, f32[64,128]{1,0:T(8,128)S(1)}, f32[3,64,128]{2,1,0:T(8,128)S(1)}, f32[2,64,1...) custom-call(f32[12,64,128]{2,1,0:T(8,128)S(1)} %pad_add_fusion.input, ...), custom_call_target="tpu_custom_call" | custom-call | tf_op jit(solution)/shard_map/pallas_call | solution.py:831
  3.8 0.7 %collective-permute-start.1 = (f32[384,128]{1,0:T(8,128)S(1)}, f32[384,128]{1,0:T(8,128)S(1)}, u32[]{:S(2)}, u32[]{:S(2)}) collective-permute-start(f32[384,128]{1,0:T(8,128)S(1)} %get-tuple-element.45.message), channel_id=1, source_target_pairs={{1,2},{2,1},{3,4},{4,3},{5,6},{6,5},{7,8},{8,7},{9,10},{10,9},{11,... | collective-permute-start | bytes 589832 | tf_op jit(solution)/shard_map/ppermute | solution.py:15
  4.5 0.0 collective-permute-done.1.across_in
  4.5 0.5 %shard_map.62 = (f32[9,32,128]{2,1,0:T(8,128)S(1)}, f32[32,128]{1,0:T(8,128)S(1)}, f32[3,64,128]{2,1,0:T(8,128)S(1)}, f32[64,128]{1,0:T(8,128)S(1)}, f32[2,64,12...) custom-call(f32[12,64,128]{2,1,0:T(8,128)S(1)} %pad_add_fusion.input, ...), custom_call_target="tpu_custom_call" | custom-call | tf_op jit(solution)/shard_map/pallas_call | solution.py:831
  5.0 8.9 %collective-permute-start.2 = (f32[9,32,128]{2,1,0:T(8,128)S(1)}, f32[9,32,128]{2,1,0:T(8,128)S(1)}, u32[]{:S(2)}, u32[]{:S(2)}) collective-permute-start(f32[9,32,128]{2,1,0:T(8,128)S(1)} %get-tuple-element.49.own), channel_id=1, source_target_pairs={{0,1},{1,0},{2,3},{3,2},{4,5},{5,4},{6,7},{7,6},{8,9},{9,8},{10,11... | collective-permute-start | bytes 442376 | tf_op jit(solution)/shard_map/ppermute | solution.py:19
  13.9 1.0 %collective-permute-done.2.within_in = f32[9,32,128]{2,1,0:T(8,128)S(1)} collective-permute-done((f32[9,32,128]{2,1,0:T(8,128)S(1)}, f32[9,32,128]{2,1,0:T(8,128)S(1)}, u32[]{:S(2)}, u32[]{:S(2)}) %collective-permute-start.2) | collective-permute-done | bytes 147488 | tf_op jit(solution)/shard_map/ppermute | solution.py:19
  14.9 0.5 %shard_map.63 = (f32[8,3,16,128]{3,2,1,0:T(8,128)S(1)}, f32[4,32,128]{2,1,0:T(8,128)S(1)}, f32[4,32,128]{2,1,0:T(8,128)S(1)}, f32[4,32,128]{2,1,0:T(8,128)S(1)},...) custom-call(f32[9,32,128]{2,1,0:T(8,128)S(1)} %get-tuple-element.49., ...), custom_call_target="tpu_custom_call" | custom-call | tf_op jit(solution)/shard_map/pallas_call | solution.py:831
  15.5 13.0 %all_to_all.5.gathered = f32[8,3,16,128]{3,2,1,0:T(8,128)S(1)} all-to-all(f32[8,3,16,128]{3,2,1,0:T(8,128)S(1)} %get-tuple-element.51), channel_id=1, replica_groups={{15,13,10,8,7,5,2,0},{14,12,11,9,6,4,3,1},{31,29,26,24,23,21,18,16},{30..., dimensions={0} | all-to-all | bytes 393216 | tf_op jit(solution)/shard_map/all_to_all | solution.py:891
  28.4 3.1 %shard_map.64 = (f32[4,64,128]{2,1,0:T(8,128)}, f32[1,16,32]{2,1,0:T(8,128)}) custom-call(s32[16]{0:T(128)S(1)} %copy-done, f32[8,3,16,128]{3,2,1,0:T(8,128)S(1)} %all_to_all.5.gathered, f32[4,32,128]{2,1,0:T(8,128)S(1)} %get-tuple-element.52.e2_in, f32[4,32,128]{2,1,0:T(8,128)S(1)} %get-tuple-element.53.s2_in, f32[4,32,128]{2,1,0:T(8,128)S(1)} %get-tuple-element.54.fx2_in, ...), custom_call_target="tpu_custom_call" | custom-call | tf_op jit(solution)/shard_map/pallas_call | solution.py:831
Async XLA Ops:
  1.7 0.7 %copy-start = (s32[16]{0:T(128)S(1)}, s32[16]{0:T(128)}, u32[]{:S(2)}) copy-start(s32[16]{0:T(128)} %owner_of.3) | copy-start | bytes 196
  1.9 1.5 %collective-permute-start = (f32[224,128]{1,0:T(8,128)S(1)}, f32[224,128]{1,0:T(8,128)S(1)}, u32[]{:S(2)}, u32[]{:S(2)}) collective-permute-start(f32[224,128]{1,0:T(8,128)S(1)} %shard_map.60), channel_id=1, source_target_pairs={{0,1},{1,0},{2,3},{3,2},{4,5},{5,4},{6,7},{7,6},{8,9},{9,8},{10,11... | collective-permute-start | bytes 344072 | tf_op jit(solution)/shard_map/ppermute | solution.py:19
  3.8 0.7 %collective-permute-start.1 = (f32[384,128]{1,0:T(8,128)S(1)}, f32[384,128]{1,0:T(8,128)S(1)}, u32[]{:S(2)}, u32[]{:S(2)}) collective-permute-start(f32[384,128]{1,0:T(8,128)S(1)} %get-tuple-element.45.message), channel_id=1, source_target_pairs={{1,2},{2,1},{3,4},{4,3},{5,6},{6,5},{7,8},{8,7},{9,10},{10,9},{11,... | collective-permute-start | bytes 589832 | tf_op jit(solution)/shard_map/ppermute | solution.py:15
  5.0 10.0 %collective-permute-start.2 = (f32[9,32,128]{2,1,0:T(8,128)S(1)}, f32[9,32,128]{2,1,0:T(8,128)S(1)}, u32[]{:S(2)}, u32[]{:S(2)}) collective-permute-start(f32[9,32,128]{2,1,0:T(8,128)S(1)} %get-tuple-element.49.own), channel_id=1, source_target_pairs={{0,1},{1,0},{2,3},{3,2},{4,5},{5,4},{6,7},{7,6},{8,9},{9,8},{10,11... | collective-permute-start | bytes 442376 | tf_op jit(solution)/shard_map/ppermute | solution.py:19

commit v24 on v23

--- a/solution.py
+++ b/solution.py
@@ -712,17 +712,6 @@
         lambda inner, faces: small_cycle(512.0, inner, faces, 1, 8, third.coarse_slot_step(), 2)
     )
 
-    fetch.wait()
-    owner = owner_here[position]
-    shape = lanes // 4, lanes
-    take = jnp.where(lanes_of(shape) == 4 * rows_of(shape) + owner // spread, 1.0, 0.0)
-    owned[0] = lax.dot_general(
-        e3[owner % spread], take, (((1,), (1,)), ((), ())),
-        precision=lax.Precision.HIGHEST, preferred_element_type=jnp.float32,
-    )
-    copies = [pltpu.make_async_copy(owned, owned_out, sems.at[0])]
-    copies[0].start()
-
     first_of_two, even2 = parities2(half, lanes)
     body2 = pl.ds(PAD, half)
     edge = jnp.zeros((PAD, lanes), jnp.float32)
@@ -754,6 +743,17 @@
         e2[j + 1, body2] = fresh[j]
     fixes2 = [jnp.where(even2, even, odd) for even, odd in zip(fresh, update2())]
 
+    fetch.wait()
+    owner = owner_here[position]
+    shape = lanes // 4, lanes
+    take = jnp.where(lanes_of(shape) == 4 * rows_of(shape) + owner // spread, 1.0, 0.0)
+    owned[0] = lax.dot_general(
+        e3[owner % spread], take, (((1,), (1,)), ((), ())),
+        precision=lax.Precision.HIGHEST, preferred_element_type=jnp.float32,
+    )
+    copies = [pltpu.make_async_copy(owned, owned_out, sems.at[0])]
+    copies[0].start()
+
     _, source, _ = three_parts(inputs)
     layers = source.shape[0]
     plane = Plane(height, lanes)

time: 31.7 us -> 32.1 us (1.013)
  Pallas kernels: 4.91 us -> 5.32 us
    pallas_call x6, Pallas kernels: 4.91 us -> 5.32 us  [call(): pl.pallas_call(kernel, out_shape=tuple(outs), in_specs=[pl.BlockSpec(memo...]
where the time goes in v24:
time: 32.1 us; the launch traced here: 31.9 us
  blocking collectives  13 us (40%)
  starting transfers between devices  10.1 us (31%)
  Pallas kernels  5.32 us (17%)
  waiting for transfers between devices  1.77 us (6%)
  other arithmetic  1.06 us (3%)
  between operations  0.69 us (2%)
    all_to_all x1, blocking collectives, on_device(): lax.all_to_all(slots, 'gx', 0, 0, axis_index_groups=kinds, tiled=True)  13 us
    ppermute x2, starting transfers between devices, within_chip(): lax.ppermute(block, 'gx', [(i, i ^ 1) for i in range(lax.axis_size('gx'))])  9.46 us
    pallas_call x6, Pallas kernels, call(): pl.pallas_call(kernel, out_shape=tuple(outs), in_specs=[pl.BlockSpec(memo...  5.32 us
    ppermute x2, waiting for transfers between devices, within_chip(): lax.ppermute(block, 'gx', [(i, i ^ 1) for i in range(lax.axis_size('gx'))])  1.77 us
    add x1, other arithmetic, on_device(): sum((jnp.pad(block, ((k * layers, (2 - k) * layers), (0, 0), (0, 0))) for...  1.06 us
    ppermute x1, starting transfers between devices, between_chips(): lax.ppermute(block, 'gx', [(i, i + 1 if i % 2 else i - 1) for i in range(...  0.68 us
  transfers between devices with their start and end apart: 3, of which 2 were waited for; matrix products, arithmetic and copies ran while one was open for 0% of the time, Pallas kernels for 1%

profile of v24, /device:TPU:0, one launch (start us, length us, event | category | flops | bytes accessed | tf_op | source)
XLA Modules:
  0.0 31.9 jit_solution(11910929780720416641)
XLA Ops:
  0.6 1.1 %pad_add_fusion.inputs = f32[12,64,128]{2,1,0:T(8,128)S(1)} fusion(f32[4,64,128]{2,1,0:T(8,128)} %param.6, f32[4,64,128]{2,1,0:T(8,128)} %param.5, f32[4,64,128]{2,1,0:T(8,128)} %param.4), kind=kLoop, calls=%fused_computation | loop fusion | flops 196608 | bytes 786432 | tf_op jit(solution)/shard_map/add | solution.py:846
  1.7 0.0 copy-start
  1.7 0.2 shard_map.60
  1.9 0.5 %collective-permute-start = (f32[224,128]{1,0:T(8,128)S(1)}, f32[224,128]{1,0:T(8,128)S(1)}, u32[]{:S(2)}, u32[]{:S(2)}) collective-permute-start(f32[224,128]{1,0:T(8,128)S(1)} %shard_map.60), channel_id=1, source_target_pairs={{0,1},{1,0},{2,3},{3,2},{4,5},{5,4},{6,7},{7,6},{8,9},{9,8},{10,11... | collective-permute-start | bytes 344072 | tf_op jit(solution)/shard_map/ppermute | solution.py:19
  2.4 0.0 copy-done
  2.4 0.2 shard_map.59
  2.6 0.8 %collective-permute-done.within_in = f32[224,128]{1,0:T(8,128)S(1)} collective-permute-done((f32[224,128]{1,0:T(8,128)S(1)}, f32[224,128]{1,0:T(8,128)S(1)}, u32[]{:S(2)}, u32[]{:S(2)}) %collective-permute-start) | collective-permute-done | bytes 114720 | tf_op jit(solution)/shard_map/ppermute | solution.py:19
  3.4 0.4 %shard_map.61 = (f32[384,128]{1,0:T(8,128)S(1)}, f32[2,32,128]{2,1,0:T(8,128)S(1)}, f32[64,128]{1,0:T(8,128)S(1)}, f32[3,64,128]{2,1,0:T(8,128)S(1)}, f32[2,64,1...) custom-call(f32[12,64,128]{2,1,0:T(8,128)S(1)} %pad_add_fusion.input, ...), custom_call_target="tpu_custom_call" | custom-call | tf_op jit(solution)/shard_map/pallas_call | solution.py:831
  3.8 0.7 %collective-permute-start.1 = (f32[384,128]{1,0:T(8,128)S(1)}, f32[384,128]{1,0:T(8,128)S(1)}, u32[]{:S(2)}, u32[]{:S(2)}) collective-permute-start(f32[384,128]{1,0:T(8,128)S(1)} %get-tuple-element.45.message), channel_id=1, source_target_pairs={{1,2},{2,1},{3,4},{4,3},{5,6},{6,5},{7,8},{8,7},{9,10},{10,9},{11,... | collective-permute-start | bytes 589832 | tf_op jit(solution)/shard_map/ppermute | solution.py:15
  4.5 0.0 collective-permute-done.1.across_in
  4.5 0.5 %shard_map.62 = (f32[9,32,128]{2,1,0:T(8,128)S(1)}, f32[32,128]{1,0:T(8,128)S(1)}, f32[3,64,128]{2,1,0:T(8,128)S(1)}, f32[64,128]{1,0:T(8,128)S(1)}, f32[2,64,12...) custom-call(f32[12,64,128]{2,1,0:T(8,128)S(1)} %pad_add_fusion.input, ...), custom_call_target="tpu_custom_call" | custom-call | tf_op jit(solution)/shard_map/pallas_call | solution.py:831
  5.0 8.9 %collective-permute-start.2 = (f32[9,32,128]{2,1,0:T(8,128)S(1)}, f32[9,32,128]{2,1,0:T(8,128)S(1)}, u32[]{:S(2)}, u32[]{:S(2)}) collective-permute-start(f32[9,32,128]{2,1,0:T(8,128)S(1)} %get-tuple-element.49.own), channel_id=1, source_target_pairs={{0,1},{1,0},{2,3},{3,2},{4,5},{5,4},{6,7},{7,6},{8,9},{9,8},{10,11... | collective-permute-start | bytes 442376 | tf_op jit(solution)/shard_map/ppermute | solution.py:19
  13.9 1.0 %collective-permute-done.2.within_in = f32[9,32,128]{2,1,0:T(8,128)S(1)} collective-permute-done((f32[9,32,128]{2,1,0:T(8,128)S(1)}, f32[9,32,128]{2,1,0:T(8,128)S(1)}, u32[]{:S(2)}, u32[]{:S(2)}) %collective-permute-start.2) | collective-permute-done | bytes 147488 | tf_op jit(solution)/shard_map/ppermute | solution.py:19
  14.9 0.5 %shard_map.63 = (f32[8,3,16,128]{3,2,1,0:T(8,128)S(1)}, f32[4,32,128]{2,1,0:T(8,128)S(1)}, f32[4,32,128]{2,1,0:T(8,128)S(1)}, f32[4,32,128]{2,1,0:T(8,128)S(1)},...) custom-call(f32[9,32,128]{2,1,0:T(8,128)S(1)} %get-tuple-element.49., ...), custom_call_target="tpu_custom_call" | custom-call | tf_op jit(solution)/shard_map/pallas_call | solution.py:831
  15.5 13.0 %all_to_all.5.gathered = f32[8,3,16,128]{3,2,1,0:T(8,128)S(1)} all-to-all(f32[8,3,16,128]{3,2,1,0:T(8,128)S(1)} %get-tuple-element.51), channel_id=1, replica_groups={{15,13,10,8,7,5,2,0},{14,12,11,9,6,4,3,1},{31,29,26,24,23,21,18,16},{30..., dimensions={0} | all-to-all | bytes 393216 | tf_op jit(solution)/shard_map/all_to_all | solution.py:891
  28.4 3.5 %shard_map.64 = (f32[4,64,128]{2,1,0:T(8,128)}, f32[1,16,32]{2,1,0:T(8,128)}) custom-call(s32[16]{0:T(128)S(1)} %copy-done, f32[8,3,16,128]{3,2,1,0:T(8,128)S(1)} %all_to_all.5.gathered, f32[4,32,128]{2,1,0:T(8,128)S(1)} %get-tuple-element.52.e2_in, f32[4,32,128]{2,1,0:T(8,128)S(1)} %get-tuple-element.53.s2_in, f32[4,32,128]{2,1,0:T(8,128)S(1)} %get-tuple-element.54.fx2_in, ...), custom_call_target="tpu_custom_call" | custom-call | tf_op jit(solution)/shard_map/pallas_call | solution.py:831
Async XLA Ops:
  1.7 0.7 %copy-start = (s32[16]{0:T(128)S(1)}, s32[16]{0:T(128)}, u32[]{:S(2)}) copy-start(s32[16]{0:T(128)} %owner_of.3) | copy-start | bytes 196
  1.9 1.5 %collective-permute-start = (f32[224,128]{1,0:T(8,128)S(1)}, f32[224,128]{1,0:T(8,128)S(1)}, u32[]{:S(2)}, u32[]{:S(2)}) collective-permute-start(f32[224,128]{1,0:T(8,128)S(1)} %shard_map.60), channel_id=1, source_target_pairs={{0,1},{1,0},{2,3},{3,2},{4,5},{5,4},{6,7},{7,6},{8,9},{9,8},{10,11... | collective-permute-start | bytes 344072 | tf_op jit(solution)/shard_map/ppermute | solution.py:19
  3.8 0.7 %collective-permute-start.1 = (f32[384,128]{1,0:T(8,128)S(1)}, f32[384,128]{1,0:T(8,128)S(1)}, u32[]{:S(2)}, u32[]{:S(2)}) collective-permute-start(f32[384,128]{1,0:T(8,128)S(1)} %get-tuple-element.45.message), channel_id=1, source_target_pairs={{1,2},{2,1},{3,4},{4,3},{5,6},{6,5},{7,8},{8,7},{9,10},{10,9},{11,... | collective-permute-start | bytes 589832 | tf_op jit(solution)/shard_map/ppermute | solution.py:15
  5.0 10.0 %collective-permute-start.2 = (f32[9,32,128]{2,1,0:T(8,128)S(1)}, f32[9,32,128]{2,1,0:T(8,128)S(1)}, u32[]{:S(2)}, u32[]{:S(2)}) collective-permute-start(f32[9,32,128]{2,1,0:T(8,128)S(1)} %get-tuple-element.49.own), channel_id=1, source_target_pairs={{0,1},{1,0},{2,3},{3,2},{4,5},{5,4},{6,7},{7,6},{8,9},{9,8},{10,11... | collective-permute-start | bytes 442376 | tf_op jit(solution)/shard_map/ppermute | solution.py:19
